TPU v7x, 32 devices: a whole 2x2x4 slice. The times are simulated.
32 devices in a mesh: ctx: 8 (over y, x, core), head: 4 (over z).
Axes of the slice: x: 2, y: 2, z: 4, core: 2. Of those that a mesh axis runs over, the one named last changes fastest.
Arguments:
- query: bfloat16 [8192, 4096], P('ctx', 'head'), may hold values from -150 to 150
- keys: bfloat16 [8192, 4096], P('ctx', 'head'), may hold values from -5.5 to 5.5, as said below
- values: bfloat16 [8192, 4096], P('ctx', 'head'), may hold values from -6 to 6
- lr_code: int32 [8192, 8], P('ctx', 'head'), may hold values from 2048 to 26623, as said below
- fast_weights: bfloat16 [8, 3, 512, 512], P('head'), may hold values from -0.25 to 0.25
- out_weight: bfloat16 [4096, 4096], P('head'), may hold values from -0.09375 to 0.09375
Outputs:
- layer_out: bfloat16 [8192, 4096], P('ctx', 'head')
- new_weights: bfloat16 [8, 3, 512, 512], P('head')
Inputs may be any that keep to these rules, and one draw needn't show every extreme that they name: `keys`: keys of order one. `lr_code`: Fixed-point learning-rate codes in units of 2**-14.
All inputs are finite; a program needn't handle non-finite values.
Results may differ from a plain program's by a relative error of at most 0.025.
Values may be sent and summed in bfloat16 or wider, within the bound.
No kernel may reach another device: no remote copies, remote signals or barrier semaphores. Data moves between devices by JAX's collectives and lax.ppermute only.
A program may use at most 192 MiB of HBM per device.

v0:
```python
import math

import jax
import jax.numpy as jnp
from jax import lax
from jax.sharding import PartitionSpec as P

FW = 512
HEAD_DIM = 128
WINDOW = 256


base_rate = 0.05


def from_behind(block, axis, distance):
    devices = range(lax.axis_size(axis))
    route = [(i - distance, i) for i in devices if i - distance in devices]
    return lax.ppermute(block, axis, route)


def attention(query, keys, values, rim_keys, rim_values, ctx_index):
    tok_rows, feat_width = query.shape
    head_count = feat_width // HEAD_DIM
    block_rows = min(512, tok_rows)
    q_all = query.reshape(tok_rows, head_count, HEAD_DIM)
    key_all = jnp.concatenate([rim_keys, keys], 0).reshape(tok_rows + WINDOW, head_count, HEAD_DIM)
    val_all = jnp.concatenate([rim_values, values], 0).reshape(
        tok_rows + WINDOW, head_count, HEAD_DIM
    )
    score_scale = 1.0 / math.sqrt(HEAD_DIM)
    shard_start = ctx_index * tok_rows

    def one_block(blk_index):
        row_start = blk_index * block_rows
        q_block = lax.dynamic_slice_in_dim(q_all, row_start, block_rows, 0)
        k_block = lax.dynamic_slice_in_dim(key_all, row_start, block_rows + WINDOW, 0)
        v_block = lax.dynamic_slice_in_dim(val_all, row_start, block_rows + WINDOW, 0)
        scores = (
            jnp.einsum("qhd,khd->hqk", q_block, k_block, preferred_element_type=jnp.float32)
            * score_scale
        )
        q_pos = shard_start + row_start + jnp.arange(block_rows, dtype=jnp.int32)[:, None]
        k_pos = (
            shard_start
            + row_start
            - WINDOW
            + jnp.arange(block_rows + WINDOW, dtype=jnp.int32)[None, :]
        )
        live = (k_pos <= q_pos) & (k_pos > q_pos - WINDOW) & (k_pos >= 0)
        scores = jnp.where(live[None], scores, jnp.float32(-1e30))
        top_score = jnp.max(scores, axis=-1, keepdims=True)
        exps = jnp.exp(scores - top_score)
        probs = (exps / jnp.sum(exps, axis=-1, keepdims=True)).astype(jnp.bfloat16)
        head_out = jnp.einsum("hqk,khd->qhd", probs, v_block, preferred_element_type=jnp.float32)
        return head_out.reshape(block_rows, feat_width)

    blocks_out = lax.map(one_block, jnp.arange(tok_rows // block_rows, dtype=jnp.int32))
    return blocks_out.reshape(tok_rows, feat_width)


def contract_rows(left, right):
    return lax.dot_general(
        left, right, (((0,), (0,)), ((), ())), preferred_element_type=jnp.float32
    )


def train_head(keys_h, values_h, rate_h, weights):
    gate_in = jnp.dot(keys_h, weights[0], preferred_element_type=jnp.float32)
    up_in = jnp.dot(keys_h, weights[1], preferred_element_type=jnp.float32)
    sigmoid_val = jax.nn.sigmoid(gate_in)
    gated_act = (gate_in * sigmoid_val * up_in).astype(jnp.bfloat16)
    pushed = (rate_h[:, None] * values_h.astype(jnp.float32)).astype(jnp.bfloat16)
    back_grad = lax.dot_general(
        pushed, weights[2], (((1,), (1,)), ((), ())), preferred_element_type=jnp.float32
    )
    d_gate = (back_grad * up_in * sigmoid_val * (1.0 + gate_in * (1.0 - sigmoid_val))).astype(
        jnp.bfloat16
    )
    d_up = (back_grad * gate_in * sigmoid_val).astype(jnp.bfloat16)
    return jnp.stack(
        [
            contract_rows(keys_h, d_gate),
            contract_rows(keys_h, d_up),
            contract_rows(gated_act, pushed),
        ]
    )


def renorm(start_w, grad_pull, step_size):
    base_w = start_w.astype(jnp.float32)
    updated = base_w + step_size[:, None, None, None] * grad_pull
    old_norm = jnp.sqrt(jnp.sum(base_w * base_w, axis=2, keepdims=True) + 1e-06)
    new_norm = jnp.sqrt(jnp.sum(updated * updated, axis=2, keepdims=True) + 1e-06)
    return (updated * (old_norm / new_norm)).astype(jnp.bfloat16)


def apply_head(query_h, weights):
    gate_in = jnp.dot(query_h, weights[0], preferred_element_type=jnp.float32)
    up_in = jnp.dot(query_h, weights[1], preferred_element_type=jnp.float32)
    gated_q = (gate_in * jax.nn.sigmoid(gate_in) * up_in).astype(jnp.bfloat16)
    head_out = jnp.dot(gated_q, weights[2], preferred_element_type=jnp.float32)
    return head_out * lax.rsqrt(jnp.mean(head_out * head_out, axis=-1, keepdims=True) + 1e-06)


def shards(query, keys, values, lr_code, fast_weights, out_weight):
    tok_rows = query.shape[0]
    contexts = lax.axis_size("ctx")
    ctx_index = lax.axis_index("ctx")
    tokens_all = tok_rows * contexts
    local_heads = fast_weights.shape[0]
    rim_keys, rim_values = from_behind(
        (keys[tok_rows - WINDOW :], values[tok_rows - WINDOW :]), "ctx", 1
    )
    rate = lr_code.astype(jnp.float32) * 2.0 ** (-14)
    rate_sum = lax.psum(jnp.sum(rate, axis=0), "ctx")
    step_size = base_rate / (math.sqrt(tokens_all) * (rate_sum / tokens_all))
    grad_pull = jnp.stack(
        [
            train_head(
                keys[:, head_idx * FW : (head_idx + 1) * FW],
                values[:, head_idx * FW : (head_idx + 1) * FW],
                rate[:, head_idx],
                fast_weights[head_idx],
            )
            for head_idx in range(local_heads)
        ]
    )
    attended = attention(query, keys, values, rim_keys, rim_values, ctx_index)
    pull_whole = lax.psum(grad_pull.astype(jnp.bfloat16), "ctx").astype(jnp.float32)
    new_weights = renorm(fast_weights, pull_whole, step_size)
    fast_out = jnp.concatenate(
        [
            apply_head(query[:, head_idx * FW : (head_idx + 1) * FW], new_weights[head_idx])
            for head_idx in range(local_heads)
        ],
        1,
    )
    merged = (attended + fast_out).astype(jnp.bfloat16)
    partial_out = jnp.dot(merged, out_weight, preferred_element_type=jnp.float32)
    layer_out = lax.psum_scatter(
        partial_out.astype(jnp.bfloat16), "head", scatter_dimension=1, tiled=True
    )
    return (layer_out, new_weights)


def solution(mesh):
    placed = (
        P("ctx", "head"),
        P("ctx", "head"),
        P("ctx", "head"),
        P("ctx", "head"),
        P("head", None, None, None),
        P("head", None),
    )
    return jax.shard_map(
        shards,
        mesh=mesh,
        in_specs=placed,
        out_specs=(P("ctx", "head"), P("head", None, None, None)),
        check_vma=False,
    )
```

profile of v0, /device:TPU:0, one launch (start us, length us, event | category | flops | bytes accessed | tf_op | source)
XLA Modules:
  0.0 408.9 jit_solution(6006026811588735507)
XLA Ops:
  7.2 0.0 all-reduce.2.cloned.1.call-start
  7.2 1.9 slice.94
  9.1 3.3 collective-permute-start
  12.4 3.9 copy.18
  16.3 2.0 slice.116
  18.3 4.5 %collective-permute-start.1 = (bf16[256,1024]{0,1:T(8,128)(2,1)}, bf16[256,1024]{0,1:T(8,128)(2,1)}, u32[]{:S(2)}, u32[]{:S(2)}) collective-permute-start(bf16[256,1024]{0,1:T(8,128)(2,1)} %slice.116), channel_id=1, source_target_pairs={{0,4},{4,8},{8,12},{12,16},{16,20},{20,24},{24,28},{1,5},{5,9},{9,... | collective-permute-start | bytes 1572872 | tf_op jit(solution)/shard_map/ppermute | solution.py:19
  22.9 1.8 fusion.53
  24.7 0.0 copy-start.14
  24.7 0.0 copy-start.10
  24.7 0.7 fusion.51
  25.4 0.1 fusion.78
  25.5 0.7 copy-done.10
  26.3 0.8 fusion.61
  27.0 1.2 fusion.29
  28.2 0.8 fusion.28
  29.1 1.4 fusion.27
  30.5 0.7 fusion.47
  31.2 0.7 fusion.45
  31.9 0.8 fusion.57
  32.7 1.2 fusion.32
  33.9 0.8 fusion.31
  34.7 1.4 fusion.30
  36.1 0.3 maximum_bitcast_fusion
  36.4 1.9 pad_maximum_fusion
  38.4 0.0 all-reduce.2.cloned.1.call-update
  38.4 0.0 reduce-scatter.2.cloned.1.call-start
  38.5 12.5 %psum.14 = f32[2]{0:T(128)S(1)} all-reduce(f32[2]{0:T(128)S(1)} %get-tuple-element.143), channel_id=1, replica_groups=mesh['ctx'=8,'head'=4] {'ctx'}, use_global_device_ids=true, to_apply=%region_5.6 | all-reduce | flops 2 | bytes 16 | tf_op jit(solution)/shard_map/psum | solution.py:116
  50.9 2.8 copy.23
  53.7 4.1 %copy.17 = bf16[1024,1024]{0,1:T(8,128)(2,1)} copy(bf16[1024,1024]{1,0:T(8,128)(2,1)} %param.8) | data formatting | bytes 4194304 | tf_op args[0]
  57.9 2.8 pad_maximum_fusion.1
  60.7 4.6 %copy.16 = bf16[1280,1024]{0,1:T(8,128)(2,1)} copy(bf16[1280,1024]{1,0:T(8,128)(2,1)} %pad_maximum_fusion.1) | data formatting | bytes 5242880 | tf_op jit(solution)/shard_map/concatenate | solution.py:28
  65.2 2.7 pad_maximum_fusion.2
  67.9 144.4 %while.13 = (s32[]{:T(128)}, f32[2,512,1024]{1,0,2:T(2,128)}, s32[2]{0:T(128)S(1)}, bf16[1280,8,128]{0,2,1:T(8,128)(2,1)}, s32[]{:T(128)}, /*index=5*/bf16[1024,...) while((s32[]{:T(128)}, f32[2,512,1024]{1,0,2:T(2,128)}, ...), condition=%wide.region_3.4_spmd, body=%wide.region_0.3_spmd.sunk | while | flops 1637355520 | bytes 76332832 | solution.py:58
  67.9 0.7 dynamic_slice.42
  69.3 8.2 %fusion.95 = f32[8,512,768]{2,1,0:T(8,128)} fusion(bf16[1280,8,128]{0,2,1:T(8,128)(2,1)} %get-tuple-element.236, s32[]{:T(128)S(6)} %select_n.37, bf16[1024,8,128]{0,2,1:T(8,128)(2,1)} %get-tuple-element.235, s32[]{:T(128)S(6)} %select_n.38), kind=kOutput, calls=%fused_computation.9.clone.1 | convolution fusion | flops 805306368 | bytes 15204360 | tf_op jit(solution)/shard_map/while/body/eval_jaxpr/qhd,khd->hqk/dot_general | solution.py:40
  77.5 0.4 and_and_fusion.2
  77.9 16.3 %fusion.96 = (f32[8,512]{1,0:T(8,128)S(1)}, f32[8,512,768]{2,1,0:T(8,128)}) fusion(f32[8,512,768]{2,1,0:T(8,128)} %fusion.95, pred[512,768]{1,0:T(8,128)(4,1)S(1)} %and_and_fusion.2), kind=kOutput, calls=%fused_computation.132.clone.1 | output fusion | flops 18875136 | bytes 25575424 | tf_op jit(solution)/shard_map/while/body/eval_jaxpr/sub | solution.py:53
  94.2 6.1 %fusion.97 = f32[8,128,512]{2,1,0:T(8,128)S(1)} fusion(f32[8,512,768]{2,1,0:T(8,128)} %get-tuple-element.202, f32[8,512]{1,0:T(8,128)S(1)} %get-tuple-element.203, bf16[1280,8,128]{0,2,1:T(8,128)(2,1)S(1)} %copy-done.12, s32[]{:T(128)S(6)} %select_n.37), kind=kOutput, calls=%fused_computation.7.clone.1 | convolution fusion | flops 811597824 | bytes 16269316 | tf_op jit(solution)/shard_map/while/body/eval_jaxpr/hqk,khd->qhd/dot_general | solution.py:55
  100.3 2.2 copy.44
  102.5 37.8 %dynamic_update_slice.9 = f32[2,512,1024]{1,0,2:T(2,128)} dynamic-update-slice(f32[2,512,1024]{1,0,2:T(2,128)} %get-tuple-element.218, f32[1,512,1024]{1,0,2:T(1,128)S(1)} %copy.44, s32[]{:T(128)S(6)} %copy.48, s32[]{:T(128)} %constant.91.clone.1..sunk, s32[]{:T(128)} %constant.91.clone.1..sunk) | dynamic-update-slice | bytes 4194308 | tf_op jit(solution)/shard_map/while/body/jit(dynamic_update_index_in_dim)/dynamic_update_slice | solution.py:58
  140.3 0.7 dynamic_slice.42
  141.6 8.1 %fusion.95 = f32[8,512,768]{2,1,0:T(8,128)} fusion(bf16[1280,8,128]{0,2,1:T(8,128)(2,1)} %get-tuple-element.236, s32[]{:T(128)S(6)} %select_n.37, bf16[1024,8,128]{0,2,1:T(8,128)(2,1)} %get-tuple-element.235, s32[]{:T(128)S(6)} %select_n.38), kind=kOutput, calls=%fused_computation.9.clone.1 | convolution fusion | flops 805306368 | bytes 15204360 | tf_op jit(solution)/shard_map/while/body/eval_jaxpr/qhd,khd->hqk/dot_general | solution.py:40
  149.8 0.4 and_and_fusion.2
  150.2 16.2 %fusion.96 = (f32[8,512]{1,0:T(8,128)S(1)}, f32[8,512,768]{2,1,0:T(8,128)}) fusion(f32[8,512,768]{2,1,0:T(8,128)} %fusion.95, pred[512,768]{1,0:T(8,128)(4,1)S(1)} %and_and_fusion.2), kind=kOutput, calls=%fused_computation.132.clone.1 | output fusion | flops 18875136 | bytes 25575424 | tf_op jit(solution)/shard_map/while/body/eval_jaxpr/sub | solution.py:53
  166.5 5.9 %fusion.97 = f32[8,128,512]{2,1,0:T(8,128)S(1)} fusion(f32[8,512,768]{2,1,0:T(8,128)} %get-tuple-element.202, f32[8,512]{1,0:T(8,128)S(1)} %get-tuple-element.203, bf16[1280,8,128]{0,2,1:T(8,128)(2,1)S(1)} %copy-done.12, s32[]{:T(128)S(6)} %select_n.37), kind=kOutput, calls=%fused_computation.7.clone.1 | convolution fusion | flops 811597824 | bytes 16269316 | tf_op jit(solution)/shard_map/while/body/eval_jaxpr/hqk,khd->qhd/dot_general | solution.py:55
  172.4 2.2 copy.44
  174.6 37.8 %dynamic_update_slice.9 = f32[2,512,1024]{1,0,2:T(2,128)} dynamic-update-slice(f32[2,512,1024]{1,0,2:T(2,128)} %get-tuple-element.218, f32[1,512,1024]{1,0,2:T(1,128)S(1)} %copy.44, s32[]{:T(128)S(6)} %copy.48, s32[]{:T(128)} %constant.91.clone.1..sunk, s32[]{:T(128)} %constant.91.clone.1..sunk) | dynamic-update-slice | bytes 4194308 | tf_op jit(solution)/shard_map/while/body/jit(dynamic_update_index_in_dim)/dynamic_update_slice | solution.py:58
  212.4 5.3 %copy.42 = f32[128,8,2,512]{3,1,2,0:T(8,128)} copy(f32[128,8,2,512]{3,2,1,0:T(2,128)} %bitcast.140) | data formatting | bytes 8388608
  217.7 3.8 fusion.14
  221.5 0.0 copy-start.8
  221.5 1.3 multiply_convert_fusion
  222.8 0.2 copy-done.8
  223.1 2.4 fusion.37
  225.4 2.1 fusion.41
  227.5 5.1 %multiply_reduce_fusion.1 = (f32[1024]{0:T(1024)S(1)}, f32[1024,512]{0,1:T(8,128)}) fusion(bf16[2,3,512,512]{2,3,1,0:T(8,128)(2,1)} %copy-done.2, f32[512,1024]{0,1:T(8,128)} %fusion.37, bf16[1024,1024]{1,0:T(8,128)(2,1)} %param.8), kind=kOutput, calls=%fused_computation.47 | convolution fusion | flops 1077935104 | bytes 6295552 | tf_op jit(solution)/shard_map/dot_general | solution.py:102
  232.6 4.7 %multiply_reduce_fusion.2 = (f32[1024]{0:T(1024)S(1)}, f32[1024,512]{0,1:T(8,128)}) fusion(bf16[2,3,512,512]{2,3,1,0:T(8,128)(2,1)S(1)} %copy-done.3, f32[512,1024]{0,1:T(8,128)} %fusion.41, bf16[1024,1024]{1,0:T(8,128)(2,1)} %param.8), kind=kOutput, calls=%fused_computation.48 | convolution fusion | flops 1077935104 | bytes 6295552 | tf_op jit(solution)/shard_map/dot_general | solution.py:102
  237.3 2.0 broadcast_multiply_fusion
  239.3 0.3 copy-done.13
  239.6 0.3 broadcast_multiply_fusion.1
  239.9 1.8 copy-done.9
  241.8 15.0 %convolution_convert_fusion = bf16[1024,4096]{1,0:T(8,128)(2,1)} fusion(bf16[1024,4096]{1,0:T(8,128)(2,1)} %param.13, f32[1024,1024]{0,1:T(8,128)S(1)} %bitcast.139, f32[1024,512]{0,1:T(8,128)S(1)} %broadcast_multiply_fusion, f32[1024,512]{0,1:T(8,128)S(1)} %broadcast_multiply_fusion.1), kind=kOutput, calls=%fused_computation.24 | convolution fusion | flops 8597274624 | bytes 25165824 | tf_op jit(solution)/shard_map/dot_general | solution.py:140
  256.8 0.0 reduce-scatter.2.cloned.1.call-update
  256.8 2.8 copy.28
  259.6 142.5 %reduce-scatter.2.cloned.1.call-done = bf16[1024,1024]{1,0:T(8,128)(2,1)} async-done(((bf16[1024,4096]{1,0:T(8,128)(2,1)}), bf16[1024,1024]{1,0:T(8,128)(2,1)}) %reduce-scatter.2.cloned.1.call-update) | async-done | bytes 2097168 | tf_op jit(solution)/shard_map/reduce_scatter | solution.py:141
  (41 shorter events, 0.1 us)
Async XLA Ops:
  7.2 210.5 %all-reduce.2.cloned.1.call-start = ((), (), s32[]{:S(2)}) async-start(), calls=%async_computation.1 | async-start | bytes 6291456 | tf_op jit(solution)/shard_map/psum | solution.py:130
  9.1 13.8 %copy-start.1 = (bf16[1024,1024]{1,0:T(8,128)(2,1)S(1)}, bf16[1024,1024]{1,0:T(8,128)(2,1)}, u32[]{:S(2)}) copy-start(bf16[1024,1024]{1,0:T(8,128)(2,1)} %param.9) | copy-start | bytes 6291460
  9.1 48.8 %collective-permute-start = (bf16[256,1024]{1,0:T(8,128)(2,1)}, bf16[256,1024]{1,0:T(8,128)(2,1)}, u32[]{:S(2)}, u32[]{:S(2)}) collective-permute-start(bf16[256,1024]{1,0:T(8,128)(2,1)} %slice.94), channel_id=1, source_target_pairs={{0,4},{4,8},{8,12},{12,16},{16,20},{20,24},{24,28},{1,5},{5,9},{9,... | collective-permute-start | bytes 1572872 | tf_op jit(solution)/shard_map/ppermute | solution.py:19
  16.3 8.4 %copy-start.6 = (bf16[2,3,512,512]{3,2,1,0:T(8,128)(2,1)S(1)}, bf16[2,3,512,512]{3,2,1,0:T(8,128)(2,1)}, u32[]{:S(2)}) copy-start(bf16[2,3,512,512]{3,2,1,0:T(8,128)(2,1)} %param.12) | copy-start | bytes 9437188
  18.3 46.9 %collective-permute-start.1 = (bf16[256,1024]{0,1:T(8,128)(2,1)}, bf16[256,1024]{0,1:T(8,128)(2,1)}, u32[]{:S(2)}, u32[]{:S(2)}) collective-permute-start(bf16[256,1024]{0,1:T(8,128)(2,1)} %slice.116), channel_id=1, source_target_pairs={{0,4},{4,8},{8,12},{12,16},{16,20},{20,24},{24,28},{1,5},{5,9},{9,... | collective-permute-start | bytes 1572872 | tf_op jit(solution)/shard_map/ppermute | solution.py:19
  24.7 0.7 copy-start.14
  24.7 1.6 copy-start.10
  38.4 12.5 %copy-start.7 = (bf16[2,3,512,512]{3,2,1,0:T(8,128)(2,1)S(1)}, bf16[2,3,512,512]{3,2,1,0:T(8,128)(2,1)}, u32[]{:S(2)}) copy-start(bf16[2,3,512,512]{3,2,1,0:T(8,128)(2,1)} %param.12) | copy-start | bytes 9437188
  38.4 363.6 %reduce-scatter.2.cloned.1.call-start = ((), (), s32[]{:S(2)}) async-start(), calls=%async_computation.2 | async-start | bytes 10485760 | tf_op jit(solution)/shard_map/reduce_scatter | solution.py:141
  53.7 4.1 %copy-start.11 = (bf16[1024,1024]{1,0:T(8,128)(2,1)S(1)}, bf16[1024,1024]{1,0:T(8,128)(2,1)}, u32[]{:S(2)}) copy-start(bf16[1024,1024]{1,0:T(8,128)(2,1)} %param.10) | copy-start | bytes 6291460
  60.6 4.6 %copy-start.5 = (bf16[1024,1024]{0,1:T(8,128)(2,1)S(1)}, bf16[1024,1024]{0,1:T(8,128)(2,1)}, u32[]{:S(2)}) copy-start(bf16[1024,1024]{0,1:T(8,128)(2,1)} %copy.18) | copy-start | bytes 6291460
  77.9 16.3 %copy-start.12 = (bf16[1280,8,128]{0,2,1:T(8,128)(2,1)S(1)}, bf16[1280,8,128]{0,2,1:T(8,128)(2,1)}, u32[]{:S(2)}) copy-start(bf16[1280,8,128]{0,2,1:T(8,128)(2,1)} %get-tuple-element.233) | copy-start | bytes 7864324 | tf_op jit(solution)/shard_map/while
  150.2 16.3 %copy-start.12 = (bf16[1280,8,128]{0,2,1:T(8,128)(2,1)S(1)}, bf16[1280,8,128]{0,2,1:T(8,128)(2,1)}, u32[]{:S(2)}) copy-start(bf16[1280,8,128]{0,2,1:T(8,128)(2,1)} %get-tuple-element.233) | copy-start | bytes 7864324 | tf_op jit(solution)/shard_map/while
  212.4 5.3 %copy-start = (bf16[2,3,512,512]{2,3,1,0:T(8,128)(2,1)S(1)}, bf16[2,3,512,512]{2,3,1,0:T(8,128)(2,1)}, u32[]{:S(2)}) copy-start(bf16[2,3,512,512]{2,3,1,0:T(8,128)(2,1)} %copy.23) | copy-start | bytes 9437188
  217.7 3.8 copy-start.4
  221.5 1.6 copy-start.8
  223.1 2.4 copy-start.2
  227.5 5.1 %copy-start.3 = (bf16[2,3,512,512]{2,3,1,0:T(8,128)(2,1)S(1)}, bf16[2,3,512,512]{2,3,1,0:T(8,128)(2,1)}, u32[]{:S(2)}) copy-start(bf16[2,3,512,512]{2,3,1,0:T(8,128)(2,1)} %copy-done.2) | copy-start | bytes 9437188
  237.3 2.2 copy-start.13
  239.6 2.2 copy-start.9
Sparse Core Ops, SparseCore 0:
  38.5 69.0 all-reduce.1
  256.9 145.0 reduce-scatter.1
where the time goes:
time: 415 us; the launch traced here: 409 us
  waiting for transfers between devices  143 us (34%)
  local copies, waits for them, and re-layouts  112 us (27%)
  matrix products  69.7 us (17%)
  other arithmetic  48.8 us (12%)
  between operations  14.2 us (3%)
  blocking collectives  12.5 us (3%)
  starting transfers between devices  7.9 us (2%)
    reduce_scatter x1, waiting for transfers between devices, shards(): lax.psum_scatter(partial_out.astype(jnp.bfloat16), 'head', scatter_dimens...  142 us
    dynamic_update_slice x4, local copies, waits for them, and re-layouts, attention(): lax.map(one_block, jnp.arange(tok_rows // block_rows, dtype=jnp.int32))  80 us
    sub x2, other arithmetic, one_block(): exps = jnp.exp(scores - top_score)  32.5 us
    unnamed x33, local copies, waits for them, and re-layouts  22 us
    dot_general x2, matrix products, one_block(): jnp.einsum('qhd,khd->hqk', q_block, k_block, preferred_element_type=jnp.f...  16.3 us
    dot_general x1, matrix products, shards(): jnp.dot(merged, out_weight, preferred_element_type=jnp.float32)  15 us
    psum x1, blocking collectives, shards(): rate_sum = lax.psum(jnp.sum(rate, axis=0), 'ctx')  12.5 us
    dot_general x2, matrix products, one_block(): jnp.einsum('hqk,khd->qhd', probs, v_block, preferred_element_type=jnp.flo...  12 us
  transfers between devices with their start and end apart: 4, of which 1 were waited for; matrix products, arithmetic and copies ran while one was open for 46% of the time, Pallas kernels for 0%

commit v1 on v0

v1 whole, which is shorter than its diff:
```python
import functools
import math

import jax
import jax.numpy as jnp
from jax import lax
from jax.experimental import pallas as pl
from jax.experimental.pallas import tpu as pltpu
from jax.sharding import PartitionSpec as P

FW = 512
HEAD_DIM = 128
WINDOW = 256
LANES = 128
BLOCKS = 3 * FW // LANES
HALF = BLOCKS // 2
THIRD = BLOCKS // 4
VMEM = 56 * 2**20

base_rate = 0.05
BF = jnp.bfloat16
F32 = jnp.float32


def mm(a, b):
    return jnp.dot(a, b, preferred_element_type=F32)


def shift(block, axis, distance):
    n = lax.axis_size(axis)
    return lax.ppermute(block, axis, [(i, i + distance) for i in range(n) if 0 <= i + distance < n])


def rotate(block, axis, distance):
    n = lax.axis_size(axis)
    return lax.ppermute(block, axis, [(i, (i + distance) % n) for i in range(n)])


def swap(block, bit):
    n = lax.axis_size("ctx")
    return lax.ppermute(block, "ctx", [(i, i ^ bit) for i in range(n)])


def sigmoid(x):
    return 1.0 / (1.0 + jnp.exp(-x))


def grads_kernel(bit_ref, rate_ref, k_ref, v_ref, w_ref, keep_ref, send_ref, dgu, gated, pushed):
    rows = k_ref.shape[0]
    tile = min(256, rows)
    w0, w1, w2 = w_ref[0, 0], w_ref[0, 1], w_ref[0, 2]
    w2t = w2.T
    for t in range(rows // tile):
        sl = pl.ds(t * tile, tile)
        k = k_ref[sl, :]
        gate = mm(k, w0)
        up = mm(k, w1)
        s = sigmoid(gate)
        rate = jnp.broadcast_to(rate_ref[0, :, sl], (LANES, tile)).T
        rate = jnp.concatenate([rate] * (FW // LANES), axis=1)
        push = (rate * v_ref[sl, :].astype(F32)).astype(BF)
        pushed[sl, :] = push
        back = mm(push, w2t)
        gs = gate * s
        gated[sl, :] = (gs * up).astype(BF)
        dgu[sl, :FW] = (back * up * s * (1.0 + gate * (1.0 - s))).astype(BF)
        dgu[sl, FW:] = (back * gs).astype(BF)
    bit = bit_ref[0]
    kt = k_ref[...].T
    gt = gated[...].T
    wide = 2 * LANES
    for b in range(BLOCKS // 2):
        if b * wide < 2 * FW:
            r = mm(kt, dgu[:, b * wide : (b + 1) * wide])
        else:
            r = mm(gt, pushed[:, b * wide - 2 * FW : (b + 1) * wide - 2 * FW])
        r = r.astype(BF)
        half, pos = (2 * b) // HALF, (2 * b) % HALF

        @pl.when(bit == half)
        def _():
            keep_ref[0, pos] = r[:, :LANES]
            keep_ref[0, pos + 1] = r[:, LANES:]

        @pl.when(bit != half)
        def _():
            send_ref[0, pos] = r[:, :LANES]
            send_ref[0, pos + 1] = r[:, LANES:]


def grads(bit, rate, keys, values, fast_weights):
    heads = fast_weights.shape[0]
    rows = keys.shape[0]
    out = jax.ShapeDtypeStruct((heads, HALF, FW, LANES), BF)
    col = pl.BlockSpec((rows, FW), lambda h: (0, h))
    blk = pl.BlockSpec((1, HALF, FW, LANES), lambda h: (h, 0, 0, 0))
    return pl.pallas_call(
        grads_kernel,
        grid=(heads,),
        in_specs=[
            pl.BlockSpec(memory_space=pltpu.SMEM),
            pl.BlockSpec((1, 1, rows), lambda h: (h, 0, 0)),
            col,
            col,
            pl.BlockSpec((1, 3, FW, FW), lambda h: (h, 0, 0, 0)),
        ],
        out_specs=[blk, blk],
        out_shape=[out, out],
        scratch_shapes=[
            pltpu.VMEM((rows, 2 * FW), BF),
            pltpu.VMEM((rows, FW), BF),
            pltpu.VMEM((rows, FW), BF),
        ],
        compiler_params=pltpu.CompilerParams(vmem_limit_bytes=VMEM),
        cost_estimate=pl.CostEstimate(
            flops=heads * 12 * rows * FW * FW,
            bytes_accessed=heads * (2 * rows * FW * 2 + 12 * FW * FW),
            transcendentals=heads * rows * FW,
        ),
    )(bit, rate, keys, values, fast_weights)


def attn_kernel(first_ref, q_ref, k_ref, v_ref, rk_ref, rv_ref, o_ref):
    rows = q_ref.shape[0]
    w = WINDOW
    row = lax.broadcasted_iota(jnp.int32, (w, w), 0)
    col = lax.broadcasted_iota(jnp.int32, (w, w), 1)
    own = col <= row
    scale = 1.0 / math.sqrt(HEAD_DIM)
    has_prev = first_ref[0] == 0
    nt = (((1,), (1,)), ((), ()))
    for b in range(rows // w):
        sl = pl.ds(b * w, w)
        q = q_ref[sl, :]
        if b == 0:
            kp, vp = rk_ref[...], rv_ref[...]
        else:
            kp, vp = k_ref[pl.ds((b - 1) * w, w), :], v_ref[pl.ds((b - 1) * w, w), :]
        s_own = lax.dot_general(q, k_ref[sl, :], nt, preferred_element_type=F32)
        s_prev = lax.dot_general(q, kp, nt, preferred_element_type=F32)
        if b == 0:
            s_prev = jnp.where(has_prev, s_prev, -1e30)
        s = jnp.where(own, s_own, s_prev) * scale
        e = jnp.exp(s - jnp.max(s, axis=1, keepdims=True))
        inv = 1.0 / jnp.sum(e, axis=1, keepdims=True)
        p = (e * inv).astype(BF)
        zero = jnp.zeros_like(p)
        o = mm(jnp.where(own, p, zero), v_ref[sl, :]) + mm(jnp.where(own, zero, p), vp)
        o_ref[sl, :] = o.astype(o_ref.dtype)


def attention(first, query, keys, values, rim_keys, rim_values):
    rows, feats = query.shape
    col = pl.BlockSpec((rows, HEAD_DIM), lambda h: (0, h))
    rim = pl.BlockSpec((WINDOW, HEAD_DIM), lambda h: (0, h))
    return pl.pallas_call(
        attn_kernel,
        grid=(feats // HEAD_DIM,),
        in_specs=[pl.BlockSpec(memory_space=pltpu.SMEM), col, col, col, rim, rim],
        out_specs=col,
        out_shape=jax.ShapeDtypeStruct((rows, feats), BF),
        compiler_params=pltpu.CompilerParams(vmem_limit_bytes=VMEM),
        cost_estimate=pl.CostEstimate(
            flops=8 * rows * feats * WINDOW,
            bytes_accessed=4 * rows * feats * 2,
            transcendentals=rows * feats // HEAD_DIM * WINDOW,
        ),
    )(first, query, keys, values, rim_keys, rim_values)


def renorm_kernel(start_ref, step_ref, base_ref, pull_ref, out_ref):
    base = base_ref[0].astype(F32)
    updated = base + step_ref[0] * pull_ref[0].astype(F32)
    old = jnp.sqrt(jnp.sum(base * base, axis=0, keepdims=True) + 1e-06)
    new = jnp.sqrt(jnp.sum(updated * updated, axis=0, keepdims=True) + 1e-06)
    out_ref[0] = (updated * (old / new)).astype(BF)


def renorm(start, step, base, pull):
    per = FW // LANES
    return pl.pallas_call(
        renorm_kernel,
        grid_spec=pltpu.PrefetchScalarGridSpec(
            num_scalar_prefetch=1,
            grid=(pull.shape[0],),
            in_specs=[
                pl.BlockSpec(memory_space=pltpu.SMEM),
                pl.BlockSpec((1, FW, LANES), lambda i, s: ((s[0] + i) // per, 0, (s[0] + i) % per)),
                pl.BlockSpec((1, FW, LANES), lambda i, s: (i, 0, 0)),
            ],
            out_specs=pl.BlockSpec((1, FW, LANES), lambda i, s: (i, 0, 0)),
        ),
        out_shape=jax.ShapeDtypeStruct(pull.shape, BF),
        cost_estimate=pl.CostEstimate(
            flops=10 * pull.size, bytes_accessed=6 * pull.size, transcendentals=0
        ),
    )(start, step, base, pull)


def apply_tile(q, att, weights):
    outs = []
    for h in range(len(weights)):
        n0, n1, n2 = weights[h]
        qh = q[:, h * FW : (h + 1) * FW]
        gate = mm(qh, n0)
        up = mm(qh, n1)
        act = (gate * sigmoid(gate) * up).astype(BF)
        y = mm(act, n2)
        y = y * lax.rsqrt(jnp.mean(y * y, axis=1, keepdims=True) + 1e-06)
        outs.append(att[:, h * FW : (h + 1) * FW].astype(F32) + y)
    return jnp.concatenate(outs, axis=1).astype(BF)


def apply_first_kernel(ids_ref, q_ref, att_ref, mine_ref, mate_ref, o_ref, nw_ref, sem):
    heads = nw_ref.shape[0]

    @pl.when(pl.program_id(0) == 0)
    def _():
        def each(act):
            for h in range(heads):
                for b in range(BLOCKS):
                    half, third, i = b // HALF, (b % HALF) // THIRD, b % THIRD
                    m, j = b // (FW // LANES), b % (FW // LANES)
                    slot = jnp.bitwise_xor(ids_ref[1 + h], third)
                    dst = nw_ref.at[h, m, :, pl.ds(j * LANES, LANES)]
                    own = ids_ref[0] == half

                    @pl.when(own)
                    def _():
                        act(pltpu.make_async_copy(mine_ref.at[h, slot, i], dst, sem.at[h, b]))

                    @pl.when(jnp.logical_not(own))
                    def _():
                        act(pltpu.make_async_copy(mate_ref.at[h, slot, i], dst, sem.at[h, b]))

        each(lambda c: c.start())
        each(lambda c: c.wait())

    weights = [[nw_ref[h, m] for m in range(3)] for h in range(heads)]
    o_ref[...] = apply_tile(q_ref[...], att_ref[...], weights)


def apply_next_kernel(q_ref, att_ref, nw_ref, o_ref):
    weights = [[nw_ref[h, m] for m in range(3)] for h in range(nw_ref.shape[0])]
    o_ref[...] = apply_tile(q_ref[...], att_ref[...], weights)


def apply_cost(rows, heads):
    return pl.CostEstimate(
        flops=heads * 6 * rows * FW * FW,
        bytes_accessed=heads * (6 * rows * FW + 12 * FW * FW),
        transcendentals=heads * rows * FW,
    )


def apply_first(ids, query, attended, mine, mate, rows):
    feats = query.shape[1]
    heads = mine.shape[0]
    tile = min(256, rows)
    row = pl.BlockSpec((tile, feats), lambda r: (r, 0))
    whole = (heads, 3, FW, FW)
    return pl.pallas_call(
        apply_first_kernel,
        grid=(rows // tile,),
        in_specs=[
            pl.BlockSpec(memory_space=pltpu.SMEM),
            row,
            row,
            pl.BlockSpec(memory_space=pl.ANY),
            pl.BlockSpec(memory_space=pl.ANY),
        ],
        out_specs=[row, pl.BlockSpec(whole, lambda r: (0, 0, 0, 0))],
        out_shape=[
            jax.ShapeDtypeStruct((rows, feats), BF),
            jax.ShapeDtypeStruct(whole, BF),
        ],
        scratch_shapes=[pltpu.SemaphoreType.DMA((heads, BLOCKS))],
        compiler_params=pltpu.CompilerParams(vmem_limit_bytes=VMEM),
        cost_estimate=apply_cost(rows, heads),
    )(ids, query, attended, mine, mate)


def apply_next(query, attended, weights, start):
    rows, feats = query.shape[0] - start, query.shape[1]
    tile = min(256, rows)
    off = start // tile
    row = pl.BlockSpec((tile, feats), lambda r: (r + off, 0))
    return pl.pallas_call(
        apply_next_kernel,
        grid=(rows // tile,),
        in_specs=[row, row, pl.BlockSpec(weights.shape, lambda r: (0, 0, 0, 0))],
        out_specs=pl.BlockSpec((tile, feats), lambda r: (r, 0)),
        out_shape=jax.ShapeDtypeStruct((rows, feats), BF),
        compiler_params=pltpu.CompilerParams(vmem_limit_bytes=VMEM),
        cost_estimate=apply_cost(rows, weights.shape[0]),
    )(query, attended, weights)


def scalars(*xs):
    return jnp.stack([jnp.asarray(x, jnp.int32) for x in xs])


def part(x, i, size):
    return lax.dynamic_slice_in_dim(x, i * size, size, 0)


def shards(query, keys, values, lr_code, fast_weights, out_weight):
    rows, feats = query.shape
    contexts, groups = lax.axis_size("ctx"), lax.axis_size("head")
    c, z = lax.axis_index("ctx"), lax.axis_index("head")
    tokens_all = rows * contexts
    heads = fast_weights.shape[0]
    bits = [1 << i for i in range(contexts.bit_length() - 1)]
    bit_of = {b: (c // b) % 2 for b in bits}

    rim_keys = shift(keys[rows - WINDOW :], "ctx", 1)
    rim_values = shift(values[rows - WINDOW :], "ctx", 1)

    rate = lr_code.T.astype(F32) * 2.0 ** (-14)
    rate_sum = lax.psum(jnp.sum(rate, axis=1), "ctx")
    step_size = base_rate / (math.sqrt(tokens_all) * (rate_sum / tokens_all))
    keep, send = grads(scalars(bit_of[1]), rate[:, None, :], keys, values, fast_weights)
    other = swap(send, 1)

    share = feats // contexts
    strip = part(out_weight, c, share)
    width = out_weight.shape[1] // groups

    def block_for(s):
        return lax.dynamic_slice_in_dim(strip, ((z + s) % groups) * width, width, 1)

    strips = jnp.stack([rotate(block_for(s), "head", s) for s in range(1, groups)])

    attended = attention(scalars(c == 0), query, keys, values, rim_keys, rim_values)

    mine = []
    second = [2, 4]
    slots = []
    for h in range(heads):
        near = second[h % 2]
        rest = [b for b in bits[1:] if b != near]
        me = bit_of[near]
        slots.append(me)
        away = swap(part(keep[h], 1 - me, THIRD) + part(other[h], 1 - me, THIRD), near)
        pull = part(keep[h], me, THIRD) + part(other[h], me, THIRD) + away
        for b in rest:
            pull = pull + swap(pull, b)
        start = bit_of[1] * HALF + me * THIRD
        new = renorm(scalars(start), step_size[h : h + 1], fast_weights[h], pull)
        mine.append(jnp.stack([new, swap(new, near)]))
    mine = jnp.stack(mine)
    mate = swap(mine, 1)

    cut = rows // 2
    ids = scalars(bit_of[1], *slots)
    merged_a, new_weights = apply_first(ids, query, attended, mine, mate, cut)

    strips, merged_a = lax.optimization_barrier((strips, merged_a))
    pieces, order = strips[None], [0]
    for b in reversed(bits):
        pieces = jnp.concatenate([pieces, swap(pieces, b)])
        order = order + [o ^ b for o in order]
    cols = jnp.zeros((groups - 1, feats, width), BF)
    for i, o in enumerate(order):
        cols = lax.dynamic_update_slice(cols, pieces[i], (0, (c ^ o) * share, 0))

    to_right, to_left = [shift(merged_a, "head", 1)], [shift(merged_a, "head", -1)]
    merged_r = apply_next(query, attended, new_weights, cut)
    partial = mm(merged_r, out_weight).astype(BF)

    def partial_for(d):
        return lax.dynamic_slice_in_dim(partial, (d % groups) * width, width, 1)

    zero = jnp.zeros((), BF)
    for t in range(1, groups):
        right = to_right[-1] + jnp.where(t <= z, zero, partial_for(z - t + groups))
        left = to_left[-1] + jnp.where(t <= groups - 1 - z, zero, partial_for(z + t))
        to_right.append(shift(right, "head", 1))
        to_left.append(shift(left, "head", -1))
    own_cols = lax.dynamic_slice_in_dim(out_weight, z * width, width, 1)
    out_a = mm(merged_a, own_cols)
    for t in range(groups - 1):
        x = jnp.where(t <= z - 1, to_right[t], to_left[groups - 2 - t])
        out_a = out_a + mm(x, cols[t])
    out_r = partial_for(z).astype(F32) + to_right[-1].astype(F32) + to_left[-1].astype(F32)
    layer_out = jnp.concatenate([out_a.astype(BF), out_r.astype(BF)])
    return (layer_out, new_weights)


def solution(mesh):
    placed = (
        P("ctx", "head"),
        P("ctx", "head"),
        P("ctx", "head"),
        P("ctx", "head"),
        P("head", None, None, None),
        P("head", None),
    )
    return jax.shard_map(
        shards,
        mesh=mesh,
        in_specs=placed,
        out_specs=(P("ctx", "head"), P("head", None, None, None)),
        check_vma=False,
    )
```

time: 415 us -> 269 us (0.65); the launches traced: 409 us -> 268 us
  local copies, waits for them, and re-layouts: 112 us -> 17.6 us
  waiting for transfers between devices: 143 us -> 89.1 us
  matrix products: 69.7 us -> 17.4 us
  Pallas kernels: 0 us -> 51.9 us
  starting transfers between devices: 7.9 us -> 51.8 us
  other arithmetic: 48.8 us -> 23.2 us
  between operations: 14.2 us -> 1.17 us
    reduce_scatter x1 -> x0, waiting for transfers between devices: 142 us -> none  [shards(): lax.psum_scatter(partial_out.astype(jnp.bfloat16), 'head', scatter_dimens...]
    ppermute x2 -> x24, waiting for transfers between devices: 0.01 us -> 89.1 us  [the longest x10 50.3 us: shift(): lax.ppermute(block, axis, [(i, i + distance) for i in range(n) if 0 <= i...]
    dynamic_update_slice x4 -> x8, local copies, waits for them, and re-layouts: 80 us -> 5.11 us  [shards(): cols = lax.dynamic_update_slice(cols, pieces[i], (0, (c ^ o) * share, 0))]
    dot_general x21 -> x5, matrix products: 69.7 us -> 17.4 us  [mm(): return jnp.dot(a, b, preferred_element_type=F32)]
    pallas_call x0 -> x6, Pallas kernels: none -> 51.9 us  [the longest x1 16.3 us: attention(): pl.pallas_call(attn_kernel, grid=(feats // HEAD_DIM,), in_specs=[pl.Block...]
    ppermute x2 -> x24, starting transfers between devices: 7.82 us -> 51.8 us  [the longest x10 32.9 us: shift(): lax.ppermute(block, axis, [(i, i + distance) for i in range(n) if 0 <= i...]
    sub x2 -> x0, other arithmetic: 32.5 us -> none  [one_block(): exps = jnp.exp(scores - top_score)]
    unnamed x33 -> x36, local copies, waits for them, and re-layouts: 22 us -> 1.34 us
  transfers between devices with their start and end apart: 4 -> 24, of which waited for: 1 -> 15; matrix products, arithmetic and copies ran while one was open for 46% -> 15% of each run, Pallas kernels for 0% -> 11%
where the time goes in v1:
time: 269 us; the launch traced here: 268 us
  waiting for transfers between devices  89.1 us (33%)
  Pallas kernels  51.9 us (19%)
  starting transfers between devices  51.8 us (19%)
  other arithmetic  23.2 us (9%)
  local copies, waits for them, and re-layouts  17.6 us (7%)
  matrix products  17.4 us (6%)
  blocking collectives  15.3 us (6%)
    ppermute x10, waiting for transfers between devices, shift(): lax.ppermute(block, axis, [(i, i + distance) for i in range(n) if 0 <= i...  50.3 us
    ppermute x10, starting transfers between devices, shift(): lax.ppermute(block, axis, [(i, i + distance) for i in range(n) if 0 <= i...  32.9 us
    ppermute x11, waiting for transfers between devices, swap(): return lax.ppermute(block, 'ctx', [(i, i ^ bit) for i in range(n)])  27.5 us
    dot_general x5, matrix products, mm(): return jnp.dot(a, b, preferred_element_type=F32)  17.4 us
    pallas_call x1, Pallas kernels, attention(): pl.pallas_call(attn_kernel, grid=(feats // HEAD_DIM,), in_specs=[pl.Block...  16.3 us
    pallas_call x1, Pallas kernels, grads(): pl.pallas_call(grads_kernel, grid=(heads,), in_specs=[pl.BlockSpec(memory...  15.8 us
    psum x1, blocking collectives, shards(): rate_sum = lax.psum(jnp.sum(rate, axis=1), 'ctx')  15.3 us
    ppermute x11, starting transfers between devices, swap(): return lax.ppermute(block, 'ctx', [(i, i ^ bit) for i in range(n)])  13.3 us
  transfers between devices with their start and end apart: 24, of which 15 were waited for; matrix products, arithmetic and copies ran while one was open for 15% of the time, Pallas kernels for 11%

profile of v1, /device:TPU:0, one launch (start us, length us, event | category | flops | bytes accessed | tf_op | source)
XLA Modules:
  0.0 267.5 jit_solution(11075316536909173013)
XLA Ops:
  2.1 15.8 %shard_map.78 = (bf16[2,6,512,128]{3,2,1,0:T(8,128)(2,1)}, bf16[2,6,512,128]{3,2,1,0:T(8,128)(2,1)}) custom-call(s32[1]{0:T(128)} %bitcast.3.bit_ref, f32[2,1,1024]{2,1,0:T(1,128)} %broadcast_in_dim.18.rate_ref, bf16[1024,1024]{1,0:T(8,128)(2,1)} %k_ref.3, bf16[1024,1024]{1,0:T(8,128)(2,1)} %v_ref.3, bf16[2,3,512,512]{3,2,1,0:T(8,128)(2,1)} %w_ref.1), custom_call_target="tpu_custom_call" | custom-call | flops 6442450944 | bytes 10485760 | tf_op jit(solution)/shard_map/pallas_call | solution.py:97
  18.3 15.3 %psum.7 = f32[2]{0:T(128)S(1)} all-reduce(f32[2]{0:T(128)S(1)} %get-tuple-element.30), channel_id=1, replica_groups=mesh['ctx'=8,'head'=4] {'ctx'}, use_global_device_ids=true, to_apply=%region_1.2 | all-reduce | flops 2 | bytes 16 | tf_op jit(solution)/shard_map/psum | solution.py:320
  33.7 1.5 fusion.23
  37.8 7.1 %collective-permute-done.6 = bf16[3,512,128]{2,1,0:T(8,128)(2,1)} collective-permute-done((bf16[3,512,128]{2,1,0:T(8,128)(2,1)}, bf16[3,512,128]{2,1,0:T(8,128)(2,1)}, u32[]{:S(2)}, u32[]{:S(2)}) %collective-permute-start.6) | collective-permute-done | bytes 393248 | tf_op jit(solution)/shard_map/ppermute | solution.py:41
  44.9 1.3 bitcast_add_fusion.1
  46.2 1.7 collective-permute-start.7
  47.8 1.3 bitcast_add_fusion
  49.1 1.6 collective-permute-start.10
  50.8 1.9 slice_bitcast_fusion.7
  52.6 2.6 collective-permute-done.7
  56.1 3.5 %shard_map.79 = bf16[3,512,128]{2,1,0:T(8,128)(2,1)} custom-call(s32[1]{0:T(128)} %bitcast.7.start_ref, f32[1]{0:T(128)} %get-tuple-element.31.step_ref, bf16[3,512,512]{2,1,0:T(8,128)(2,1)} %get-tuple-element.23.base_ref, bf16[3,512,128]{2,1,0:T(8,128)(2,1)} %add.221.pull_ref), custom_call_target="tpu_custom_call" | custom-call | flops 1966080 | bytes 1179648 | tf_op jit(solution)/shard_map/pallas_call | solution.py:181
  59.6 2.5 collective-permute-start.8
  62.1 1.8 add.230.pull_ref
  63.9 3.5 %shard_map.80 = bf16[3,512,128]{2,1,0:T(8,128)(2,1)} custom-call(s32[1]{0:T(128)} %bitcast.15.start_ref, f32[1]{0:T(128)} %get-tuple-element.32.step_ref, bf16[3,512,512]{2,1,0:T(8,128)(2,1)} %get-tuple-element.24.base_ref, bf16[3,512,128]{2,1,0:T(8,128)(2,1)} %add.230.pull_ref), custom_call_target="tpu_custom_call" | custom-call | flops 1966080 | bytes 1179648 | tf_op jit(solution)/shard_map/pallas_call | solution.py:181
  67.5 1.7 collective-permute-start.11
  69.7 6.9 %collective-permute-done.11 = bf16[3,512,128]{2,1,0:T(8,128)(2,1)S(1)} collective-permute-done((bf16[3,512,128]{2,1,0:T(8,128)(2,1)}, bf16[3,512,128]{2,1,0:T(8,128)(2,1)S(1)}, u32[]{:S(2)}, u32[]{:S(2)}) %collective-permute-start.11) | collective-permute-done | bytes 393248 | tf_op jit(solution)/shard_map/ppermute | solution.py:41
  76.7 1.1 maximum_bitcast_fusion.1
  78.0 2.0 fusion.22
  80.1 1.6 collective-permute-start
  81.7 1.9 slice.61
  83.6 1.7 collective-permute-start.3
  85.2 1.9 slice.62
  87.1 2.6 collective-permute-start.4
  89.7 2.7 %collective-permute-start.1 = (bf16[128,1024]{1,0:T(8,128)(2,1)S(1)}, bf16[128,1024]{1,0:T(8,128)(2,1)}, u32[]{:S(2)}, u32[]{:S(2)}) collective-permute-start(bf16[128,1024]{1,0:T(8,128)(2,1)S(1)} %get-tuple-element.16), channel_id=1, source_target_pairs={{0,2},{1,3},{2,0},{3,1},{4,6},{5,7},{6,4},{7,5},{8,10},{9,11},{10,... | collective-permute-start | bytes 786440 | tf_op jit(solution)/shard_map/ppermute | solution.py:36
  92.4 1.3 collective-permute-start.2
  94.3 11.3 %collective-permute-done.1 = bf16[128,1024]{1,0:T(8,128)(2,1)} collective-permute-done((bf16[128,1024]{1,0:T(8,128)(2,1)S(1)}, bf16[128,1024]{1,0:T(8,128)(2,1)}, u32[]{:S(2)}, u32[]{:S(2)}) %collective-permute-start.1) | collective-permute-done | bytes 262176 | tf_op jit(solution)/shard_map/ppermute | solution.py:36
  105.6 1.2 pad_maximum_fusion.4
  107.8 16.3 %shard_map.77.att_ref = bf16[1024,1024]{1,0:T(8,128)(2,1)} custom-call(s32[1]{0:T(128)} %bitcast.6.first_ref, bf16[1024,1024]{1,0:T(8,128)(2,1)} %q_ref.5, bf16[1024,1024]{1,0:T(8,128)(2,1)} %k_ref.3, bf16[1024,1024]{1,0:T(8,128)(2,1)} %v_ref.3, bf16[256,1024]{1,0:T(8,128)(2,1)} %copy-done.14, bf16[256,1024]{1,0:T(8,128)(2,1)} %copy-done.15), custom_call_target="tpu_custom_call" | custom-call | flops 2147483648 | bytes 8388608 | tf_op jit(solution)/shard_map/pallas_call | solution.py:156
  124.2 7.1 %shard_map.81 = (bf16[512,1024]{1,0:T(8,128)(2,1)}, bf16[2,3,512,512]{3,2,1,0:T(8,128)(2,1)}) custom-call(s32[3]{0:T(128)} %pad_add_fusion.ids_ref, bf16[1024,1024]{1,0:T(8,128)(2,1)} %q_ref.5, bf16[1024,1024]{1,0:T(8,128)(2,1)} %shard_map.77.att_ref, bf16[2,2,3,512,128]{4,3,2,1,0:T(8,128)(2,1)} %copy-done.2, ...), custom_call_target="tpu_custom_call" | custom-call | flops 1610612736 | bytes 9437184 | tf_op jit(solution)/shard_map/pallas_call | solution.py:262
  131.3 1.9 collective-permute-start.17
  133.2 7.0 %collective-permute-start.13 = (bf16[512,1024]{1,0:T(8,128)(2,1)}, bf16[512,1024]{1,0:T(8,128)(2,1)S(1)}, u32[]{:S(2)}, u32[]{:S(2)}) collective-permute-start(bf16[512,1024]{1,0:T(8,128)(2,1)} %get-tuple-element.11), channel_id=1, source_target_pairs={{0,1},{1,2},{2,3},{4,5},{5,6},{6,7},{8,9},{9,10},{10,11},{12,13},{... | collective-permute-start | bytes 3145736 | tf_op jit(solution)/shard_map/ppermute | solution.py:31
  140.2 1.5 collective-permute-start.14
  141.7 5.6 %shard_map.82 = bf16[512,1024]{1,0:T(8,128)(2,1)} custom-call(bf16[1024,1024]{1,0:T(8,128)(2,1)} %q_ref.5, bf16[1024,1024]{1,0:T(8,128)(2,1)} %shard_map.77.att_ref, bf16[2,3,512,512]{3,2,1,0:T(8,128)(2,1)} %get-tuple-element.7.nw_ref), custom_call_target="tpu_custom_call" | custom-call | flops 1610612736 | bytes 9437184 | tf_op jit(solution)/shard_map/pallas_call | solution.py:288
  147.3 1.8 collective-permute-done.17
  149.2 2.8 %collective-permute-start.18 = (bf16[2,3,128,1024]{3,2,1,0:T(8,128)(2,1)S(1)}, bf16[2,3,128,1024]{3,2,1,0:T(8,128)(2,1)S(1)}, u32[]{:S(2)}, u32[]{:S(2)}) collective-permute-start(bf16[2,3,128,1024]{3,2,1,0:T(8,128)(2,1)S(1)} %pad_maximum_fusion.3), channel_id=1, source_target_pairs={{0,8},{4,12},{8,0},{12,4},{16,24},{20,28},{24,16},{28,20},{1,9},{5... | collective-permute-start | bytes 4718600 | tf_op jit(solution)/shard_map/ppermute | solution.py:41
  152.1 8.1 %convolution_convert_fusion = bf16[512,4096]{1,0:T(8,128)(2,1)S(1)} fusion(bf16[512,1024]{1,0:T(8,128)(2,1)S(1)} %copy-done.13, bf16[1024,4096]{1,0:T(8,128)(2,1)} %param.11), kind=kOutput, calls=%fused_computation | convolution fusion | flops 4297064448 | bytes 13631488 | tf_op jit(solution)/shard_map/dot_general | solution.py:26
  160.2 1.9 collective-permute-done.13
  162.1 4.1 %collective-permute-done.14 = bf16[512,1024]{1,0:T(8,128)(2,1)S(1)} collective-permute-done((bf16[512,1024]{1,0:T(8,128)(2,1)}, bf16[512,1024]{1,0:T(8,128)(2,1)S(1)}, u32[]{:S(2)}, u32[]{:S(2)}) %collective-permute-start.14) | collective-permute-done | bytes 1048608 | tf_op jit(solution)/shard_map/ppermute | solution.py:31
  166.1 2.3 select_add_fusion.3
  168.5 1.3 collective-permute-start.15
  169.8 5.5 %collective-permute-start.20 = (bf16[512,1024]{1,0:T(8,128)(2,1)}, bf16[512,1024]{1,0:T(8,128)(2,1)}, u32[]{:S(2)}, u32[]{:S(2)}) collective-permute-start(bf16[512,1024]{1,0:T(8,128)(2,1)} %get-tuple-element.21), channel_id=1, source_target_pairs={{0,1},{1,2},{2,3},{4,5},{5,6},{6,7},{8,9},{9,10},{10,11},{12,13},{... | collective-permute-start | bytes 3145736 | tf_op jit(solution)/shard_map/ppermute | solution.py:31
  175.3 8.6 %collective-permute-done.18 = bf16[2,3,128,1024]{3,2,1,0:T(8,128)(2,1)S(1)} collective-permute-done((bf16[2,3,128,1024]{3,2,1,0:T(8,128)(2,1)S(1)}, bf16[2,3,128,1024]{3,2,1,0:T(8,128)(2,1)S(1)}, u32[]{:S(2)}, u32[]{:S(2)}) %collective-permute-start.18) | collective-permute-done | bytes 1572896 | tf_op jit(solution)/shard_map/ppermute | solution.py:41
  183.9 1.9 pad_maximum_fusion
  185.9 7.7 %collective-permute-done.15 = bf16[512,1024]{1,0:T(8,128)(2,1)} collective-permute-done((bf16[512,1024]{1,0:T(8,128)(2,1)}, bf16[512,1024]{1,0:T(8,128)(2,1)}, u32[]{:S(2)}, u32[]{:S(2)}) %collective-permute-start.15) | collective-permute-done | bytes 1048608 | tf_op jit(solution)/shard_map/ppermute | solution.py:31
  193.6 1.2 collective-permute-done.20
  194.8 4.0 %select_add_fusion.2 = (bf16[512,1024]{1,0:T(8,128)(2,1)}, bf16[512,1024]{1,0:T(8,128)(2,1)}) fusion(bf16[512,1024]{1,0:T(8,128)(2,1)} %collective-permute-done.20, pred[]{:T(512)S(6)} %ge.33, bf16[512,4096]{1,0:T(8,128)(2,1)} %copy-done, s32[]{:T(128)S(6)} %select_n.185, bf16[512,1024]{1,0:T(8,128)(2,1)} %collective-permute-done.15, pred[]{:T(512)S(6)} %ge.29), kind=kLoop, calls=%fused_computation.20 | loop fusion | flops 5242880 | bytes 5242886 | tf_op jit(solution)/shard_map/add | solution.py:376
  198.7 1.3 collective-permute-start.16
  200.0 6.0 %collective-permute-start.21 = (bf16[512,1024]{1,0:T(8,128)(2,1)}, bf16[512,1024]{1,0:T(8,128)(2,1)}, u32[]{:S(2)}, u32[]{:S(2)}) collective-permute-start(bf16[512,1024]{1,0:T(8,128)(2,1)} %get-tuple-element.19), channel_id=1, source_target_pairs={{0,1},{1,2},{2,3},{4,5},{5,6},{6,7},{8,9},{9,10},{10,11},{12,13},{... | collective-permute-start | bytes 3145736 | tf_op jit(solution)/shard_map/ppermute | solution.py:31
  206.9 16.4 %collective-permute-done.16 = bf16[512,1024]{1,0:T(8,128)(2,1)} collective-permute-done((bf16[512,1024]{1,0:T(8,128)(2,1)}, bf16[512,1024]{1,0:T(8,128)(2,1)}, u32[]{:S(2)}, u32[]{:S(2)}) %collective-permute-start.16) | collective-permute-done | bytes 1048608 | tf_op jit(solution)/shard_map/ppermute | solution.py:31
  223.4 1.2 collective-permute-done.21
  224.5 2.5 select_add_fusion.1
  227.1 4.5 %collective-permute-start.22 = (bf16[512,1024]{1,0:T(8,128)(2,1)S(1)}, bf16[512,1024]{1,0:T(8,128)(2,1)S(1)}, u32[]{:S(2)}, u32[]{:S(2)}) collective-permute-start(bf16[512,1024]{1,0:T(8,128)(2,1)S(1)} %get-tuple-element.17), channel_id=1, source_target_pairs={{0,1},{1,2},{2,3},{4,5},{5,6},{6,7},{8,9},{9,10},{10,11},{12,13},{... | collective-permute-start | bytes 3145736 | tf_op jit(solution)/shard_map/ppermute | solution.py:31
  231.6 1.5 collective-permute-start.23
  233.1 2.8 %fusion.3 = f32[512,1024]{1,0:T(8,128)S(1)} fusion(bf16[512,1024]{1,0:T(8,128)(2,1)S(1)} %copy-done.17, bf16[1024,4096]{1,0:T(8,128)(2,1)} %param.11, s32[]{:T(128)S(6)} %select_n.199), kind=kOutput, calls=%fused_computation.11 | convolution fusion | flops 1073741824 | bytes 5242884 | tf_op jit(solution)/shard_map/dot_general | solution.py:26
  236.2 13.6 %collective-permute-done.22 = bf16[512,1024]{1,0:T(8,128)(2,1)S(1)} collective-permute-done((bf16[512,1024]{1,0:T(8,128)(2,1)S(1)}, bf16[512,1024]{1,0:T(8,128)(2,1)S(1)}, u32[]{:S(2)}, u32[]{:S(2)}) %collective-permute-start.22) | collective-permute-done | bytes 1048608 | tf_op jit(solution)/shard_map/ppermute | solution.py:31
  249.7 4.2 %collective-permute-done.23 = bf16[512,1024]{1,0:T(8,128)(2,1)S(1)} collective-permute-done((bf16[512,1024]{1,0:T(8,128)(2,1)S(1)}, bf16[512,1024]{1,0:T(8,128)(2,1)S(1)}, u32[]{:S(2)}, u32[]{:S(2)}) %collective-permute-start.23) | collective-permute-done | bytes 1048608 | tf_op jit(solution)/shard_map/ppermute | solution.py:31
  254.6 1.2 fusion.16
  255.8 1.3 fusion.15
  257.1 1.2 fusion.14
  258.3 1.2 fusion.13
  259.5 2.5 fusion.2
  262.0 2.6 fusion.1
  264.6 1.4 add_convert_fusion.1
  266.0 1.5 pad_maximum_fusion.1
  (69 shorter events, 9.4 us)
Async XLA Ops:
  17.8 17.3 %collective-permute-start.5 = (bf16[2,6,512,128]{3,2,1,0:T(8,128)(2,1)}, bf16[2,6,512,128]{3,2,1,0:T(8,128)(2,1)S(1)}, u32[]{:S(2)}, u32[]{:S(2)}) collective-permute-start(bf16[2,6,512,128]{3,2,1,0:T(8,128)(2,1)} %get-tuple-element.9), channel_id=1, source_target_pairs={{0,4},{4,0},{8,12},{12,8},{16,20},{20,16},{24,28},{28,24},{1,5},{5... | collective-permute-start | bytes 4718600 | tf_op jit(solution)/shard_map/ppermute | solution.py:41
  35.1 1.1 copy-start.8
  35.1 1.3 copy-start.6
  35.3 1.4 copy-start.7
  35.3 1.9 copy-start.9
  36.3 8.6 %collective-permute-start.6 = (bf16[3,512,128]{2,1,0:T(8,128)(2,1)}, bf16[3,512,128]{2,1,0:T(8,128)(2,1)}, u32[]{:S(2)}, u32[]{:S(2)}) collective-permute-start(bf16[3,512,128]{2,1,0:T(8,128)(2,1)} %add_bitcast_fusion.1), channel_id=1, source_target_pairs={{0,8},{4,12},{8,0},{12,4},{16,24},{20,28},{24,16},{28,20},{1,9},{5... | collective-permute-start | bytes 1179656 | tf_op jit(solution)/shard_map/ppermute | solution.py:41
  36.4 14.3 %copy-start.5 = (bf16[2,3,512,512]{3,2,1,0:T(8,128)(2,1)S(1)}, bf16[2,3,512,512]{3,2,1,0:T(8,128)(2,1)}, u32[]{:S(2)}) copy-start(bf16[2,3,512,512]{3,2,1,0:T(8,128)(2,1)} %w_ref.1) | copy-start | bytes 9437188
  36.7 11.2 %collective-permute-start.9 = (bf16[3,512,128]{2,1,0:T(8,128)(2,1)S(1)}, bf16[3,512,128]{2,1,0:T(8,128)(2,1)}, u32[]{:S(2)}, u32[]{:S(2)}) collective-permute-start(bf16[3,512,128]{2,1,0:T(8,128)(2,1)S(1)} %add_bitcast_fusion), channel_id=1, source_target_pairs={{0,16},{4,20},{8,24},{12,28},{16,0},{20,4},{24,8},{28,12},{1,17},{... | collective-permute-start | bytes 1179656 | tf_op jit(solution)/shard_map/ppermute | solution.py:41
  46.2 9.1 %collective-permute-start.7 = (bf16[3,512,128]{2,1,0:T(8,128)(2,1)S(1)}, bf16[3,512,128]{2,1,0:T(8,128)(2,1)S(1)}, u32[]{:S(2)}, u32[]{:S(2)}) collective-permute-start(bf16[3,512,128]{2,1,0:T(8,128)(2,1)S(1)} %bitcast_add_fusion.1), channel_id=1, source_target_pairs={{0,16},{4,20},{8,24},{12,28},{16,0},{20,4},{24,8},{28,12},{1,17},{... | collective-permute-start | bytes 1179656 | tf_op jit(solution)/shard_map/ppermute | solution.py:41
  49.1 13.0 %collective-permute-start.10 = (bf16[3,512,128]{2,1,0:T(8,128)(2,1)S(1)}, bf16[3,512,128]{2,1,0:T(8,128)(2,1)}, u32[]{:S(2)}, u32[]{:S(2)}) collective-permute-start(bf16[3,512,128]{2,1,0:T(8,128)(2,1)S(1)} %bitcast_add_fusion), channel_id=1, source_target_pairs={{0,8},{4,12},{8,0},{12,4},{16,24},{20,28},{24,16},{28,20},{1,9},{5... | collective-permute-start | bytes 1179656 | tf_op jit(solution)/shard_map/ppermute | solution.py:41
  59.6 10.1 %copy-start.10 = (bf16[3,512,128]{2,1,0:T(8,128)(2,1)S(1)}, bf16[3,512,128]{2,1,0:T(8,128)(2,1)}, u32[]{:S(2)}) copy-start(bf16[3,512,128]{2,1,0:T(8,128)(2,1)} %shard_map.79) | copy-start | bytes 1179652
  59.6 10.0 %collective-permute-start.8 = (bf16[3,512,128]{2,1,0:T(8,128)(2,1)}, bf16[3,512,128]{2,1,0:T(8,128)(2,1)S(1)}, u32[]{:S(2)}, u32[]{:S(2)}) collective-permute-start(bf16[3,512,128]{2,1,0:T(8,128)(2,1)} %shard_map.79), channel_id=1, source_target_pairs={{0,8},{4,12},{8,0},{12,4},{16,24},{20,28},{24,16},{28,20},{1,9},{5... | collective-permute-start | bytes 1179656 | tf_op jit(solution)/shard_map/ppermute | solution.py:41
  67.5 9.2 %collective-permute-start.11 = (bf16[3,512,128]{2,1,0:T(8,128)(2,1)}, bf16[3,512,128]{2,1,0:T(8,128)(2,1)S(1)}, u32[]{:S(2)}, u32[]{:S(2)}) collective-permute-start(bf16[3,512,128]{2,1,0:T(8,128)(2,1)} %shard_map.80), channel_id=1, source_target_pairs={{0,16},{4,20},{8,24},{12,28},{16,0},{20,4},{24,8},{28,12},{1,17},{... | collective-permute-start | bytes 1179656 | tf_op jit(solution)/shard_map/ppermute | solution.py:41
  77.9 29.0 %copy-start.2 = (bf16[2,2,3,512,128]{4,3,2,1,0:T(8,128)(2,1)}, bf16[2,2,3,512,128]{4,3,2,1,0:T(8,128)(2,1)S(1)}, u32[]{:S(2)}) copy-start(bf16[2,2,3,512,128]{4,3,2,1,0:T(8,128)(2,1)S(1)} %pad_maximum_fusion.2.mine_ref) | copy-start | bytes 4718596
  77.9 46.3 %collective-permute-start.12 = (bf16[2,2,3,512,128]{4,3,2,1,0:T(8,128)(2,1)S(1)}, bf16[2,2,3,512,128]{4,3,2,1,0:T(8,128)(2,1)}, u32[]{:S(2)}, u32[]{:S(2)}) collective-permute-start(bf16[2,2,3,512,128]{4,3,2,1,0:T(8,128)(2,1)S(1)} %pad_maximum_fusion.2.mine_ref), channel_id=1, source_target_pairs={{0,4},{4,0},{8,12},{12,8},{16,20},{20,16},{24,28},{28,24},{1,5},{5... | collective-permute-start | bytes 4718600 | tf_op jit(solution)/shard_map/ppermute | solution.py:41
  80.1 12.3 %collective-permute-start = (bf16[128,1024]{1,0:T(8,128)(2,1)S(1)}, bf16[128,1024]{1,0:T(8,128)(2,1)S(1)}, u32[]{:S(2)}, u32[]{:S(2)}) collective-permute-start(bf16[128,1024]{1,0:T(8,128)(2,1)S(1)} %get-tuple-element.14), channel_id=1, source_target_pairs={{0,1},{1,2},{2,3},{3,0},{4,5},{5,6},{6,7},{7,4},{8,9},{9,10},{10,1... | collective-permute-start | bytes 786440 | tf_op jit(solution)/shard_map/ppermute | solution.py:36
  83.6 23.3 %collective-permute-start.3 = (bf16[256,1024]{1,0:T(8,128)(2,1)}, bf16[256,1024]{1,0:T(8,128)(2,1)S(1)}, u32[]{:S(2)}, u32[]{:S(2)}) collective-permute-start(bf16[256,1024]{1,0:T(8,128)(2,1)} %slice.61), channel_id=1, source_target_pairs={{0,4},{4,8},{8,12},{12,16},{16,20},{20,24},{24,28},{1,5},{5,9},{9,... | collective-permute-start | bytes 1572872 | tf_op jit(solution)/shard_map/ppermute | solution.py:31
  87.1 19.8 %collective-permute-start.4 = (bf16[256,1024]{1,0:T(8,128)(2,1)}, bf16[256,1024]{1,0:T(8,128)(2,1)S(1)}, u32[]{:S(2)}, u32[]{:S(2)}) collective-permute-start(bf16[256,1024]{1,0:T(8,128)(2,1)} %slice.62), channel_id=1, source_target_pairs={{0,4},{4,8},{8,12},{12,16},{16,20},{20,24},{24,28},{1,5},{5,9},{9,... | collective-permute-start | bytes 1572872 | tf_op jit(solution)/shard_map/ppermute | solution.py:31
  89.7 15.9 %collective-permute-start.1 = (bf16[128,1024]{1,0:T(8,128)(2,1)S(1)}, bf16[128,1024]{1,0:T(8,128)(2,1)}, u32[]{:S(2)}, u32[]{:S(2)}) collective-permute-start(bf16[128,1024]{1,0:T(8,128)(2,1)S(1)} %get-tuple-element.16), channel_id=1, source_target_pairs={{0,2},{1,3},{2,0},{3,1},{4,6},{5,7},{6,4},{7,5},{8,10},{9,11},{10,... | collective-permute-start | bytes 786440 | tf_op jit(solution)/shard_map/ppermute | solution.py:36
  92.4 13.2 %copy-start.16 = (bf16[128,1024]{1,0:T(8,128)(2,1)}, bf16[128,1024]{1,0:T(8,128)(2,1)S(1)}, u32[]{:S(2)}) copy-start(bf16[128,1024]{1,0:T(8,128)(2,1)S(1)} %collective-permute-done) | copy-start | bytes 786436
  92.4 13.2 %collective-permute-start.2 = (bf16[128,1024]{1,0:T(8,128)(2,1)S(1)}, bf16[128,1024]{1,0:T(8,128)(2,1)}, u32[]{:S(2)}, u32[]{:S(2)}) collective-permute-start(bf16[128,1024]{1,0:T(8,128)(2,1)S(1)} %get-tuple-element.15), channel_id=1, source_target_pairs={{0,3},{1,0},{2,1},{3,2},{4,7},{5,4},{6,5},{7,6},{8,11},{9,8},{10,9... | collective-permute-start | bytes 786440 | tf_op jit(solution)/shard_map/ppermute | solution.py:36
  106.9 0.8 copy-start.14
  106.9 0.9 copy-start.15
  131.3 17.8 %collective-permute-start.17 = (bf16[1,3,128,1024]{3,2,1,0:T(8,128)(2,1)S(1)}, bf16[1,3,128,1024]{3,2,1,0:T(8,128)(2,1)S(1)}, u32[]{:S(2)}, u32[]{:S(2)}) collective-permute-start(bf16[1,3,128,1024]{3,2,1,0:T(8,128)(2,1)S(1)} %bitcast.72), channel_id=1, source_target_pairs={{0,16},{4,20},{8,24},{12,28},{16,0},{20,4},{24,8},{28,12},{1,17},{... | collective-permute-start | bytes 2359304 | tf_op jit(solution)/shard_map/ppermute | solution.py:41
  133.2 28.9 %collective-permute-start.13 = (bf16[512,1024]{1,0:T(8,128)(2,1)}, bf16[512,1024]{1,0:T(8,128)(2,1)S(1)}, u32[]{:S(2)}, u32[]{:S(2)}) collective-permute-start(bf16[512,1024]{1,0:T(8,128)(2,1)} %get-tuple-element.11), channel_id=1, source_target_pairs={{0,1},{1,2},{2,3},{4,5},{5,6},{6,7},{8,9},{9,10},{10,11},{12,13},{... | collective-permute-start | bytes 3145736 | tf_op jit(solution)/shard_map/ppermute | solution.py:31
  140.2 25.9 %collective-permute-start.14 = (bf16[512,1024]{1,0:T(8,128)(2,1)}, bf16[512,1024]{1,0:T(8,128)(2,1)S(1)}, u32[]{:S(2)}, u32[]{:S(2)}) collective-permute-start(bf16[512,1024]{1,0:T(8,128)(2,1)} %get-tuple-element.11), channel_id=1, source_target_pairs={{1,0},{2,1},{3,2},{5,4},{6,5},{7,6},{9,8},{10,9},{11,10},{13,12},{... | collective-permute-start | bytes 3145736 | tf_op jit(solution)/shard_map/ppermute | solution.py:31
  147.3 4.7 %copy-start.13 = (bf16[512,1024]{1,0:T(8,128)(2,1)S(1)}, bf16[512,1024]{1,0:T(8,128)(2,1)}, u32[]{:S(2)}) copy-start(bf16[512,1024]{1,0:T(8,128)(2,1)} %shard_map.82) | copy-start | bytes 3145732
  149.2 34.7 %collective-permute-start.18 = (bf16[2,3,128,1024]{3,2,1,0:T(8,128)(2,1)S(1)}, bf16[2,3,128,1024]{3,2,1,0:T(8,128)(2,1)S(1)}, u32[]{:S(2)}, u32[]{:S(2)}) collective-permute-start(bf16[2,3,128,1024]{3,2,1,0:T(8,128)(2,1)S(1)} %pad_maximum_fusion.3), channel_id=1, source_target_pairs={{0,8},{4,12},{8,0},{12,4},{16,24},{20,28},{24,16},{28,20},{1,9},{5... | collective-permute-start | bytes 4718600 | tf_op jit(solution)/shard_map/ppermute | solution.py:41
  160.2 8.3 %copy-start = (bf16[512,4096]{1,0:T(8,128)(2,1)}, bf16[512,4096]{1,0:T(8,128)(2,1)S(1)}, u32[]{:S(2)}) copy-start(bf16[512,4096]{1,0:T(8,128)(2,1)S(1)} %convolution_convert_fusion) | copy-start | bytes 12582916
  162.1 6.4 %copy-start.11 = (bf16[512,1024]{1,0:T(8,128)(2,1)}, bf16[512,1024]{1,0:T(8,128)(2,1)S(1)}, u32[]{:S(2)}) copy-start(bf16[512,1024]{1,0:T(8,128)(2,1)S(1)} %collective-permute-done.13) | copy-start | bytes 3145732
  166.1 2.3 copy-start.3
  168.5 25.1 %collective-permute-start.15 = (bf16[512,1024]{1,0:T(8,128)(2,1)}, bf16[512,1024]{1,0:T(8,128)(2,1)}, u32[]{:S(2)}, u32[]{:S(2)}) collective-permute-start(bf16[512,1024]{1,0:T(8,128)(2,1)} %get-tuple-element.22), channel_id=1, source_target_pairs={{1,0},{2,1},{3,2},{5,4},{6,5},{7,6},{9,8},{10,9},{11,10},{13,12},{... | collective-permute-start | bytes 3145736 | tf_op jit(solution)/shard_map/ppermute | solution.py:31
  169.8 25.0 %collective-permute-start.20 = (bf16[512,1024]{1,0:T(8,128)(2,1)}, bf16[512,1024]{1,0:T(8,128)(2,1)}, u32[]{:S(2)}, u32[]{:S(2)}) collective-permute-start(bf16[512,1024]{1,0:T(8,128)(2,1)} %get-tuple-element.21), channel_id=1, source_target_pairs={{0,1},{1,2},{2,3},{4,5},{5,6},{6,7},{8,9},{9,10},{10,11},{12,13},{... | collective-permute-start | bytes 3145736 | tf_op jit(solution)/shard_map/ppermute | solution.py:31
  185.9 68.7 %collective-permute-start.19 = (bf16[4,3,128,1024]{3,2,1,0:T(8,128)(2,1)}, bf16[4,3,128,1024]{3,2,1,0:T(8,128)(2,1)}, u32[]{:S(2)}, u32[]{:S(2)}) collective-permute-start(bf16[4,3,128,1024]{3,2,1,0:T(8,128)(2,1)} %pad_maximum_fusion), channel_id=1, source_target_pairs={{0,4},{4,0},{8,12},{12,8},{16,20},{20,16},{24,28},{28,24},{1,5},{5... | collective-permute-start | bytes 9437192 | tf_op jit(solution)/shard_map/ppermute | solution.py:41
  198.7 24.6 %collective-permute-start.16 = (bf16[512,1024]{1,0:T(8,128)(2,1)}, bf16[512,1024]{1,0:T(8,128)(2,1)}, u32[]{:S(2)}, u32[]{:S(2)}) collective-permute-start(bf16[512,1024]{1,0:T(8,128)(2,1)} %get-tuple-element.20), channel_id=1, source_target_pairs={{1,0},{2,1},{3,2},{5,4},{6,5},{7,6},{9,8},{10,9},{11,10},{13,12},{... | collective-permute-start | bytes 3145736 | tf_op jit(solution)/shard_map/ppermute | solution.py:31
  200.0 24.5 %collective-permute-start.21 = (bf16[512,1024]{1,0:T(8,128)(2,1)}, bf16[512,1024]{1,0:T(8,128)(2,1)}, u32[]{:S(2)}, u32[]{:S(2)}) collective-permute-start(bf16[512,1024]{1,0:T(8,128)(2,1)} %get-tuple-element.19), channel_id=1, source_target_pairs={{0,1},{1,2},{2,3},{4,5},{5,6},{6,7},{8,9},{9,10},{10,11},{12,13},{... | collective-permute-start | bytes 3145736 | tf_op jit(solution)/shard_map/ppermute | solution.py:31
  206.0 18.5 %copy-start.1 = (bf16[512,4096]{1,0:T(8,128)(2,1)S(1)}, bf16[512,4096]{1,0:T(8,128)(2,1)}, u32[]{:S(2)}) copy-start(bf16[512,4096]{1,0:T(8,128)(2,1)} %copy-done) | copy-start | bytes 12582916
  206.9 26.2 %copy-start.17 = (bf16[512,1024]{1,0:T(8,128)(2,1)S(1)}, bf16[512,1024]{1,0:T(8,128)(2,1)}, u32[]{:S(2)}) copy-start(bf16[512,1024]{1,0:T(8,128)(2,1)} %get-tuple-element.11) | copy-start | bytes 3145732
  227.1 22.6 %collective-permute-start.22 = (bf16[512,1024]{1,0:T(8,128)(2,1)S(1)}, bf16[512,1024]{1,0:T(8,128)(2,1)S(1)}, u32[]{:S(2)}, u32[]{:S(2)}) collective-permute-start(bf16[512,1024]{1,0:T(8,128)(2,1)S(1)} %get-tuple-element.17), channel_id=1, source_target_pairs={{0,1},{1,2},{2,3},{4,5},{5,6},{6,7},{8,9},{9,10},{10,11},{12,13},{... | collective-permute-start | bytes 3145736 | tf_op jit(solution)/shard_map/ppermute | solution.py:31
  231.6 22.4 %collective-permute-start.23 = (bf16[512,1024]{1,0:T(8,128)(2,1)S(1)}, bf16[512,1024]{1,0:T(8,128)(2,1)S(1)}, u32[]{:S(2)}, u32[]{:S(2)}) collective-permute-start(bf16[512,1024]{1,0:T(8,128)(2,1)S(1)} %get-tuple-element.18), channel_id=1, source_target_pairs={{1,0},{2,1},{3,2},{5,4},{6,5},{7,6},{9,8},{10,9},{11,10},{13,12},{... | collective-permute-start | bytes 3145736 | tf_op jit(solution)/shard_map/ppermute | solution.py:31
  255.8 3.7 %copy-start.12 = (bf16[512,1024]{1,0:T(8,128)(2,1)S(1)}, bf16[512,1024]{1,0:T(8,128)(2,1)}, u32[]{:S(2)}) copy-start(bf16[512,1024]{1,0:T(8,128)(2,1)} %copy-done.11) | copy-start | bytes 3145732
  262.0 2.6 copy-start.4

commit v2 on v0

v2 whole, which is shorter than its diff:
```python
import functools
import math

import jax
import jax.numpy as jnp
from jax import lax
from jax.experimental import pallas as pl
from jax.experimental.pallas import tpu as pltpu
from jax.sharding import PartitionSpec as P

FW = 512
HEAD_DIM = 128
WINDOW = 256
LANES = 128
PER = FW // LANES
BLOCKS = 3 * PER
HALF = BLOCKS // 2
THIRD = BLOCKS // 4
TAIL = 16
VMEM = 56 * 2**20

base_rate = 0.05
BF = jnp.bfloat16
F32 = jnp.float32
NT = (((1,), (1,)), ((), ()))

ANY = pl.BlockSpec(memory_space=pl.ANY)
SMEM = pl.BlockSpec(memory_space=pltpu.SMEM)
PARAMS = pltpu.CompilerParams(vmem_limit_bytes=VMEM)


def mm(a, b):
    return jnp.dot(a, b, preferred_element_type=F32)


def shift(block, axis, distance):
    n = lax.axis_size(axis)
    return lax.ppermute(block, axis, [(i, i + distance) for i in range(n) if 0 <= i + distance < n])


def rotate(block, axis, distance):
    n = lax.axis_size(axis)
    return lax.ppermute(block, axis, [(i, (i + distance) % n) for i in range(n)])


def swap(block, bit):
    n = lax.axis_size("ctx")
    return lax.ppermute(block, "ctx", [(i, i ^ bit) for i in range(n)])


def sigmoid(x):
    return 0.5 * jnp.tanh(0.5 * x) + 0.5


def full(shape):
    return pl.BlockSpec(shape, lambda *_: (0,) * len(shape))


def cost(flops, bytes_accessed, transcendentals=0):
    return pl.CostEstimate(
        flops=int(flops), bytes_accessed=int(bytes_accessed), transcendentals=int(transcendentals)
    )


def split_rows(x):
    hi = x.astype(BF).astype(F32)
    mid = (x - hi).astype(BF).astype(F32)
    lo = x - hi - mid
    row = lax.broadcasted_iota(jnp.int32, (TAIL, LANES), 0)
    return jnp.where(row == 0, hi, jnp.where(row == 1, mid, jnp.where(row == 2, lo, 0.0))).astype(BF)


def join_rows(tail):
    return jnp.sum(tail.astype(F32), axis=0, keepdims=True)


def grads_kernel(bit_ref, rate_ref, k_ref, v_ref, w_ref, keep_ref, send_ref, dgu, gated, pushed):
    rows = k_ref.shape[0]
    tile = min(256, rows)
    wide = 2 * LANES
    for t in range(rows // tile):
        sl = pl.ds(t * tile, tile)
        k = k_ref[sl, :]
        rate = jnp.broadcast_to(rate_ref[0, :, sl], (LANES, tile)).T
        rate = jnp.concatenate([rate] * PER, axis=1)
        push = (rate * v_ref[sl, :].astype(F32)).astype(BF)
        pushed[sl, :] = push
        for j in range(FW // wide):
            cs = slice(j * wide, (j + 1) * wide)
            gate = mm(k, w_ref[0, 0, :, cs])
            up = mm(k, w_ref[0, 1, :, cs])
            back = lax.dot_general(push, w_ref[0, 2, cs, :], NT, preferred_element_type=F32)
            s = sigmoid(gate)
            gs = gate * s
            gated[sl, cs] = (gs * up).astype(BF)
            dgu[sl, cs] = (back * up * (s + gs * (1.0 - s))).astype(BF)
            dgu[sl, FW + j * wide : FW + (j + 1) * wide] = (back * gs).astype(BF)
    bit = bit_ref[0]
    tail = split_rows(jnp.broadcast_to(jnp.sum(rate_ref[0], axis=1, keepdims=True), (1, LANES)))
    keep_ref[pl.ds(HALF * FW, TAIL), :] = tail
    send_ref[pl.ds(HALF * FW, TAIL), :] = tail
    kt = k_ref[...].T
    gt = gated[...].T
    for b in range(BLOCKS // 2):
        if b * wide < 2 * FW:
            r = mm(kt, dgu[:, b * wide : (b + 1) * wide])
        else:
            r = mm(gt, pushed[:, b * wide - 2 * FW : (b + 1) * wide - 2 * FW])
        r = r.astype(BF)
        half, pos = (2 * b) // HALF, (2 * b) % HALF

        @pl.when(bit == half)
        def _():
            keep_ref[pl.ds(pos * FW, FW), :] = r[:, :LANES]
            keep_ref[pl.ds((pos + 1) * FW, FW), :] = r[:, LANES:]

        @pl.when(bit != half)
        def _():
            send_ref[pl.ds(pos * FW, FW), :] = r[:, :LANES]
            send_ref[pl.ds((pos + 1) * FW, FW), :] = r[:, LANES:]


def grads(h, bit, rate, keys, values, fast_weights):
    rows = keys.shape[0]
    shape = (HALF * FW + TAIL, LANES)
    out = jax.ShapeDtypeStruct(shape, BF)
    col = pl.BlockSpec((rows, FW), lambda i: (0, h))
    return pl.pallas_call(
        grads_kernel,
        grid=(1,),
        in_specs=[
            SMEM,
            pl.BlockSpec((1, 1, rows), lambda i: (h, 0, 0)),
            col,
            col,
            pl.BlockSpec((1, 3, FW, FW), lambda i: (h, 0, 0, 0)),
        ],
        out_specs=[full(shape), full(shape)],
        out_shape=[out, out],
        scratch_shapes=[
            pltpu.VMEM((rows, 2 * FW), BF),
            pltpu.VMEM((rows, FW), BF),
            pltpu.VMEM((rows, FW), BF),
        ],
        compiler_params=PARAMS,
        cost_estimate=cost(12 * rows * FW * FW, 4 * rows * FW + 12 * FW * FW, rows * FW),
    )(bit, rate, keys, values, fast_weights)


def split_kernel(bit_ref, keep_ref, other_ref, keep_out, send_out):
    n = THIRD * FW
    mine = pl.ds(pl.multiple_of(bit_ref[0] * n, n), n)
    theirs = pl.ds(pl.multiple_of((1 - bit_ref[0]) * n, n), n)
    keep_out[pl.ds(0, n), :] = keep_ref[mine, :] + other_ref[mine, :]
    send_out[pl.ds(0, n), :] = keep_ref[theirs, :] + other_ref[theirs, :]
    tail = pl.ds(HALF * FW, TAIL)
    rate = split_rows(join_rows(keep_ref[tail, :]) + join_rows(other_ref[tail, :]))
    keep_out[pl.ds(n, TAIL), :] = rate
    send_out[pl.ds(n, TAIL), :] = rate


def split(bit, keep, other):
    shape = (THIRD * FW + TAIL, LANES)
    out = jax.ShapeDtypeStruct(shape, BF)
    return pl.pallas_call(
        split_kernel,
        grid=(1,),
        in_specs=[SMEM, full(keep.shape), full(keep.shape)],
        out_specs=[full(shape), full(shape)],
        out_shape=[out, out],
        compiler_params=PARAMS,
        cost_estimate=cost(keep.size, 6 * keep.size),
    )(bit, keep, other)


def total_kernel(a_ref, b_ref, *rest):
    o_ref = rest[-1]
    n = THIRD * FW
    o_ref[pl.ds(0, n), :] = a_ref[pl.ds(0, n), :] + b_ref[pl.ds(0, n), :]
    tail = pl.ds(n, TAIL)
    o_ref[tail, :] = split_rows(join_rows(a_ref[tail, :]) + join_rows(b_ref[tail, :]))


def total(a, b, after):
    return pl.pallas_call(
        total_kernel,
        grid=(1,),
        in_specs=[full(a.shape), full(a.shape)] + [ANY] * len(after),
        out_specs=full(a.shape),
        out_shape=jax.ShapeDtypeStruct(a.shape, BF),
        compiler_params=PARAMS,
        cost_estimate=cost(a.size, 6 * a.size),
    )(a, b, *after)


def renorm_kernel(tokens_all, start_ref, base_ref, a_ref, b_ref, *rest):
    o_ref = rest[-1]
    tail = pl.ds(THIRD * FW, TAIL)
    rate_sum = join_rows(a_ref[tail, :]) + join_rows(b_ref[tail, :])
    step = base_rate / (math.sqrt(tokens_all) * (rate_sum / tokens_all))
    for i in range(THIRD):
        sl = pl.ds(i * FW, FW)
        pull = a_ref[sl, :].astype(F32) + b_ref[sl, :].astype(F32)
        at = start_ref[0] + i
        col = pl.ds(pl.multiple_of((at % PER) * LANES, LANES), LANES)
        base = base_ref[0, at // PER, :, col].astype(F32)
        updated = base + step * pull
        old = jnp.sqrt(jnp.sum(base * base, axis=0, keepdims=True) + 1e-06)
        new = jnp.sqrt(jnp.sum(updated * updated, axis=0, keepdims=True) + 1e-06)
        o_ref[i] = (updated * (old / new)).astype(BF)


def renorm(h, start, tokens_all, fast_weights, a, b, after):
    shape = (THIRD, FW, LANES)
    return pl.pallas_call(
        functools.partial(renorm_kernel, tokens_all),
        grid=(1,),
        in_specs=[
            SMEM,
            pl.BlockSpec((1, 3, FW, FW), lambda i: (h, 0, 0, 0)),
            full(a.shape),
            full(a.shape),
        ]
        + [ANY] * len(after),
        out_specs=full(shape),
        out_shape=jax.ShapeDtypeStruct(shape, BF),
        compiler_params=PARAMS,
        cost_estimate=cost(10 * a.size, 6 * FW * FW + 6 * a.size),
    )(start, fast_weights, a, b, *after)


def attn_kernel(first_ref, q_ref, k_ref, v_ref, rk_ref, rv_ref, *rest):
    o_ref = rest[-1]
    rows = q_ref.shape[0]
    w, d = WINDOW, HEAD_DIM
    row = lax.broadcasted_iota(jnp.int32, (w, w), 0)
    col = lax.broadcasted_iota(jnp.int32, (w, w), 1)
    own = col <= row
    factor = math.log2(math.e) / math.sqrt(d)
    has_prev = first_ref[0] == 0
    ones = jnp.ones((2 * w, LANES), BF)
    for h in range(q_ref.shape[1] // d):
        cs = slice(h * d, (h + 1) * d)
        for b in range(rows // w):
            sl = pl.ds(b * w, w)
            if b == 0:
                k2 = jnp.concatenate([rk_ref[:, cs], k_ref[sl, cs]], axis=0)
                v2 = jnp.concatenate([rv_ref[:, cs], v_ref[sl, cs]], axis=0)
            else:
                both = pl.ds((b - 1) * w, 2 * w)
                k2, v2 = k_ref[both, cs], v_ref[both, cs]
            s2 = lax.dot_general(q_ref[sl, cs], k2, NT, preferred_element_type=F32)
            prev = s2[:, :w]
            if b == 0:
                prev = jnp.where(has_prev, prev, -1e30)
            s = jnp.where(own, s2[:, w:], prev)
            e = jnp.exp2((s - jnp.max(s, axis=1, keepdims=True)) * factor).astype(BF)
            zero = jnp.zeros_like(e)
            e2 = jnp.concatenate([jnp.where(own, zero, e), jnp.where(own, e, zero)], axis=1)
            o = mm(e2, jnp.concatenate([v2, ones], axis=1))
            o_ref[sl, cs] = (o[:, :d] / o[:, d:]).astype(o_ref.dtype)


def attention(piece, width, first, query, keys, values, rim_keys, rim_values, after):
    rows = query.shape[0]
    col = pl.BlockSpec((rows, width), lambda i: (0, piece))
    rim = pl.BlockSpec((WINDOW, width), lambda i: (0, piece))
    return pl.pallas_call(
        attn_kernel,
        grid=(1,),
        in_specs=[SMEM, col, col, col, rim, rim] + [ANY] * len(after),
        out_specs=full((rows, width)),
        out_shape=jax.ShapeDtypeStruct((rows, width), BF),
        compiler_params=PARAMS,
        cost_estimate=cost(
            8 * rows * width * WINDOW, 8 * rows * width, rows * width // HEAD_DIM * WINDOW
        ),
    )(first, query, keys, values, rim_keys, rim_values, *after)


def apply_tile(q, att, w_ref, act):
    wide = 2 * LANES
    for j in range(FW // wide):
        cs = slice(j * wide, (j + 1) * wide)
        gate = mm(q, w_ref[0, :, cs])
        up = mm(q, w_ref[1, :, cs])
        act[:, cs] = (gate * sigmoid(gate) * up).astype(BF)
    y = mm(act[...], w_ref[2])
    y = y * lax.rsqrt(jnp.mean(y * y, axis=1, keepdims=True) + 1e-06)
    return (att.astype(F32) + y).astype(BF)


def joined(refs):
    return jnp.concatenate([r[...] for r in refs], axis=1)


def apply_first_kernel(pieces, ids_ref, q_ref, *rest):
    att_refs, rest = rest[:pieces], rest[pieces:]
    mine_ref, mate_ref = rest[:2]
    o_ref, nw_ref, act, sem = rest[-4:]

    @pl.when(pl.program_id(0) == 0)
    def _():
        def each(do):
            for b in range(BLOCKS):
                half, third, i = b // HALF, (b % HALF) // THIRD, b % THIRD
                slot = jnp.bitwise_xor(ids_ref[1], third)
                dst = nw_ref.at[b // PER, :, pl.ds((b % PER) * LANES, LANES)]
                own = ids_ref[0] == half

                @pl.when(own)
                def _():
                    do(pltpu.make_async_copy(mine_ref.at[slot, i], dst, sem.at[b]))

                @pl.when(jnp.logical_not(own))
                def _():
                    do(pltpu.make_async_copy(mate_ref.at[slot, i], dst, sem.at[b]))

        each(lambda c: c.start())
        each(lambda c: c.wait())

    o_ref[...] = apply_tile(q_ref[...], joined(att_refs), nw_ref, act)


def apply_next_kernel(pieces, q_ref, *rest):
    nw_ref, o_ref, act = rest[pieces:]
    o_ref[...] = apply_tile(q_ref[...], joined(rest[:pieces]), nw_ref, act)


def apply_cost(rows):
    return cost(6 * rows * FW * FW, 6 * rows * FW + 6 * FW * FW, rows * FW)


def apply_first(h, ids, query, attended, mine, mate, rows, after):
    tile = min(256, rows)
    att = pl.BlockSpec((tile, attended[0].shape[1]), lambda r: (r, 0))
    whole = (3, FW, FW)
    return pl.pallas_call(
        functools.partial(apply_first_kernel, len(attended)),
        grid=(rows // tile,),
        in_specs=[SMEM, pl.BlockSpec((tile, FW), lambda r: (r, h))]
        + [att] * len(attended)
        + [ANY] * (2 + len(after)),
        out_specs=[pl.BlockSpec((tile, FW), lambda r: (r, 0)), full(whole)],
        out_shape=[jax.ShapeDtypeStruct((rows, FW), BF), jax.ShapeDtypeStruct(whole, BF)],
        scratch_shapes=[pltpu.VMEM((tile, FW), BF), pltpu.SemaphoreType.DMA((BLOCKS,))],
        compiler_params=PARAMS,
        cost_estimate=apply_cost(rows),
    )(ids, query, *attended, mine, mate, *after)


def apply_next(h, query, attended, weights, start):
    rows = query.shape[0] - start
    tile = min(256, rows)
    off = start // tile
    att = pl.BlockSpec((tile, attended[0].shape[1]), lambda r: (r + off, 0))
    return pl.pallas_call(
        functools.partial(apply_next_kernel, len(attended)),
        grid=(rows // tile,),
        in_specs=[pl.BlockSpec((tile, FW), lambda r: (r + off, h))]
        + [att] * len(attended)
        + [full(weights.shape)],
        out_specs=pl.BlockSpec((tile, FW), lambda r: (r, 0)),
        out_shape=jax.ShapeDtypeStruct((rows, FW), BF),
        scratch_shapes=[pltpu.VMEM((tile, FW), BF)],
        compiler_params=PARAMS,
        cost_estimate=apply_cost(rows),
    )(query, *attended, weights)


def partial_kernel(heads, *refs):
    x_refs, w_ref, o_ref = refs[:heads], refs[heads], refs[heads + 1]
    for j in range(w_ref.shape[1] // FW):
        cs = pl.ds(j * FW, FW)
        o_ref[0, :, cs] = mm(joined(x_refs), w_ref[:, cs]).astype(BF)


def partials(merged, out_weight, groups):
    rows = merged[0].shape[0]
    depth, width = out_weight.shape[0], out_weight.shape[1] // groups
    return pl.pallas_call(
        functools.partial(partial_kernel, len(merged)),
        grid=(groups,),
        in_specs=[full(m.shape) for m in merged]
        + [pl.BlockSpec((depth, width), lambda d: (0, d))],
        out_specs=pl.BlockSpec((1, rows, width), lambda d: (d, 0, 0)),
        out_shape=jax.ShapeDtypeStruct((groups, rows, width), BF),
        compiler_params=PARAMS,
        cost_estimate=cost(
            2 * rows * depth * width * groups, 2 * (rows * width + depth * width) * groups
        ),
    )(*merged, out_weight)


def ring_kernel(ids_ref, right_ref, left_ref, pr_ref, pl_ref, ro_ref, lo_ref):
    zero = jnp.zeros((), BF)
    ro_ref[...] = right_ref[...] + jnp.where(ids_ref[2] > 0, pr_ref[0], zero)
    lo_ref[...] = left_ref[...] + jnp.where(ids_ref[3] > 0, pl_ref[0], zero)


def ring_step(ids, wave, right, left, partial):
    rows, width = right.shape
    out = jax.ShapeDtypeStruct(right.shape, BF)
    own = pl.BlockSpec((rows, width), lambda i, s: (0, 0))
    return pl.pallas_call(
        ring_kernel,
        grid_spec=pltpu.PrefetchScalarGridSpec(
            num_scalar_prefetch=1,
            grid=(1,),
            in_specs=[
                own,
                own,
                pl.BlockSpec((1, rows, width), lambda i, s: (s[0], 0, wave)),
                pl.BlockSpec((1, rows, width), lambda i, s: (s[1], 0, wave)),
            ],
            out_specs=[own, own],
        ),
        out_shape=[out, out],
        compiler_params=PARAMS,
        cost_estimate=cost(2 * right.size, 12 * right.size),
    )(ids, right, left, partial, partial)


def gathered_kernel(n, heads, parts, ids_ref, pos_ref, *refs):
    own_refs, refs = refs[:heads], refs[heads:]
    rights, refs = refs[: (n - 1) * heads], refs[(n - 1) * heads :]
    lefts, refs = refs[: (n - 1) * heads], refs[(n - 1) * heads :]
    w_ref, near_ref, far_ref, o_ref, x, cols, acc, xsem, wsem = refs
    share = near_ref.shape[2]
    near = near_ref.shape[0]

    def each(do):
        for t in range(n - 1):
            for h in range(heads):
                dst = x.at[t, :, pl.ds(h * FW, FW)]
                sem = xsem.at[t, h]
                from_left = ids_ref[t] > 0

                @pl.when(from_left)
                def _():
                    do(pltpu.make_async_copy(rights[t * heads + h], dst, sem))

                @pl.when(jnp.logical_not(from_left))
                def _():
                    do(pltpu.make_async_copy(lefts[(n - 2 - t) * heads + h], dst, sem))

        for p in range(parts):
            src = near_ref.at[p] if p < near else far_ref.at[p - near]
            to = pl.ds(pl.multiple_of(pos_ref[p] * share, share), share)
            do(pltpu.make_async_copy(src, cols.at[:, to, :], wsem.at[p]))

    each(lambda c: c.start())
    acc[...] = mm(joined(own_refs), w_ref[...])
    each(lambda c: c.wait())
    for t in range(n - 1):
        acc[...] += mm(x[t], cols[t])
    o_ref[...] = acc[...].astype(BF)


def gathered(z, from_left, positions, merged, rights, lefts, out_weight, near, far, rows_all):
    n, heads, parts = len(rights) + 1, len(merged), near.shape[0] + far.shape[0]
    rows, feats = merged[0].shape[0], out_weight.shape[0]
    width = out_weight.shape[1] // n
    ids = jnp.concatenate([from_left, z[None]])
    flat = lambda xs: [x for step in xs for x in step]
    return pl.pallas_call(
        functools.partial(gathered_kernel, n, heads, parts),
        grid_spec=pltpu.PrefetchScalarGridSpec(
            num_scalar_prefetch=2,
            grid=(1,),
            in_specs=[full(m.shape) for m in merged]
            + [ANY] * (2 * (n - 1) * heads)
            + [pl.BlockSpec((feats, width), lambda i, s, p: (0, s[n - 1])), ANY, ANY],
            out_specs=pl.BlockSpec((rows, width), lambda i, s, p: (0, 0)),
            scratch_shapes=[
                pltpu.VMEM((n - 1, rows, feats), BF),
                pltpu.VMEM((n - 1, feats, width), BF),
                pltpu.VMEM((rows, width), F32),
                pltpu.SemaphoreType.DMA((n - 1, heads)),
                pltpu.SemaphoreType.DMA((parts,)),
            ],
        ),
        out_shape=jax.ShapeDtypeStruct((rows_all, width), BF),
        compiler_params=PARAMS,
        cost_estimate=cost(2 * rows * feats * n * width, 2 * n * (rows * feats + feats * width)),
    )(ids, positions, *merged, *flat(rights), *flat(lefts), out_weight, near, far)


def finish_kernel(ids_ref, out_ref, p_ref, right_ref, left_ref, o_ref):
    o_ref[...] = (
        p_ref[0].astype(F32) + right_ref[...].astype(F32) + left_ref[...].astype(F32)
    ).astype(BF)


def finish(z, wave, out, partial, right, left):
    rows, width = right.shape
    own = pl.BlockSpec((rows, width), lambda i, s: (0, 0))
    off = out.shape[0] // rows - 1
    return pl.pallas_call(
        finish_kernel,
        grid_spec=pltpu.PrefetchScalarGridSpec(
            num_scalar_prefetch=1,
            grid=(1,),
            in_specs=[
                ANY,
                pl.BlockSpec((1, rows, width), lambda i, s: (s[0], 0, wave)),
                own,
                own,
            ],
            out_specs=pl.BlockSpec((rows, width), lambda i, s: (off, wave)),
        ),
        out_shape=jax.ShapeDtypeStruct(out.shape, BF),
        input_output_aliases={1: 0},
        compiler_params=PARAMS,
        cost_estimate=cost(2 * right.size, 8 * right.size),
    )(z[None], out, partial, right, left)


def scalars(*xs):
    return jnp.stack([jnp.asarray(x, jnp.int32) for x in xs])


def shards(query, keys, values, lr_code, fast_weights, out_weight):
    rows, feats = query.shape
    contexts, groups = lax.axis_size("ctx"), lax.axis_size("head")
    c, z = lax.axis_index("ctx"), lax.axis_index("head")
    tokens_all = rows * contexts
    heads = fast_weights.shape[0]
    bits = [1 << i for i in range(contexts.bit_length() - 1)]
    bit_of = {b: (c // b) % 2 for b in bits}

    rim_keys = shift(keys[rows - WINDOW :], "ctx", 1)
    rim_values = shift(values[rows - WINDOW :], "ctx", 1)

    share, width = feats // contexts, out_weight.shape[1] // groups

    def block_for(s):
        return lax.dynamic_slice(
            out_weight, (c * share, ((z + s) % groups) * width), (share, width)
        )

    strips = [rotate(block_for(s), "head", s) for s in range(1, groups)]

    rate = lr_code.T.astype(F32)[:, None, :] * 2.0 ** (-14)
    order = [[bits[1 + h % 2]] for h in range(heads)]
    order = [o + [b for b in bits[1:] if b != o[0]] for o in order]
    core = scalars(bit_of[1])
    keep, other = [], []
    for h in range(heads):
        k, s = grads(h, core, rate, keys, values, fast_weights)
        keep.append(k)
        other.append(swap(s, 1))
    split_up = [split(scalars(bit_of[order[h][0]]), keep[h], other[h]) for h in range(heads)]
    away = [swap(split_up[h][1], order[h][0]) for h in range(heads)]

    per_head = 2
    piece_width = FW // per_head
    pieces = []

    def attend(after):
        pieces.append(
            attention(
                len(pieces),
                piece_width,
                scalars(c == 0),
                query,
                keys,
                values,
                rim_keys,
                rim_values,
                after,
            )
        )
        return pieces[-1]

    att = attend([split_up[h][1] for h in range(heads)])
    pull, far = [], []
    for h in range(heads):
        p = total(split_up[h][0], away[h], [att])
        for b in order[h][1:-1]:
            p = total(p, swap(p, b), [])
        pull.append(p)
        far.append(swap(p, order[h][-1]))
        att = attend([p])
    new = []
    for h in range(heads):
        start = scalars(bit_of[1] * HALF + bit_of[order[h][0]] * THIRD)
        after = [att] + (strips if h == 0 else [])
        new.append(renorm(h, start, tokens_all, fast_weights, pull[h], far[h], after))
    while len(pieces) < per_head * heads:
        att = attend(new)
    mine = [jnp.stack([new[h], swap(new[h], order[h][0])]) for h in range(heads)]
    mate = [swap(mine[h], 1) for h in range(heads)]

    cut = rows // 2
    merged, weights = [], []
    for h in range(heads):
        ids = scalars(bit_of[1], bit_of[order[h][0]])
        own = pieces[h * per_head : (h + 1) * per_head]
        m, w = apply_first(h, ids, query, own, mine[h], mate[h], cut, [att])
        merged.append(m)
        weights.append(w)
    to_right = [[shift(m, "head", 1) for m in merged]]
    to_left = [[shift(m, "head", -1) for m in merged]]
    rest = [
        apply_next(h, query, pieces[h * per_head : (h + 1) * per_head], weights[h], cut)
        for h in range(heads)
    ]
    partial = partials(rest, out_weight, groups)
    for t in range(1, groups):
        ids = scalars((z - t) % groups, (z + t) % groups, t > z, t > groups - 1 - z)
        sent = [
            ring_step(ids, h, to_right[-1][h], to_left[-1][h], partial) for h in range(heads)
        ]
        to_right.append([shift(s[0], "head", 1) for s in sent])
        to_left.append([shift(s[1], "head", -1) for s in sent])

    near = jnp.stack(strips)[None]
    places = [0]
    for b in reversed(bits[1:]):
        near = jnp.concatenate([near, swap(near, b)])
        places = places + [p ^ b for p in places]
    other_half = swap(near, 1)
    places = places + [p ^ 1 for p in places]
    positions = jnp.bitwise_xor(c, jnp.array(places, jnp.int32))
    from_left = scalars(*[t <= z - 1 for t in range(groups - 1)])
    out = gathered(
        z, from_left, positions, merged, to_right[:-1], to_left[:-1], out_weight, near, other_half, rows
    )
    for h in range(heads):
        out = finish(z, h, out, partial, to_right[-1][h], to_left[-1][h])
    return (out, jnp.stack(weights))


def solution(mesh):
    placed = (
        P("ctx", "head"),
        P("ctx", "head"),
        P("ctx", "head"),
        P("ctx", "head"),
        P("head", None, None, None),
        P("head", None),
    )
    return jax.shard_map(
        shards,
        mesh=mesh,
        in_specs=placed,
        out_specs=(P("ctx", "head"), P("head", None, None, None)),
        check_vma=False,
    )
```

time: 415 us -> 273 us (0.66); the launches traced: 409 us -> 272 us
  Pallas kernels: 0 us -> 109 us
  local copies, waits for them, and re-layouts: 112 us -> 15.9 us
  waiting for transfers between devices: 143 us -> 59.5 us
  matrix products: 69.7 us -> 0 us
  starting transfers between devices: 7.9 us -> 76.1 us
  other arithmetic: 48.8 us -> 10.1 us
  between operations: 14.2 us -> 1.17 us
  blocking collectives: 12.5 us -> 0 us
    reduce_scatter x1 -> x0, waiting for transfers between devices: 142 us -> none  [shards(): lax.psum_scatter(partial_out.astype(jnp.bfloat16), 'head', scatter_dimens...]
    pallas_call x0 -> x26, Pallas kernels: none -> 109 us  [the longest x6 19.7 us: ring_step(): pl.pallas_call(ring_kernel, grid_spec=pltpu.PrefetchScalarGridSpec(num_sc...]
    dynamic_update_slice x4 -> x0, local copies, waits for them, and re-layouts: 80 us -> none  [attention(): lax.map(one_block, jnp.arange(tok_rows // block_rows, dtype=jnp.int32))]
    dot_general x21 -> x0, matrix products: 69.7 us -> none  [the longest x2 16.3 us: one_block(): jnp.einsum('qhd,khd->hqk', q_block, k_block, preferred_element_type=jnp.f...]
    ppermute x2 -> x34, starting transfers between devices: 7.82 us -> 76.1 us  [the longest x18 48.5 us: shift(): lax.ppermute(block, axis, [(i, i + distance) for i in range(n) if 0 <= i...]
    ppermute x2 -> x34, waiting for transfers between devices: 0.01 us -> 59.5 us  [the longest x13 30.8 us: swap(): return lax.ppermute(block, 'ctx', [(i, i ^ bit) for i in range(n)])]
    sub x2 -> x0, other arithmetic: 32.5 us -> none  [one_block(): exps = jnp.exp(scores - top_score)]
    psum x1 -> x0, blocking collectives: 12.5 us -> none  [shards(): rate_sum = lax.psum(jnp.sum(rate, axis=0), 'ctx')]
  transfers between devices with their start and end apart: 4 -> 34, of which waited for: 1 -> 10; matrix products, arithmetic and copies ran while one was open for 46% -> 5% of each run, Pallas kernels for 0% -> 39%
where the time goes in v2:
time: 273 us; the launch traced here: 272 us
  Pallas kernels  109 us (40%)
  starting transfers between devices  76.1 us (28%)
  waiting for transfers between devices  59.5 us (22%)
  local copies, waits for them, and re-layouts  15.9 us (6%)
  other arithmetic  10.1 us (4%)
    ppermute x18, starting transfers between devices, shift(): lax.ppermute(block, axis, [(i, i + distance) for i in range(n) if 0 <= i...  48.5 us
    ppermute x13, waiting for transfers between devices, swap(): return lax.ppermute(block, 'ctx', [(i, i ^ bit) for i in range(n)])  30.8 us
    ppermute x13, starting transfers between devices, swap(): return lax.ppermute(block, 'ctx', [(i, i ^ bit) for i in range(n)])  20.5 us
    pallas_call x6, Pallas kernels, ring_step(): pl.pallas_call(ring_kernel, grid_spec=pltpu.PrefetchScalarGridSpec(num_sc...  19.7 us
    pallas_call x2, Pallas kernels, grads(): pl.pallas_call(grads_kernel, grid=(1,), in_specs=[SMEM, pl.BlockSpec((1,...  18.5 us
    ppermute x3, waiting for transfers between devices, rotate(): lax.ppermute(block, axis, [(i, (i + distance) % n) for i in range(n)])  15.8 us
    pallas_call x4, Pallas kernels, attention(): pl.pallas_call(attn_kernel, grid=(1,), in_specs=[SMEM, col, col, col, rim...  15.1 us
    ppermute x18, waiting for transfers between devices, shift(): lax.ppermute(block, axis, [(i, i + distance) for i in range(n) if 0 <= i...  12.9 us
  transfers between devices with their start and end apart: 34, of which 10 were waited for; matrix products, arithmetic and copies ran while one was open for 5% of the time, Pallas kernels for 39%

profile of v2, /device:TPU:0, one launch (start us, length us, event | category | flops | bytes accessed | tf_op | source)
XLA Modules:
  0.0 272.0 jit_solution(18307711064365275574)
XLA Ops:
  1.9 3.1 %collective-permute-start.7 = (bf16[128,1024]{1,0:T(8,128)(2,1)S(1)}, bf16[128,1024]{1,0:T(8,128)(2,1)S(1)}, u32[]{:S(2)}, u32[]{:S(2)}) collective-permute-start(bf16[128,1024]{1,0:T(8,128)(2,1)S(1)} %get-tuple-element.52), channel_id=1, source_target_pairs={{0,1},{1,2},{2,3},{3,0},{4,5},{5,6},{6,7},{7,4},{8,9},{9,10},{10,1... | collective-permute-start | bytes 786440 | tf_op jit(solution)/shard_map/ppermute | solution.py:43
  4.9 2.6 collective-permute-start.8
  7.5 1.3 collective-permute-start.9
  8.9 5.4 %collective-permute-done.7.rest_1_ = bf16[128,1024]{1,0:T(8,128)(2,1)S(1)} collective-permute-done((bf16[128,1024]{1,0:T(8,128)(2,1)S(1)}, bf16[128,1024]{1,0:T(8,128)(2,1)S(1)}, u32[]{:S(2)}, u32[]{:S(2)}) %collective-permute-start.7) | collective-permute-done | bytes 262176 | tf_op jit(solution)/shard_map/ppermute | solution.py:43
  14.2 10.4 %collective-permute-done.8.rest_2_ = bf16[128,1024]{1,0:T(8,128)(2,1)S(1)} collective-permute-done((bf16[128,1024]{1,0:T(8,128)(2,1)S(1)}, bf16[128,1024]{1,0:T(8,128)(2,1)S(1)}, u32[]{:S(2)}, u32[]{:S(2)}) %collective-permute-start.8) | collective-permute-done | bytes 262176 | tf_op jit(solution)/shard_map/ppermute | solution.py:43
  25.5 1.6 collective-permute-start.27
  27.7 9.2 %shard_map.86 = (bf16[3088,128]{1,0:T(8,128)(2,1)}, bf16[3088,128]{1,0:T(8,128)(2,1)}) custom-call(s32[1]{0:T(128)} %bitcast.4.bit_ref, f32[2,1,1024]{2,1,0:T(1,128)} %mul.37.rate_ref, bf16[1024,1024]{1,0:T(8,128)(2,1)} %k_ref.11, bf16[1024,1024]{1,0:T(8,128)(2,1)} %v_ref.11, bf16[2,3,512,512]{3,2,1,0:T(8,128)(2,1)} %base_ref.3), custom_call_target="tpu_custom_call" | custom-call | flops 3221225472 | bytes 5242880 | tf_op jit(solution)/shard_map/pallas_call | solution.py:128
  37.0 9.3 %shard_map.88 = (bf16[3088,128]{1,0:T(8,128)(2,1)}, bf16[3088,128]{1,0:T(8,128)(2,1)}) custom-call(s32[1]{0:T(128)} %bitcast.4.bit_ref, f32[2,1,1024]{2,1,0:T(1,128)} %mul.37.rate_ref, bf16[1024,1024]{1,0:T(8,128)(2,1)} %k_ref.11, bf16[1024,1024]{1,0:T(8,128)(2,1)} %v_ref.11, bf16[2,3,512,512]{3,2,1,0:T(8,128)(2,1)} %base_ref.3), custom_call_target="tpu_custom_call" | custom-call | flops 3221225472 | bytes 5242880 | tf_op jit(solution)/shard_map/pallas_call | solution.py:128
  46.9 1.6 collective-permute-start.28
  48.5 1.9 slice.6
  50.3 1.7 collective-permute-start
  52.0 1.9 slice.7
  53.9 3.0 %collective-permute-start.1 = (bf16[256,1024]{1,0:T(8,128)(2,1)}, bf16[256,1024]{1,0:T(8,128)(2,1)S(1)}, u32[]{:S(2)}, u32[]{:S(2)}) collective-permute-start(bf16[256,1024]{1,0:T(8,128)(2,1)} %slice.7), channel_id=1, source_target_pairs={{0,4},{4,8},{8,12},{12,16},{16,20},{20,24},{24,28},{1,5},{5,9},{9,... | collective-permute-start | bytes 1572872 | tf_op jit(solution)/shard_map/ppermute | solution.py:38
  57.0 2.6 shard_map.87
  59.5 1.4 collective-permute-start.4
  60.9 2.5 shard_map.89
  64.4 3.8 %shard_map.90.rest_0_ = bf16[1024,256]{1,0:T(8,128)(2,1)} custom-call(s32[1]{0:T(128)} %bitcast.6.first_ref, bf16[1024,1024]{1,0:T(8,128)(2,1)} %q_ref.15, bf16[1024,1024]{1,0:T(8,128)(2,1)} %k_ref.11, bf16[1024,1024]{1,0:T(8,128)(2,1)} %v_ref.11, bf16[256,1024]{1,0:T(8,128)(2,1)} %copy-done.1, bf16[256,1024]{1,0:T(8,128)(2,1)} %copy-done.2, ...), custom_call_target="tpu_custom_call" | custom-call | flops 536870912 | bytes 2097152 | tf_op jit(solution)/shard_map/pallas_call | solution.py:268
  68.2 24.6 %collective-permute-done.4.b_ref = bf16[1552,128]{1,0:T(8,128)(2,1)S(1)} collective-permute-done((bf16[1552,128]{1,0:T(8,128)(2,1)}, bf16[1552,128]{1,0:T(8,128)(2,1)S(1)}, u32[]{:S(2)}, u32[]{:S(2)}) %collective-permute-start.4) | collective-permute-done | bytes 397344 | tf_op jit(solution)/shard_map/ppermute | solution.py:48
  93.5 2.0 shard_map.91.rest_0_.a_ref
  95.5 12.1 %collective-permute-start.5 = (bf16[1552,128]{1,0:T(8,128)(2,1)}, bf16[1552,128]{1,0:T(8,128)(2,1)S(1)}, u32[]{:S(2)}, u32[]{:S(2)}) collective-permute-start(bf16[1552,128]{1,0:T(8,128)(2,1)} %shard_map.91.rest_0_.a_ref), channel_id=1, source_target_pairs={{0,16},{4,20},{8,24},{12,28},{16,0},{20,4},{24,8},{28,12},{1,17},{... | collective-permute-start | bytes 1191944 | tf_op jit(solution)/shard_map/ppermute | solution.py:48
  107.5 3.8 %shard_map.92.rest_0_.rest_1_ = bf16[1024,256]{1,0:T(8,128)(2,1)} custom-call(s32[1]{0:T(128)} %bitcast.6.first_ref, bf16[1024,1024]{1,0:T(8,128)(2,1)} %q_ref.15, bf16[1024,1024]{1,0:T(8,128)(2,1)} %k_ref.11, bf16[1024,1024]{1,0:T(8,128)(2,1)} %v_ref.11, bf16[256,1024]{1,0:T(8,128)(2,1)} %copy-done.1, bf16[256,1024]{1,0:T(8,128)(2,1)} %copy-done.2, ...), custom_call_target="tpu_custom_call" | custom-call | flops 536870912 | bytes 2097152 | tf_op jit(solution)/shard_map/pallas_call | solution.py:268
  112.0 2.0 shard_map.93.rest_0_.a_ref
  114.6 3.8 %shard_map.94.rest_0_ = bf16[1024,256]{1,0:T(8,128)(2,1)} custom-call(s32[1]{0:T(128)} %bitcast.6.first_ref, bf16[1024,1024]{1,0:T(8,128)(2,1)} %q_ref.15, bf16[1024,1024]{1,0:T(8,128)(2,1)} %k_ref.11, bf16[1024,1024]{1,0:T(8,128)(2,1)} %v_ref.11, bf16[256,1024]{1,0:T(8,128)(2,1)} %copy-done.1, bf16[256,1024]{1,0:T(8,128)(2,1)} %copy-done.2, ...), custom_call_target="tpu_custom_call" | custom-call | flops 536870912 | bytes 2097152 | tf_op jit(solution)/shard_map/pallas_call | solution.py:268
  119.1 2.7 %shard_map.95.rest_0_ = bf16[3,512,128]{2,1,0:T(8,128)(2,1)} custom-call(s32[1]{0:T(128)} %bitcast.9.start_ref, bf16[2,3,512,512]{3,2,1,0:T(8,128)(2,1)} %base_ref.3, bf16[1552,128]{1,0:T(8,128)(2,1)} %shard_map.91.rest_0_.a_ref, bf16[1552,128]{1,0:T(8,128)(2,1)} %copy-done.22, bf16[1024,256]{1,0:T(8,128)(2,1)} %shard_map.94.rest_0_, ...), custom_call_target="tpu_custom_call" | custom-call | flops 1986560 | bytes 2764800 | tf_op jit(solution)/shard_map/pallas_call | solution.py:215
  121.8 1.5 collective-permute-start.10
  124.7 2.9 %shard_map.96.rest_1_ = bf16[3,512,128]{2,1,0:T(8,128)(2,1)} custom-call(s32[1]{0:T(128)} %bitcast.12.start_ref, bf16[2,3,512,512]{3,2,1,0:T(8,128)(2,1)} %base_ref.3, bf16[1552,128]{1,0:T(8,128)(2,1)} %shard_map.93.rest_0_.a_ref, bf16[1552,128]{1,0:T(8,128)(2,1)} %copy-done.21, bf16[1024,256]{1,0:T(8,128)(2,1)} %shard_map.94.rest_0_), custom_call_target="tpu_custom_call" | custom-call | flops 1986560 | bytes 2764800 | tf_op jit(solution)/shard_map/pallas_call | solution.py:215
  127.5 1.3 collective-permute-start.13
  128.8 1.7 pad_maximum_fusion.refs_15_
  130.6 1.4 collective-permute-done.10
  133.0 4.2 %collective-permute-done.13 = bf16[3,512,128]{2,1,0:T(8,128)(2,1)S(1)} collective-permute-done((bf16[3,512,128]{2,1,0:T(8,128)(2,1)}, bf16[3,512,128]{2,1,0:T(8,128)(2,1)S(1)}, u32[]{:S(2)}, u32[]{:S(2)}) %collective-permute-start.13) | collective-permute-done | bytes 393248 | tf_op jit(solution)/shard_map/ppermute | solution.py:48
  140.1 3.8 %shard_map.97.rest_4_.rest_1_ = bf16[1024,256]{1,0:T(8,128)(2,1)} custom-call(s32[1]{0:T(128)} %bitcast.6.first_ref, bf16[1024,1024]{1,0:T(8,128)(2,1)} %q_ref.15, bf16[1024,1024]{1,0:T(8,128)(2,1)} %k_ref.11, bf16[1024,1024]{1,0:T(8,128)(2,1)} %v_ref.11, bf16[256,1024]{1,0:T(8,128)(2,1)} %copy-done.1, bf16[256,1024]{1,0:T(8,128)(2,1)} %copy-done.2, ...), custom_call_target="tpu_custom_call" | custom-call | flops 536870912 | bytes 2097152 | tf_op jit(solution)/shard_map/pallas_call | solution.py:268
  143.9 4.8 %shard_map.98 = (bf16[512,512]{1,0:T(8,128)(2,1)}, bf16[3,512,512]{2,1,0:T(8,128)(2,1)}) custom-call(s32[2]{0:T(128)} %pad_add_fusion.1.ids_ref, bf16[1024,1024]{1,0:T(8,128)(2,1)} %q_ref.15, bf16[1024,256]{1,0:T(8,128)(2,1)} %shard_map.90.rest_0_, bf16[1024,256]{1,0:T(8,128)(2,1)} %shard_map.92.rest_0_.rest_1_, ...), custom_call_target="tpu_custom_call" | custom-call | flops 805306368 | bytes 3145728 | tf_op jit(solution)/shard_map/pallas_call | solution.py:338
  148.7 7.9 %collective-permute-start.15 = (bf16[512,512]{1,0:T(8,128)(2,1)}, bf16[512,512]{1,0:T(8,128)(2,1)S(1)}, u32[]{:S(2)}, u32[]{:S(2)}) collective-permute-start(bf16[512,512]{1,0:T(8,128)(2,1)} %get-tuple-element.34.refs_0_), channel_id=1, source_target_pairs={{0,1},{1,2},{2,3},{4,5},{5,6},{6,7},{8,9},{9,10},{10,11},{12,13},{... | collective-permute-start | bytes 1572872 | tf_op jit(solution)/shard_map/ppermute | solution.py:38
  156.6 1.3 collective-permute-start.17
  157.9 4.8 %shard_map.99 = (bf16[512,512]{1,0:T(8,128)(2,1)}, bf16[3,512,512]{2,1,0:T(8,128)(2,1)}) custom-call(s32[2]{0:T(128)} %pad_add_fusion.2.ids_ref, bf16[1024,1024]{1,0:T(8,128)(2,1)} %q_ref.15, bf16[1024,256]{1,0:T(8,128)(2,1)} %shard_map.94.rest_0_, bf16[1024,256]{1,0:T(8,128)(2,1)} %shard_map.97.rest_4_.rest_1_, ...), custom_call_target="tpu_custom_call" | custom-call | flops 805306368 | bytes 3145728 | tf_op jit(solution)/shard_map/pallas_call | solution.py:338
  162.7 4.6 %collective-permute-start.16 = (bf16[512,512]{1,0:T(8,128)(2,1)}, bf16[512,512]{1,0:T(8,128)(2,1)S(1)}, u32[]{:S(2)}, u32[]{:S(2)}) collective-permute-start(bf16[512,512]{1,0:T(8,128)(2,1)} %get-tuple-element.35.refs_1_), channel_id=1, source_target_pairs={{0,1},{1,2},{2,3},{4,5},{5,6},{6,7},{8,9},{9,10},{10,11},{12,13},{... | collective-permute-start | bytes 1572872 | tf_op jit(solution)/shard_map/ppermute | solution.py:38
  167.3 1.5 collective-permute-start.19
  168.9 3.8 %shard_map.100.refs_0_ = bf16[512,512]{1,0:T(8,128)(2,1)} custom-call(bf16[1024,1024]{1,0:T(8,128)(2,1)} %q_ref.15, bf16[1024,256]{1,0:T(8,128)(2,1)} %shard_map.90.rest_0_, bf16[1024,256]{1,0:T(8,128)(2,1)} %shard_map.92.rest_0_.rest_1_, bf16[3,512,512]{2,1,0:T(8,128)(2,1)} %get-tuple-element.36.rest_2_), custom_call_target="tpu_custom_call" | custom-call | flops 805306368 | bytes 3145728 | tf_op jit(solution)/shard_map/pallas_call | solution.py:357
  172.6 3.8 %shard_map.101.refs_1_ = bf16[512,512]{1,0:T(8,128)(2,1)} custom-call(bf16[1024,1024]{1,0:T(8,128)(2,1)} %q_ref.15, bf16[1024,256]{1,0:T(8,128)(2,1)} %shard_map.94.rest_0_, bf16[1024,256]{1,0:T(8,128)(2,1)} %shard_map.97.rest_4_.rest_1_, bf16[3,512,512]{2,1,0:T(8,128)(2,1)} %get-tuple-element.37.rest_2_), custom_call_target="tpu_custom_call" | custom-call | flops 805306368 | bytes 3145728 | tf_op jit(solution)/shard_map/pallas_call | solution.py:357
  176.4 8.7 %shard_map.102.pr_ref.pl_ref.p_ref = bf16[4,512,1024]{2,1,0:T(8,128)(2,1)} custom-call(bf16[512,512]{1,0:T(8,128)(2,1)} %shard_map.100.refs_0_, bf16[512,512]{1,0:T(8,128)(2,1)} %shard_map.101.refs_1_, bf16[1024,4096]{1,0:T(8,128)(2,1)} %refs_14_.1), custom_call_target="tpu_custom_call" | custom-call | flops 4294967296 | bytes 12582912 | tf_op jit(solution)/shard_map/pallas_call | solution.py:381
  186.7 3.3 %shard_map.103 = (bf16[512,512]{1,0:T(8,128)(2,1)}, bf16[512,512]{1,0:T(8,128)(2,1)}) custom-call(s32[4]{0:T(128)} %pad_add_fusion.3.ids_ref, bf16[512,512]{1,0:T(8,128)(2,1)} %copy-done.11, bf16[512,512]{1,0:T(8,128)(2,1)} %copy-done.12, bf16[4,512,1024]{2,1,0:T(8,128)(2,1)} %shard_map.102.pr_ref.pl_ref.p_ref, ...), custom_call_target="tpu_custom_call" | custom-call | flops 524288 | bytes 3145728 | tf_op jit(solution)/shard_map/pallas_call | solution.py:405
  190.0 5.3 %collective-permute-start.18 = (bf16[512,512]{1,0:T(8,128)(2,1)}, bf16[512,512]{1,0:T(8,128)(2,1)}, u32[]{:S(2)}, u32[]{:S(2)}) collective-permute-start(bf16[512,512]{1,0:T(8,128)(2,1)} %get-tuple-element.38), channel_id=1, source_target_pairs={{0,1},{1,2},{2,3},{4,5},{5,6},{6,7},{8,9},{9,10},{10,11},{12,13},{... | collective-permute-start | bytes 1572872 | tf_op jit(solution)/shard_map/ppermute | solution.py:38
  195.3 1.3 collective-permute-start.21
  198.2 3.3 %shard_map.104 = (bf16[512,512]{1,0:T(8,128)(2,1)}, bf16[512,512]{1,0:T(8,128)(2,1)}) custom-call(s32[4]{0:T(128)} %pad_add_fusion.3.ids_ref, bf16[512,512]{1,0:T(8,128)(2,1)} %copy-done.13, bf16[512,512]{1,0:T(8,128)(2,1)} %copy-done.14, bf16[4,512,1024]{2,1,0:T(8,128)(2,1)} %shard_map.102.pr_ref.pl_ref.p_ref, ...), custom_call_target="tpu_custom_call" | custom-call | flops 524288 | bytes 3145728 | tf_op jit(solution)/shard_map/pallas_call | solution.py:405
  201.5 5.3 %collective-permute-start.20 = (bf16[512,512]{1,0:T(8,128)(2,1)}, bf16[512,512]{1,0:T(8,128)(2,1)}, u32[]{:S(2)}, u32[]{:S(2)}) collective-permute-start(bf16[512,512]{1,0:T(8,128)(2,1)} %get-tuple-element.39), channel_id=1, source_target_pairs={{0,1},{1,2},{2,3},{4,5},{5,6},{6,7},{8,9},{9,10},{10,11},{12,13},{... | collective-permute-start | bytes 1572872 | tf_op jit(solution)/shard_map/ppermute | solution.py:38
  208.8 1.9 collective-permute-done.21.left_ref.refs_10_
  210.6 3.3 %shard_map.105 = (bf16[512,512]{1,0:T(8,128)(2,1)}, bf16[512,512]{1,0:T(8,128)(2,1)}) custom-call(s32[4]{0:T(128)} %pad_add_fusion.4.ids_ref, bf16[512,512]{1,0:T(8,128)(2,1)} %collective-permute-done.18.right_ref.refs_4_, bf16[512,512]{1,0:T(8,128)(2,1)} %collective-permute-done.21.left_ref.refs_10_, bf16[4,512,1024]{2,1,0:T(8,128)(2,1)} %shard_map.102.pr_ref.pl_ref.p_ref, ...), custom_call_target="tpu_custom_call" | custom-call | flops 524288 | bytes 3145728 | tf_op jit(solution)/shard_map/pallas_call | solution.py:405
  213.9 3.6 %collective-permute-start.22 = (bf16[512,512]{1,0:T(8,128)(2,1)}, bf16[512,512]{1,0:T(8,128)(2,1)}, u32[]{:S(2)}, u32[]{:S(2)}) collective-permute-start(bf16[512,512]{1,0:T(8,128)(2,1)} %get-tuple-element.41), channel_id=1, source_target_pairs={{0,1},{1,2},{2,3},{4,5},{5,6},{6,7},{8,9},{9,10},{10,11},{12,13},{... | collective-permute-start | bytes 1572872 | tf_op jit(solution)/shard_map/ppermute | solution.py:38
  217.5 1.4 collective-permute-start.25
  219.0 3.9 %collective-permute-done.23.left_ref.refs_11_ = bf16[512,512]{1,0:T(8,128)(2,1)} collective-permute-done((bf16[512,512]{1,0:T(8,128)(2,1)}, bf16[512,512]{1,0:T(8,128)(2,1)}, u32[]{:S(2)}, u32[]{:S(2)}) %collective-permute-start.23) | collective-permute-done | bytes 524320 | tf_op jit(solution)/shard_map/ppermute | solution.py:38
  222.9 3.3 %shard_map.106 = (bf16[512,512]{1,0:T(8,128)(2,1)}, bf16[512,512]{1,0:T(8,128)(2,1)}) custom-call(s32[4]{0:T(128)} %pad_add_fusion.4.ids_ref, bf16[512,512]{1,0:T(8,128)(2,1)} %collective-permute-done.20.right_ref.refs_5_, bf16[512,512]{1,0:T(8,128)(2,1)} %collective-permute-done.23.left_ref.refs_11_, bf16[4,512,1024]{2,1,0:T(8,128)(2,1)} %shard_map.102.pr_ref.pl_ref.p_ref, ...), custom_call_target="tpu_custom_call" | custom-call | flops 524288 | bytes 3145728 | tf_op jit(solution)/shard_map/pallas_call | solution.py:405
  226.2 2.8 %collective-permute-start.24 = (bf16[512,512]{1,0:T(8,128)(2,1)}, bf16[512,512]{1,0:T(8,128)(2,1)}, u32[]{:S(2)}, u32[]{:S(2)}) collective-permute-start(bf16[512,512]{1,0:T(8,128)(2,1)} %get-tuple-element.43), channel_id=1, source_target_pairs={{0,1},{1,2},{2,3},{4,5},{5,6},{6,7},{8,9},{9,10},{10,11},{12,13},{... | collective-permute-start | bytes 1572872 | tf_op jit(solution)/shard_map/ppermute | solution.py:38
  232.1 2.6 collective-permute-done.25.refs_12_.left_ref
  234.7 3.3 %shard_map.108 = (bf16[512,512]{1,0:T(8,128)(2,1)}, bf16[512,512]{1,0:T(8,128)(2,1)}) custom-call(s32[4]{0:T(128)} %pad_add_fusion.5.ids_ref, bf16[512,512]{1,0:T(8,128)(2,1)} %collective-permute-done.22.refs_6_.right_ref, bf16[512,512]{1,0:T(8,128)(2,1)} %collective-permute-done.25.refs_12_.left_ref, bf16[4,512,1024]{2,1,0:T(8,128)(2,1)} %shard_map.102.pr_ref.pl_ref.p_ref, ...), custom_call_target="tpu_custom_call" | custom-call | flops 524288 | bytes 3145728 | tf_op jit(solution)/shard_map/pallas_call | solution.py:405
  238.0 1.9 collective-permute-start.30
  240.0 1.6 collective-permute-start.31
  241.5 4.5 %collective-permute-done.26.refs_13_.left_ref = bf16[512,512]{1,0:T(8,128)(2,1)} collective-permute-done((bf16[512,512]{1,0:T(8,128)(2,1)}, bf16[512,512]{1,0:T(8,128)(2,1)}, u32[]{:S(2)}, u32[]{:S(2)}) %collective-permute-start.26) | collective-permute-done | bytes 524320 | tf_op jit(solution)/shard_map/ppermute | solution.py:38
  246.0 3.3 %shard_map.110 = (bf16[512,512]{1,0:T(8,128)(2,1)}, bf16[512,512]{1,0:T(8,128)(2,1)}) custom-call(s32[4]{0:T(128)} %pad_add_fusion.5.ids_ref, bf16[512,512]{1,0:T(8,128)(2,1)} %collective-permute-done.24.refs_7_.right_ref, bf16[512,512]{1,0:T(8,128)(2,1)} %collective-permute-done.26.refs_13_.left_ref, bf16[4,512,1024]{2,1,0:T(8,128)(2,1)} %shard_map.102.pr_ref.pl_ref.p_ref, ...), custom_call_target="tpu_custom_call" | custom-call | flops 524288 | bytes 3145728 | tf_op jit(solution)/shard_map/pallas_call | solution.py:405
  249.3 1.5 collective-permute-start.32
  250.8 1.3 collective-permute-start.33
  252.1 1.9 pad_maximum_fusion.1
  254.0 10.8 %shard_map.107.out_ref = bf16[1024,1024]{1,0:T(8,128)(2,1)} custom-call(s32[4]{0:T(128)} %pad_add_fusion.ids_ref, s32[8]{0:T(128)} %broadcast_xor_fusion.pos_ref, bf16[512,512]{1,0:T(8,128)(2,1)} %get-tuple-element.34.refs_0_, bf16[512,512]{1,0:T(8,128)(2,1)} %get-tuple-element.35.refs_1_, bf16[512,512]{1,0:T(8,128)(2,1)} %copy-done.11, ...), custom_call_target="tpu_custom_call" | custom-call | flops 4294967296 | bytes 12582912 | tf_op jit(solution)/shard_map/pallas_call | solution.py:466
  266.5 2.3 shard_map.109.out_ref
  269.6 2.3 shard_map.111
  (102 shorter events, 22.9 us)
Async XLA Ops:
  0.6 26.5 %copy-start.25 = (s32[1024,2]{0,1:T(2,128)S(1)}, s32[1024,2]{0,1:T(2,128)}, u32[]{:S(2)}) copy-start(s32[1024,2]{0,1:T(2,128)} %param.10) | copy-start | bytes 24580
  1.9 12.4 %collective-permute-start.7 = (bf16[128,1024]{1,0:T(8,128)(2,1)S(1)}, bf16[128,1024]{1,0:T(8,128)(2,1)S(1)}, u32[]{:S(2)}, u32[]{:S(2)}) collective-permute-start(bf16[128,1024]{1,0:T(8,128)(2,1)S(1)} %get-tuple-element.52), channel_id=1, source_target_pairs={{0,1},{1,2},{2,3},{3,0},{4,5},{5,6},{6,7},{7,4},{8,9},{9,10},{10,1... | collective-permute-start | bytes 786440 | tf_op jit(solution)/shard_map/ppermute | solution.py:43
  4.9 19.7 %collective-permute-start.8 = (bf16[128,1024]{1,0:T(8,128)(2,1)S(1)}, bf16[128,1024]{1,0:T(8,128)(2,1)S(1)}, u32[]{:S(2)}, u32[]{:S(2)}) collective-permute-start(bf16[128,1024]{1,0:T(8,128)(2,1)S(1)} %get-tuple-element.51), channel_id=1, source_target_pairs={{0,2},{1,3},{2,0},{3,1},{4,6},{5,7},{6,4},{7,5},{8,10},{9,11},{10,... | collective-permute-start | bytes 786440 | tf_op jit(solution)/shard_map/ppermute | solution.py:43
  7.5 17.1 %collective-permute-start.9 = (bf16[128,1024]{1,0:T(8,128)(2,1)S(1)}, bf16[128,1024]{1,0:T(8,128)(2,1)S(1)}, u32[]{:S(2)}, u32[]{:S(2)}) collective-permute-start(bf16[128,1024]{1,0:T(8,128)(2,1)S(1)} %get-tuple-element.50), channel_id=1, source_target_pairs={{0,3},{1,0},{2,1},{3,2},{4,7},{5,4},{6,5},{7,6},{8,11},{9,8},{10,9... | collective-permute-start | bytes 786440 | tf_op jit(solution)/shard_map/ppermute | solution.py:43
  14.2 22.7 %copy-start.15 = (bf16[128,1024]{1,0:T(8,128)(2,1)}, bf16[128,1024]{1,0:T(8,128)(2,1)S(1)}, u32[]{:S(2)}) copy-start(bf16[128,1024]{1,0:T(8,128)(2,1)S(1)} %collective-permute-done.7.rest_1_) | copy-start | bytes 786436
  24.6 0.7 copy-start.16
  24.6 0.8 copy-start.17
  25.5 21.2 %copy-start.3 = (bf16[1,3,128,1024]{3,2,1,0:T(8,128)(2,1)}, bf16[1,3,128,1024]{3,2,1,0:T(8,128)(2,1)S(1)}, u32[]{:S(2)}) copy-start(bf16[1,3,128,1024]{3,2,1,0:T(8,128)(2,1)S(1)} %maximum_bitcast_fusion) | copy-start | bytes 2359300
  25.5 21.2 %collective-permute-start.27 = (bf16[1,3,128,1024]{3,2,1,0:T(8,128)(2,1)S(1)}, bf16[1,3,128,1024]{3,2,1,0:T(8,128)(2,1)S(1)}, u32[]{:S(2)}, u32[]{:S(2)}) collective-permute-start(bf16[1,3,128,1024]{3,2,1,0:T(8,128)(2,1)S(1)} %maximum_bitcast_fusion), channel_id=1, source_target_pairs={{0,16},{4,20},{8,24},{12,28},{16,0},{20,4},{24,8},{28,12},{1,17},{... | collective-permute-start | bytes 2359304 | tf_op jit(solution)/shard_map/ppermute | solution.py:48
  37.0 20.0 %collective-permute-start.2 = (bf16[3088,128]{1,0:T(8,128)(2,1)}, bf16[3088,128]{1,0:T(8,128)(2,1)}, u32[]{:S(2)}, u32[]{:S(2)}) collective-permute-start(bf16[3088,128]{1,0:T(8,128)(2,1)} %get-tuple-element.27), channel_id=1, source_target_pairs={{0,4},{4,0},{8,12},{12,8},{16,20},{20,16},{24,28},{28,24},{1,5},{5... | collective-permute-start | bytes 2371592 | tf_op jit(solution)/shard_map/ppermute | solution.py:48
  46.3 14.7 %collective-permute-start.3 = (bf16[3088,128]{1,0:T(8,128)(2,1)}, bf16[3088,128]{1,0:T(8,128)(2,1)}, u32[]{:S(2)}, u32[]{:S(2)}) collective-permute-start(bf16[3088,128]{1,0:T(8,128)(2,1)} %get-tuple-element.30), channel_id=1, source_target_pairs={{0,4},{4,0},{8,12},{12,8},{16,20},{20,16},{24,28},{28,24},{1,5},{5... | collective-permute-start | bytes 2371592 | tf_op jit(solution)/shard_map/ppermute | solution.py:48
  46.8 5.3 %copy-start.9 = (bf16[1,3,128,1024]{3,2,1,0:T(8,128)(2,1)}, bf16[1,3,128,1024]{3,2,1,0:T(8,128)(2,1)S(1)}, u32[]{:S(2)}) copy-start(bf16[1,3,128,1024]{3,2,1,0:T(8,128)(2,1)S(1)} %collective-permute-done.27) | copy-start | bytes 2359300
  46.9 81.9 %collective-permute-start.28 = (bf16[2,3,128,1024]{3,2,1,0:T(8,128)(2,1)S(1)}, bf16[2,3,128,1024]{3,2,1,0:T(8,128)(2,1)}, u32[]{:S(2)}, u32[]{:S(2)}) collective-permute-start(bf16[2,3,128,1024]{3,2,1,0:T(8,128)(2,1)S(1)} %pad_maximum_fusion.2), channel_id=1, source_target_pairs={{0,8},{4,12},{8,0},{12,4},{16,24},{20,28},{24,16},{28,20},{1,9},{5... | collective-permute-start | bytes 4718600 | tf_op jit(solution)/shard_map/ppermute | solution.py:48
  50.3 13.1 %collective-permute-start = (bf16[256,1024]{1,0:T(8,128)(2,1)}, bf16[256,1024]{1,0:T(8,128)(2,1)S(1)}, u32[]{:S(2)}, u32[]{:S(2)}) collective-permute-start(bf16[256,1024]{1,0:T(8,128)(2,1)} %slice.6), channel_id=1, source_target_pairs={{0,4},{4,8},{8,12},{12,16},{16,20},{20,24},{24,28},{1,5},{5,9},{9,... | collective-permute-start | bytes 1572872 | tf_op jit(solution)/shard_map/ppermute | solution.py:38
  53.9 9.6 %collective-permute-start.1 = (bf16[256,1024]{1,0:T(8,128)(2,1)}, bf16[256,1024]{1,0:T(8,128)(2,1)S(1)}, u32[]{:S(2)}, u32[]{:S(2)}) collective-permute-start(bf16[256,1024]{1,0:T(8,128)(2,1)} %slice.7), channel_id=1, source_target_pairs={{0,4},{4,8},{8,12},{12,16},{16,20},{20,24},{24,28},{1,5},{5,9},{9,... | collective-permute-start | bytes 1572872 | tf_op jit(solution)/shard_map/ppermute | solution.py:38
  59.5 33.2 %collective-permute-start.4 = (bf16[1552,128]{1,0:T(8,128)(2,1)}, bf16[1552,128]{1,0:T(8,128)(2,1)S(1)}, u32[]{:S(2)}, u32[]{:S(2)}) collective-permute-start(bf16[1552,128]{1,0:T(8,128)(2,1)} %get-tuple-element.28.rest_0_), channel_id=1, source_target_pairs={{0,8},{4,12},{8,0},{12,4},{16,24},{20,28},{24,16},{28,20},{1,9},{5... | collective-permute-start | bytes 1191944 | tf_op jit(solution)/shard_map/ppermute | solution.py:48
  63.5 47.8 %collective-permute-start.6 = (bf16[1552,128]{1,0:T(8,128)(2,1)}, bf16[1552,128]{1,0:T(8,128)(2,1)S(1)}, u32[]{:S(2)}, u32[]{:S(2)}) collective-permute-start(bf16[1552,128]{1,0:T(8,128)(2,1)} %get-tuple-element.31.rest_1_), channel_id=1, source_target_pairs={{0,16},{4,20},{8,24},{12,28},{16,0},{20,4},{24,8},{28,12},{1,17},{... | collective-permute-start | bytes 1191944 | tf_op jit(solution)/shard_map/ppermute | solution.py:48
  63.5 0.8 copy-start.1
  63.5 0.9 copy-start.2
  92.8 0.7 copy-start.23
  95.5 22.9 %collective-permute-start.5 = (bf16[1552,128]{1,0:T(8,128)(2,1)}, bf16[1552,128]{1,0:T(8,128)(2,1)S(1)}, u32[]{:S(2)}, u32[]{:S(2)}) collective-permute-start(bf16[1552,128]{1,0:T(8,128)(2,1)} %shard_map.91.rest_0_.a_ref), channel_id=1, source_target_pairs={{0,16},{4,20},{8,24},{12,28},{16,0},{20,4},{24,8},{28,12},{1,17},{... | collective-permute-start | bytes 1191944 | tf_op jit(solution)/shard_map/ppermute | solution.py:48
  111.3 0.7 copy-start.24
  114.0 9.9 %collective-permute-start.12 = (bf16[1552,128]{1,0:T(8,128)(2,1)}, bf16[1552,128]{1,0:T(8,128)(2,1)S(1)}, u32[]{:S(2)}, u32[]{:S(2)}) collective-permute-start(bf16[1552,128]{1,0:T(8,128)(2,1)} %shard_map.93.rest_0_.a_ref), channel_id=1, source_target_pairs={{0,8},{4,12},{8,0},{12,4},{16,24},{20,28},{24,16},{28,20},{1,9},{5... | collective-permute-start | bytes 1191944 | tf_op jit(solution)/shard_map/ppermute | solution.py:48
  118.3 0.7 copy-start.22
  121.8 10.2 %collective-permute-start.10 = (bf16[3,512,128]{2,1,0:T(8,128)(2,1)}, bf16[3,512,128]{2,1,0:T(8,128)(2,1)S(1)}, u32[]{:S(2)}, u32[]{:S(2)}) collective-permute-start(bf16[3,512,128]{2,1,0:T(8,128)(2,1)} %shard_map.95.rest_0_), channel_id=1, source_target_pairs={{0,8},{4,12},{8,0},{12,4},{16,24},{20,28},{24,16},{28,20},{1,9},{5... | collective-permute-start | bytes 1179656 | tf_op jit(solution)/shard_map/ppermute | solution.py:48
  123.9 0.7 copy-start.21
  124.6 4.2 %copy-start.4 = (bf16[1,3,128,1024]{3,2,1,0:T(8,128)(2,1)S(1)}, bf16[1,3,128,1024]{3,2,1,0:T(8,128)(2,1)}, u32[]{:S(2)}) copy-start(bf16[1,3,128,1024]{3,2,1,0:T(8,128)(2,1)} %copy-done.3) | copy-start | bytes 2359300
  124.6 4.2 %copy-start.10 = (bf16[1,3,128,1024]{3,2,1,0:T(8,128)(2,1)S(1)}, bf16[1,3,128,1024]{3,2,1,0:T(8,128)(2,1)}, u32[]{:S(2)}) copy-start(bf16[1,3,128,1024]{3,2,1,0:T(8,128)(2,1)} %copy-done.9) | copy-start | bytes 2359300
  127.5 4.5 %copy-start.7 = (bf16[3,512,128]{2,1,0:T(8,128)(2,1)S(1)}, bf16[3,512,128]{2,1,0:T(8,128)(2,1)}, u32[]{:S(2)}) copy-start(bf16[3,512,128]{2,1,0:T(8,128)(2,1)} %shard_map.95.rest_0_) | copy-start | bytes 1179652
  127.5 9.7 %copy-start.8 = (bf16[3,512,128]{2,1,0:T(8,128)(2,1)S(1)}, bf16[3,512,128]{2,1,0:T(8,128)(2,1)}, u32[]{:S(2)}) copy-start(bf16[3,512,128]{2,1,0:T(8,128)(2,1)} %shard_map.96.rest_1_) | copy-start | bytes 1179652
  127.5 9.7 %collective-permute-start.13 = (bf16[3,512,128]{2,1,0:T(8,128)(2,1)}, bf16[3,512,128]{2,1,0:T(8,128)(2,1)S(1)}, u32[]{:S(2)}, u32[]{:S(2)}) collective-permute-start(bf16[3,512,128]{2,1,0:T(8,128)(2,1)} %shard_map.96.rest_1_), channel_id=1, source_target_pairs={{0,16},{4,20},{8,24},{12,28},{16,0},{20,4},{24,8},{28,12},{1,17},{... | collective-permute-start | bytes 1179656 | tf_op jit(solution)/shard_map/ppermute | solution.py:48
  130.5 13.4 %copy-start = (bf16[4,3,128,1024]{3,2,1,0:T(8,128)(2,1)}, bf16[4,3,128,1024]{3,2,1,0:T(8,128)(2,1)S(1)}, u32[]{:S(2)}) copy-start(bf16[4,3,128,1024]{3,2,1,0:T(8,128)(2,1)S(1)} %pad_maximum_fusion.refs_15_) | copy-start | bytes 9437188
  130.6 123.5 %collective-permute-start.29 = (bf16[4,3,128,1024]{3,2,1,0:T(8,128)(2,1)S(1)}, bf16[4,3,128,1024]{3,2,1,0:T(8,128)(2,1)}, u32[]{:S(2)}, u32[]{:S(2)}) collective-permute-start(bf16[4,3,128,1024]{3,2,1,0:T(8,128)(2,1)S(1)} %pad_maximum_fusion.refs_15_), channel_id=1, source_target_pairs={{0,4},{4,0},{8,12},{12,8},{16,20},{20,16},{24,28},{28,24},{1,5},{5... | collective-permute-start | bytes 9437192 | tf_op jit(solution)/shard_map/ppermute | solution.py:48
  133.0 10.9 %collective-permute-start.11 = (bf16[2,3,512,128]{3,2,1,0:T(8,128)(2,1)}, bf16[2,3,512,128]{3,2,1,0:T(8,128)(2,1)}, u32[]{:S(2)}, u32[]{:S(2)}) collective-permute-start(bf16[2,3,512,128]{3,2,1,0:T(8,128)(2,1)} %pad_maximum_fusion.3.rest_2_), channel_id=1, source_target_pairs={{0,4},{4,0},{8,12},{12,8},{16,20},{20,16},{24,28},{28,24},{1,5},{5... | collective-permute-start | bytes 2359304 | tf_op jit(solution)/shard_map/ppermute | solution.py:48
  138.2 19.7 %collective-permute-start.14 = (bf16[2,3,512,128]{3,2,1,0:T(8,128)(2,1)}, bf16[2,3,512,128]{3,2,1,0:T(8,128)(2,1)}, u32[]{:S(2)}, u32[]{:S(2)}) collective-permute-start(bf16[2,3,512,128]{3,2,1,0:T(8,128)(2,1)} %pad_maximum_fusion.4.rest_2_), channel_id=1, source_target_pairs={{0,4},{4,0},{8,12},{12,8},{16,20},{20,16},{24,28},{28,24},{1,5},{5... | collective-permute-start | bytes 2359304 | tf_op jit(solution)/shard_map/ppermute | solution.py:48
  148.7 36.4 %collective-permute-start.15 = (bf16[512,512]{1,0:T(8,128)(2,1)}, bf16[512,512]{1,0:T(8,128)(2,1)S(1)}, u32[]{:S(2)}, u32[]{:S(2)}) collective-permute-start(bf16[512,512]{1,0:T(8,128)(2,1)} %get-tuple-element.34.refs_0_), channel_id=1, source_target_pairs={{0,1},{1,2},{2,3},{4,5},{5,6},{6,7},{8,9},{9,10},{10,11},{12,13},{... | collective-permute-start | bytes 1572872 | tf_op jit(solution)/shard_map/ppermute | solution.py:38
  156.6 28.5 %collective-permute-start.17 = (bf16[512,512]{1,0:T(8,128)(2,1)}, bf16[512,512]{1,0:T(8,128)(2,1)S(1)}, u32[]{:S(2)}, u32[]{:S(2)}) collective-permute-start(bf16[512,512]{1,0:T(8,128)(2,1)} %get-tuple-element.34.refs_0_), channel_id=1, source_target_pairs={{1,0},{2,1},{3,2},{5,4},{6,5},{7,6},{9,8},{10,9},{11,10},{13,12},{... | collective-permute-start | bytes 1572872 | tf_op jit(solution)/shard_map/ppermute | solution.py:38
  162.7 33.9 %collective-permute-start.16 = (bf16[512,512]{1,0:T(8,128)(2,1)}, bf16[512,512]{1,0:T(8,128)(2,1)S(1)}, u32[]{:S(2)}, u32[]{:S(2)}) collective-permute-start(bf16[512,512]{1,0:T(8,128)(2,1)} %get-tuple-element.35.refs_1_), channel_id=1, source_target_pairs={{0,1},{1,2},{2,3},{4,5},{5,6},{6,7},{8,9},{9,10},{10,11},{12,13},{... | collective-permute-start | bytes 1572872 | tf_op jit(solution)/shard_map/ppermute | solution.py:38
  167.3 29.3 %collective-permute-start.19 = (bf16[512,512]{1,0:T(8,128)(2,1)}, bf16[512,512]{1,0:T(8,128)(2,1)S(1)}, u32[]{:S(2)}, u32[]{:S(2)}) collective-permute-start(bf16[512,512]{1,0:T(8,128)(2,1)} %get-tuple-element.35.refs_1_), channel_id=1, source_target_pairs={{1,0},{2,1},{3,2},{5,4},{6,5},{7,6},{9,8},{10,9},{11,10},{13,12},{... | collective-permute-start | bytes 1572872 | tf_op jit(solution)/shard_map/ppermute | solution.py:38
  185.1 0.8 copy-start.11
  185.9 0.8 copy-start.12
  190.0 18.8 %collective-permute-start.18 = (bf16[512,512]{1,0:T(8,128)(2,1)}, bf16[512,512]{1,0:T(8,128)(2,1)}, u32[]{:S(2)}, u32[]{:S(2)}) collective-permute-start(bf16[512,512]{1,0:T(8,128)(2,1)} %get-tuple-element.38), channel_id=1, source_target_pairs={{0,1},{1,2},{2,3},{4,5},{5,6},{6,7},{8,9},{9,10},{10,11},{12,13},{... | collective-permute-start | bytes 1572872 | tf_op jit(solution)/shard_map/ppermute | solution.py:38
  195.3 15.3 %collective-permute-start.21 = (bf16[512,512]{1,0:T(8,128)(2,1)}, bf16[512,512]{1,0:T(8,128)(2,1)}, u32[]{:S(2)}, u32[]{:S(2)}) collective-permute-start(bf16[512,512]{1,0:T(8,128)(2,1)} %get-tuple-element.40), channel_id=1, source_target_pairs={{1,0},{2,1},{3,2},{5,4},{6,5},{7,6},{9,8},{10,9},{11,10},{13,12},{... | collective-permute-start | bytes 1572872 | tf_op jit(solution)/shard_map/ppermute | solution.py:38
  196.6 0.8 copy-start.13
  197.4 0.8 copy-start.14
  201.5 17.4 %collective-permute-start.20 = (bf16[512,512]{1,0:T(8,128)(2,1)}, bf16[512,512]{1,0:T(8,128)(2,1)}, u32[]{:S(2)}, u32[]{:S(2)}) collective-permute-start(bf16[512,512]{1,0:T(8,128)(2,1)} %get-tuple-element.39), channel_id=1, source_target_pairs={{0,1},{1,2},{2,3},{4,5},{5,6},{6,7},{8,9},{9,10},{10,11},{12,13},{... | collective-permute-start | bytes 1572872 | tf_op jit(solution)/shard_map/ppermute | solution.py:38
  206.9 16.0 %collective-permute-start.23 = (bf16[512,512]{1,0:T(8,128)(2,1)}, bf16[512,512]{1,0:T(8,128)(2,1)}, u32[]{:S(2)}, u32[]{:S(2)}) collective-permute-start(bf16[512,512]{1,0:T(8,128)(2,1)} %get-tuple-element.42), channel_id=1, source_target_pairs={{1,0},{2,1},{3,2},{5,4},{6,5},{7,6},{9,8},{10,9},{11,10},{13,12},{... | collective-permute-start | bytes 1572872 | tf_op jit(solution)/shard_map/ppermute | solution.py:38
  213.9 18.2 %collective-permute-start.22 = (bf16[512,512]{1,0:T(8,128)(2,1)}, bf16[512,512]{1,0:T(8,128)(2,1)}, u32[]{:S(2)}, u32[]{:S(2)}) collective-permute-start(bf16[512,512]{1,0:T(8,128)(2,1)} %get-tuple-element.41), channel_id=1, source_target_pairs={{0,1},{1,2},{2,3},{4,5},{5,6},{6,7},{8,9},{9,10},{10,11},{12,13},{... | collective-permute-start | bytes 1572872 | tf_op jit(solution)/shard_map/ppermute | solution.py:38
  217.5 14.0 %copy-start.26 = (s32[8]{0:T(128)S(1)}, s32[8]{0:T(128)}, u32[]{:S(2)}) copy-start(s32[8]{0:T(128)} %constant.113.clone) | copy-start | bytes 100
  217.5 17.2 %collective-permute-start.25 = (bf16[512,512]{1,0:T(8,128)(2,1)}, bf16[512,512]{1,0:T(8,128)(2,1)}, u32[]{:S(2)}, u32[]{:S(2)}) collective-permute-start(bf16[512,512]{1,0:T(8,128)(2,1)} %get-tuple-element.44), channel_id=1, source_target_pairs={{1,0},{2,1},{3,2},{5,4},{6,5},{7,6},{9,8},{10,9},{11,10},{13,12},{... | collective-permute-start | bytes 1572872 | tf_op jit(solution)/shard_map/ppermute | solution.py:38
  226.2 15.4 %collective-permute-start.24 = (bf16[512,512]{1,0:T(8,128)(2,1)}, bf16[512,512]{1,0:T(8,128)(2,1)}, u32[]{:S(2)}, u32[]{:S(2)}) collective-permute-start(bf16[512,512]{1,0:T(8,128)(2,1)} %get-tuple-element.43), channel_id=1, source_target_pairs={{0,1},{1,2},{2,3},{4,5},{5,6},{6,7},{8,9},{9,10},{10,11},{12,13},{... | collective-permute-start | bytes 1572872 | tf_op jit(solution)/shard_map/ppermute | solution.py:38
  229.0 17.1 %collective-permute-start.26 = (bf16[512,512]{1,0:T(8,128)(2,1)}, bf16[512,512]{1,0:T(8,128)(2,1)}, u32[]{:S(2)}, u32[]{:S(2)}) collective-permute-start(bf16[512,512]{1,0:T(8,128)(2,1)} %get-tuple-element.45), channel_id=1, source_target_pairs={{1,0},{2,1},{3,2},{5,4},{6,5},{7,6},{9,8},{10,9},{11,10},{13,12},{... | collective-permute-start | bytes 1572872 | tf_op jit(solution)/shard_map/ppermute | solution.py:38
  238.0 26.8 %collective-permute-start.30 = (bf16[512,512]{1,0:T(8,128)(2,1)}, bf16[512,512]{1,0:T(8,128)(2,1)S(1)}, u32[]{:S(2)}, u32[]{:S(2)}) collective-permute-start(bf16[512,512]{1,0:T(8,128)(2,1)} %get-tuple-element.46), channel_id=1, source_target_pairs={{0,1},{1,2},{2,3},{4,5},{5,6},{6,7},{8,9},{9,10},{10,11},{12,13},{... | collective-permute-start | bytes 1572872 | tf_op jit(solution)/shard_map/ppermute | solution.py:38
  239.9 12.1 %copy-start.5 = (bf16[3,512,512]{2,1,0:T(8,128)(2,1)S(1)}, bf16[3,512,512]{2,1,0:T(8,128)(2,1)}, u32[]{:S(2)}) copy-start(bf16[3,512,512]{2,1,0:T(8,128)(2,1)} %get-tuple-element.36.rest_2_) | copy-start | bytes 4718596
  240.0 12.1 %copy-start.6 = (bf16[3,512,512]{2,1,0:T(8,128)(2,1)S(1)}, bf16[3,512,512]{2,1,0:T(8,128)(2,1)}, u32[]{:S(2)}) copy-start(bf16[3,512,512]{2,1,0:T(8,128)(2,1)} %get-tuple-element.37.rest_2_) | copy-start | bytes 4718596
  240.0 24.9 %collective-permute-start.31 = (bf16[512,512]{1,0:T(8,128)(2,1)}, bf16[512,512]{1,0:T(8,128)(2,1)S(1)}, u32[]{:S(2)}, u32[]{:S(2)}) collective-permute-start(bf16[512,512]{1,0:T(8,128)(2,1)} %get-tuple-element.47), channel_id=1, source_target_pairs={{1,0},{2,1},{3,2},{5,4},{6,5},{7,6},{9,8},{10,9},{11,10},{13,12},{... | collective-permute-start | bytes 1572872 | tf_op jit(solution)/shard_map/ppermute | solution.py:38
  249.3 19.5 %collective-permute-start.32 = (bf16[512,512]{1,0:T(8,128)(2,1)}, bf16[512,512]{1,0:T(8,128)(2,1)S(1)}, u32[]{:S(2)}, u32[]{:S(2)}) collective-permute-start(bf16[512,512]{1,0:T(8,128)(2,1)} %get-tuple-element.48), channel_id=1, source_target_pairs={{0,1},{1,2},{2,3},{4,5},{5,6},{6,7},{8,9},{9,10},{10,11},{12,13},{... | collective-permute-start | bytes 1572872 | tf_op jit(solution)/shard_map/ppermute | solution.py:38
  250.8 18.0 %collective-permute-start.33 = (bf16[512,512]{1,0:T(8,128)(2,1)}, bf16[512,512]{1,0:T(8,128)(2,1)}, u32[]{:S(2)}, u32[]{:S(2)}) collective-permute-start(bf16[512,512]{1,0:T(8,128)(2,1)} %get-tuple-element.49), channel_id=1, source_target_pairs={{1,0},{2,1},{3,2},{5,4},{6,5},{7,6},{9,8},{10,9},{11,10},{13,12},{... | collective-permute-start | bytes 1572872 | tf_op jit(solution)/shard_map/ppermute | solution.py:38
  264.9 0.8 copy-start.18
  265.7 0.8 copy-start.19
  268.8 0.8 copy-start.20

commit v3 on v0

v3 whole, which is shorter than its diff:
```python
import functools
import math

import jax
import jax.numpy as jnp
from jax import lax
from jax.experimental import pallas as pl
from jax.experimental.pallas import tpu as pltpu
from jax.sharding import PartitionSpec as P

FW = 512
HEAD_DIM = 128
WINDOW = 256
LANES = 128
PER = FW // LANES
BLOCKS = 3 * PER
HALF = BLOCKS // 2
THIRD = BLOCKS // 4
TAIL = 16

base_rate = 0.05
BF = jnp.bfloat16
F32 = jnp.float32
NT = (((1,), (1,)), ((), ()))

CORE, FIRST, NEAR = 0, 1, 2

ANY = pl.BlockSpec(memory_space=pl.ANY)
HBM = pl.BlockSpec(memory_space=pltpu.HBM)
SMEM = pl.BlockSpec(memory_space=pltpu.SMEM)


def room(mib):
    return pltpu.CompilerParams(vmem_limit_bytes=mib * 2**20)


def mm(a, b):
    return jnp.dot(a, b, preferred_element_type=F32)


def shift(block, axis, distance):
    n = lax.axis_size(axis)
    return lax.ppermute(block, axis, [(i, i + distance) for i in range(n) if 0 <= i + distance < n])


def rotate(block, axis, distance):
    n = lax.axis_size(axis)
    return lax.ppermute(block, axis, [(i, (i + distance) % n) for i in range(n)])


def swap(block, bit):
    n = lax.axis_size("ctx")
    return lax.ppermute(block, "ctx", [(i, i ^ bit) for i in range(n)])


def sigmoid(x):
    return 0.5 * jnp.tanh(0.5 * x) + 0.5


def full(shape):
    return pl.BlockSpec(shape, lambda *_: (0,) * len(shape))


def cost(microseconds):
    return pl.CostEstimate(
        flops=int(microseconds * 0.12e9), bytes_accessed=0, transcendentals=0
    )


def strip_copy(ids_ref, at, w_hbm, o_ref, sem):
    share, width = o_ref.shape
    rows = pl.ds(pl.multiple_of(ids_ref[at] * share, share), share)
    cols = pl.ds(pl.multiple_of(ids_ref[at + 1] * width, width), width)
    return pltpu.make_async_copy(w_hbm.at[rows, cols], o_ref, sem)


def split_rows(x):
    hi = x.astype(BF).astype(F32)
    mid = (x - hi).astype(BF).astype(F32)
    lo = x - hi - mid
    row = lax.broadcasted_iota(jnp.int32, (TAIL, LANES), 0)
    return jnp.where(row == 0, hi, jnp.where(row == 1, mid, jnp.where(row == 2, lo, 0.0))).astype(BF)


def join_rows(tail):
    return jnp.sum(tail.astype(F32), axis=0, keepdims=True)


def grads_kernel(h, at, ids_ref, code_ref, k_hbm, v_hbm, w_hbm, *refs):
    k_ref, v_ref, w_ref, lhs, rhs, sem, ksem, vsem = refs[-8:]
    cols = pl.ds(h * FW, FW)
    rows = k_ref.shape[0]
    tile = min(256, rows)
    copies = [[pltpu.make_async_copy(w_hbm.at[pl.ds(h, 1)], w_ref, sem.at[0])]]
    for t in range(rows // tile):
        sl = pl.ds(t * tile, tile)
        copies.append(
            [
                pltpu.make_async_copy(k_hbm.at[sl, cols], k_ref.at[sl, :], ksem.at[t]),
                pltpu.make_async_copy(v_hbm.at[sl, cols], v_ref.at[sl, :], vsem.at[t]),
            ]
        )
    later = []
    if h == 0:
        ow_hbm, keep_ref, send_ref, rim_ref = refs[:4]
        strip_refs = refs[4:-8]
        last = pl.ds(k_hbm.shape[0] - WINDOW, WINDOW)
        later = [
            pltpu.make_async_copy(k_hbm.at[last, :], rim_ref.at[pl.ds(0, WINDOW), :], sem.at[3]),
            pltpu.make_async_copy(
                v_hbm.at[last, :], rim_ref.at[pl.ds(WINDOW, WINDOW), :], sem.at[4]
            ),
        ] + [
            strip_copy(ids_ref, at + 2 * i, ow_hbm, strip_ref, sem.at[5 + i])
            for i, strip_ref in enumerate(strip_refs)
        ]
    else:
        keep_ref, send_ref = refs[-10:-8]
    for copy in sum(copies, []) + later:
        copy.start()
    copies[0][0].wait()
    wide = 2 * LANES
    codes = code_ref[h : h + 1, :].astype(F32) * 2.0 ** (-14)
    for t in range(rows // tile):
        for copy in copies[1 + t]:
            copy.wait()
        sl = pl.ds(t * tile, tile)
        k = k_ref[sl, :]
        rate = jnp.broadcast_to(codes[:, t * tile : (t + 1) * tile], (LANES, tile)).T
        rate = jnp.concatenate([rate] * PER, axis=1)
        push = (rate * v_ref[sl, :].astype(F32)).astype(BF)
        rhs[sl, 2 * FW :] = push
        for j in range(FW // wide):
            cs = slice(j * wide, (j + 1) * wide)
            gate = mm(k, w_ref[0, 0, :, cs])
            up = mm(k, w_ref[0, 1, :, cs])
            back = lax.dot_general(push, w_ref[0, 2, cs, :], NT, preferred_element_type=F32)
            s = sigmoid(gate)
            gs = gate * s
            lhs[FW + j * wide : FW + (j + 1) * wide, sl] = (gs * up).astype(BF).T
            rhs[sl, cs] = (back * up * (s + gs * (1.0 - s))).astype(BF)
            rhs[sl, FW + j * wide : FW + (j + 1) * wide] = (back * gs).astype(BF)
    lhs[:FW, :] = k_ref[...].T
    tail = split_rows(jnp.broadcast_to(jnp.sum(codes, axis=1, keepdims=True), (1, LANES)))
    pairs = HALF // 2
    for ref, half in ((send_ref, 1 - ids_ref[CORE]), (keep_ref, ids_ref[CORE])):
        ref[pl.ds(HALF * FW, TAIL), :] = tail
        for i in range(pairs):
            pair = half * pairs + i
            left = (pair >= 2 * FW // wide).astype(jnp.int32) * FW
            left = lhs[pl.ds(pl.multiple_of(left, FW), FW), :]
            right = rhs[:, pl.ds(pl.multiple_of(pair * wide, wide), wide)]
            r = mm(left, right).astype(BF)
            ref[pl.ds(2 * i * FW, FW), :] = r[:, :LANES]
            ref[pl.ds((2 * i + 1) * FW, FW), :] = r[:, LANES:]
    for copy in later:
        copy.wait()


def grads(h, at, ids, codes, keys, values, fast_weights, out_weight, strips, after):
    rows, feats = keys.shape
    shape = (HALF * FW + TAIL, LANES)
    outs = [shape, shape] + ([(2 * WINDOW, feats)] + strips if h == 0 else [])
    more = [out_weight] if h == 0 else after
    return pl.pallas_call(
        functools.partial(grads_kernel, h, at),
        grid=(1,),
        in_specs=[SMEM, full(codes.shape), HBM, HBM, HBM]
        + ([HBM] if h == 0 else [ANY] * len(more)),
        out_specs=[full(x) for x in outs],
        out_shape=[jax.ShapeDtypeStruct(x, BF) for x in outs],
        scratch_shapes=[
            pltpu.VMEM((rows, FW), BF),
            pltpu.VMEM((rows, FW), BF),
            pltpu.VMEM((1, 3, FW, FW), BF),
            pltpu.VMEM((2 * FW, rows), BF),
            pltpu.VMEM((rows, 3 * FW), BF),
            pltpu.SemaphoreType.DMA((5 + len(strips),)),
            pltpu.SemaphoreType.DMA((rows // min(256, rows),)),
            pltpu.SemaphoreType.DMA((rows // min(256, rows),)),
        ],
        compiler_params=room(58),
        cost_estimate=cost(8 * rows / 1024),
    )(ids, codes, keys, values, fast_weights, *more)


def fetch(refs, scratch, sem):
    copies = [pltpu.make_async_copy(r, scratch.at[i], sem.at[i]) for i, r in enumerate(refs)]
    for c in copies:
        c.start()
    for c in copies:
        c.wait()


def pair(x):
    return [pltpu.VMEM((2,) + x.shape, x.dtype), pltpu.SemaphoreType.DMA((2,))]


def split_kernel(h, ids_ref, keep_hbm, other_hbm, *refs):
    keep_out, send_out, both, sem = refs[-4:]
    fetch((keep_hbm, other_hbm), both, sem)
    keep_ref, other_ref = both.at[0], both.at[1]
    n = THIRD * FW
    bit = ids_ref[NEAR + h]
    mine = pl.ds(pl.multiple_of(bit * n, n), n)
    theirs = pl.ds(pl.multiple_of((1 - bit) * n, n), n)
    keep_out[pl.ds(0, n), :] = keep_ref[mine, :] + other_ref[mine, :]
    send_out[pl.ds(0, n), :] = keep_ref[theirs, :] + other_ref[theirs, :]
    tail = pl.ds(HALF * FW, TAIL)
    rate = split_rows(join_rows(keep_ref[tail, :]) + join_rows(other_ref[tail, :]))
    keep_out[pl.ds(n, TAIL), :] = rate
    send_out[pl.ds(n, TAIL), :] = rate


def split(h, ids, keep, other, after):
    shape = (THIRD * FW + TAIL, LANES)
    out = jax.ShapeDtypeStruct(shape, BF)
    return pl.pallas_call(
        functools.partial(split_kernel, h),
        grid=(1,),
        in_specs=[SMEM] + [ANY] * (2 + len(after)),
        out_specs=[full(shape), full(shape)],
        out_shape=[out, out],
        scratch_shapes=pair(keep),
        compiler_params=room(12),
        cost_estimate=cost(0.9),
    )(ids, keep, other, *after)


def total_kernel(a_hbm, b_hbm, *rest):
    o_ref, both, sem = rest[-3:]
    fetch((a_hbm, b_hbm), both, sem)
    a_ref, b_ref = both.at[0], both.at[1]
    n = THIRD * FW
    o_ref[pl.ds(0, n), :] = a_ref[pl.ds(0, n), :] + b_ref[pl.ds(0, n), :]
    tail = pl.ds(n, TAIL)
    o_ref[tail, :] = split_rows(join_rows(a_ref[tail, :]) + join_rows(b_ref[tail, :]))


def total(a, b, after):
    return pl.pallas_call(
        total_kernel,
        grid=(1,),
        in_specs=[ANY] * (2 + len(after)),
        out_specs=full(a.shape),
        out_shape=jax.ShapeDtypeStruct(a.shape, BF),
        scratch_shapes=pair(a),
        compiler_params=room(8),
        cost_estimate=cost(0.5),
    )(a, b, *after)


def renorm_kernel(heads, tokens_all, ids_ref, base_ref, *refs):
    outs, (both, sem) = refs[-2 - heads : -2], refs[-2:]
    fetch(refs[: 2 * heads], both, sem)
    tail = pl.ds(THIRD * FW, TAIL)
    for h in range(heads):
        a_ref, b_ref = both.at[2 * h], both.at[2 * h + 1]
        start = ids_ref[CORE] * HALF + ids_ref[NEAR + h] * THIRD
        rate_sum = join_rows(a_ref[tail, :]) + join_rows(b_ref[tail, :])
        step = base_rate / (math.sqrt(tokens_all) * (rate_sum / tokens_all))
        for i in range(THIRD):
            sl = pl.ds(i * FW, FW)
            pull = a_ref[sl, :].astype(F32) + b_ref[sl, :].astype(F32)
            at = start + i
            col = pl.ds(pl.multiple_of((at % PER) * LANES, LANES), LANES)
            base = base_ref[h, at // PER, :, col].astype(F32)
            updated = base + step * pull
            old = jnp.sqrt(jnp.sum(base * base, axis=0, keepdims=True) + 1e-06)
            new = jnp.sqrt(jnp.sum(updated * updated, axis=0, keepdims=True) + 1e-06)
            outs[h][i] = (updated * (old / new)).astype(BF)


def renorm(ids, tokens_all, fast_weights, pulls, after):
    heads, one = fast_weights.shape[0], pulls[0].shape
    shape = (THIRD, FW, LANES)
    return pl.pallas_call(
        functools.partial(renorm_kernel, heads, tokens_all),
        grid=(1,),
        in_specs=[SMEM, full(fast_weights.shape)] + [ANY] * (len(pulls) + len(after)),
        out_specs=[full(shape)] * heads,
        out_shape=[jax.ShapeDtypeStruct(shape, BF)] * heads,
        scratch_shapes=[
            pltpu.VMEM((2 * heads,) + one, BF),
            pltpu.SemaphoreType.DMA((2 * heads,)),
        ],
        compiler_params=room(24),
        cost_estimate=cost(2.1),
    )(ids, fast_weights, *pulls, *after)


def attn_kernel(ids_ref, q_ref, k_ref, v_ref, rim_ref, *rest):
    o_ref = rest[-1]
    rows = q_ref.shape[0]
    w, d = WINDOW, HEAD_DIM
    row = lax.broadcasted_iota(jnp.int32, (w, w), 0)
    col = lax.broadcasted_iota(jnp.int32, (w, w), 1)
    own = col <= row
    factor = math.log2(math.e) / math.sqrt(d)
    has_prev = ids_ref[FIRST] == 0
    ones = jnp.ones((2 * w, LANES), BF)
    for h in range(q_ref.shape[1] // d):
        cs = slice(h * d, (h + 1) * d)
        for b in range(rows // w):
            sl = pl.ds(b * w, w)
            if b == 0:
                k2 = jnp.concatenate([rim_ref[:w, cs], k_ref[sl, cs]], axis=0)
                v2 = jnp.concatenate([rim_ref[w:, cs], v_ref[sl, cs]], axis=0)
            else:
                both = pl.ds((b - 1) * w, 2 * w)
                k2, v2 = k_ref[both, cs], v_ref[both, cs]
            s2 = lax.dot_general(q_ref[sl, cs], k2, NT, preferred_element_type=F32)
            prev = s2[:, :w]
            if b == 0:
                prev = jnp.where(has_prev, prev, -1e30)
            s = jnp.where(own, s2[:, w:], prev)
            e = jnp.exp2((s - jnp.max(s, axis=1, keepdims=True)) * factor).astype(BF)
            zero = jnp.zeros_like(e)
            e2 = jnp.concatenate([jnp.where(own, zero, e), jnp.where(own, e, zero)], axis=1)
            o = mm(e2, jnp.concatenate([v2, ones], axis=1))
            o_ref[sl, cs] = (o[:, :d] / o[:, d:]).astype(o_ref.dtype)


def attention(piece, width, ids, query, keys, values, rim, after):
    rows = query.shape[0]
    col = pl.BlockSpec((rows, width), lambda i: (0, piece))
    of_rim = pl.BlockSpec((2 * WINDOW, width), lambda i: (0, piece))
    return pl.pallas_call(
        attn_kernel,
        grid=(1,),
        in_specs=[SMEM, col, col, col, of_rim] + [ANY] * len(after),
        out_specs=full((rows, width)),
        out_shape=jax.ShapeDtypeStruct((rows, width), BF),
        compiler_params=room(16),
        cost_estimate=cost(2.1 * rows * width / 2**18),
    )(ids, query, keys, values, rim, *after)


def apply_tile(q, att, weights, act):
    wide = 2 * LANES
    rows = q.shape[0]
    for j in range(FW // wide):
        cs = slice(j * wide, (j + 1) * wide)
        gate = mm(q, weights[0, :, cs])
        up = mm(q, weights[1, :, cs])
        act[:rows, cs] = (gate * sigmoid(gate) * up).astype(BF)
    y = mm(act[:rows, :], weights[2])
    y = y * lax.rsqrt(jnp.mean(y * y, axis=1, keepdims=True) + 1e-06)
    return (att.astype(F32) + y).astype(BF)


def apply_kernel(h, pieces, ids_ref, q_hbm, *refs):
    att_hbm, refs = refs[:pieces], refs[pieces:]
    blocks = refs[:4]
    lo_ref, hi_ref, nw_hbm, q, att, nw, act, sem, bsem, osem = refs[-10:]
    rows = q.shape[0]
    core, near = ids_ref[CORE], ids_ref[NEAR + h]
    copies = [pltpu.make_async_copy(q_hbm.at[:, pl.ds(h * FW, FW)], q, sem.at[0])]
    for i, a in enumerate(att_hbm):
        to = att.at[:, pl.ds(i * a.shape[1], a.shape[1])]
        copies.append(pltpu.make_async_copy(a, to, sem.at[1 + i]))
    for n, src in enumerate(blocks):
        half, third = core ^ (n // 2), near ^ (n % 2)
        for i in range(THIRD):
            b = half * HALF + third * THIRD + i
            col = pl.ds(pl.multiple_of((b % PER) * LANES, LANES), LANES)
            dst = nw.at[b // PER, :, col]
            copies.append(pltpu.make_async_copy(src.at[i], dst, bsem.at[n, i]))
    for c in copies:
        c.start()
    for c in copies:
        c.wait()
    out = pltpu.make_async_copy(nw, nw_hbm.at[h], osem)
    out.start()
    cut = lo_ref.shape[0]
    for ref, start in ((lo_ref, 0), (hi_ref, cut)):
        sl = pl.ds(start, ref.shape[0])
        ref[...] = apply_tile(q[sl, :], att[sl, :], nw, act)
    out.wait()


def apply(h, heads, ids, query, attended, blocks, cut, whole, after):
    rows, pieces = query.shape[0], len(attended)
    shape = (heads, 3, FW, FW)
    extra = ([] if whole is None else [whole]) + after
    alias = {} if whole is None else {2 + pieces + len(blocks): 2}
    sizes = [(cut, FW), (rows - cut, FW)]
    return pl.pallas_call(
        functools.partial(apply_kernel, h, pieces),
        grid=(1,),
        in_specs=[SMEM] + [ANY] * (1 + pieces + len(blocks) + len(extra)),
        out_specs=[full(x) for x in sizes] + [ANY],
        out_shape=[jax.ShapeDtypeStruct(x, BF) for x in sizes + [shape]],
        input_output_aliases=alias,
        scratch_shapes=[
            pltpu.VMEM((rows, FW), BF),
            pltpu.VMEM((rows, FW), BF),
            pltpu.VMEM((3, FW, FW), BF),
            pltpu.VMEM((max(cut, rows - cut), FW), BF),
            pltpu.SemaphoreType.DMA((1 + pieces,)),
            pltpu.SemaphoreType.DMA((4, THIRD)),
            pltpu.SemaphoreType.DMA,
        ],
        compiler_params=room(20),
        cost_estimate=cost(3.3 * rows / 1024),
    )(ids, query, *attended, *blocks, *extra)


def joined(refs):
    return jnp.concatenate([r[...] for r in refs], axis=1)


def partial_kernel(heads, *refs):
    x_refs, w_ref = refs[:heads], refs[heads]
    o_ref, x = refs[-2:]

    @pl.when(pl.program_id(0) == 0)
    def _():
        for h in range(heads):
            x[:, h * FW : (h + 1) * FW] = x_refs[h][...]

    o_ref[0] = mm(x[...], w_ref[...]).astype(BF)


def partials(merged, out_weight, groups, after):
    rows, heads = merged[0].shape[0], len(merged)
    feats, width = out_weight.shape[0], out_weight.shape[1] // groups
    return pl.pallas_call(
        functools.partial(partial_kernel, heads),
        grid=(groups,),
        in_specs=[full(m.shape) for m in merged]
        + [pl.BlockSpec((feats, width), lambda d: (0, d))]
        + [ANY] * len(after),
        out_specs=pl.BlockSpec((1, rows, width), lambda d: (d, 0, 0)),
        out_shape=jax.ShapeDtypeStruct((groups, rows, width), BF),
        scratch_shapes=[pltpu.VMEM((rows, feats), BF)],
        compiler_params=room(24),
        cost_estimate=cost(1 * rows / 512),
    )(*merged, out_weight, *after)


def stack_kernel(n, *refs):
    o_ref = refs[-1]
    at = 0
    for r in refs[:n]:
        o_ref[pl.ds(at, r.shape[0])] = r[...]
        at += r.shape[0]


def stack(parts, after):
    shape = (sum(p.shape[0] for p in parts),) + parts[0].shape[1:]
    return pl.pallas_call(
        functools.partial(stack_kernel, len(parts)),
        grid=(1,),
        in_specs=[full(p.shape) for p in parts] + [ANY] * len(after),
        out_specs=full(shape),
        out_shape=jax.ShapeDtypeStruct(shape, BF),
        compiler_params=room(20),
        cost_estimate=cost(0.1),
    )(*parts, *after)


def ring_kernel(t, n, at, tail, wave, ids_ref, right_hbm, left_hbm, p_hbm, *refs):
    ro_ref, lo_ref, x_hbm, got, own, sem, xsem = refs[-7:]
    width = right_hbm.shape[1]
    cols = pl.ds(wave * width, width)
    copies = [
        pltpu.make_async_copy(right_hbm, got.at[0], sem.at[0]),
        pltpu.make_async_copy(p_hbm.at[ids_ref[at], :, cols], own.at[0], sem.at[1]),
        pltpu.make_async_copy(left_hbm, got.at[1], sem.at[2]),
        pltpu.make_async_copy(p_hbm.at[ids_ref[at + 1], :, cols], own.at[1], sem.at[3]),
    ]
    for c in copies:
        c.start()
    zero = jnp.zeros((), BF)
    for i, ref in enumerate((ro_ref, lo_ref)):
        copies[2 * i].wait()
        copies[2 * i + 1].wait()
        ref[...] = got[i] + jnp.where(ids_ref[at + 2 + i] > 0, own[i], zero)
    for i, (slot, here) in enumerate(((t - 1, t <= ids_ref[tail]), (n - 1 - t, t < n - ids_ref[tail]))):

        @pl.when(here)
        def _():
            keep = pltpu.make_async_copy(got.at[i], x_hbm.at[slot, :, cols], xsem.at[i])
            keep.start()
            keep.wait()


def ring_step(t, n, ids, at, tail, wave, right, left, partial, x, after):
    out = jax.ShapeDtypeStruct(right.shape, BF)
    kept = jax.ShapeDtypeStruct((n - 1, right.shape[0], partial.shape[2]), BF)
    more = ([] if x is None else [x]) + after
    return pl.pallas_call(
        functools.partial(ring_kernel, t, n, at, tail, wave),
        grid=(1,),
        in_specs=[SMEM] + [ANY] * (3 + len(more)),
        out_specs=[full(right.shape)] * 2 + [ANY],
        out_shape=[out, out, kept],
        input_output_aliases={} if x is None else {4: 2},
        scratch_shapes=[
            pltpu.VMEM((2,) + right.shape, BF),
            pltpu.VMEM((2,) + right.shape, BF),
            pltpu.SemaphoreType.DMA((4,)),
            pltpu.SemaphoreType.DMA((2,)),
        ],
        compiler_params=room(12),
        cost_estimate=cost(30),
    )(ids, right, left, partial, *more)


def gathered_kernel(n, heads, parts, at, ids_ref, *refs):
    own_refs, refs = refs[:heads], refs[heads:]
    x_hbm, refs = refs[0], refs[1:]
    w_ref, near_ref, far_ref = refs[:3]
    o_ref, x, cols, acc, xsem, wsem = refs[-6:]
    share = near_ref.shape[2]
    near = near_ref.shape[0]

    def each(steps, do):
        for t in steps:
            do(t, pltpu.make_async_copy(x_hbm.at[t], x.at[t], xsem.at[t]))
            for p in range(parts):
                src = near_ref.at[p, t] if p < near else far_ref.at[p - near, t]
                to = ids_ref[at + 1 + p] * share
                to = pl.ds(pl.multiple_of(to, share), share)
                do(t, pltpu.make_async_copy(src, cols.at[t, to, :], wsem.at[t, p]))

    each(range(n - 1), lambda t, c: c.start())
    acc[...] = mm(joined(own_refs), w_ref[...])
    for t in range(n - 1):
        each((t,), lambda t, c: c.wait())
        if t < n - 2:
            acc[...] += mm(x[t], cols[t])
        else:
            o_ref[...] = (acc[...] + mm(x[t], cols[t])).astype(BF)


def gathered(ids, at, merged, x, out_weight, near, far, rows_all, after):
    n, heads, parts = x.shape[0] + 1, len(merged), near.shape[0] + far.shape[0]
    rows, feats = merged[0].shape[0], out_weight.shape[0]
    width = out_weight.shape[1] // n
    return pl.pallas_call(
        functools.partial(gathered_kernel, n, heads, parts, at),
        grid_spec=pltpu.PrefetchScalarGridSpec(
            num_scalar_prefetch=1,
            grid=(1,),
            in_specs=[full(m.shape) for m in merged]
            + [ANY]
            + [pl.BlockSpec((feats, width), lambda i, s: (0, s[at])), ANY, ANY]
            + [ANY] * len(after),
            out_specs=pl.BlockSpec((rows, width), lambda i, s: (0, 0)),
            scratch_shapes=[
                pltpu.VMEM((n - 1, rows, feats), BF),
                pltpu.VMEM((n - 1, feats, width), BF),
                pltpu.VMEM((rows, width), F32),
                pltpu.SemaphoreType.DMA((n - 1,)),
                pltpu.SemaphoreType.DMA((n - 1, parts)),
            ],
        ),
        out_shape=jax.ShapeDtypeStruct((rows_all, width), BF),
        compiler_params=room(48),
        cost_estimate=cost(9 * rows / 512),
    )(
        ids, *merged, x, out_weight, near, far, *after
    )


def finish_kernel(at, wave, ids_ref, right_hbm, left_hbm, p_hbm, out_in, o_hbm, got, own, sem):
    del out_in
    rows, width = own.shape
    cols = pl.ds(wave * width, width)
    copies = [
        pltpu.make_async_copy(right_hbm, got.at[0], sem.at[0]),
        pltpu.make_async_copy(left_hbm, got.at[1], sem.at[1]),
        pltpu.make_async_copy(p_hbm.at[ids_ref[at], :, cols], own, sem.at[2]),
    ]
    for c in copies:
        c.start()
    for c in copies:
        c.wait()
    total = own[...].astype(F32) + (got[0].astype(F32) + got[1].astype(F32))
    own[...] = total.astype(BF)
    last = pl.ds(o_hbm.shape[0] - rows, rows)
    out = pltpu.make_async_copy(own, o_hbm.at[last, cols], sem.at[3])
    out.start()
    out.wait()


def finish(ids, at, wave, right, left, partial, out):
    return pl.pallas_call(
        functools.partial(finish_kernel, at, wave),
        grid=(1,),
        in_specs=[SMEM] + [ANY] * 4,
        out_specs=ANY,
        out_shape=jax.ShapeDtypeStruct(out.shape, BF),
        input_output_aliases={4: 0},
        scratch_shapes=[
            pltpu.VMEM((2,) + right.shape, BF),
            pltpu.VMEM(right.shape, BF),
            pltpu.SemaphoreType.DMA((4,)),
        ],
        compiler_params=room(12),
        cost_estimate=cost(30),
    )(ids, right, left, partial, out)


def scalars(*xs):
    return jnp.stack([jnp.asarray(x, jnp.int32) for x in xs])


def shards(query, keys, values, lr_code, fast_weights, out_weight):
    rows, feats = query.shape
    contexts, groups = lax.axis_size("ctx"), lax.axis_size("head")
    c, z = lax.axis_index("ctx"), lax.axis_index("head")
    tokens_all = rows * contexts
    heads = fast_weights.shape[0]
    bits = [1 << i for i in range(contexts.bit_length() - 1)]
    bit_of = {b: (c // b) % 2 for b in bits}
    order = [[bits[1 + h % 2]] for h in range(heads)]
    order = [o + [b for b in bits[1:] if b != o[0]] for o in order]
    spread = bits[2::-1]
    places = [0]
    for b in spread:
        places = places + [p ^ b for p in places]
    share, width = feats // len(places), out_weight.shape[1] // groups
    ids = [bit_of[1], c == 0] + [bit_of[o[0]] for o in order]
    step_at = [len(ids) + 4 * (t - 1) for t in range(groups)]
    for t in range(1, groups):
        ids += [(z - t) % groups, (z + t) % groups, t > z, t > groups - 1 - z]
    tail_at = len(ids)
    ids += [z] + [(c % len(places)) ^ p for p in places]
    strip_at = len(ids)
    for s in range(1, groups):
        ids += [c % len(places), (z + s) % groups]
    ids = scalars(*ids)

    keep, other = [], []
    for h in range(heads):
        g = grads(
            h,
            strip_at,
            ids,
            lr_code.T,
            keys,
            values,
            fast_weights,
            out_weight,
            [(share, width)] * (groups - 1),
            keep[-1:],
        )
        keep.append(g[0])
        other.append(swap(g[1], 1))
        if h == 0:
            rim = shift(g[2], "ctx", 1)
            strips = [rotate(x, "head", s + 1) for s, x in enumerate(g[3:])]
    split_up = []
    for h in range(heads):
        before = [s[1] for s in split_up[-1:]] or [rim]
        split_up.append(split(h, ids, keep[h], other[h], before))
    away = [swap(split_up[h][1], order[h][0]) for h in range(heads)]

    per_head = 2
    pieces = []

    def attend(after):
        i = len(pieces)
        pieces.append(attention(i, FW // per_head, ids, query, keys, values, rim, after))
        return pieces[-1]

    att = attend([s[1] for s in split_up])
    pull, far = [], []
    for h in range(heads):
        more = strips[1:2] if h == heads - 1 else []
        p = total(split_up[h][0], away[h], [att] + pull + more)
        for b in order[h][1:-1]:
            p = total(p, swap(p, b), [])
        pull.append(p)
        far.append(swap(p, order[h][-1]))
        att = attend([p])
    while len(pieces) < per_head * heads:
        att = attend([att])
    both = [x for h in range(heads) for x in (pull[h], far[h])]
    new = renorm(ids, tokens_all, fast_weights, both, [att] + strips[:1])

    cut = rows // 2
    merged, rest, weights = [], [], None
    for h in range(heads):
        b = order[h][0]
        near = swap(new[h], b)
        blocks = [new[h], near, swap(new[h], 1), swap(near, 1)]
        own = pieces[h * per_head : (h + 1) * per_head]
        m, r, weights = apply(h, heads, ids, query, own, blocks, cut, weights, strips)
        merged.append(m)
        rest.append(r)
    to_right = [[shift(m, "head", 1) for m in merged]]
    to_left = [[shift(m, "head", -1) for m in merged]]

    near = stack([s[None] for s in strips], [merged[-1]])
    partial = partials(rest, out_weight, groups, [near])
    near = near.reshape((1,) + near.shape)
    after = near
    x = None
    for t in range(1, groups):
        right, left = [], []
        for h in range(heads):
            r, l, x = ring_step(
                t,
                groups,
                ids,
                step_at[t],
                tail_at,
                h,
                to_right[t - 1][h],
                to_left[t - 1][h],
                partial,
                x,
                [after],
            )
            after = l
            right.append(shift(r, "head", 1))
            left.append(shift(l, "head", -1))
        to_right.append(right)
        to_left.append(left)
        due = spread[:1] if t == 1 else spread[1:-1] if t == groups - 1 else []
        for b in due:
            near = stack([near, swap(near, b)], [after])
    out = gathered(
        ids,
        tail_at,
        merged,
        x,
        out_weight,
        near,
        swap(near, 1),
        rows,
        [after],
    )
    for h in range(heads):
        out = finish(ids, tail_at, h, to_right[-1][h], to_left[-1][h], partial, out)
    return (out, weights)


def solution(mesh):
    placed = (
        P("ctx", "head"),
        P("ctx", "head"),
        P("ctx", "head"),
        P("ctx", "head"),
        P("head", None, None, None),
        P("head", None),
    )
    return jax.shard_map(
        shards,
        mesh=mesh,
        in_specs=placed,
        out_specs=(P("ctx", "head"), P("head", None, None, None)),
        check_vma=False,
    )
```

time: 415 us -> 193 us (0.47); the launches traced: 409 us -> 193 us
  local copies, waits for them, and re-layouts: 112 us -> 3.64 us
  waiting for transfers between devices: 143 us -> 54.9 us
  matrix products: 69.7 us -> 0 us
  starting transfers between devices: 7.9 us -> 71.7 us
  Pallas kernels: 0 us -> 61 us
  other arithmetic: 48.8 us -> 0.01 us
  between operations: 14.2 us -> 1.56 us
  blocking collectives: 12.5 us -> 0 us
    reduce_scatter x1 -> x0, waiting for transfers between devices: 142 us -> none  [shards(): lax.psum_scatter(partial_out.astype(jnp.bfloat16), 'head', scatter_dimens...]
    dynamic_update_slice x4 -> x0, local copies, waits for them, and re-layouts: 80 us -> none  [attention(): lax.map(one_block, jnp.arange(tok_rows // block_rows, dtype=jnp.int32))]
    dot_general x21 -> x0, matrix products: 69.7 us -> none  [the longest x2 16.3 us: one_block(): jnp.einsum('qhd,khd->hqk', q_block, k_block, preferred_element_type=jnp.f...]
    ppermute x2 -> x35, starting transfers between devices: 7.82 us -> 71.7 us  [the longest x17 48.1 us: shift(): lax.ppermute(block, axis, [(i, i + distance) for i in range(n) if 0 <= i...]
    pallas_call x0 -> x26, Pallas kernels: none -> 61 us  [the longest x2 17.2 us: grads(): pl.pallas_call(functools.partial(grads_kernel, h, at), grid=(1,), in_spec...]
    ppermute x2 -> x35, waiting for transfers between devices: 0.01 us -> 54.9 us  [the longest x17 31.9 us: shift(): lax.ppermute(block, axis, [(i, i + distance) for i in range(n) if 0 <= i...]
    sub x2 -> x0, other arithmetic: 32.5 us -> none  [one_block(): exps = jnp.exp(scores - top_score)]
    unnamed x33 -> x32, local copies, waits for them, and re-layouts: 22 us -> 2.95 us
  transfers between devices with their start and end apart: 4 -> 35, of which waited for: 1 -> 16; matrix products, arithmetic and copies ran while one was open for 46% -> 0% of each run, Pallas kernels for 0% -> 25%
where the time goes in v3:
time: 193 us
  starting transfers between devices  71.7 us (37%)
  Pallas kernels  61 us (32%)
  waiting for transfers between devices  54.9 us (28%)
  local copies, waits for them, and re-layouts  3.64 us (2%)
    ppermute x17, starting transfers between devices, shift(): lax.ppermute(block, axis, [(i, i + distance) for i in range(n) if 0 <= i...  48.1 us
    ppermute x17, waiting for transfers between devices, shift(): lax.ppermute(block, axis, [(i, i + distance) for i in range(n) if 0 <= i...  31.9 us
    pallas_call x2, Pallas kernels, grads(): pl.pallas_call(functools.partial(grads_kernel, h, at), grid=(1,), in_spec...  17.2 us
    ppermute x15, starting transfers between devices, swap(): return lax.ppermute(block, 'ctx', [(i, i ^ bit) for i in range(n)])  16.4 us
    ppermute x3, waiting for transfers between devices, rotate(): lax.ppermute(block, axis, [(i, (i + distance) % n) for i in range(n)])  14.7 us
    pallas_call x1, Pallas kernels, gathered(): pl.pallas_call(functools.partial(gathered_kernel, n, heads, parts, at), g...  8.73 us
    ppermute x15, waiting for transfers between devices, swap(): return lax.ppermute(block, 'ctx', [(i, i ^ bit) for i in range(n)])  8.29 us
    pallas_call x4, Pallas kernels, attention(): pl.pallas_call(attn_kernel, grid=(1,), in_specs=[SMEM, col, col, col, of_...  8.26 us
  transfers between devices with their start and end apart: 35, of which 16 were waited for; matrix products, arithmetic and copies ran while one was open for 0% of the time, Pallas kernels for 25%

profile of v3, /device:TPU:0, one launch (start us, length us, event | category | flops | bytes accessed | tf_op | source)
XLA Modules:
  0.0 192.8 jit_solution(18246535450799997420)
XLA Ops:
  0.8 0.7 stack.137.ids_ref
  1.5 8.7 %shard_map.77 = (bf16[3088,128]{1,0:T(8,128)(2,1)}, bf16[3088,128]{1,0:T(8,128)(2,1)}, bf16[512,1024]{1,0:T(8,128)(2,1)}, bf16[128,1024]{1,0:T(8,128)(2,1)}, bf1...) custom-call(s32[31]{0:T(128)} %stack.137.ids_ref, s32[2,1024]{1,0:T(2,128)} %bitcast.38, bf16[1024,1024]{1,0:T(8,128)(2,1)} %k_ref.7, ...), custom_call_target="tpu_custom_call" | custom-call | flops 960000000 | tf_op jit(solution)/shard_map/pallas_call | solution.py:165
  10.2 2.6 %collective-permute-start = (bf16[512,1024]{1,0:T(8,128)(2,1)}, bf16[512,1024]{1,0:T(8,128)(2,1)S(1)}, u32[]{:S(2)}, u32[]{:S(2)}) collective-permute-start(bf16[512,1024]{1,0:T(8,128)(2,1)} %get-tuple-element.40), channel_id=1, source_target_pairs={{0,4},{4,8},{8,12},{12,16},{16,20},{20,24},{24,28},{1,5},{5,9},{9,... | collective-permute-start | bytes 3145736 | tf_op jit(solution)/shard_map/ppermute | solution.py:43
  12.8 2.6 %collective-permute-start.2 = (bf16[3088,128]{1,0:T(8,128)(2,1)}, bf16[3088,128]{1,0:T(8,128)(2,1)S(1)}, u32[]{:S(2)}, u32[]{:S(2)}) collective-permute-start(bf16[3088,128]{1,0:T(8,128)(2,1)} %get-tuple-element.44), channel_id=1, source_target_pairs={{0,4},{4,0},{8,12},{12,8},{16,20},{20,16},{24,28},{28,24},{1,5},{5... | collective-permute-start | bytes 2371592 | tf_op jit(solution)/shard_map/ppermute | solution.py:53
  15.4 8.5 %shard_map.78 = (bf16[3088,128]{1,0:T(8,128)(2,1)}, bf16[3088,128]{1,0:T(8,128)(2,1)}) custom-call(s32[31]{0:T(128)} %stack.137.ids_ref, s32[2,1024]{1,0:T(2,128)} %bitcast.39, bf16[1024,1024]{1,0:T(8,128)(2,1)} %k_ref.7, bf16[1024,1024]{1,0:T(8,128)(2,1)} %v_ref.7, bf16[2,3,512,512]{3,2,1,0:T(8,128)(2,1)} %base_ref.1, ...), custom_call_target="tpu_custom_call" | custom-call | flops 960000000 | tf_op jit(solution)/shard_map/pallas_call | solution.py:165
  24.1 0.9 shard_map.79
  24.9 5.4 %collective-permute-start.4 = (bf16[1552,128]{1,0:T(8,128)(2,1)S(1)}, bf16[1552,128]{1,0:T(8,128)(2,1)S(1)}, u32[]{:S(2)}, u32[]{:S(2)}) collective-permute-start(bf16[1552,128]{1,0:T(8,128)(2,1)S(1)} %get-tuple-element.45.refs_0_.rest_0_), channel_id=1, source_target_pairs={{0,8},{4,12},{8,0},{12,4},{16,24},{20,28},{24,16},{28,20},{1,9},{5... | collective-permute-start | bytes 1191944 | tf_op jit(solution)/shard_map/ppermute | solution.py:53
  30.4 1.1 copy-done.8
  31.5 0.9 shard_map.80
  32.4 1.6 collective-permute-start.3
  34.0 2.6 %collective-permute-start.5 = (bf16[128,1024]{1,0:T(8,128)(2,1)S(1)}, bf16[128,1024]{1,0:T(8,128)(2,1)S(1)}, u32[]{:S(2)}, u32[]{:S(2)}) collective-permute-start(bf16[128,1024]{1,0:T(8,128)(2,1)S(1)} %copy-done.13), channel_id=1, source_target_pairs={{0,2},{1,3},{2,0},{3,1},{4,6},{5,7},{6,4},{7,5},{8,10},{9,11},{10,... | collective-permute-start | bytes 786440 | tf_op jit(solution)/shard_map/ppermute | solution.py:48
  36.6 2.1 %shard_map.81.rest_0_.refs_0_ = bf16[1024,256]{1,0:T(8,128)(2,1)S(1)} custom-call(s32[31]{0:T(128)S(1)} %copy-done.9, bf16[1024,1024]{1,0:T(8,128)(2,1)S(1)} %copy-done.2, bf16[1024,1024]{1,0:T(8,128)(2,1)S(1)} %copy-done, bf16[1024,1024]{1,0:T(8,128)(2,1)S(1)} %copy-done.1, bf16[512,1024]{1,0:T(8,128)(2,1)S(1)} %collective-permute-done.refs_0_.rim_ref, ...), custom_call_target="tpu_custom_call" | custom-call | flops 252000000 | tf_op jit(solution)/shard_map/pallas_call | solution.py:328
  38.6 0.6 collective-permute-done.4.b_hbm
  39.7 2.1 %shard_map.83.rest_0_.refs_1_ = bf16[1024,256]{1,0:T(8,128)(2,1)S(1)} custom-call(s32[31]{0:T(128)S(1)} %copy-done.9, bf16[1024,1024]{1,0:T(8,128)(2,1)S(1)} %copy-done.2, bf16[1024,1024]{1,0:T(8,128)(2,1)S(1)} %copy-done, bf16[1024,1024]{1,0:T(8,128)(2,1)S(1)} %copy-done.1, bf16[512,1024]{1,0:T(8,128)(2,1)S(1)} %collective-permute-done.refs_0_.rim_ref, ...), custom_call_target="tpu_custom_call" | custom-call | flops 252000000 | tf_op jit(solution)/shard_map/pallas_call | solution.py:328
  41.8 4.4 %collective-permute-done.5.rest_2_.refs_7_.refs_8_ = bf16[128,1024]{1,0:T(8,128)(2,1)S(1)} collective-permute-done((bf16[128,1024]{1,0:T(8,128)(2,1)S(1)}, bf16[128,1024]{1,0:T(8,128)(2,1)S(1)}, u32[]{:S(2)}, u32[]{:S(2)}) %collective-permute-start.5) | collective-permute-done | bytes 262176 | tf_op jit(solution)/shard_map/ppermute | solution.py:48
  46.7 1.8 collective-permute-start.7
  49.0 0.7 collective-permute-start.8
  49.7 2.1 %shard_map.85.rest_0_.refs_0_ = bf16[1024,256]{1,0:T(8,128)(2,1)S(1)} custom-call(s32[31]{0:T(128)S(1)} %copy-done.9, bf16[1024,1024]{1,0:T(8,128)(2,1)S(1)} %copy-done.2, bf16[1024,1024]{1,0:T(8,128)(2,1)S(1)} %copy-done, bf16[1024,1024]{1,0:T(8,128)(2,1)S(1)} %copy-done.1, bf16[512,1024]{1,0:T(8,128)(2,1)S(1)} %collective-permute-done.refs_0_.rim_ref, ...), custom_call_target="tpu_custom_call" | custom-call | flops 252000000 | tf_op jit(solution)/shard_map/pallas_call | solution.py:328
  51.8 2.1 %shard_map.86.refs_4_.refs_1_ = bf16[1024,256]{1,0:T(8,128)(2,1)S(1)} custom-call(s32[31]{0:T(128)S(1)} %copy-done.9, bf16[1024,1024]{1,0:T(8,128)(2,1)S(1)} %copy-done.2, bf16[1024,1024]{1,0:T(8,128)(2,1)S(1)} %copy-done, bf16[1024,1024]{1,0:T(8,128)(2,1)S(1)} %copy-done.1, bf16[512,1024]{1,0:T(8,128)(2,1)S(1)} %collective-permute-done.refs_0_.rim_ref, ...), custom_call_target="tpu_custom_call" | custom-call | flops 252000000 | tf_op jit(solution)/shard_map/pallas_call | solution.py:328
  53.8 4.6 %collective-permute-done.8.refs_5_.refs_6_.refs_7_ = bf16[128,1024]{1,0:T(8,128)(2,1)S(1)} collective-permute-done((bf16[128,1024]{1,0:T(8,128)(2,1)S(1)}, bf16[128,1024]{1,0:T(8,128)(2,1)S(1)}, u32[]{:S(2)}, u32[]{:S(2)}) %collective-permute-start.8) | collective-permute-done | bytes 262176 | tf_op jit(solution)/shard_map/ppermute | solution.py:48
  58.4 2.1 %shard_map.87 = (bf16[3,512,128]{2,1,0:T(8,128)(2,1)S(1)}, bf16[3,512,128]{2,1,0:T(8,128)(2,1)S(1)}) custom-call(s32[31]{0:T(128)S(1)} %copy-done.9, bf16[2,3,512,512]{3,2,1,0:T(8,128)(2,1)S(1)} %copy-done.3, bf16[1552,128]{1,0:T(8,128)(2,1)S(1)} %shard_map.82.rest_0_.rest_1_.refs_0_, bf16[1552,128]{1,0:T(8,128)(2,1)S(1)} %collective-permute-done.6.refs_1_, ...), custom_call_target="tpu_custom_call" | custom-call | flops 252000000 | tf_op jit(solution)/shard_map/pallas_call | solution.py:277
  60.5 1.6 collective-permute-start.12
  62.4 7.7 %collective-permute-done.12.refs_3_ = bf16[3,512,128]{2,1,0:T(8,128)(2,1)S(1)} collective-permute-done((bf16[3,512,128]{2,1,0:T(8,128)(2,1)S(1)}, bf16[3,512,128]{2,1,0:T(8,128)(2,1)S(1)}, u32[]{:S(2)}, u32[]{:S(2)}) %collective-permute-start.12) | collective-permute-done | bytes 393248 | tf_op jit(solution)/shard_map/ppermute | solution.py:53
  70.1 4.0 %collective-permute-start.15 = (bf16[128,1024]{1,0:T(8,128)(2,1)S(1)}, bf16[128,1024]{1,0:T(8,128)(2,1)S(1)}, u32[]{:S(2)}, u32[]{:S(2)}) collective-permute-start(bf16[128,1024]{1,0:T(8,128)(2,1)S(1)} %copy-done.11), channel_id=1, source_target_pairs={{0,3},{1,0},{2,1},{3,2},{4,7},{5,4},{6,5},{7,6},{8,11},{9,8},{10,9... | collective-permute-start | bytes 786440 | tf_op jit(solution)/shard_map/ppermute | solution.py:48
  74.6 5.7 %collective-permute-done.15.refs_8_.refs_9_ = bf16[128,1024]{1,0:T(8,128)(2,1)S(1)} collective-permute-done((bf16[128,1024]{1,0:T(8,128)(2,1)S(1)}, bf16[128,1024]{1,0:T(8,128)(2,1)S(1)}, u32[]{:S(2)}, u32[]{:S(2)}) %collective-permute-start.15) | collective-permute-done | bytes 262176 | tf_op jit(solution)/shard_map/ppermute | solution.py:48
  80.3 3.2 %shard_map.88 = (bf16[512,512]{1,0:T(8,128)(2,1)S(1)}, bf16[512,512]{1,0:T(8,128)(2,1)S(1)}, bf16[2,3,512,512]{3,2,1,0:T(8,128)(2,1)}) custom-call(s32[31]{0:T(128)S(1)} %copy-done.9, bf16[1024,1024]{1,0:T(8,128)(2,1)S(1)} %copy-done.2, bf16[1024,256]{1,0:T(8,128)(2,1)S(1)} %shard_map.81.rest_0_.refs_0_, bf16[1024,256]{1,0:T(8,128)(2,1)S(1)} %shard_map.83.rest_0_.refs_1_, ...), custom_call_target="tpu_custom_call" | custom-call | flops 396000000 | tf_op jit(solution)/shard_map/pallas_call | solution.py:388
  83.6 1.6 collective-permute-start.18
  85.2 1.3 collective-permute-start.19
  86.5 3.2 %shard_map.89 = (bf16[512,512]{1,0:T(8,128)(2,1)S(1)}, bf16[512,512]{1,0:T(8,128)(2,1)S(1)}, bf16[2,3,512,512]{3,2,1,0:T(8,128)(2,1)}) custom-call(s32[31]{0:T(128)S(1)} %copy-done.9, bf16[1024,1024]{1,0:T(8,128)(2,1)S(1)} %copy-done.2, bf16[1024,256]{1,0:T(8,128)(2,1)S(1)} %shard_map.85.rest_0_.refs_0_, ...), custom_call_target="tpu_custom_call", output_to_operand_aliasing={{2}: (8, {})} | custom-call | flops 396000000 | tf_op jit(solution)/shard_map/pallas_call | solution.py:388
  89.8 4.7 %collective-permute-start.16 = (bf16[512,512]{1,0:T(8,128)(2,1)S(1)}, bf16[512,512]{1,0:T(8,128)(2,1)S(1)}, u32[]{:S(2)}, u32[]{:S(2)}) collective-permute-start(bf16[512,512]{1,0:T(8,128)(2,1)S(1)} %get-tuple-element.55.refs_3_.refs_1_), channel_id=1, source_target_pairs={{0,1},{1,2},{2,3},{4,5},{5,6},{6,7},{8,9},{9,10},{10,11},{12,13},{... | collective-permute-start | bytes 1572872 | tf_op jit(solution)/shard_map/ppermute | solution.py:43
  94.5 1.3 collective-permute-start.17
  95.9 1.4 collective-permute-start.32
  97.3 5.7 %shard_map.91.p_hbm = bf16[4,512,1024]{2,1,0:T(8,128)(2,1)S(1)} custom-call(bf16[512,512]{1,0:T(8,128)(2,1)S(1)} %get-tuple-element.56.refs_0_, bf16[512,512]{1,0:T(8,128)(2,1)S(1)} %get-tuple-element.57.refs_1_, bf16[1024,4096]{1,0:T(8,128)(2,1)S(1)} %bitcast.31, bf16[3,128,1024]{2,1,0:T(8,128)(2,1)S(1)} %shard_map.90.refs_3_), custom_call_target="tpu_custom_call" | custom-call | flops 120000000 | tf_op jit(solution)/shard_map/pallas_call | solution.py:428
  103.1 1.0 shard_map.92
  104.1 6.2 %collective-permute-start.22 = (bf16[512,512]{1,0:T(8,128)(2,1)S(1)}, bf16[512,512]{1,0:T(8,128)(2,1)S(1)}, u32[]{:S(2)}, u32[]{:S(2)}) collective-permute-start(bf16[512,512]{1,0:T(8,128)(2,1)S(1)} %get-tuple-element.63), channel_id=1, source_target_pairs={{0,1},{1,2},{2,3},{4,5},{5,6},{6,7},{8,9},{9,10},{10,11},{12,13},{... | collective-permute-start | bytes 1572872 | tf_op jit(solution)/shard_map/ppermute | solution.py:43
  110.2 1.3 collective-permute-start.23
  111.5 0.7 collective-permute-done.17.left_hbm
  112.3 1.0 shard_map.93
  113.3 5.8 %collective-permute-start.20 = (bf16[512,512]{1,0:T(8,128)(2,1)S(1)}, bf16[512,512]{1,0:T(8,128)(2,1)S(1)}, u32[]{:S(2)}, u32[]{:S(2)}) collective-permute-start(bf16[512,512]{1,0:T(8,128)(2,1)S(1)} %get-tuple-element.61), channel_id=1, source_target_pairs={{0,1},{1,2},{2,3},{4,5},{5,6},{6,7},{8,9},{9,10},{10,11},{12,13},{... | collective-permute-start | bytes 1572872 | tf_op jit(solution)/shard_map/ppermute | solution.py:43
  119.1 1.6 collective-permute-start.21
  121.3 1.3 collective-permute-done.22.right_hbm
  122.6 4.4 %collective-permute-done.23.left_hbm = bf16[512,512]{1,0:T(8,128)(2,1)S(1)} collective-permute-done((bf16[512,512]{1,0:T(8,128)(2,1)S(1)}, bf16[512,512]{1,0:T(8,128)(2,1)S(1)}, u32[]{:S(2)}, u32[]{:S(2)}) %collective-permute-start.23) | collective-permute-done | bytes 524320 | tf_op jit(solution)/shard_map/ppermute | solution.py:43
  127.0 1.0 shard_map.94
  128.0 3.9 %collective-permute-start.26 = (bf16[512,512]{1,0:T(8,128)(2,1)S(1)}, bf16[512,512]{1,0:T(8,128)(2,1)S(1)}, u32[]{:S(2)}, u32[]{:S(2)}) collective-permute-start(bf16[512,512]{1,0:T(8,128)(2,1)S(1)} %get-tuple-element.69), channel_id=1, source_target_pairs={{0,1},{1,2},{2,3},{4,5},{5,6},{6,7},{8,9},{9,10},{10,11},{12,13},{... | collective-permute-start | bytes 1572872 | tf_op jit(solution)/shard_map/ppermute | solution.py:43
  132.0 1.3 collective-permute-start.27
  133.8 4.4 %collective-permute-done.21.left_hbm = bf16[512,512]{1,0:T(8,128)(2,1)S(1)} collective-permute-done((bf16[512,512]{1,0:T(8,128)(2,1)S(1)}, bf16[512,512]{1,0:T(8,128)(2,1)S(1)}, u32[]{:S(2)}, u32[]{:S(2)}) %collective-permute-start.21) | collective-permute-done | bytes 524320 | tf_op jit(solution)/shard_map/ppermute | solution.py:43
  138.2 1.0 shard_map.95
  139.2 3.9 %collective-permute-start.24 = (bf16[512,512]{1,0:T(8,128)(2,1)S(1)}, bf16[512,512]{1,0:T(8,128)(2,1)S(1)}, u32[]{:S(2)}, u32[]{:S(2)}) collective-permute-start(bf16[512,512]{1,0:T(8,128)(2,1)S(1)} %get-tuple-element.67), channel_id=1, source_target_pairs={{0,1},{1,2},{2,3},{4,5},{5,6},{6,7},{8,9},{9,10},{10,11},{12,13},{... | collective-permute-start | bytes 1572872 | tf_op jit(solution)/shard_map/ppermute | solution.py:43
  143.2 1.3 collective-permute-start.25
  145.0 4.4 %collective-permute-done.27.left_hbm = bf16[512,512]{1,0:T(8,128)(2,1)S(1)} collective-permute-done((bf16[512,512]{1,0:T(8,128)(2,1)S(1)}, bf16[512,512]{1,0:T(8,128)(2,1)S(1)}, u32[]{:S(2)}, u32[]{:S(2)}) %collective-permute-start.27) | collective-permute-done | bytes 524320 | tf_op jit(solution)/shard_map/ppermute | solution.py:43
  149.5 1.0 shard_map.96
  150.5 3.7 %collective-permute-done.24.right_hbm = bf16[512,512]{1,0:T(8,128)(2,1)S(1)} collective-permute-done((bf16[512,512]{1,0:T(8,128)(2,1)S(1)}, bf16[512,512]{1,0:T(8,128)(2,1)S(1)}, u32[]{:S(2)}, u32[]{:S(2)}) %collective-permute-start.24) | collective-permute-done | bytes 524320 | tf_op jit(solution)/shard_map/ppermute | solution.py:43
  154.1 4.1 %collective-permute-done.25.left_hbm = bf16[512,512]{1,0:T(8,128)(2,1)S(1)} collective-permute-done((bf16[512,512]{1,0:T(8,128)(2,1)S(1)}, bf16[512,512]{1,0:T(8,128)(2,1)S(1)}, u32[]{:S(2)}, u32[]{:S(2)}) %collective-permute-start.25) | collective-permute-done | bytes 524320 | tf_op jit(solution)/shard_map/ppermute | solution.py:43
  158.3 1.0 shard_map.97
  159.6 4.1 %collective-permute-start.30 = (bf16[512,512]{1,0:T(8,128)(2,1)S(1)}, bf16[512,512]{1,0:T(8,128)(2,1)S(1)}, u32[]{:S(2)}, u32[]{:S(2)}) collective-permute-start(bf16[512,512]{1,0:T(8,128)(2,1)S(1)} %get-tuple-element.75), channel_id=1, source_target_pairs={{0,1},{1,2},{2,3},{4,5},{5,6},{6,7},{8,9},{9,10},{10,11},{12,13},{... | collective-permute-start | bytes 1572872 | tf_op jit(solution)/shard_map/ppermute | solution.py:43
  163.7 1.3 collective-permute-start.31
  165.0 4.6 %collective-permute-start.28 = (bf16[512,512]{1,0:T(8,128)(2,1)S(1)}, bf16[512,512]{1,0:T(8,128)(2,1)S(1)}, u32[]{:S(2)}, u32[]{:S(2)}) collective-permute-start(bf16[512,512]{1,0:T(8,128)(2,1)S(1)} %get-tuple-element.73), channel_id=1, source_target_pairs={{0,1},{1,2},{2,3},{4,5},{5,6},{6,7},{8,9},{9,10},{10,11},{12,13},{... | collective-permute-start | bytes 1572872 | tf_op jit(solution)/shard_map/ppermute | solution.py:43
  169.6 1.3 collective-permute-start.29
  170.9 1.7 copy-done.10
  172.7 8.7 %shard_map.100.out_in = bf16[1024,1024]{1,0:T(8,128)(2,1)} custom-call(s32[31]{0:T(128)S(1)} %copy-done.9, bf16[512,512]{1,0:T(8,128)(2,1)S(1)} %get-tuple-element.58.refs_0_, bf16[512,512]{1,0:T(8,128)(2,1)S(1)} %get-tuple-element.55.refs_3_.refs_1_, bf16[3,512,1024]{2,1,0:T(8,128)(2,1)S(1)} %get-tuple-element.76.refs_2_, bf16[1024,4096]{1,0:T(8,128)(2,1)} %refs_3_.1, ...), custom_call_target="tpu_custom_call" | custom-call | flops 1080000000 | tf_op jit(solution)/shard_map/pallas_call | solution.py:542
  181.5 1.7 shard_map.101.out_in
  183.2 3.6 %collective-permute-done.28.right_hbm = bf16[512,512]{1,0:T(8,128)(2,1)S(1)} collective-permute-done((bf16[512,512]{1,0:T(8,128)(2,1)S(1)}, bf16[512,512]{1,0:T(8,128)(2,1)S(1)}, u32[]{:S(2)}, u32[]{:S(2)}) %collective-permute-start.28) | collective-permute-done | bytes 524320 | tf_op jit(solution)/shard_map/ppermute | solution.py:43
  186.7 4.1 %collective-permute-done.29.left_hbm = bf16[512,512]{1,0:T(8,128)(2,1)S(1)} collective-permute-done((bf16[512,512]{1,0:T(8,128)(2,1)S(1)}, bf16[512,512]{1,0:T(8,128)(2,1)S(1)}, u32[]{:S(2)}, u32[]{:S(2)}) %collective-permute-start.29) | collective-permute-done | bytes 524320 | tf_op jit(solution)/shard_map/ppermute | solution.py:43
  190.9 1.7 shard_map.102
  (66 shorter events, 4.6 us)
Async XLA Ops:
  10.2 13.9 %collective-permute-start = (bf16[512,1024]{1,0:T(8,128)(2,1)}, bf16[512,1024]{1,0:T(8,128)(2,1)S(1)}, u32[]{:S(2)}, u32[]{:S(2)}) collective-permute-start(bf16[512,1024]{1,0:T(8,128)(2,1)} %get-tuple-element.40), channel_id=1, source_target_pairs={{0,4},{4,8},{8,12},{12,16},{16,20},{20,24},{24,28},{1,5},{5,9},{9,... | collective-permute-start | bytes 3145736 | tf_op jit(solution)/shard_map/ppermute | solution.py:43
  12.8 11.2 %collective-permute-start.2 = (bf16[3088,128]{1,0:T(8,128)(2,1)}, bf16[3088,128]{1,0:T(8,128)(2,1)S(1)}, u32[]{:S(2)}, u32[]{:S(2)}) collective-permute-start(bf16[3088,128]{1,0:T(8,128)(2,1)} %get-tuple-element.44), channel_id=1, source_target_pairs={{0,4},{4,0},{8,12},{12,8},{16,20},{20,16},{24,28},{28,24},{1,5},{5... | collective-permute-start | bytes 2371592 | tf_op jit(solution)/shard_map/ppermute | solution.py:53
  15.4 8.7 %copy-start.7 = (bf16[3088,128]{1,0:T(8,128)(2,1)S(1)}, bf16[3088,128]{1,0:T(8,128)(2,1)}, u32[]{:S(2)}) copy-start(bf16[3088,128]{1,0:T(8,128)(2,1)} %get-tuple-element.41.refs_0_.keep_hbm) | copy-start | bytes 2371588
  15.4 8.7 %copy-start.9 = (s32[31]{0:T(128)S(1)}, s32[31]{0:T(128)}, u32[]{:S(2)}) copy-start(s32[31]{0:T(128)} %stack.137.ids_ref) | copy-start | bytes 376
  15.4 18.6 %copy-start.13 = (bf16[128,1024]{1,0:T(8,128)(2,1)S(1)}, bf16[128,1024]{1,0:T(8,128)(2,1)}, u32[]{:S(2)}) copy-start(bf16[128,1024]{1,0:T(8,128)(2,1)} %get-tuple-element.49) | copy-start | bytes 786436
  15.4 21.2 %copy-start.2 = (bf16[1024,1024]{1,0:T(8,128)(2,1)S(1)}, bf16[1024,1024]{1,0:T(8,128)(2,1)}, u32[]{:S(2)}) copy-start(bf16[1024,1024]{1,0:T(8,128)(2,1)} %q_hbm.3) | copy-start | bytes 6291460
  23.9 12.7 %copy-start = (bf16[1024,1024]{1,0:T(8,128)(2,1)S(1)}, bf16[1024,1024]{1,0:T(8,128)(2,1)}, u32[]{:S(2)}) copy-start(bf16[1024,1024]{1,0:T(8,128)(2,1)} %k_ref.7) | copy-start | bytes 6291460
  23.9 12.6 %copy-start.1 = (bf16[1024,1024]{1,0:T(8,128)(2,1)S(1)}, bf16[1024,1024]{1,0:T(8,128)(2,1)}, u32[]{:S(2)}) copy-start(bf16[1024,1024]{1,0:T(8,128)(2,1)} %v_ref.7) | copy-start | bytes 6291460
  23.9 6.4 %collective-permute-start.1 = (bf16[3088,128]{1,0:T(8,128)(2,1)}, bf16[3088,128]{1,0:T(8,128)(2,1)S(1)}, u32[]{:S(2)}, u32[]{:S(2)}) collective-permute-start(bf16[3088,128]{1,0:T(8,128)(2,1)} %get-tuple-element.43), channel_id=1, source_target_pairs={{0,4},{4,0},{8,12},{12,8},{16,20},{20,16},{24,28},{28,24},{1,5},{5... | collective-permute-start | bytes 2371592 | tf_op jit(solution)/shard_map/ppermute | solution.py:53
  24.9 14.3 %collective-permute-start.4 = (bf16[1552,128]{1,0:T(8,128)(2,1)S(1)}, bf16[1552,128]{1,0:T(8,128)(2,1)S(1)}, u32[]{:S(2)}, u32[]{:S(2)}) collective-permute-start(bf16[1552,128]{1,0:T(8,128)(2,1)S(1)} %get-tuple-element.45.refs_0_.rest_0_), channel_id=1, source_target_pairs={{0,8},{4,12},{8,0},{12,4},{16,24},{20,28},{24,16},{28,20},{1,9},{5... | collective-permute-start | bytes 1191944 | tf_op jit(solution)/shard_map/ppermute | solution.py:53
  30.4 1.1 copy-start.8
  32.4 13.8 %collective-permute-start.3 = (bf16[1552,128]{1,0:T(8,128)(2,1)S(1)}, bf16[1552,128]{1,0:T(8,128)(2,1)S(1)}, u32[]{:S(2)}, u32[]{:S(2)}) collective-permute-start(bf16[1552,128]{1,0:T(8,128)(2,1)S(1)} %get-tuple-element.47.rest_1_), channel_id=1, source_target_pairs={{0,16},{4,20},{8,24},{12,28},{16,0},{20,4},{24,8},{28,12},{1,17},{... | collective-permute-start | bytes 1191944 | tf_op jit(solution)/shard_map/ppermute | solution.py:53
  34.0 12.2 %collective-permute-start.5 = (bf16[128,1024]{1,0:T(8,128)(2,1)S(1)}, bf16[128,1024]{1,0:T(8,128)(2,1)S(1)}, u32[]{:S(2)}, u32[]{:S(2)}) collective-permute-start(bf16[128,1024]{1,0:T(8,128)(2,1)S(1)} %copy-done.13), channel_id=1, source_target_pairs={{0,2},{1,3},{2,0},{3,1},{4,6},{5,7},{6,4},{7,5},{8,10},{9,11},{10,... | collective-permute-start | bytes 786440 | tf_op jit(solution)/shard_map/ppermute | solution.py:48
  39.7 9.3 %copy-start.12 = (bf16[128,1024]{1,0:T(8,128)(2,1)S(1)}, bf16[128,1024]{1,0:T(8,128)(2,1)}, u32[]{:S(2)}) copy-start(bf16[128,1024]{1,0:T(8,128)(2,1)} %get-tuple-element.50) | copy-start | bytes 786436
  46.7 11.7 %collective-permute-start.7 = (bf16[1552,128]{1,0:T(8,128)(2,1)S(1)}, bf16[1552,128]{1,0:T(8,128)(2,1)S(1)}, u32[]{:S(2)}, u32[]{:S(2)}) collective-permute-start(bf16[1552,128]{1,0:T(8,128)(2,1)S(1)} %shard_map.84.rest_0_.refs_2_), channel_id=1, source_target_pairs={{0,8},{4,12},{8,0},{12,4},{16,24},{20,28},{24,16},{28,20},{1,9},{5... | collective-permute-start | bytes 1191944 | tf_op jit(solution)/shard_map/ppermute | solution.py:53
  48.5 9.9 %collective-permute-start.6 = (bf16[1552,128]{1,0:T(8,128)(2,1)S(1)}, bf16[1552,128]{1,0:T(8,128)(2,1)S(1)}, u32[]{:S(2)}, u32[]{:S(2)}) collective-permute-start(bf16[1552,128]{1,0:T(8,128)(2,1)S(1)} %shard_map.82.rest_0_.rest_1_.refs_0_), channel_id=1, source_target_pairs={{0,16},{4,20},{8,24},{12,28},{16,0},{20,4},{24,8},{28,12},{1,17},{... | collective-permute-start | bytes 1191944 | tf_op jit(solution)/shard_map/ppermute | solution.py:53
  49.0 9.4 %collective-permute-start.8 = (bf16[128,1024]{1,0:T(8,128)(2,1)S(1)}, bf16[128,1024]{1,0:T(8,128)(2,1)S(1)}, u32[]{:S(2)}, u32[]{:S(2)}) collective-permute-start(bf16[128,1024]{1,0:T(8,128)(2,1)S(1)} %copy-done.12), channel_id=1, source_target_pairs={{0,1},{1,2},{2,3},{3,0},{4,5},{5,6},{6,7},{7,4},{8,9},{9,10},{10,1... | collective-permute-start | bytes 786440 | tf_op jit(solution)/shard_map/ppermute | solution.py:48
  51.7 6.7 %copy-start.3 = (bf16[2,3,512,512]{3,2,1,0:T(8,128)(2,1)S(1)}, bf16[2,3,512,512]{3,2,1,0:T(8,128)(2,1)}, u32[]{:S(2)}) copy-start(bf16[2,3,512,512]{3,2,1,0:T(8,128)(2,1)} %base_ref.1) | copy-start | bytes 9437188
  53.8 16.3 %copy-start.11 = (bf16[128,1024]{1,0:T(8,128)(2,1)S(1)}, bf16[128,1024]{1,0:T(8,128)(2,1)}, u32[]{:S(2)}) copy-start(bf16[128,1024]{1,0:T(8,128)(2,1)} %get-tuple-element.53) | copy-start | bytes 786436
  60.5 9.6 %collective-permute-start.12 = (bf16[3,512,128]{2,1,0:T(8,128)(2,1)S(1)}, bf16[3,512,128]{2,1,0:T(8,128)(2,1)S(1)}, u32[]{:S(2)}, u32[]{:S(2)}) collective-permute-start(bf16[3,512,128]{2,1,0:T(8,128)(2,1)S(1)} %get-tuple-element.52.refs_2_), channel_id=1, source_target_pairs={{0,8},{4,12},{8,0},{12,4},{16,24},{20,28},{24,16},{28,20},{1,9},{5... | collective-permute-start | bytes 1179656 | tf_op jit(solution)/shard_map/ppermute | solution.py:53
  62.1 12.3 %collective-permute-start.9 = (bf16[3,512,128]{2,1,0:T(8,128)(2,1)S(1)}, bf16[3,512,128]{2,1,0:T(8,128)(2,1)S(1)}, u32[]{:S(2)}, u32[]{:S(2)}) collective-permute-start(bf16[3,512,128]{2,1,0:T(8,128)(2,1)S(1)} %get-tuple-element.51.refs_2_), channel_id=1, source_target_pairs={{0,16},{4,20},{8,24},{12,28},{16,0},{20,4},{24,8},{28,12},{1,17},{... | collective-permute-start | bytes 1179656 | tf_op jit(solution)/shard_map/ppermute | solution.py:53
  62.4 17.9 %collective-permute-start.13 = (bf16[3,512,128]{2,1,0:T(8,128)(2,1)S(1)}, bf16[3,512,128]{2,1,0:T(8,128)(2,1)S(1)}, u32[]{:S(2)}, u32[]{:S(2)}) collective-permute-start(bf16[3,512,128]{2,1,0:T(8,128)(2,1)S(1)} %get-tuple-element.52.refs_2_), channel_id=1, source_target_pairs={{0,4},{4,0},{8,12},{12,8},{16,20},{20,16},{24,28},{28,24},{1,5},{5... | collective-permute-start | bytes 1179656 | tf_op jit(solution)/shard_map/ppermute | solution.py:53
  70.1 10.3 %collective-permute-start.14 = (bf16[3,512,128]{2,1,0:T(8,128)(2,1)S(1)}, bf16[3,512,128]{2,1,0:T(8,128)(2,1)S(1)}, u32[]{:S(2)}, u32[]{:S(2)}) collective-permute-start(bf16[3,512,128]{2,1,0:T(8,128)(2,1)S(1)} %collective-permute-done.12.refs_3_), channel_id=1, source_target_pairs={{0,4},{4,0},{8,12},{12,8},{16,20},{20,16},{24,28},{28,24},{1,5},{5... | collective-permute-start | bytes 1179656 | tf_op jit(solution)/shard_map/ppermute | solution.py:53
  70.1 10.2 %collective-permute-start.15 = (bf16[128,1024]{1,0:T(8,128)(2,1)S(1)}, bf16[128,1024]{1,0:T(8,128)(2,1)S(1)}, u32[]{:S(2)}, u32[]{:S(2)}) collective-permute-start(bf16[128,1024]{1,0:T(8,128)(2,1)S(1)} %copy-done.11), channel_id=1, source_target_pairs={{0,3},{1,0},{2,1},{3,2},{4,7},{5,4},{6,5},{7,6},{8,11},{9,8},{10,9... | collective-permute-start | bytes 786440 | tf_op jit(solution)/shard_map/ppermute | solution.py:48
  74.1 12.4 %collective-permute-start.10 = (bf16[3,512,128]{2,1,0:T(8,128)(2,1)S(1)}, bf16[3,512,128]{2,1,0:T(8,128)(2,1)S(1)}, u32[]{:S(2)}, u32[]{:S(2)}) collective-permute-start(bf16[3,512,128]{2,1,0:T(8,128)(2,1)S(1)} %get-tuple-element.51.refs_2_), channel_id=1, source_target_pairs={{0,4},{4,0},{8,12},{12,8},{16,20},{20,16},{24,28},{28,24},{1,5},{5... | collective-permute-start | bytes 1179656 | tf_op jit(solution)/shard_map/ppermute | solution.py:53
  74.3 12.2 %collective-permute-start.11 = (bf16[3,512,128]{2,1,0:T(8,128)(2,1)S(1)}, bf16[3,512,128]{2,1,0:T(8,128)(2,1)S(1)}, u32[]{:S(2)}, u32[]{:S(2)}) collective-permute-start(bf16[3,512,128]{2,1,0:T(8,128)(2,1)S(1)} %collective-permute-done.9.refs_3_), channel_id=1, source_target_pairs={{0,4},{4,0},{8,12},{12,8},{16,20},{20,16},{24,28},{28,24},{1,5},{5... | collective-permute-start | bytes 1179656 | tf_op jit(solution)/shard_map/ppermute | solution.py:53
  80.3 17.0 %slice-start = ((s8[8388608]{0:T(1024)(128)(4,1)}), s8[4194304]{0:T(1024)(128)(4,1)S(1)}, s32[]{:S(2)}) async-start(s8[8388608]{0:T(1024)(128)(4,1)} %bitcast.30), calls=%async_computation | async-start | bytes 8388608
  83.6 19.5 %collective-permute-start.18 = (bf16[512,512]{1,0:T(8,128)(2,1)S(1)}, bf16[512,512]{1,0:T(8,128)(2,1)S(1)}, u32[]{:S(2)}, u32[]{:S(2)}) collective-permute-start(bf16[512,512]{1,0:T(8,128)(2,1)S(1)} %get-tuple-element.58.refs_0_), channel_id=1, source_target_pairs={{0,1},{1,2},{2,3},{4,5},{5,6},{6,7},{8,9},{9,10},{10,11},{12,13},{... | collective-permute-start | bytes 1572872 | tf_op jit(solution)/shard_map/ppermute | solution.py:43
  85.2 17.8 %collective-permute-start.19 = (bf16[512,512]{1,0:T(8,128)(2,1)S(1)}, bf16[512,512]{1,0:T(8,128)(2,1)S(1)}, u32[]{:S(2)}, u32[]{:S(2)}) collective-permute-start(bf16[512,512]{1,0:T(8,128)(2,1)S(1)} %get-tuple-element.58.refs_0_), channel_id=1, source_target_pairs={{1,0},{2,1},{3,2},{5,4},{6,5},{7,6},{9,8},{10,9},{11,10},{13,12},{... | collective-permute-start | bytes 1572872 | tf_op jit(solution)/shard_map/ppermute | solution.py:43
  86.5 10.8 %slice-start.1 = ((s8[8388608]{0:T(1024)(128)(4,1)}), s8[4194304]{0:T(1024)(128)(4,1)S(1)}, s32[]{:S(2)}) async-start(s8[8388608]{0:T(1024)(128)(4,1)} %bitcast.30), calls=%async_computation.1 | async-start | bytes 8388608
  89.8 21.7 %collective-permute-start.16 = (bf16[512,512]{1,0:T(8,128)(2,1)S(1)}, bf16[512,512]{1,0:T(8,128)(2,1)S(1)}, u32[]{:S(2)}, u32[]{:S(2)}) collective-permute-start(bf16[512,512]{1,0:T(8,128)(2,1)S(1)} %get-tuple-element.55.refs_3_.refs_1_), channel_id=1, source_target_pairs={{0,1},{1,2},{2,3},{4,5},{5,6},{6,7},{8,9},{9,10},{10,11},{12,13},{... | collective-permute-start | bytes 1572872 | tf_op jit(solution)/shard_map/ppermute | solution.py:43
  94.5 17.7 %collective-permute-start.17 = (bf16[512,512]{1,0:T(8,128)(2,1)S(1)}, bf16[512,512]{1,0:T(8,128)(2,1)S(1)}, u32[]{:S(2)}, u32[]{:S(2)}) collective-permute-start(bf16[512,512]{1,0:T(8,128)(2,1)S(1)} %get-tuple-element.55.refs_3_.refs_1_), channel_id=1, source_target_pairs={{1,0},{2,1},{3,2},{5,4},{6,5},{7,6},{9,8},{10,9},{11,10},{13,12},{... | collective-permute-start | bytes 1572872 | tf_op jit(solution)/shard_map/ppermute | solution.py:43
  95.9 24.7 %collective-permute-start.32 = (bf16[1,3,128,1024]{3,2,1,0:T(8,128)(2,1)S(1)}, bf16[1,3,128,1024]{3,2,1,0:T(8,128)(2,1)S(1)}, u32[]{:S(2)}, u32[]{:S(2)}) collective-permute-start(bf16[1,3,128,1024]{3,2,1,0:T(8,128)(2,1)S(1)} %bitcast.32), channel_id=1, source_target_pairs={{0,16},{4,20},{8,24},{12,28},{16,0},{20,4},{24,8},{28,12},{1,17},{... | collective-permute-start | bytes 2359304 | tf_op jit(solution)/shard_map/ppermute | solution.py:53
  103.0 55.2 %copy-start.5 = (bf16[4,512,1024]{2,1,0:T(8,128)(2,1)}, bf16[4,512,1024]{2,1,0:T(8,128)(2,1)S(1)}, u32[]{:S(2)}) copy-start(bf16[4,512,1024]{2,1,0:T(8,128)(2,1)S(1)} %shard_map.91.p_hbm) | copy-start | bytes 12582916
  104.1 18.5 %collective-permute-start.22 = (bf16[512,512]{1,0:T(8,128)(2,1)S(1)}, bf16[512,512]{1,0:T(8,128)(2,1)S(1)}, u32[]{:S(2)}, u32[]{:S(2)}) collective-permute-start(bf16[512,512]{1,0:T(8,128)(2,1)S(1)} %get-tuple-element.63), channel_id=1, source_target_pairs={{0,1},{1,2},{2,3},{4,5},{5,6},{6,7},{8,9},{9,10},{10,11},{12,13},{... | collective-permute-start | bytes 1572872 | tf_op jit(solution)/shard_map/ppermute | solution.py:43
  110.2 16.8 %collective-permute-start.23 = (bf16[512,512]{1,0:T(8,128)(2,1)S(1)}, bf16[512,512]{1,0:T(8,128)(2,1)S(1)}, u32[]{:S(2)}, u32[]{:S(2)}) collective-permute-start(bf16[512,512]{1,0:T(8,128)(2,1)S(1)} %get-tuple-element.60.refs_1_), channel_id=1, source_target_pairs={{1,0},{2,1},{3,2},{5,4},{6,5},{7,6},{9,8},{10,9},{11,10},{13,12},{... | collective-permute-start | bytes 1572872 | tf_op jit(solution)/shard_map/ppermute | solution.py:43
  113.3 20.5 %collective-permute-start.20 = (bf16[512,512]{1,0:T(8,128)(2,1)S(1)}, bf16[512,512]{1,0:T(8,128)(2,1)S(1)}, u32[]{:S(2)}, u32[]{:S(2)}) collective-permute-start(bf16[512,512]{1,0:T(8,128)(2,1)S(1)} %get-tuple-element.61), channel_id=1, source_target_pairs={{0,1},{1,2},{2,3},{4,5},{5,6},{6,7},{8,9},{9,10},{10,11},{12,13},{... | collective-permute-start | bytes 1572872 | tf_op jit(solution)/shard_map/ppermute | solution.py:43
  119.1 19.1 %collective-permute-start.21 = (bf16[512,512]{1,0:T(8,128)(2,1)S(1)}, bf16[512,512]{1,0:T(8,128)(2,1)S(1)}, u32[]{:S(2)}, u32[]{:S(2)}) collective-permute-start(bf16[512,512]{1,0:T(8,128)(2,1)S(1)} %get-tuple-element.62.refs_1_.refs_2_), channel_id=1, source_target_pairs={{1,0},{2,1},{3,2},{5,4},{6,5},{7,6},{9,8},{10,9},{11,10},{13,12},{... | collective-permute-start | bytes 1572872 | tf_op jit(solution)/shard_map/ppermute | solution.py:43
  120.8 38.5 %collective-permute-start.33 = (bf16[2,3,128,1024]{3,2,1,0:T(8,128)(2,1)S(1)}, bf16[2,3,128,1024]{3,2,1,0:T(8,128)(2,1)S(1)}, u32[]{:S(2)}, u32[]{:S(2)}) collective-permute-start(bf16[2,3,128,1024]{3,2,1,0:T(8,128)(2,1)S(1)} %shard_map.98.refs_0_), channel_id=1, source_target_pairs={{0,8},{4,12},{8,0},{12,4},{16,24},{20,28},{24,16},{28,20},{1,9},{5... | collective-permute-start | bytes 4718600 | tf_op jit(solution)/shard_map/ppermute | solution.py:53
  128.0 17.0 %collective-permute-start.26 = (bf16[512,512]{1,0:T(8,128)(2,1)S(1)}, bf16[512,512]{1,0:T(8,128)(2,1)S(1)}, u32[]{:S(2)}, u32[]{:S(2)}) collective-permute-start(bf16[512,512]{1,0:T(8,128)(2,1)S(1)} %get-tuple-element.69), channel_id=1, source_target_pairs={{0,1},{1,2},{2,3},{4,5},{5,6},{6,7},{8,9},{9,10},{10,11},{12,13},{... | collective-permute-start | bytes 1572872 | tf_op jit(solution)/shard_map/ppermute | solution.py:43
  132.0 17.5 %collective-permute-start.27 = (bf16[512,512]{1,0:T(8,128)(2,1)S(1)}, bf16[512,512]{1,0:T(8,128)(2,1)S(1)}, u32[]{:S(2)}, u32[]{:S(2)}) collective-permute-start(bf16[512,512]{1,0:T(8,128)(2,1)S(1)} %get-tuple-element.66.refs_1_), channel_id=1, source_target_pairs={{1,0},{2,1},{3,2},{5,4},{6,5},{7,6},{9,8},{10,9},{11,10},{13,12},{... | collective-permute-start | bytes 1572872 | tf_op jit(solution)/shard_map/ppermute | solution.py:43
  139.2 14.9 %collective-permute-start.24 = (bf16[512,512]{1,0:T(8,128)(2,1)S(1)}, bf16[512,512]{1,0:T(8,128)(2,1)S(1)}, u32[]{:S(2)}, u32[]{:S(2)}) collective-permute-start(bf16[512,512]{1,0:T(8,128)(2,1)S(1)} %get-tuple-element.67), channel_id=1, source_target_pairs={{0,1},{1,2},{2,3},{4,5},{5,6},{6,7},{8,9},{9,10},{10,11},{12,13},{... | collective-permute-start | bytes 1572872 | tf_op jit(solution)/shard_map/ppermute | solution.py:43
  143.2 15.1 %collective-permute-start.25 = (bf16[512,512]{1,0:T(8,128)(2,1)S(1)}, bf16[512,512]{1,0:T(8,128)(2,1)S(1)}, u32[]{:S(2)}, u32[]{:S(2)}) collective-permute-start(bf16[512,512]{1,0:T(8,128)(2,1)S(1)} %get-tuple-element.68.refs_1_), channel_id=1, source_target_pairs={{1,0},{2,1},{3,2},{5,4},{6,5},{7,6},{9,8},{10,9},{11,10},{13,12},{... | collective-permute-start | bytes 1572872 | tf_op jit(solution)/shard_map/ppermute | solution.py:43
  159.5 13.2 %copy-start.4 = (bf16[4,3,128,1024]{3,2,1,0:T(8,128)(2,1)}, bf16[4,3,128,1024]{3,2,1,0:T(8,128)(2,1)S(1)}, u32[]{:S(2)}) copy-start(bf16[4,3,128,1024]{3,2,1,0:T(8,128)(2,1)S(1)} %shard_map.99.refs_4_) | copy-start | bytes 9437188
  159.5 11.4 %collective-permute-start.34 = (bf16[4,3,128,1024]{3,2,1,0:T(8,128)(2,1)S(1)}, bf16[4,3,128,1024]{3,2,1,0:T(8,128)(2,1)S(1)}, u32[]{:S(2)}, u32[]{:S(2)}) collective-permute-start(bf16[4,3,128,1024]{3,2,1,0:T(8,128)(2,1)S(1)} %shard_map.99.refs_4_), channel_id=1, source_target_pairs={{0,4},{4,0},{8,12},{12,8},{16,20},{20,16},{24,28},{28,24},{1,5},{5... | collective-permute-start | bytes 9437192 | tf_op jit(solution)/shard_map/ppermute | solution.py:53
  159.6 21.8 %collective-permute-start.30 = (bf16[512,512]{1,0:T(8,128)(2,1)S(1)}, bf16[512,512]{1,0:T(8,128)(2,1)S(1)}, u32[]{:S(2)}, u32[]{:S(2)}) collective-permute-start(bf16[512,512]{1,0:T(8,128)(2,1)S(1)} %get-tuple-element.75), channel_id=1, source_target_pairs={{0,1},{1,2},{2,3},{4,5},{5,6},{6,7},{8,9},{9,10},{10,11},{12,13},{... | collective-permute-start | bytes 1572872 | tf_op jit(solution)/shard_map/ppermute | solution.py:43
  163.7 17.7 %collective-permute-start.31 = (bf16[512,512]{1,0:T(8,128)(2,1)S(1)}, bf16[512,512]{1,0:T(8,128)(2,1)S(1)}, u32[]{:S(2)}, u32[]{:S(2)}) collective-permute-start(bf16[512,512]{1,0:T(8,128)(2,1)S(1)} %get-tuple-element.72.refs_1_), channel_id=1, source_target_pairs={{1,0},{2,1},{3,2},{5,4},{6,5},{7,6},{9,8},{10,9},{11,10},{13,12},{... | collective-permute-start | bytes 1572872 | tf_op jit(solution)/shard_map/ppermute | solution.py:43
  165.0 21.7 %collective-permute-start.28 = (bf16[512,512]{1,0:T(8,128)(2,1)S(1)}, bf16[512,512]{1,0:T(8,128)(2,1)S(1)}, u32[]{:S(2)}, u32[]{:S(2)}) collective-permute-start(bf16[512,512]{1,0:T(8,128)(2,1)S(1)} %get-tuple-element.73), channel_id=1, source_target_pairs={{0,1},{1,2},{2,3},{4,5},{5,6},{6,7},{8,9},{9,10},{10,11},{12,13},{... | collective-permute-start | bytes 1572872 | tf_op jit(solution)/shard_map/ppermute | solution.py:43
  169.6 21.3 %collective-permute-start.29 = (bf16[512,512]{1,0:T(8,128)(2,1)S(1)}, bf16[512,512]{1,0:T(8,128)(2,1)S(1)}, u32[]{:S(2)}, u32[]{:S(2)}) collective-permute-start(bf16[512,512]{1,0:T(8,128)(2,1)S(1)} %get-tuple-element.74.refs_2_.refs_6_), channel_id=1, source_target_pairs={{1,0},{2,1},{3,2},{5,4},{6,5},{7,6},{9,8},{10,9},{11,10},{13,12},{... | collective-permute-start | bytes 1572872 | tf_op jit(solution)/shard_map/ppermute | solution.py:43
  170.9 1.8 copy-start.10
  172.7 8.8 %copy-start.6 = (bf16[4,512,1024]{2,1,0:T(8,128)(2,1)S(1)}, bf16[4,512,1024]{2,1,0:T(8,128)(2,1)}, u32[]{:S(2)}) copy-start(bf16[4,512,1024]{2,1,0:T(8,128)(2,1)} %copy-done.5) | copy-start | bytes 12582916

commit v4 on v3

--- a/solution.py
+++ b/solution.py
@@ -26,7 +26,6 @@
 CORE, FIRST, NEAR = 0, 1, 2
 
 ANY = pl.BlockSpec(memory_space=pl.ANY)
-HBM = pl.BlockSpec(memory_space=pltpu.HBM)
 SMEM = pl.BlockSpec(memory_space=pltpu.SMEM)
 
 
@@ -86,44 +85,30 @@
     return jnp.sum(tail.astype(F32), axis=0, keepdims=True)
 
 
-def grads_kernel(h, at, ids_ref, code_ref, k_hbm, v_hbm, w_hbm, *refs):
-    k_ref, v_ref, w_ref, lhs, rhs, sem, ksem, vsem = refs[-8:]
-    cols = pl.ds(h * FW, FW)
+def grads_kernel(h, at, ids_ref, code_ref, k_ref, v_ref, w_ref, *refs):
+    lhs, rhs, sem = refs[-3:]
+    copies = []
+    if h == 0:
+        k_hbm, v_hbm, ow_hbm, keep_ref, send_ref, rim_ref = refs[:6]
+        last = pl.ds(k_hbm.shape[0] - WINDOW, WINDOW)
+        copies = [
+            pltpu.make_async_copy(k_hbm.at[last, :], rim_ref.at[pl.ds(0, WINDOW), :], sem.at[0]),
+            pltpu.make_async_copy(
+                v_hbm.at[last, :], rim_ref.at[pl.ds(WINDOW, WINDOW), :], sem.at[1]
+            ),
+        ] + [
+            strip_copy(ids_ref, at + 2 * i, ow_hbm, strip_ref, sem.at[2 + i])
+            for i, strip_ref in enumerate(refs[6:-3])
+        ]
+    else:
+        keep_ref, send_ref = refs[-5:-3]
+    for copy in copies:
+        copy.start()
     rows = k_ref.shape[0]
     tile = min(256, rows)
-    copies = [[pltpu.make_async_copy(w_hbm.at[pl.ds(h, 1)], w_ref, sem.at[0])]]
-    for t in range(rows // tile):
-        sl = pl.ds(t * tile, tile)
-        copies.append(
-            [
-                pltpu.make_async_copy(k_hbm.at[sl, cols], k_ref.at[sl, :], ksem.at[t]),
-                pltpu.make_async_copy(v_hbm.at[sl, cols], v_ref.at[sl, :], vsem.at[t]),
-            ]
-        )
-    later = []
-    if h == 0:
-        ow_hbm, keep_ref, send_ref, rim_ref = refs[:4]
-        strip_refs = refs[4:-8]
-        last = pl.ds(k_hbm.shape[0] - WINDOW, WINDOW)
-        later = [
-            pltpu.make_async_copy(k_hbm.at[last, :], rim_ref.at[pl.ds(0, WINDOW), :], sem.at[3]),
-            pltpu.make_async_copy(
-                v_hbm.at[last, :], rim_ref.at[pl.ds(WINDOW, WINDOW), :], sem.at[4]
-            ),
-        ] + [
-            strip_copy(ids_ref, at + 2 * i, ow_hbm, strip_ref, sem.at[5 + i])
-            for i, strip_ref in enumerate(strip_refs)
-        ]
-    else:
-        keep_ref, send_ref = refs[-10:-8]
-    for copy in sum(copies, []) + later:
-        copy.start()
-    copies[0][0].wait()
     wide = 2 * LANES
     codes = code_ref[h : h + 1, :].astype(F32) * 2.0 ** (-14)
     for t in range(rows // tile):
-        for copy in copies[1 + t]:
-            copy.wait()
         sl = pl.ds(t * tile, tile)
         k = k_ref[sl, :]
         rate = jnp.broadcast_to(codes[:, t * tile : (t + 1) * tile], (LANES, tile)).T
@@ -153,7 +138,7 @@
             r = mm(left, right).astype(BF)
             ref[pl.ds(2 * i * FW, FW), :] = r[:, :LANES]
             ref[pl.ds((2 * i + 1) * FW, FW), :] = r[:, LANES:]
-    for copy in later:
+    for copy in copies:
         copy.wait()
 
 
@@ -161,23 +146,25 @@
     rows, feats = keys.shape
     shape = (HALF * FW + TAIL, LANES)
     outs = [shape, shape] + ([(2 * WINDOW, feats)] + strips if h == 0 else [])
-    more = [out_weight] if h == 0 else after
+    more = [keys, values, out_weight] if h == 0 else after
+    col = pl.BlockSpec((rows, FW), lambda i: (0, h))
     return pl.pallas_call(
         functools.partial(grads_kernel, h, at),
         grid=(1,),
-        in_specs=[SMEM, full(codes.shape), HBM, HBM, HBM]
-        + ([HBM] if h == 0 else [ANY] * len(more)),
+        in_specs=[
+            SMEM,
+            full(codes.shape),
+            col,
+            col,
+            pl.BlockSpec((1, 3, FW, FW), lambda i: (h, 0, 0, 0)),
+        ]
+        + [ANY] * len(more),
         out_specs=[full(x) for x in outs],
         out_shape=[jax.ShapeDtypeStruct(x, BF) for x in outs],
         scratch_shapes=[
-            pltpu.VMEM((rows, FW), BF),
-            pltpu.VMEM((rows, FW), BF),
-            pltpu.VMEM((1, 3, FW, FW), BF),
             pltpu.VMEM((2 * FW, rows), BF),
             pltpu.VMEM((rows, 3 * FW), BF),
-            pltpu.SemaphoreType.DMA((5 + len(strips),)),
-            pltpu.SemaphoreType.DMA((rows // min(256, rows),)),
-            pltpu.SemaphoreType.DMA((rows // min(256, rows),)),
+            pltpu.SemaphoreType.DMA((2 + len(strips),)),
         ],
         compiler_params=room(58),
         cost_estimate=cost(8 * rows / 1024),
@@ -655,7 +642,7 @@
             strips = [rotate(x, "head", s + 1) for s, x in enumerate(g[3:])]
     split_up = []
     for h in range(heads):
-        before = [s[1] for s in split_up[-1:]] or [rim]
+        before = [split_up[0][1], rim] if h else []
         split_up.append(split(h, ids, keep[h], other[h], before))
     away = [swap(split_up[h][1], order[h][0]) for h in range(heads)]
 
@@ -689,7 +676,7 @@
         near = swap(new[h], b)
         blocks = [new[h], near, swap(new[h], 1), swap(near, 1)]
         own = pieces[h * per_head : (h + 1) * per_head]
-        m, r, weights = apply(h, heads, ids, query, own, blocks, cut, weights, strips)
+        m, r, weights = apply(h, heads, ids, query, own, blocks, cut, weights, strips[2:] if h else [])
         merged.append(m)
         rest.append(r)
     to_right = [[shift(m, "head", 1) for m in merged]]
@@ -719,11 +706,11 @@
             after = l
             right.append(shift(r, "head", 1))
             left.append(shift(l, "head", -1))
+            due = {(1, heads - 1): spread[:1], (groups - 1, heads - 1): spread[1:-1]}
+            for b in due.get((t, h), []):
+                near = stack([near, swap(near, b)], [after])
         to_right.append(right)
         to_left.append(left)
-        due = spread[:1] if t == 1 else spread[1:-1] if t == groups - 1 else []
-        for b in due:
-            near = stack([near, swap(near, b)], [after])
     out = gathered(
         ids,
         tail_at,

time: 193 us -> 202 us (1.047)
  waiting for transfers between devices: 54.9 us -> 67.1 us
    ppermute x3, waiting for transfers between devices: 14.7 us -> 25.1 us  [rotate(): lax.ppermute(block, axis, [(i, (i + distance) % n) for i in range(n)])]
    ppermute x17, starting transfers between devices: 48.1 us -> 44.9 us  [shift(): lax.ppermute(block, axis, [(i, i + distance) for i in range(n) if 0 <= i...]
  transfers between devices with their start and end apart: 35 -> 35, of which waited for: 16 -> 17; matrix products, arithmetic and copies ran while one was open for 0% -> 0% of each run, Pallas kernels for 25% -> 23%
where the time goes in v4:
time: 202 us
  starting transfers between devices  69.7 us (35%)
  waiting for transfers between devices  67.1 us (33%)
  Pallas kernels  59.7 us (30%)
  local copies, waits for them, and re-layouts  3.64 us (2%)
    ppermute x17, starting transfers between devices, shift(): lax.ppermute(block, axis, [(i, i + distance) for i in range(n) if 0 <= i...  44.9 us
    ppermute x17, waiting for transfers between devices, shift(): lax.ppermute(block, axis, [(i, i + distance) for i in range(n) if 0 <= i...  32.5 us
    ppermute x3, waiting for transfers between devices, rotate(): lax.ppermute(block, axis, [(i, (i + distance) % n) for i in range(n)])  25.1 us
    pallas_call x2, Pallas kernels, grads(): pl.pallas_call(functools.partial(grads_kernel, h, at), grid=(1,), in_spec...  16 us
    ppermute x15, starting transfers between devices, swap(): return lax.ppermute(block, 'ctx', [(i, i ^ bit) for i in range(n)])  15.9 us
    ppermute x15, waiting for transfers between devices, swap(): return lax.ppermute(block, 'ctx', [(i, i ^ bit) for i in range(n)])  9.55 us
    ppermute x3, starting transfers between devices, rotate(): lax.ppermute(block, axis, [(i, (i + distance) % n) for i in range(n)])  8.9 us
    pallas_call x1, Pallas kernels, gathered(): pl.pallas_call(functools.partial(gathered_kernel, n, heads, parts, at), g...  8.73 us
  transfers between devices with their start and end apart: 35, of which 17 were waited for; matrix products, arithmetic and copies ran while one was open for 0% of the time, Pallas kernels for 23%

profile of v4, /device:TPU:0, one launch (start us, length us, event | category | flops | bytes accessed | tf_op | source)
XLA Modules:
  0.0 201.7 jit_solution(16138879719989637648)
XLA Ops:
  0.8 0.7 stack.137.ids_ref
  1.5 8.7 %shard_map.77 = (bf16[3088,128]{1,0:T(8,128)(2,1)}, bf16[3088,128]{1,0:T(8,128)(2,1)}, bf16[512,1024]{1,0:T(8,128)(2,1)}, bf16[128,1024]{1,0:T(8,128)(2,1)}, bf1...) custom-call(s32[31]{0:T(128)} %stack.137.ids_ref, s32[2,1024]{1,0:T(2,128)} %bitcast.38, bf16[1024,1024]{1,0:T(8,128)(2,1)} %k_ref.11, ...), custom_call_target="tpu_custom_call" | custom-call | flops 960000000 | tf_op jit(solution)/shard_map/pallas_call | solution.py:151
  10.2 2.6 %collective-permute-start = (bf16[512,1024]{1,0:T(8,128)(2,1)}, bf16[512,1024]{1,0:T(8,128)(2,1)S(1)}, u32[]{:S(2)}, u32[]{:S(2)}) collective-permute-start(bf16[512,1024]{1,0:T(8,128)(2,1)} %get-tuple-element.40), channel_id=1, source_target_pairs={{0,4},{4,8},{8,12},{12,16},{16,20},{20,24},{24,28},{1,5},{5,9},{9,... | collective-permute-start | bytes 3145736 | tf_op jit(solution)/shard_map/ppermute | solution.py:42
  12.9 2.6 %collective-permute-start.2 = (bf16[3088,128]{1,0:T(8,128)(2,1)}, bf16[3088,128]{1,0:T(8,128)(2,1)S(1)}, u32[]{:S(2)}, u32[]{:S(2)}) collective-permute-start(bf16[3088,128]{1,0:T(8,128)(2,1)} %get-tuple-element.44), channel_id=1, source_target_pairs={{0,4},{4,0},{8,12},{12,8},{16,20},{20,16},{24,28},{28,24},{1,5},{5... | collective-permute-start | bytes 2371592 | tf_op jit(solution)/shard_map/ppermute | solution.py:52
  15.5 7.2 %shard_map.78 = (bf16[3088,128]{1,0:T(8,128)(2,1)}, bf16[3088,128]{1,0:T(8,128)(2,1)}) custom-call(s32[31]{0:T(128)} %stack.137.ids_ref, s32[2,1024]{1,0:T(2,128)} %bitcast.39, bf16[1024,1024]{1,0:T(8,128)(2,1)} %k_ref.11, bf16[1024,1024]{1,0:T(8,128)(2,1)} %v_ref.11, bf16[2,3,512,512]{3,2,1,0:T(8,128)(2,1)} %base_ref.1, ...), custom_call_target="tpu_custom_call" | custom-call | flops 960000000 | tf_op jit(solution)/shard_map/pallas_call | solution.py:151
  22.8 0.9 shard_map.79
  23.7 1.6 collective-permute-start.4
  25.3 1.1 copy-done.8
  26.4 0.9 shard_map.80
  27.3 6.8 %collective-permute-start.3 = (bf16[1552,128]{1,0:T(8,128)(2,1)S(1)}, bf16[1552,128]{1,0:T(8,128)(2,1)S(1)}, u32[]{:S(2)}, u32[]{:S(2)}) collective-permute-start(bf16[1552,128]{1,0:T(8,128)(2,1)S(1)} %get-tuple-element.47.rest_1_), channel_id=1, source_target_pairs={{0,16},{4,20},{8,24},{12,28},{16,0},{20,4},{24,8},{28,12},{1,17},{... | collective-permute-start | bytes 1191944 | tf_op jit(solution)/shard_map/ppermute | solution.py:52
  34.1 2.6 %collective-permute-start.5 = (bf16[128,1024]{1,0:T(8,128)(2,1)S(1)}, bf16[128,1024]{1,0:T(8,128)(2,1)S(1)}, u32[]{:S(2)}, u32[]{:S(2)}) collective-permute-start(bf16[128,1024]{1,0:T(8,128)(2,1)S(1)} %copy-done.13), channel_id=1, source_target_pairs={{0,2},{1,3},{2,0},{3,1},{4,6},{5,7},{6,4},{7,5},{8,10},{9,11},{10,... | collective-permute-start | bytes 786440 | tf_op jit(solution)/shard_map/ppermute | solution.py:47
  36.7 2.1 %shard_map.81.rest_0_.refs_0_ = bf16[1024,256]{1,0:T(8,128)(2,1)S(1)} custom-call(s32[31]{0:T(128)S(1)} %copy-done.9, bf16[1024,1024]{1,0:T(8,128)(2,1)S(1)} %copy-done.2, bf16[1024,1024]{1,0:T(8,128)(2,1)S(1)} %copy-done, bf16[1024,1024]{1,0:T(8,128)(2,1)S(1)} %copy-done.1, bf16[512,1024]{1,0:T(8,128)(2,1)S(1)} %collective-permute-done.refs_1_.rim_ref, ...), custom_call_target="tpu_custom_call" | custom-call | flops 252000000 | tf_op jit(solution)/shard_map/pallas_call | solution.py:315
  39.4 2.1 %shard_map.83.rest_0_.refs_1_ = bf16[1024,256]{1,0:T(8,128)(2,1)S(1)} custom-call(s32[31]{0:T(128)S(1)} %copy-done.9, bf16[1024,1024]{1,0:T(8,128)(2,1)S(1)} %copy-done.2, bf16[1024,1024]{1,0:T(8,128)(2,1)S(1)} %copy-done, bf16[1024,1024]{1,0:T(8,128)(2,1)S(1)} %copy-done.1, bf16[512,1024]{1,0:T(8,128)(2,1)S(1)} %collective-permute-done.refs_1_.rim_ref, ...), custom_call_target="tpu_custom_call" | custom-call | flops 252000000 | tf_op jit(solution)/shard_map/pallas_call | solution.py:315
  41.5 5.5 %collective-permute-done.5.rest_2_ = bf16[128,1024]{1,0:T(8,128)(2,1)S(1)} collective-permute-done((bf16[128,1024]{1,0:T(8,128)(2,1)S(1)}, bf16[128,1024]{1,0:T(8,128)(2,1)S(1)}, u32[]{:S(2)}, u32[]{:S(2)}) %collective-permute-start.5) | collective-permute-done | bytes 262176 | tf_op jit(solution)/shard_map/ppermute | solution.py:47
  47.8 0.8 collective-permute-start.8
  48.6 2.1 %shard_map.85.rest_0_.refs_0_ = bf16[1024,256]{1,0:T(8,128)(2,1)S(1)} custom-call(s32[31]{0:T(128)S(1)} %copy-done.9, bf16[1024,1024]{1,0:T(8,128)(2,1)S(1)} %copy-done.2, bf16[1024,1024]{1,0:T(8,128)(2,1)S(1)} %copy-done, bf16[1024,1024]{1,0:T(8,128)(2,1)S(1)} %copy-done.1, bf16[512,1024]{1,0:T(8,128)(2,1)S(1)} %collective-permute-done.refs_1_.rim_ref, ...), custom_call_target="tpu_custom_call" | custom-call | flops 252000000 | tf_op jit(solution)/shard_map/pallas_call | solution.py:315
  50.7 2.1 %shard_map.86.refs_4_.refs_1_ = bf16[1024,256]{1,0:T(8,128)(2,1)S(1)} custom-call(s32[31]{0:T(128)S(1)} %copy-done.9, bf16[1024,1024]{1,0:T(8,128)(2,1)S(1)} %copy-done.2, bf16[1024,1024]{1,0:T(8,128)(2,1)S(1)} %copy-done, bf16[1024,1024]{1,0:T(8,128)(2,1)S(1)} %copy-done.1, bf16[512,1024]{1,0:T(8,128)(2,1)S(1)} %collective-permute-done.refs_1_.rim_ref, ...), custom_call_target="tpu_custom_call" | custom-call | flops 252000000 | tf_op jit(solution)/shard_map/pallas_call | solution.py:315
  52.7 5.2 %collective-permute-done.8.refs_5_ = bf16[128,1024]{1,0:T(8,128)(2,1)S(1)} collective-permute-done((bf16[128,1024]{1,0:T(8,128)(2,1)S(1)}, bf16[128,1024]{1,0:T(8,128)(2,1)S(1)}, u32[]{:S(2)}, u32[]{:S(2)}) %collective-permute-start.8) | collective-permute-done | bytes 262176 | tf_op jit(solution)/shard_map/ppermute | solution.py:47
  57.9 2.1 %shard_map.87 = (bf16[3,512,128]{2,1,0:T(8,128)(2,1)S(1)}, bf16[3,512,128]{2,1,0:T(8,128)(2,1)S(1)}) custom-call(s32[31]{0:T(128)S(1)} %copy-done.9, bf16[2,3,512,512]{3,2,1,0:T(8,128)(2,1)S(1)} %copy-done.3, bf16[1552,128]{1,0:T(8,128)(2,1)S(1)} %shard_map.82.rest_0_.rest_1_.refs_0_, bf16[1552,128]{1,0:T(8,128)(2,1)S(1)} %collective-permute-done.6.refs_1_, ...), custom_call_target="tpu_custom_call" | custom-call | flops 252000000 | tf_op jit(solution)/shard_map/pallas_call | solution.py:264
  60.0 1.5 collective-permute-start.12
  61.9 8.3 %collective-permute-done.12.refs_3_ = bf16[3,512,128]{2,1,0:T(8,128)(2,1)S(1)} collective-permute-done((bf16[3,512,128]{2,1,0:T(8,128)(2,1)S(1)}, bf16[3,512,128]{2,1,0:T(8,128)(2,1)S(1)}, u32[]{:S(2)}, u32[]{:S(2)}) %collective-permute-start.12) | collective-permute-done | bytes 393248 | tf_op jit(solution)/shard_map/ppermute | solution.py:52
  71.1 0.9 collective-permute-done.14.refs_5_
  71.9 3.2 %shard_map.88 = (bf16[512,512]{1,0:T(8,128)(2,1)S(1)}, bf16[512,512]{1,0:T(8,128)(2,1)S(1)}, bf16[2,3,512,512]{3,2,1,0:T(8,128)(2,1)}) custom-call(s32[31]{0:T(128)S(1)} %copy-done.9, bf16[1024,1024]{1,0:T(8,128)(2,1)S(1)} %copy-done.2, bf16[1024,256]{1,0:T(8,128)(2,1)S(1)} %shard_map.81.rest_0_.refs_0_, bf16[1024,256]{1,0:T(8,128)(2,1)S(1)} %shard_map.83.rest_0_.refs_1_, ...), custom_call_target="tpu_custom_call" | custom-call | flops 396000000 | tf_op jit(solution)/shard_map/pallas_call | solution.py:375
  75.2 3.5 %collective-permute-start.18 = (bf16[512,512]{1,0:T(8,128)(2,1)S(1)}, bf16[512,512]{1,0:T(8,128)(2,1)S(1)}, u32[]{:S(2)}, u32[]{:S(2)}) collective-permute-start(bf16[512,512]{1,0:T(8,128)(2,1)S(1)} %get-tuple-element.58.refs_0_), channel_id=1, source_target_pairs={{0,1},{1,2},{2,3},{4,5},{5,6},{6,7},{8,9},{9,10},{10,11},{12,13},{... | collective-permute-start | bytes 1572872 | tf_op jit(solution)/shard_map/ppermute | solution.py:42
  78.7 1.3 collective-permute-start.19
  80.0 5.5 %collective-permute-start.15 = (bf16[128,1024]{1,0:T(8,128)(2,1)S(1)}, bf16[128,1024]{1,0:T(8,128)(2,1)S(1)}, u32[]{:S(2)}, u32[]{:S(2)}) collective-permute-start(bf16[128,1024]{1,0:T(8,128)(2,1)S(1)} %copy-done.11), channel_id=1, source_target_pairs={{0,3},{1,0},{2,1},{3,2},{4,7},{5,4},{6,5},{7,6},{8,11},{9,8},{10,9... | collective-permute-start | bytes 786440 | tf_op jit(solution)/shard_map/ppermute | solution.py:47
  85.5 14.4 %collective-permute-done.15.refs_7_ = bf16[128,1024]{1,0:T(8,128)(2,1)S(1)} collective-permute-done((bf16[128,1024]{1,0:T(8,128)(2,1)S(1)}, bf16[128,1024]{1,0:T(8,128)(2,1)S(1)}, u32[]{:S(2)}, u32[]{:S(2)}) %collective-permute-start.15) | collective-permute-done | bytes 262176 | tf_op jit(solution)/shard_map/ppermute | solution.py:47
  99.9 3.2 %shard_map.89 = (bf16[512,512]{1,0:T(8,128)(2,1)S(1)}, bf16[512,512]{1,0:T(8,128)(2,1)S(1)}, bf16[2,3,512,512]{3,2,1,0:T(8,128)(2,1)}) custom-call(s32[31]{0:T(128)S(1)} %copy-done.9, bf16[1024,1024]{1,0:T(8,128)(2,1)S(1)} %copy-done.2, bf16[1024,256]{1,0:T(8,128)(2,1)S(1)} %shard_map.85.rest_0_.refs_0_, ...), custom_call_target="tpu_custom_call", output_to_operand_aliasing={{2}: (8, {})} | custom-call | flops 396000000 | tf_op jit(solution)/shard_map/pallas_call | solution.py:375
  103.1 4.1 %collective-permute-start.16 = (bf16[512,512]{1,0:T(8,128)(2,1)S(1)}, bf16[512,512]{1,0:T(8,128)(2,1)S(1)}, u32[]{:S(2)}, u32[]{:S(2)}) collective-permute-start(bf16[512,512]{1,0:T(8,128)(2,1)S(1)} %get-tuple-element.55.refs_3_.refs_1_), channel_id=1, source_target_pairs={{0,1},{1,2},{2,3},{4,5},{5,6},{6,7},{8,9},{9,10},{10,11},{12,13},{... | collective-permute-start | bytes 1572872 | tf_op jit(solution)/shard_map/ppermute | solution.py:42
  107.3 1.3 collective-permute-start.17
  109.1 5.7 %shard_map.91.p_hbm = bf16[4,512,1024]{2,1,0:T(8,128)(2,1)S(1)} custom-call(bf16[512,512]{1,0:T(8,128)(2,1)S(1)} %get-tuple-element.56.refs_0_, bf16[512,512]{1,0:T(8,128)(2,1)S(1)} %get-tuple-element.57.refs_1_, bf16[1024,4096]{1,0:T(8,128)(2,1)S(1)} %bitcast.31, bf16[3,128,1024]{2,1,0:T(8,128)(2,1)S(1)} %shard_map.90.refs_3_), custom_call_target="tpu_custom_call" | custom-call | flops 120000000 | tf_op jit(solution)/shard_map/pallas_call | solution.py:415
  114.8 1.0 shard_map.92
  115.8 4.7 %collective-permute-start.22 = (bf16[512,512]{1,0:T(8,128)(2,1)S(1)}, bf16[512,512]{1,0:T(8,128)(2,1)S(1)}, u32[]{:S(2)}, u32[]{:S(2)}) collective-permute-start(bf16[512,512]{1,0:T(8,128)(2,1)S(1)} %get-tuple-element.63), channel_id=1, source_target_pairs={{0,1},{1,2},{2,3},{4,5},{5,6},{6,7},{8,9},{9,10},{10,11},{12,13},{... | collective-permute-start | bytes 1572872 | tf_op jit(solution)/shard_map/ppermute | solution.py:42
  120.5 1.3 collective-permute-start.23
  122.0 1.0 shard_map.93
  123.0 4.5 %collective-permute-start.20 = (bf16[512,512]{1,0:T(8,128)(2,1)S(1)}, bf16[512,512]{1,0:T(8,128)(2,1)S(1)}, u32[]{:S(2)}, u32[]{:S(2)}) collective-permute-start(bf16[512,512]{1,0:T(8,128)(2,1)S(1)} %get-tuple-element.61), channel_id=1, source_target_pairs={{0,1},{1,2},{2,3},{4,5},{5,6},{6,7},{8,9},{9,10},{10,11},{12,13},{... | collective-permute-start | bytes 1572872 | tf_op jit(solution)/shard_map/ppermute | solution.py:42
  127.5 1.6 collective-permute-start.21
  129.2 1.5 collective-permute-start.33
  130.7 2.1 %collective-permute-done.22.right_hbm = bf16[512,512]{1,0:T(8,128)(2,1)S(1)} collective-permute-done((bf16[512,512]{1,0:T(8,128)(2,1)S(1)}, bf16[512,512]{1,0:T(8,128)(2,1)S(1)}, u32[]{:S(2)}, u32[]{:S(2)}) %collective-permute-start.22) | collective-permute-done | bytes 524320 | tf_op jit(solution)/shard_map/ppermute | solution.py:42
  132.8 4.4 %collective-permute-done.23.left_hbm = bf16[512,512]{1,0:T(8,128)(2,1)S(1)} collective-permute-done((bf16[512,512]{1,0:T(8,128)(2,1)S(1)}, bf16[512,512]{1,0:T(8,128)(2,1)S(1)}, u32[]{:S(2)}, u32[]{:S(2)}) %collective-permute-start.23) | collective-permute-done | bytes 524320 | tf_op jit(solution)/shard_map/ppermute | solution.py:42
  137.2 1.0 shard_map.94
  138.2 3.6 %collective-permute-start.26 = (bf16[512,512]{1,0:T(8,128)(2,1)S(1)}, bf16[512,512]{1,0:T(8,128)(2,1)S(1)}, u32[]{:S(2)}, u32[]{:S(2)}) collective-permute-start(bf16[512,512]{1,0:T(8,128)(2,1)S(1)} %get-tuple-element.69), channel_id=1, source_target_pairs={{0,1},{1,2},{2,3},{4,5},{5,6},{6,7},{8,9},{9,10},{10,11},{12,13},{... | collective-permute-start | bytes 1572872 | tf_op jit(solution)/shard_map/ppermute | solution.py:42
  141.9 1.3 collective-permute-start.27
  143.2 0.9 collective-permute-done.20.right_hbm
  144.0 4.4 %collective-permute-done.21.left_hbm = bf16[512,512]{1,0:T(8,128)(2,1)S(1)} collective-permute-done((bf16[512,512]{1,0:T(8,128)(2,1)S(1)}, bf16[512,512]{1,0:T(8,128)(2,1)S(1)}, u32[]{:S(2)}, u32[]{:S(2)}) %collective-permute-start.21) | collective-permute-done | bytes 524320 | tf_op jit(solution)/shard_map/ppermute | solution.py:42
  148.5 1.0 shard_map.95
  149.5 3.6 %collective-permute-start.24 = (bf16[512,512]{1,0:T(8,128)(2,1)S(1)}, bf16[512,512]{1,0:T(8,128)(2,1)S(1)}, u32[]{:S(2)}, u32[]{:S(2)}) collective-permute-start(bf16[512,512]{1,0:T(8,128)(2,1)S(1)} %get-tuple-element.67), channel_id=1, source_target_pairs={{0,1},{1,2},{2,3},{4,5},{5,6},{6,7},{8,9},{9,10},{10,11},{12,13},{... | collective-permute-start | bytes 1572872 | tf_op jit(solution)/shard_map/ppermute | solution.py:42
  153.1 1.3 collective-permute-start.25
  154.4 0.9 collective-permute-done.26.right_hbm
  155.3 4.4 %collective-permute-done.27.left_hbm = bf16[512,512]{1,0:T(8,128)(2,1)S(1)} collective-permute-done((bf16[512,512]{1,0:T(8,128)(2,1)S(1)}, bf16[512,512]{1,0:T(8,128)(2,1)S(1)}, u32[]{:S(2)}, u32[]{:S(2)}) %collective-permute-start.27) | collective-permute-done | bytes 524320 | tf_op jit(solution)/shard_map/ppermute | solution.py:42
  159.7 1.0 shard_map.96
  160.7 3.2 %collective-permute-done.24.right_hbm = bf16[512,512]{1,0:T(8,128)(2,1)S(1)} collective-permute-done((bf16[512,512]{1,0:T(8,128)(2,1)S(1)}, bf16[512,512]{1,0:T(8,128)(2,1)S(1)}, u32[]{:S(2)}, u32[]{:S(2)}) %collective-permute-start.24) | collective-permute-done | bytes 524320 | tf_op jit(solution)/shard_map/ppermute | solution.py:42
  164.0 4.1 %collective-permute-done.25.left_hbm = bf16[512,512]{1,0:T(8,128)(2,1)S(1)} collective-permute-done((bf16[512,512]{1,0:T(8,128)(2,1)S(1)}, bf16[512,512]{1,0:T(8,128)(2,1)S(1)}, u32[]{:S(2)}, u32[]{:S(2)}) %collective-permute-start.25) | collective-permute-done | bytes 524320 | tf_op jit(solution)/shard_map/ppermute | solution.py:42
  168.1 1.0 shard_map.97
  169.4 3.2 %collective-permute-start.30 = (bf16[512,512]{1,0:T(8,128)(2,1)S(1)}, bf16[512,512]{1,0:T(8,128)(2,1)S(1)}, u32[]{:S(2)}, u32[]{:S(2)}) collective-permute-start(bf16[512,512]{1,0:T(8,128)(2,1)S(1)} %get-tuple-element.75), channel_id=1, source_target_pairs={{0,1},{1,2},{2,3},{4,5},{5,6},{6,7},{8,9},{9,10},{10,11},{12,13},{... | collective-permute-start | bytes 1572872 | tf_op jit(solution)/shard_map/ppermute | solution.py:42
  172.6 1.3 collective-permute-start.31
  173.9 4.6 %collective-permute-start.28 = (bf16[512,512]{1,0:T(8,128)(2,1)S(1)}, bf16[512,512]{1,0:T(8,128)(2,1)S(1)}, u32[]{:S(2)}, u32[]{:S(2)}) collective-permute-start(bf16[512,512]{1,0:T(8,128)(2,1)S(1)} %get-tuple-element.73), channel_id=1, source_target_pairs={{0,1},{1,2},{2,3},{4,5},{5,6},{6,7},{8,9},{9,10},{10,11},{12,13},{... | collective-permute-start | bytes 1572872 | tf_op jit(solution)/shard_map/ppermute | solution.py:42
  178.5 1.3 collective-permute-start.29
  179.8 1.7 copy-done.10
  181.6 8.7 %shard_map.100.out_in = bf16[1024,1024]{1,0:T(8,128)(2,1)} custom-call(s32[31]{0:T(128)S(1)} %copy-done.9, bf16[512,512]{1,0:T(8,128)(2,1)S(1)} %get-tuple-element.58.refs_0_, bf16[512,512]{1,0:T(8,128)(2,1)S(1)} %get-tuple-element.55.refs_3_.refs_1_, bf16[3,512,1024]{2,1,0:T(8,128)(2,1)S(1)} %get-tuple-element.76.refs_2_, bf16[1024,4096]{1,0:T(8,128)(2,1)} %refs_3_.1, ...), custom_call_target="tpu_custom_call" | custom-call | flops 1080000000 | tf_op jit(solution)/shard_map/pallas_call | solution.py:529
  190.4 1.7 shard_map.101.out_in
  192.1 3.6 %collective-permute-done.28.right_hbm = bf16[512,512]{1,0:T(8,128)(2,1)S(1)} collective-permute-done((bf16[512,512]{1,0:T(8,128)(2,1)S(1)}, bf16[512,512]{1,0:T(8,128)(2,1)S(1)}, u32[]{:S(2)}, u32[]{:S(2)}) %collective-permute-start.28) | collective-permute-done | bytes 524320 | tf_op jit(solution)/shard_map/ppermute | solution.py:42
  195.7 4.1 %collective-permute-done.29.left_hbm = bf16[512,512]{1,0:T(8,128)(2,1)S(1)} collective-permute-done((bf16[512,512]{1,0:T(8,128)(2,1)S(1)}, bf16[512,512]{1,0:T(8,128)(2,1)S(1)}, u32[]{:S(2)}, u32[]{:S(2)}) %collective-permute-start.29) | collective-permute-done | bytes 524320 | tf_op jit(solution)/shard_map/ppermute | solution.py:42
  199.8 1.7 shard_map.102
  (66 shorter events, 3.9 us)
Async XLA Ops:
  10.2 15.0 %collective-permute-start = (bf16[512,1024]{1,0:T(8,128)(2,1)}, bf16[512,1024]{1,0:T(8,128)(2,1)S(1)}, u32[]{:S(2)}, u32[]{:S(2)}) collective-permute-start(bf16[512,1024]{1,0:T(8,128)(2,1)} %get-tuple-element.40), channel_id=1, source_target_pairs={{0,4},{4,8},{8,12},{12,16},{16,20},{20,24},{24,28},{1,5},{5,9},{9,... | collective-permute-start | bytes 3145736 | tf_op jit(solution)/shard_map/ppermute | solution.py:42
  12.9 10.0 %collective-permute-start.2 = (bf16[3088,128]{1,0:T(8,128)(2,1)}, bf16[3088,128]{1,0:T(8,128)(2,1)S(1)}, u32[]{:S(2)}, u32[]{:S(2)}) collective-permute-start(bf16[3088,128]{1,0:T(8,128)(2,1)} %get-tuple-element.44), channel_id=1, source_target_pairs={{0,4},{4,0},{8,12},{12,8},{16,20},{20,16},{24,28},{28,24},{1,5},{5... | collective-permute-start | bytes 2371592 | tf_op jit(solution)/shard_map/ppermute | solution.py:52
  15.5 7.4 %copy-start.7 = (bf16[3088,128]{1,0:T(8,128)(2,1)S(1)}, bf16[3088,128]{1,0:T(8,128)(2,1)}, u32[]{:S(2)}) copy-start(bf16[3088,128]{1,0:T(8,128)(2,1)} %get-tuple-element.41.refs_0_.keep_hbm) | copy-start | bytes 2371588
  15.5 7.4 %copy-start.9 = (s32[31]{0:T(128)S(1)}, s32[31]{0:T(128)}, u32[]{:S(2)}) copy-start(s32[31]{0:T(128)} %stack.137.ids_ref) | copy-start | bytes 376
  15.5 18.6 %copy-start.13 = (bf16[128,1024]{1,0:T(8,128)(2,1)S(1)}, bf16[128,1024]{1,0:T(8,128)(2,1)}, u32[]{:S(2)}) copy-start(bf16[128,1024]{1,0:T(8,128)(2,1)} %get-tuple-element.49) | copy-start | bytes 786436
  15.5 21.2 %copy-start.2 = (bf16[1024,1024]{1,0:T(8,128)(2,1)S(1)}, bf16[1024,1024]{1,0:T(8,128)(2,1)}, u32[]{:S(2)}) copy-start(bf16[1024,1024]{1,0:T(8,128)(2,1)} %q_hbm.3) | copy-start | bytes 6291460
  22.7 14.0 %copy-start = (bf16[1024,1024]{1,0:T(8,128)(2,1)S(1)}, bf16[1024,1024]{1,0:T(8,128)(2,1)}, u32[]{:S(2)}) copy-start(bf16[1024,1024]{1,0:T(8,128)(2,1)} %k_ref.11) | copy-start | bytes 6291460
  22.7 14.0 %copy-start.1 = (bf16[1024,1024]{1,0:T(8,128)(2,1)S(1)}, bf16[1024,1024]{1,0:T(8,128)(2,1)}, u32[]{:S(2)}) copy-start(bf16[1024,1024]{1,0:T(8,128)(2,1)} %v_ref.11) | copy-start | bytes 6291460
  22.7 2.6 %collective-permute-start.1 = (bf16[3088,128]{1,0:T(8,128)(2,1)}, bf16[3088,128]{1,0:T(8,128)(2,1)S(1)}, u32[]{:S(2)}, u32[]{:S(2)}) collective-permute-start(bf16[3088,128]{1,0:T(8,128)(2,1)} %get-tuple-element.43), channel_id=1, source_target_pairs={{0,4},{4,0},{8,12},{12,8},{16,20},{20,16},{24,28},{28,24},{1,5},{5... | collective-permute-start | bytes 2371592 | tf_op jit(solution)/shard_map/ppermute | solution.py:52
  23.7 15.1 %collective-permute-start.4 = (bf16[1552,128]{1,0:T(8,128)(2,1)S(1)}, bf16[1552,128]{1,0:T(8,128)(2,1)S(1)}, u32[]{:S(2)}, u32[]{:S(2)}) collective-permute-start(bf16[1552,128]{1,0:T(8,128)(2,1)S(1)} %get-tuple-element.45.refs_0_.rest_0_), channel_id=1, source_target_pairs={{0,8},{4,12},{8,0},{12,4},{16,24},{20,28},{24,16},{28,20},{1,9},{5... | collective-permute-start | bytes 1191944 | tf_op jit(solution)/shard_map/ppermute | solution.py:52
  25.3 1.1 copy-start.8
  27.3 19.8 %collective-permute-start.3 = (bf16[1552,128]{1,0:T(8,128)(2,1)S(1)}, bf16[1552,128]{1,0:T(8,128)(2,1)S(1)}, u32[]{:S(2)}, u32[]{:S(2)}) collective-permute-start(bf16[1552,128]{1,0:T(8,128)(2,1)S(1)} %get-tuple-element.47.rest_1_), channel_id=1, source_target_pairs={{0,16},{4,20},{8,24},{12,28},{16,0},{20,4},{24,8},{28,12},{1,17},{... | collective-permute-start | bytes 1191944 | tf_op jit(solution)/shard_map/ppermute | solution.py:52
  34.1 13.0 %collective-permute-start.5 = (bf16[128,1024]{1,0:T(8,128)(2,1)S(1)}, bf16[128,1024]{1,0:T(8,128)(2,1)S(1)}, u32[]{:S(2)}, u32[]{:S(2)}) collective-permute-start(bf16[128,1024]{1,0:T(8,128)(2,1)S(1)} %copy-done.13), channel_id=1, source_target_pairs={{0,2},{1,3},{2,0},{3,1},{4,6},{5,7},{6,4},{7,5},{8,10},{9,11},{10,... | collective-permute-start | bytes 786440 | tf_op jit(solution)/shard_map/ppermute | solution.py:47
  39.3 8.5 %copy-start.12 = (bf16[128,1024]{1,0:T(8,128)(2,1)S(1)}, bf16[128,1024]{1,0:T(8,128)(2,1)}, u32[]{:S(2)}) copy-start(bf16[128,1024]{1,0:T(8,128)(2,1)} %get-tuple-element.50) | copy-start | bytes 786436
  39.3 18.6 %collective-permute-start.6 = (bf16[1552,128]{1,0:T(8,128)(2,1)S(1)}, bf16[1552,128]{1,0:T(8,128)(2,1)S(1)}, u32[]{:S(2)}, u32[]{:S(2)}) collective-permute-start(bf16[1552,128]{1,0:T(8,128)(2,1)S(1)} %shard_map.82.rest_0_.rest_1_.refs_0_), channel_id=1, source_target_pairs={{0,16},{4,20},{8,24},{12,28},{16,0},{20,4},{24,8},{28,12},{1,17},{... | collective-permute-start | bytes 1191944 | tf_op jit(solution)/shard_map/ppermute | solution.py:52
  47.5 10.3 %collective-permute-start.7 = (bf16[1552,128]{1,0:T(8,128)(2,1)S(1)}, bf16[1552,128]{1,0:T(8,128)(2,1)S(1)}, u32[]{:S(2)}, u32[]{:S(2)}) collective-permute-start(bf16[1552,128]{1,0:T(8,128)(2,1)S(1)} %shard_map.84.rest_0_.refs_2_), channel_id=1, source_target_pairs={{0,8},{4,12},{8,0},{12,4},{16,24},{20,28},{24,16},{28,20},{1,9},{5... | collective-permute-start | bytes 1191944 | tf_op jit(solution)/shard_map/ppermute | solution.py:52
  47.8 10.1 %collective-permute-start.8 = (bf16[128,1024]{1,0:T(8,128)(2,1)S(1)}, bf16[128,1024]{1,0:T(8,128)(2,1)S(1)}, u32[]{:S(2)}, u32[]{:S(2)}) collective-permute-start(bf16[128,1024]{1,0:T(8,128)(2,1)S(1)} %copy-done.12), channel_id=1, source_target_pairs={{0,1},{1,2},{2,3},{3,0},{4,5},{5,6},{6,7},{7,4},{8,9},{9,10},{10,1... | collective-permute-start | bytes 786440 | tf_op jit(solution)/shard_map/ppermute | solution.py:47
  50.7 7.2 %copy-start.3 = (bf16[2,3,512,512]{3,2,1,0:T(8,128)(2,1)S(1)}, bf16[2,3,512,512]{3,2,1,0:T(8,128)(2,1)}, u32[]{:S(2)}) copy-start(bf16[2,3,512,512]{3,2,1,0:T(8,128)(2,1)} %base_ref.1) | copy-start | bytes 9437188
  57.9 51.2 %slice-start = ((s8[8388608]{0:T(1024)(128)(4,1)}), s8[4194304]{0:T(1024)(128)(4,1)S(1)}, s32[]{:S(2)}) async-start(s8[8388608]{0:T(1024)(128)(4,1)} %bitcast.30), calls=%async_computation | async-start | bytes 8388608
  60.0 20.0 %copy-start.11 = (bf16[128,1024]{1,0:T(8,128)(2,1)S(1)}, bf16[128,1024]{1,0:T(8,128)(2,1)}, u32[]{:S(2)}) copy-start(bf16[128,1024]{1,0:T(8,128)(2,1)} %get-tuple-element.54) | copy-start | bytes 786436
  60.0 10.2 %collective-permute-start.12 = (bf16[3,512,128]{2,1,0:T(8,128)(2,1)S(1)}, bf16[3,512,128]{2,1,0:T(8,128)(2,1)S(1)}, u32[]{:S(2)}, u32[]{:S(2)}) collective-permute-start(bf16[3,512,128]{2,1,0:T(8,128)(2,1)S(1)} %get-tuple-element.52.refs_2_), channel_id=1, source_target_pairs={{0,8},{4,12},{8,0},{12,4},{16,24},{20,28},{24,16},{28,20},{1,9},{5... | collective-permute-start | bytes 1179656 | tf_op jit(solution)/shard_map/ppermute | solution.py:52
  61.5 47.5 %slice-start.1 = ((s8[8388608]{0:T(1024)(128)(4,1)}), s8[4194304]{0:T(1024)(128)(4,1)S(1)}, s32[]{:S(2)}) async-start(s8[8388608]{0:T(1024)(128)(4,1)} %bitcast.30), calls=%async_computation.1 | async-start | bytes 8388608
  61.5 9.5 %collective-permute-start.9 = (bf16[3,512,128]{2,1,0:T(8,128)(2,1)S(1)}, bf16[3,512,128]{2,1,0:T(8,128)(2,1)S(1)}, u32[]{:S(2)}, u32[]{:S(2)}) collective-permute-start(bf16[3,512,128]{2,1,0:T(8,128)(2,1)S(1)} %get-tuple-element.51.refs_2_), channel_id=1, source_target_pairs={{0,16},{4,20},{8,24},{12,28},{16,0},{20,4},{24,8},{28,12},{1,17},{... | collective-permute-start | bytes 1179656 | tf_op jit(solution)/shard_map/ppermute | solution.py:52
  61.9 9.2 %collective-permute-start.13 = (bf16[3,512,128]{2,1,0:T(8,128)(2,1)S(1)}, bf16[3,512,128]{2,1,0:T(8,128)(2,1)S(1)}, u32[]{:S(2)}, u32[]{:S(2)}) collective-permute-start(bf16[3,512,128]{2,1,0:T(8,128)(2,1)S(1)} %get-tuple-element.52.refs_2_), channel_id=1, source_target_pairs={{0,4},{4,0},{8,12},{12,8},{16,20},{20,16},{24,28},{28,24},{1,5},{5... | collective-permute-start | bytes 1179656 | tf_op jit(solution)/shard_map/ppermute | solution.py:52
  70.2 1.7 collective-permute-start.14
  70.2 29.7 %collective-permute-start.10 = (bf16[3,512,128]{2,1,0:T(8,128)(2,1)S(1)}, bf16[3,512,128]{2,1,0:T(8,128)(2,1)S(1)}, u32[]{:S(2)}, u32[]{:S(2)}) collective-permute-start(bf16[3,512,128]{2,1,0:T(8,128)(2,1)S(1)} %get-tuple-element.51.refs_2_), channel_id=1, source_target_pairs={{0,4},{4,0},{8,12},{12,8},{16,20},{20,16},{24,28},{28,24},{1,5},{5... | collective-permute-start | bytes 1179656 | tf_op jit(solution)/shard_map/ppermute | solution.py:52
  71.1 28.8 %collective-permute-start.11 = (bf16[3,512,128]{2,1,0:T(8,128)(2,1)S(1)}, bf16[3,512,128]{2,1,0:T(8,128)(2,1)S(1)}, u32[]{:S(2)}, u32[]{:S(2)}) collective-permute-start(bf16[3,512,128]{2,1,0:T(8,128)(2,1)S(1)} %collective-permute-done.9.refs_3_), channel_id=1, source_target_pairs={{0,4},{4,0},{8,12},{12,8},{16,20},{20,16},{24,28},{28,24},{1,5},{5... | collective-permute-start | bytes 1179656 | tf_op jit(solution)/shard_map/ppermute | solution.py:52
  75.2 39.6 %collective-permute-start.18 = (bf16[512,512]{1,0:T(8,128)(2,1)S(1)}, bf16[512,512]{1,0:T(8,128)(2,1)S(1)}, u32[]{:S(2)}, u32[]{:S(2)}) collective-permute-start(bf16[512,512]{1,0:T(8,128)(2,1)S(1)} %get-tuple-element.58.refs_0_), channel_id=1, source_target_pairs={{0,1},{1,2},{2,3},{4,5},{5,6},{6,7},{8,9},{9,10},{10,11},{12,13},{... | collective-permute-start | bytes 1572872 | tf_op jit(solution)/shard_map/ppermute | solution.py:42
  78.7 36.1 %collective-permute-start.19 = (bf16[512,512]{1,0:T(8,128)(2,1)S(1)}, bf16[512,512]{1,0:T(8,128)(2,1)S(1)}, u32[]{:S(2)}, u32[]{:S(2)}) collective-permute-start(bf16[512,512]{1,0:T(8,128)(2,1)S(1)} %get-tuple-element.58.refs_0_), channel_id=1, source_target_pairs={{1,0},{2,1},{3,2},{5,4},{6,5},{7,6},{9,8},{10,9},{11,10},{13,12},{... | collective-permute-start | bytes 1572872 | tf_op jit(solution)/shard_map/ppermute | solution.py:42
  80.0 19.9 %collective-permute-start.15 = (bf16[128,1024]{1,0:T(8,128)(2,1)S(1)}, bf16[128,1024]{1,0:T(8,128)(2,1)S(1)}, u32[]{:S(2)}, u32[]{:S(2)}) collective-permute-start(bf16[128,1024]{1,0:T(8,128)(2,1)S(1)} %copy-done.11), channel_id=1, source_target_pairs={{0,3},{1,0},{2,1},{3,2},{4,7},{5,4},{6,5},{7,6},{8,11},{9,8},{10,9... | collective-permute-start | bytes 786440 | tf_op jit(solution)/shard_map/ppermute | solution.py:47
  103.1 18.7 %collective-permute-start.16 = (bf16[512,512]{1,0:T(8,128)(2,1)S(1)}, bf16[512,512]{1,0:T(8,128)(2,1)S(1)}, u32[]{:S(2)}, u32[]{:S(2)}) collective-permute-start(bf16[512,512]{1,0:T(8,128)(2,1)S(1)} %get-tuple-element.55.refs_3_.refs_1_), channel_id=1, source_target_pairs={{0,1},{1,2},{2,3},{4,5},{5,6},{6,7},{8,9},{9,10},{10,11},{12,13},{... | collective-permute-start | bytes 1572872 | tf_op jit(solution)/shard_map/ppermute | solution.py:42
  107.3 14.8 %collective-permute-start.17 = (bf16[512,512]{1,0:T(8,128)(2,1)S(1)}, bf16[512,512]{1,0:T(8,128)(2,1)S(1)}, u32[]{:S(2)}, u32[]{:S(2)}) collective-permute-start(bf16[512,512]{1,0:T(8,128)(2,1)S(1)} %get-tuple-element.55.refs_3_.refs_1_), channel_id=1, source_target_pairs={{1,0},{2,1},{3,2},{5,4},{6,5},{7,6},{9,8},{10,9},{11,10},{13,12},{... | collective-permute-start | bytes 1572872 | tf_op jit(solution)/shard_map/ppermute | solution.py:42
  108.6 20.4 %collective-permute-start.32 = (bf16[1,3,128,1024]{3,2,1,0:T(8,128)(2,1)S(1)}, bf16[1,3,128,1024]{3,2,1,0:T(8,128)(2,1)S(1)}, u32[]{:S(2)}, u32[]{:S(2)}) collective-permute-start(bf16[1,3,128,1024]{3,2,1,0:T(8,128)(2,1)S(1)} %bitcast.32), channel_id=1, source_target_pairs={{0,16},{4,20},{8,24},{12,28},{16,0},{20,4},{24,8},{28,12},{1,17},{... | collective-permute-start | bytes 2359304 | tf_op jit(solution)/shard_map/ppermute | solution.py:52
  114.8 53.3 %copy-start.5 = (bf16[4,512,1024]{2,1,0:T(8,128)(2,1)}, bf16[4,512,1024]{2,1,0:T(8,128)(2,1)S(1)}, u32[]{:S(2)}) copy-start(bf16[4,512,1024]{2,1,0:T(8,128)(2,1)S(1)} %shard_map.91.p_hbm) | copy-start | bytes 12582916
  115.8 17.0 %collective-permute-start.22 = (bf16[512,512]{1,0:T(8,128)(2,1)S(1)}, bf16[512,512]{1,0:T(8,128)(2,1)S(1)}, u32[]{:S(2)}, u32[]{:S(2)}) collective-permute-start(bf16[512,512]{1,0:T(8,128)(2,1)S(1)} %get-tuple-element.63), channel_id=1, source_target_pairs={{0,1},{1,2},{2,3},{4,5},{5,6},{6,7},{8,9},{9,10},{10,11},{12,13},{... | collective-permute-start | bytes 1572872 | tf_op jit(solution)/shard_map/ppermute | solution.py:42
  120.5 16.8 %collective-permute-start.23 = (bf16[512,512]{1,0:T(8,128)(2,1)S(1)}, bf16[512,512]{1,0:T(8,128)(2,1)S(1)}, u32[]{:S(2)}, u32[]{:S(2)}) collective-permute-start(bf16[512,512]{1,0:T(8,128)(2,1)S(1)} %get-tuple-element.60.refs_1_), channel_id=1, source_target_pairs={{1,0},{2,1},{3,2},{5,4},{6,5},{7,6},{9,8},{10,9},{11,10},{13,12},{... | collective-permute-start | bytes 1572872 | tf_op jit(solution)/shard_map/ppermute | solution.py:42
  123.0 21.0 %collective-permute-start.20 = (bf16[512,512]{1,0:T(8,128)(2,1)S(1)}, bf16[512,512]{1,0:T(8,128)(2,1)S(1)}, u32[]{:S(2)}, u32[]{:S(2)}) collective-permute-start(bf16[512,512]{1,0:T(8,128)(2,1)S(1)} %get-tuple-element.61), channel_id=1, source_target_pairs={{0,1},{1,2},{2,3},{4,5},{5,6},{6,7},{8,9},{9,10},{10,11},{12,13},{... | collective-permute-start | bytes 1572872 | tf_op jit(solution)/shard_map/ppermute | solution.py:42
  127.5 21.0 %collective-permute-start.21 = (bf16[512,512]{1,0:T(8,128)(2,1)S(1)}, bf16[512,512]{1,0:T(8,128)(2,1)S(1)}, u32[]{:S(2)}, u32[]{:S(2)}) collective-permute-start(bf16[512,512]{1,0:T(8,128)(2,1)S(1)} %get-tuple-element.62.refs_1_.refs_2_), channel_id=1, source_target_pairs={{1,0},{2,1},{3,2},{5,4},{6,5},{7,6},{9,8},{10,9},{11,10},{13,12},{... | collective-permute-start | bytes 1572872 | tf_op jit(solution)/shard_map/ppermute | solution.py:42
  129.2 40.0 %collective-permute-start.33 = (bf16[2,3,128,1024]{3,2,1,0:T(8,128)(2,1)S(1)}, bf16[2,3,128,1024]{3,2,1,0:T(8,128)(2,1)S(1)}, u32[]{:S(2)}, u32[]{:S(2)}) collective-permute-start(bf16[2,3,128,1024]{3,2,1,0:T(8,128)(2,1)S(1)} %shard_map.98.refs_0_), channel_id=1, source_target_pairs={{0,8},{4,12},{8,0},{12,4},{16,24},{20,28},{24,16},{28,20},{1,9},{5... | collective-permute-start | bytes 4718600 | tf_op jit(solution)/shard_map/ppermute | solution.py:52
  138.2 17.0 %collective-permute-start.26 = (bf16[512,512]{1,0:T(8,128)(2,1)S(1)}, bf16[512,512]{1,0:T(8,128)(2,1)S(1)}, u32[]{:S(2)}, u32[]{:S(2)}) collective-permute-start(bf16[512,512]{1,0:T(8,128)(2,1)S(1)} %get-tuple-element.69), channel_id=1, source_target_pairs={{0,1},{1,2},{2,3},{4,5},{5,6},{6,7},{8,9},{9,10},{10,11},{12,13},{... | collective-permute-start | bytes 1572872 | tf_op jit(solution)/shard_map/ppermute | solution.py:42
  141.9 17.8 %collective-permute-start.27 = (bf16[512,512]{1,0:T(8,128)(2,1)S(1)}, bf16[512,512]{1,0:T(8,128)(2,1)S(1)}, u32[]{:S(2)}, u32[]{:S(2)}) collective-permute-start(bf16[512,512]{1,0:T(8,128)(2,1)S(1)} %get-tuple-element.66.refs_1_), channel_id=1, source_target_pairs={{1,0},{2,1},{3,2},{5,4},{6,5},{7,6},{9,8},{10,9},{11,10},{13,12},{... | collective-permute-start | bytes 1572872 | tf_op jit(solution)/shard_map/ppermute | solution.py:42
  149.5 14.5 %collective-permute-start.24 = (bf16[512,512]{1,0:T(8,128)(2,1)S(1)}, bf16[512,512]{1,0:T(8,128)(2,1)S(1)}, u32[]{:S(2)}, u32[]{:S(2)}) collective-permute-start(bf16[512,512]{1,0:T(8,128)(2,1)S(1)} %get-tuple-element.67), channel_id=1, source_target_pairs={{0,1},{1,2},{2,3},{4,5},{5,6},{6,7},{8,9},{9,10},{10,11},{12,13},{... | collective-permute-start | bytes 1572872 | tf_op jit(solution)/shard_map/ppermute | solution.py:42
  153.1 15.0 %collective-permute-start.25 = (bf16[512,512]{1,0:T(8,128)(2,1)S(1)}, bf16[512,512]{1,0:T(8,128)(2,1)S(1)}, u32[]{:S(2)}, u32[]{:S(2)}) collective-permute-start(bf16[512,512]{1,0:T(8,128)(2,1)S(1)} %get-tuple-element.68.refs_1_), channel_id=1, source_target_pairs={{1,0},{2,1},{3,2},{5,4},{6,5},{7,6},{9,8},{10,9},{11,10},{13,12},{... | collective-permute-start | bytes 1572872 | tf_op jit(solution)/shard_map/ppermute | solution.py:42
  169.3 12.3 %copy-start.4 = (bf16[4,3,128,1024]{3,2,1,0:T(8,128)(2,1)}, bf16[4,3,128,1024]{3,2,1,0:T(8,128)(2,1)S(1)}, u32[]{:S(2)}) copy-start(bf16[4,3,128,1024]{3,2,1,0:T(8,128)(2,1)S(1)} %shard_map.99.refs_4_) | copy-start | bytes 9437188
  169.3 10.5 %collective-permute-start.34 = (bf16[4,3,128,1024]{3,2,1,0:T(8,128)(2,1)S(1)}, bf16[4,3,128,1024]{3,2,1,0:T(8,128)(2,1)S(1)}, u32[]{:S(2)}, u32[]{:S(2)}) collective-permute-start(bf16[4,3,128,1024]{3,2,1,0:T(8,128)(2,1)S(1)} %shard_map.99.refs_4_), channel_id=1, source_target_pairs={{0,4},{4,0},{8,12},{12,8},{16,20},{20,16},{24,28},{28,24},{1,5},{5... | collective-permute-start | bytes 9437192 | tf_op jit(solution)/shard_map/ppermute | solution.py:52
  169.4 20.9 %collective-permute-start.30 = (bf16[512,512]{1,0:T(8,128)(2,1)S(1)}, bf16[512,512]{1,0:T(8,128)(2,1)S(1)}, u32[]{:S(2)}, u32[]{:S(2)}) collective-permute-start(bf16[512,512]{1,0:T(8,128)(2,1)S(1)} %get-tuple-element.75), channel_id=1, source_target_pairs={{0,1},{1,2},{2,3},{4,5},{5,6},{6,7},{8,9},{9,10},{10,11},{12,13},{... | collective-permute-start | bytes 1572872 | tf_op jit(solution)/shard_map/ppermute | solution.py:42
  172.6 17.7 %collective-permute-start.31 = (bf16[512,512]{1,0:T(8,128)(2,1)S(1)}, bf16[512,512]{1,0:T(8,128)(2,1)S(1)}, u32[]{:S(2)}, u32[]{:S(2)}) collective-permute-start(bf16[512,512]{1,0:T(8,128)(2,1)S(1)} %get-tuple-element.72.refs_1_), channel_id=1, source_target_pairs={{1,0},{2,1},{3,2},{5,4},{6,5},{7,6},{9,8},{10,9},{11,10},{13,12},{... | collective-permute-start | bytes 1572872 | tf_op jit(solution)/shard_map/ppermute | solution.py:42
  173.9 21.7 %collective-permute-start.28 = (bf16[512,512]{1,0:T(8,128)(2,1)S(1)}, bf16[512,512]{1,0:T(8,128)(2,1)S(1)}, u32[]{:S(2)}, u32[]{:S(2)}) collective-permute-start(bf16[512,512]{1,0:T(8,128)(2,1)S(1)} %get-tuple-element.73), channel_id=1, source_target_pairs={{0,1},{1,2},{2,3},{4,5},{5,6},{6,7},{8,9},{9,10},{10,11},{12,13},{... | collective-permute-start | bytes 1572872 | tf_op jit(solution)/shard_map/ppermute | solution.py:42
  178.5 21.3 %collective-permute-start.29 = (bf16[512,512]{1,0:T(8,128)(2,1)S(1)}, bf16[512,512]{1,0:T(8,128)(2,1)S(1)}, u32[]{:S(2)}, u32[]{:S(2)}) collective-permute-start(bf16[512,512]{1,0:T(8,128)(2,1)S(1)} %get-tuple-element.74.refs_2_.refs_6_), channel_id=1, source_target_pairs={{1,0},{2,1},{3,2},{5,4},{6,5},{7,6},{9,8},{10,9},{11,10},{13,12},{... | collective-permute-start | bytes 1572872 | tf_op jit(solution)/shard_map/ppermute | solution.py:42
  179.8 1.8 copy-start.10
  181.6 8.8 %copy-start.6 = (bf16[4,512,1024]{2,1,0:T(8,128)(2,1)S(1)}, bf16[4,512,1024]{2,1,0:T(8,128)(2,1)}, u32[]{:S(2)}) copy-start(bf16[4,512,1024]{2,1,0:T(8,128)(2,1)} %copy-done.5) | copy-start | bytes 12582916

commit v5 on v4

--- a/solution.py
+++ b/solution.py
@@ -654,20 +654,19 @@
         pieces.append(attention(i, FW // per_head, ids, query, keys, values, rim, after))
         return pieces[-1]
 
-    att = attend([s[1] for s in split_up])
+    att = attend([s[1] for s in split_up] + strips[1:2])
     pull, far = [], []
     for h in range(heads):
-        more = strips[1:2] if h == heads - 1 else []
-        p = total(split_up[h][0], away[h], [att] + pull + more)
+        p = total(split_up[h][0], away[h], [att] + pull)
         for b in order[h][1:-1]:
             p = total(p, swap(p, b), [])
         pull.append(p)
         far.append(swap(p, order[h][-1]))
-        att = attend([p])
+        att = attend([p] + (strips[:1] if h == heads - 1 else []))
     while len(pieces) < per_head * heads:
         att = attend([att])
     both = [x for h in range(heads) for x in (pull[h], far[h])]
-    new = renorm(ids, tokens_all, fast_weights, both, [att] + strips[:1])
+    new = renorm(ids, tokens_all, fast_weights, both, [att] + strips[2:])
 
     cut = rows // 2
     merged, rest, weights = [], [], None
@@ -676,7 +675,7 @@
         near = swap(new[h], b)
         blocks = [new[h], near, swap(new[h], 1), swap(near, 1)]
         own = pieces[h * per_head : (h + 1) * per_head]
-        m, r, weights = apply(h, heads, ids, query, own, blocks, cut, weights, strips[2:] if h else [])
+        m, r, weights = apply(h, heads, ids, query, own, blocks, cut, weights, [])
         merged.append(m)
         rest.append(r)
     to_right = [[shift(m, "head", 1) for m in merged]]

time: 202 us -> 196 us (0.970)
  waiting for transfers between devices: 67.1 us -> 62.4 us
    ppermute x3, waiting for transfers between devices: 25.1 us -> 17.6 us  [rotate(): lax.ppermute(block, axis, [(i, (i + distance) % n) for i in range(n)])]
    ppermute x17, waiting for transfers between devices: 32.5 us -> 37.7 us  [shift(): lax.ppermute(block, axis, [(i, i + distance) for i in range(n) if 0 <= i...]
    ppermute x15, waiting for transfers between devices: 9.55 us -> 7.04 us  [swap(): return lax.ppermute(block, 'ctx', [(i, i ^ bit) for i in range(n)])]
    ppermute x3, starting transfers between devices: 8.9 us -> 6.41 us  [rotate(): lax.ppermute(block, axis, [(i, (i + distance) % n) for i in range(n)])]
  transfers between devices with their start and end apart: 35 -> 35, of which waited for: 17 -> 15; matrix products, arithmetic and copies ran while one was open for 0% -> 0% of each run, Pallas kernels for 23% -> 24%
where the time goes in v5:
time: 196 us; the launch traced here: 195 us
  starting transfers between devices  68.1 us (35%)
  waiting for transfers between devices  62.4 us (32%)
  Pallas kernels  59.7 us (30%)
  local copies, waits for them, and re-layouts  3.64 us (2%)
    ppermute x17, starting transfers between devices, shift(): lax.ppermute(block, axis, [(i, i + distance) for i in range(n) if 0 <= i...  44.9 us
    ppermute x17, waiting for transfers between devices, shift(): lax.ppermute(block, axis, [(i, i + distance) for i in range(n) if 0 <= i...  37.7 us
    ppermute x3, waiting for transfers between devices, rotate(): lax.ppermute(block, axis, [(i, (i + distance) % n) for i in range(n)])  17.6 us
    ppermute x15, starting transfers between devices, swap(): return lax.ppermute(block, 'ctx', [(i, i ^ bit) for i in range(n)])  16.8 us
    pallas_call x2, Pallas kernels, grads(): pl.pallas_call(functools.partial(grads_kernel, h, at), grid=(1,), in_spec...  16 us
    pallas_call x1, Pallas kernels, gathered(): pl.pallas_call(functools.partial(gathered_kernel, n, heads, parts, at), g...  8.73 us
    pallas_call x4, Pallas kernels, attention(): pl.pallas_call(attn_kernel, grid=(1,), in_specs=[SMEM, col, col, col, of_...  8.26 us
    ppermute x15, waiting for transfers between devices, swap(): return lax.ppermute(block, 'ctx', [(i, i ^ bit) for i in range(n)])  7.04 us
  transfers between devices with their start and end apart: 35, of which 15 were waited for; matrix products, arithmetic and copies ran while one was open for 0% of the time, Pallas kernels for 24%

profile of v5, /device:TPU:0, one launch (start us, length us, event | category | flops | bytes accessed | tf_op | source)
XLA Modules:
  0.0 195.4 jit_solution(16879062983809699808)
XLA Ops:
  0.8 0.7 stack.137.ids_ref
  1.5 8.7 %shard_map.77 = (bf16[3088,128]{1,0:T(8,128)(2,1)}, bf16[3088,128]{1,0:T(8,128)(2,1)}, bf16[512,1024]{1,0:T(8,128)(2,1)}, bf16[128,1024]{1,0:T(8,128)(2,1)}, bf1...) custom-call(s32[31]{0:T(128)} %stack.137.ids_ref, s32[2,1024]{1,0:T(2,128)} %bitcast.38, bf16[1024,1024]{1,0:T(8,128)(2,1)} %k_ref.11, ...), custom_call_target="tpu_custom_call" | custom-call | flops 960000000 | tf_op jit(solution)/shard_map/pallas_call | solution.py:151
  10.2 2.6 %collective-permute-start = (bf16[512,1024]{1,0:T(8,128)(2,1)}, bf16[512,1024]{1,0:T(8,128)(2,1)S(1)}, u32[]{:S(2)}, u32[]{:S(2)}) collective-permute-start(bf16[512,1024]{1,0:T(8,128)(2,1)} %get-tuple-element.40), channel_id=1, source_target_pairs={{0,4},{4,8},{8,12},{12,16},{16,20},{20,24},{24,28},{1,5},{5,9},{9,... | collective-permute-start | bytes 3145736 | tf_op jit(solution)/shard_map/ppermute | solution.py:42
  12.9 2.6 %collective-permute-start.2 = (bf16[3088,128]{1,0:T(8,128)(2,1)}, bf16[3088,128]{1,0:T(8,128)(2,1)S(1)}, u32[]{:S(2)}, u32[]{:S(2)}) collective-permute-start(bf16[3088,128]{1,0:T(8,128)(2,1)} %get-tuple-element.44), channel_id=1, source_target_pairs={{0,4},{4,0},{8,12},{12,8},{16,20},{20,16},{24,28},{28,24},{1,5},{5... | collective-permute-start | bytes 2371592 | tf_op jit(solution)/shard_map/ppermute | solution.py:52
  15.5 7.2 %shard_map.78 = (bf16[3088,128]{1,0:T(8,128)(2,1)}, bf16[3088,128]{1,0:T(8,128)(2,1)}) custom-call(s32[31]{0:T(128)} %stack.137.ids_ref, s32[2,1024]{1,0:T(2,128)} %bitcast.39, bf16[1024,1024]{1,0:T(8,128)(2,1)} %k_ref.11, bf16[1024,1024]{1,0:T(8,128)(2,1)} %v_ref.11, bf16[2,3,512,512]{3,2,1,0:T(8,128)(2,1)} %base_ref.1, ...), custom_call_target="tpu_custom_call" | custom-call | flops 960000000 | tf_op jit(solution)/shard_map/pallas_call | solution.py:151
  22.8 0.9 shard_map.79
  23.7 1.6 collective-permute-start.4
  25.3 1.1 copy-done.8
  26.4 0.9 shard_map.80
  27.3 6.8 %collective-permute-start.3 = (bf16[1552,128]{1,0:T(8,128)(2,1)S(1)}, bf16[1552,128]{1,0:T(8,128)(2,1)S(1)}, u32[]{:S(2)}, u32[]{:S(2)}) collective-permute-start(bf16[1552,128]{1,0:T(8,128)(2,1)S(1)} %get-tuple-element.47.rest_1_), channel_id=1, source_target_pairs={{0,16},{4,20},{8,24},{12,28},{16,0},{20,4},{24,8},{28,12},{1,17},{... | collective-permute-start | bytes 1191944 | tf_op jit(solution)/shard_map/ppermute | solution.py:52
  34.1 2.6 %collective-permute-start.5 = (bf16[128,1024]{1,0:T(8,128)(2,1)S(1)}, bf16[128,1024]{1,0:T(8,128)(2,1)S(1)}, u32[]{:S(2)}, u32[]{:S(2)}) collective-permute-start(bf16[128,1024]{1,0:T(8,128)(2,1)S(1)} %copy-done.13), channel_id=1, source_target_pairs={{0,2},{1,3},{2,0},{3,1},{4,6},{5,7},{6,4},{7,5},{8,10},{9,11},{10,... | collective-permute-start | bytes 786440 | tf_op jit(solution)/shard_map/ppermute | solution.py:47
  36.7 10.4 %collective-permute-done.5.rest_2_ = bf16[128,1024]{1,0:T(8,128)(2,1)S(1)} collective-permute-done((bf16[128,1024]{1,0:T(8,128)(2,1)S(1)}, bf16[128,1024]{1,0:T(8,128)(2,1)S(1)}, u32[]{:S(2)}, u32[]{:S(2)}) %collective-permute-start.5) | collective-permute-done | bytes 262176 | tf_op jit(solution)/shard_map/ppermute | solution.py:47
  47.0 2.1 %shard_map.81.rest_0_.refs_0_ = bf16[1024,256]{1,0:T(8,128)(2,1)S(1)} custom-call(s32[31]{0:T(128)S(1)} %copy-done.9, bf16[1024,1024]{1,0:T(8,128)(2,1)S(1)} %copy-done.2, bf16[1024,1024]{1,0:T(8,128)(2,1)S(1)} %copy-done, bf16[1024,1024]{1,0:T(8,128)(2,1)S(1)} %copy-done.1, bf16[512,1024]{1,0:T(8,128)(2,1)S(1)} %collective-permute-done.refs_1_.rim_ref, ...), custom_call_target="tpu_custom_call" | custom-call | flops 252000000 | tf_op jit(solution)/shard_map/pallas_call | solution.py:315
  50.1 2.1 %shard_map.83.rest_0_.refs_1_ = bf16[1024,256]{1,0:T(8,128)(2,1)S(1)} custom-call(s32[31]{0:T(128)S(1)} %copy-done.9, bf16[1024,1024]{1,0:T(8,128)(2,1)S(1)} %copy-done.2, bf16[1024,1024]{1,0:T(8,128)(2,1)S(1)} %copy-done, bf16[1024,1024]{1,0:T(8,128)(2,1)S(1)} %copy-done.1, bf16[512,1024]{1,0:T(8,128)(2,1)S(1)} %collective-permute-done.refs_1_.rim_ref, ...), custom_call_target="tpu_custom_call" | custom-call | flops 252000000 | tf_op jit(solution)/shard_map/pallas_call | solution.py:315
  52.7 1.5 collective-permute-start.8
  54.2 0.7 collective-permute-start.6
  54.9 3.2 %collective-permute-start.9 = (bf16[128,1024]{1,0:T(8,128)(2,1)S(1)}, bf16[128,1024]{1,0:T(8,128)(2,1)S(1)}, u32[]{:S(2)}, u32[]{:S(2)}) collective-permute-start(bf16[128,1024]{1,0:T(8,128)(2,1)S(1)} %copy-done.11), channel_id=1, source_target_pairs={{0,3},{1,0},{2,1},{3,2},{4,7},{5,4},{6,5},{7,6},{8,11},{9,8},{10,9... | collective-permute-start | bytes 786440 | tf_op jit(solution)/shard_map/ppermute | solution.py:47
  58.0 7.3 %collective-permute-done.6.rest_1_ = bf16[128,1024]{1,0:T(8,128)(2,1)S(1)} collective-permute-done((bf16[128,1024]{1,0:T(8,128)(2,1)S(1)}, bf16[128,1024]{1,0:T(8,128)(2,1)S(1)}, u32[]{:S(2)}, u32[]{:S(2)}) %collective-permute-start.6) | collective-permute-done | bytes 262176 | tf_op jit(solution)/shard_map/ppermute | solution.py:47
  65.3 2.1 %shard_map.85.rest_0_.refs_0_ = bf16[1024,256]{1,0:T(8,128)(2,1)S(1)} custom-call(s32[31]{0:T(128)S(1)} %copy-done.9, bf16[1024,1024]{1,0:T(8,128)(2,1)S(1)} %copy-done.2, bf16[1024,1024]{1,0:T(8,128)(2,1)S(1)} %copy-done, bf16[1024,1024]{1,0:T(8,128)(2,1)S(1)} %copy-done.1, bf16[512,1024]{1,0:T(8,128)(2,1)S(1)} %collective-permute-done.refs_1_.rim_ref, ...), custom_call_target="tpu_custom_call" | custom-call | flops 252000000 | tf_op jit(solution)/shard_map/pallas_call | solution.py:315
  67.4 2.1 %shard_map.86.refs_4_.refs_1_ = bf16[1024,256]{1,0:T(8,128)(2,1)S(1)} custom-call(s32[31]{0:T(128)S(1)} %copy-done.9, bf16[1024,1024]{1,0:T(8,128)(2,1)S(1)} %copy-done.2, bf16[1024,1024]{1,0:T(8,128)(2,1)S(1)} %copy-done, bf16[1024,1024]{1,0:T(8,128)(2,1)S(1)} %copy-done.1, bf16[512,1024]{1,0:T(8,128)(2,1)S(1)} %collective-permute-done.refs_1_.rim_ref, ...), custom_call_target="tpu_custom_call" | custom-call | flops 252000000 | tf_op jit(solution)/shard_map/pallas_call | solution.py:315
  69.5 2.1 %shard_map.87 = (bf16[3,512,128]{2,1,0:T(8,128)(2,1)S(1)}, bf16[3,512,128]{2,1,0:T(8,128)(2,1)S(1)}) custom-call(s32[31]{0:T(128)S(1)} %copy-done.9, bf16[2,3,512,512]{3,2,1,0:T(8,128)(2,1)S(1)} %copy-done.3, bf16[1552,128]{1,0:T(8,128)(2,1)S(1)} %shard_map.82.rest_0_.rest_1_.refs_0_, bf16[1552,128]{1,0:T(8,128)(2,1)S(1)} %collective-permute-done.7.refs_1_, ...), custom_call_target="tpu_custom_call" | custom-call | flops 252000000 | tf_op jit(solution)/shard_map/pallas_call | solution.py:264
  72.2 1.7 collective-permute-start.10
  73.9 5.8 %collective-permute-done.13.refs_3_ = bf16[3,512,128]{2,1,0:T(8,128)(2,1)S(1)} collective-permute-done((bf16[3,512,128]{2,1,0:T(8,128)(2,1)S(1)}, bf16[3,512,128]{2,1,0:T(8,128)(2,1)S(1)}, u32[]{:S(2)}, u32[]{:S(2)}) %collective-permute-start.13) | collective-permute-done | bytes 393248 | tf_op jit(solution)/shard_map/ppermute | solution.py:52
  80.2 1.2 collective-permute-done.15.refs_5_
  81.4 3.2 %shard_map.88 = (bf16[512,512]{1,0:T(8,128)(2,1)S(1)}, bf16[512,512]{1,0:T(8,128)(2,1)S(1)}, bf16[2,3,512,512]{3,2,1,0:T(8,128)(2,1)}) custom-call(s32[31]{0:T(128)S(1)} %copy-done.9, bf16[1024,1024]{1,0:T(8,128)(2,1)S(1)} %copy-done.2, bf16[1024,256]{1,0:T(8,128)(2,1)S(1)} %shard_map.81.rest_0_.refs_0_, bf16[1024,256]{1,0:T(8,128)(2,1)S(1)} %shard_map.83.rest_0_.refs_1_, ...), custom_call_target="tpu_custom_call" | custom-call | flops 396000000 | tf_op jit(solution)/shard_map/pallas_call | solution.py:375
  84.7 5.3 %collective-permute-start.18 = (bf16[512,512]{1,0:T(8,128)(2,1)S(1)}, bf16[512,512]{1,0:T(8,128)(2,1)S(1)}, u32[]{:S(2)}, u32[]{:S(2)}) collective-permute-start(bf16[512,512]{1,0:T(8,128)(2,1)S(1)} %get-tuple-element.58.refs_0_), channel_id=1, source_target_pairs={{0,1},{1,2},{2,3},{4,5},{5,6},{6,7},{8,9},{9,10},{10,11},{12,13},{... | collective-permute-start | bytes 1572872 | tf_op jit(solution)/shard_map/ppermute | solution.py:42
  89.9 1.3 collective-permute-start.19
  91.3 3.2 %shard_map.89 = (bf16[512,512]{1,0:T(8,128)(2,1)S(1)}, bf16[512,512]{1,0:T(8,128)(2,1)S(1)}, bf16[2,3,512,512]{3,2,1,0:T(8,128)(2,1)}) custom-call(s32[31]{0:T(128)S(1)} %copy-done.9, bf16[1024,1024]{1,0:T(8,128)(2,1)S(1)} %copy-done.2, bf16[1024,256]{1,0:T(8,128)(2,1)S(1)} %shard_map.85.rest_0_.refs_0_, ...), custom_call_target="tpu_custom_call", output_to_operand_aliasing={{2}: (8, {})} | custom-call | flops 396000000 | tf_op jit(solution)/shard_map/pallas_call | solution.py:375
  94.5 4.6 %collective-permute-start.16 = (bf16[512,512]{1,0:T(8,128)(2,1)S(1)}, bf16[512,512]{1,0:T(8,128)(2,1)S(1)}, u32[]{:S(2)}, u32[]{:S(2)}) collective-permute-start(bf16[512,512]{1,0:T(8,128)(2,1)S(1)} %get-tuple-element.55.refs_3_.refs_1_), channel_id=1, source_target_pairs={{0,1},{1,2},{2,3},{4,5},{5,6},{6,7},{8,9},{9,10},{10,11},{12,13},{... | collective-permute-start | bytes 1572872 | tf_op jit(solution)/shard_map/ppermute | solution.py:42
  99.1 1.3 collective-permute-start.17
  101.1 5.7 %shard_map.91.p_hbm = bf16[4,512,1024]{2,1,0:T(8,128)(2,1)S(1)} custom-call(bf16[512,512]{1,0:T(8,128)(2,1)S(1)} %get-tuple-element.56.refs_0_, bf16[512,512]{1,0:T(8,128)(2,1)S(1)} %get-tuple-element.57.refs_1_, bf16[1024,4096]{1,0:T(8,128)(2,1)S(1)} %bitcast.31, bf16[3,128,1024]{2,1,0:T(8,128)(2,1)S(1)} %shard_map.90.refs_3_), custom_call_target="tpu_custom_call" | custom-call | flops 120000000 | tf_op jit(solution)/shard_map/pallas_call | solution.py:415
  106.8 1.0 shard_map.92
  107.9 4.7 %collective-permute-start.22 = (bf16[512,512]{1,0:T(8,128)(2,1)S(1)}, bf16[512,512]{1,0:T(8,128)(2,1)S(1)}, u32[]{:S(2)}, u32[]{:S(2)}) collective-permute-start(bf16[512,512]{1,0:T(8,128)(2,1)S(1)} %get-tuple-element.63), channel_id=1, source_target_pairs={{0,1},{1,2},{2,3},{4,5},{5,6},{6,7},{8,9},{9,10},{10,11},{12,13},{... | collective-permute-start | bytes 1572872 | tf_op jit(solution)/shard_map/ppermute | solution.py:42
  112.5 1.3 collective-permute-start.23
  113.8 4.0 %collective-permute-done.17.left_hbm = bf16[512,512]{1,0:T(8,128)(2,1)S(1)} collective-permute-done((bf16[512,512]{1,0:T(8,128)(2,1)S(1)}, bf16[512,512]{1,0:T(8,128)(2,1)S(1)}, u32[]{:S(2)}, u32[]{:S(2)}) %collective-permute-start.17) | collective-permute-done | bytes 524320 | tf_op jit(solution)/shard_map/ppermute | solution.py:42
  117.9 1.0 shard_map.93
  118.9 3.2 %collective-permute-start.20 = (bf16[512,512]{1,0:T(8,128)(2,1)S(1)}, bf16[512,512]{1,0:T(8,128)(2,1)S(1)}, u32[]{:S(2)}, u32[]{:S(2)}) collective-permute-start(bf16[512,512]{1,0:T(8,128)(2,1)S(1)} %get-tuple-element.61), channel_id=1, source_target_pairs={{0,1},{1,2},{2,3},{4,5},{5,6},{6,7},{8,9},{9,10},{10,11},{12,13},{... | collective-permute-start | bytes 1572872 | tf_op jit(solution)/shard_map/ppermute | solution.py:42
  122.1 1.6 collective-permute-start.21
  124.0 0.9 collective-permute-done.22.right_hbm
  124.9 4.4 %collective-permute-done.23.left_hbm = bf16[512,512]{1,0:T(8,128)(2,1)S(1)} collective-permute-done((bf16[512,512]{1,0:T(8,128)(2,1)S(1)}, bf16[512,512]{1,0:T(8,128)(2,1)S(1)}, u32[]{:S(2)}, u32[]{:S(2)}) %collective-permute-start.23) | collective-permute-done | bytes 524320 | tf_op jit(solution)/shard_map/ppermute | solution.py:42
  129.3 1.0 shard_map.94
  130.3 3.1 %collective-permute-start.26 = (bf16[512,512]{1,0:T(8,128)(2,1)S(1)}, bf16[512,512]{1,0:T(8,128)(2,1)S(1)}, u32[]{:S(2)}, u32[]{:S(2)}) collective-permute-start(bf16[512,512]{1,0:T(8,128)(2,1)S(1)} %get-tuple-element.69), channel_id=1, source_target_pairs={{0,1},{1,2},{2,3},{4,5},{5,6},{6,7},{8,9},{9,10},{10,11},{12,13},{... | collective-permute-start | bytes 1572872 | tf_op jit(solution)/shard_map/ppermute | solution.py:42
  133.4 1.3 collective-permute-start.27
  134.7 1.4 collective-permute-done.20.right_hbm
  136.1 4.4 %collective-permute-done.21.left_hbm = bf16[512,512]{1,0:T(8,128)(2,1)S(1)} collective-permute-done((bf16[512,512]{1,0:T(8,128)(2,1)S(1)}, bf16[512,512]{1,0:T(8,128)(2,1)S(1)}, u32[]{:S(2)}, u32[]{:S(2)}) %collective-permute-start.21) | collective-permute-done | bytes 524320 | tf_op jit(solution)/shard_map/ppermute | solution.py:42
  140.5 1.0 shard_map.95
  141.5 3.1 %collective-permute-start.24 = (bf16[512,512]{1,0:T(8,128)(2,1)S(1)}, bf16[512,512]{1,0:T(8,128)(2,1)S(1)}, u32[]{:S(2)}, u32[]{:S(2)}) collective-permute-start(bf16[512,512]{1,0:T(8,128)(2,1)S(1)} %get-tuple-element.67), channel_id=1, source_target_pairs={{0,1},{1,2},{2,3},{4,5},{5,6},{6,7},{8,9},{9,10},{10,11},{12,13},{... | collective-permute-start | bytes 1572872 | tf_op jit(solution)/shard_map/ppermute | solution.py:42
  144.6 1.3 collective-permute-start.25
  145.9 1.4 collective-permute-done.26.right_hbm
  147.3 4.4 %collective-permute-done.27.left_hbm = bf16[512,512]{1,0:T(8,128)(2,1)S(1)} collective-permute-done((bf16[512,512]{1,0:T(8,128)(2,1)S(1)}, bf16[512,512]{1,0:T(8,128)(2,1)S(1)}, u32[]{:S(2)}, u32[]{:S(2)}) %collective-permute-start.27) | collective-permute-done | bytes 524320 | tf_op jit(solution)/shard_map/ppermute | solution.py:42
  151.8 1.0 shard_map.96
  152.8 4.8 %collective-permute-done.24.right_hbm = bf16[512,512]{1,0:T(8,128)(2,1)S(1)} collective-permute-done((bf16[512,512]{1,0:T(8,128)(2,1)S(1)}, bf16[512,512]{1,0:T(8,128)(2,1)S(1)}, u32[]{:S(2)}, u32[]{:S(2)}) %collective-permute-start.24) | collective-permute-done | bytes 524320 | tf_op jit(solution)/shard_map/ppermute | solution.py:42
  157.6 4.1 %collective-permute-done.25.left_hbm = bf16[512,512]{1,0:T(8,128)(2,1)S(1)} collective-permute-done((bf16[512,512]{1,0:T(8,128)(2,1)S(1)}, bf16[512,512]{1,0:T(8,128)(2,1)S(1)}, u32[]{:S(2)}, u32[]{:S(2)}) %collective-permute-start.25) | collective-permute-done | bytes 524320 | tf_op jit(solution)/shard_map/ppermute | solution.py:42
  161.7 1.0 shard_map.97
  163.0 3.3 %collective-permute-start.30 = (bf16[512,512]{1,0:T(8,128)(2,1)S(1)}, bf16[512,512]{1,0:T(8,128)(2,1)S(1)}, u32[]{:S(2)}, u32[]{:S(2)}) collective-permute-start(bf16[512,512]{1,0:T(8,128)(2,1)S(1)} %get-tuple-element.75), channel_id=1, source_target_pairs={{0,1},{1,2},{2,3},{4,5},{5,6},{6,7},{8,9},{9,10},{10,11},{12,13},{... | collective-permute-start | bytes 1572872 | tf_op jit(solution)/shard_map/ppermute | solution.py:42
  166.4 1.3 collective-permute-start.31
  167.7 4.6 %collective-permute-start.28 = (bf16[512,512]{1,0:T(8,128)(2,1)S(1)}, bf16[512,512]{1,0:T(8,128)(2,1)S(1)}, u32[]{:S(2)}, u32[]{:S(2)}) collective-permute-start(bf16[512,512]{1,0:T(8,128)(2,1)S(1)} %get-tuple-element.73), channel_id=1, source_target_pairs={{0,1},{1,2},{2,3},{4,5},{5,6},{6,7},{8,9},{9,10},{10,11},{12,13},{... | collective-permute-start | bytes 1572872 | tf_op jit(solution)/shard_map/ppermute | solution.py:42
  172.2 1.3 collective-permute-start.29
  173.6 1.7 copy-done.10
  175.3 8.7 %shard_map.100.out_in = bf16[1024,1024]{1,0:T(8,128)(2,1)} custom-call(s32[31]{0:T(128)S(1)} %copy-done.9, bf16[512,512]{1,0:T(8,128)(2,1)S(1)} %get-tuple-element.58.refs_0_, bf16[512,512]{1,0:T(8,128)(2,1)S(1)} %get-tuple-element.55.refs_3_.refs_1_, bf16[3,512,1024]{2,1,0:T(8,128)(2,1)S(1)} %get-tuple-element.76.refs_2_, bf16[1024,4096]{1,0:T(8,128)(2,1)} %refs_3_.1, ...), custom_call_target="tpu_custom_call" | custom-call | flops 1080000000 | tf_op jit(solution)/shard_map/pallas_call | solution.py:529
  184.1 1.7 shard_map.101.out_in
  185.8 3.6 %collective-permute-done.28.right_hbm = bf16[512,512]{1,0:T(8,128)(2,1)S(1)} collective-permute-done((bf16[512,512]{1,0:T(8,128)(2,1)S(1)}, bf16[512,512]{1,0:T(8,128)(2,1)S(1)}, u32[]{:S(2)}, u32[]{:S(2)}) %collective-permute-start.28) | collective-permute-done | bytes 524320 | tf_op jit(solution)/shard_map/ppermute | solution.py:42
  189.4 4.1 %collective-permute-done.29.left_hbm = bf16[512,512]{1,0:T(8,128)(2,1)S(1)} collective-permute-done((bf16[512,512]{1,0:T(8,128)(2,1)S(1)}, bf16[512,512]{1,0:T(8,128)(2,1)S(1)}, u32[]{:S(2)}, u32[]{:S(2)}) %collective-permute-start.29) | collective-permute-done | bytes 524320 | tf_op jit(solution)/shard_map/ppermute | solution.py:42
  193.5 1.7 shard_map.102
  (66 shorter events, 4.1 us)
Async XLA Ops:
  10.2 15.0 %collective-permute-start = (bf16[512,1024]{1,0:T(8,128)(2,1)}, bf16[512,1024]{1,0:T(8,128)(2,1)S(1)}, u32[]{:S(2)}, u32[]{:S(2)}) collective-permute-start(bf16[512,1024]{1,0:T(8,128)(2,1)} %get-tuple-element.40), channel_id=1, source_target_pairs={{0,4},{4,8},{8,12},{12,16},{16,20},{20,24},{24,28},{1,5},{5,9},{9,... | collective-permute-start | bytes 3145736 | tf_op jit(solution)/shard_map/ppermute | solution.py:42
  12.9 10.0 %collective-permute-start.2 = (bf16[3088,128]{1,0:T(8,128)(2,1)}, bf16[3088,128]{1,0:T(8,128)(2,1)S(1)}, u32[]{:S(2)}, u32[]{:S(2)}) collective-permute-start(bf16[3088,128]{1,0:T(8,128)(2,1)} %get-tuple-element.44), channel_id=1, source_target_pairs={{0,4},{4,0},{8,12},{12,8},{16,20},{20,16},{24,28},{28,24},{1,5},{5... | collective-permute-start | bytes 2371592 | tf_op jit(solution)/shard_map/ppermute | solution.py:52
  15.5 7.4 %copy-start.7 = (bf16[3088,128]{1,0:T(8,128)(2,1)S(1)}, bf16[3088,128]{1,0:T(8,128)(2,1)}, u32[]{:S(2)}) copy-start(bf16[3088,128]{1,0:T(8,128)(2,1)} %get-tuple-element.41.refs_0_.keep_hbm) | copy-start | bytes 2371588
  15.5 7.4 %copy-start.9 = (s32[31]{0:T(128)S(1)}, s32[31]{0:T(128)}, u32[]{:S(2)}) copy-start(s32[31]{0:T(128)} %stack.137.ids_ref) | copy-start | bytes 376
  15.5 18.6 %copy-start.13 = (bf16[128,1024]{1,0:T(8,128)(2,1)S(1)}, bf16[128,1024]{1,0:T(8,128)(2,1)}, u32[]{:S(2)}) copy-start(bf16[128,1024]{1,0:T(8,128)(2,1)} %get-tuple-element.49) | copy-start | bytes 786436
  15.5 31.6 %copy-start.2 = (bf16[1024,1024]{1,0:T(8,128)(2,1)S(1)}, bf16[1024,1024]{1,0:T(8,128)(2,1)}, u32[]{:S(2)}) copy-start(bf16[1024,1024]{1,0:T(8,128)(2,1)} %q_hbm.3) | copy-start | bytes 6291460
  22.7 24.4 %copy-start = (bf16[1024,1024]{1,0:T(8,128)(2,1)S(1)}, bf16[1024,1024]{1,0:T(8,128)(2,1)}, u32[]{:S(2)}) copy-start(bf16[1024,1024]{1,0:T(8,128)(2,1)} %k_ref.11) | copy-start | bytes 6291460
  22.7 24.3 %copy-start.1 = (bf16[1024,1024]{1,0:T(8,128)(2,1)S(1)}, bf16[1024,1024]{1,0:T(8,128)(2,1)}, u32[]{:S(2)}) copy-start(bf16[1024,1024]{1,0:T(8,128)(2,1)} %v_ref.11) | copy-start | bytes 6291460
  22.7 2.6 %collective-permute-start.1 = (bf16[3088,128]{1,0:T(8,128)(2,1)}, bf16[3088,128]{1,0:T(8,128)(2,1)S(1)}, u32[]{:S(2)}, u32[]{:S(2)}) collective-permute-start(bf16[3088,128]{1,0:T(8,128)(2,1)} %get-tuple-element.43), channel_id=1, source_target_pairs={{0,4},{4,0},{8,12},{12,8},{16,20},{20,16},{24,28},{28,24},{1,5},{5... | collective-permute-start | bytes 2371592 | tf_op jit(solution)/shard_map/ppermute | solution.py:52
  23.7 25.4 %collective-permute-start.4 = (bf16[1552,128]{1,0:T(8,128)(2,1)S(1)}, bf16[1552,128]{1,0:T(8,128)(2,1)S(1)}, u32[]{:S(2)}, u32[]{:S(2)}) collective-permute-start(bf16[1552,128]{1,0:T(8,128)(2,1)S(1)} %get-tuple-element.45.refs_0_.rest_0_), channel_id=1, source_target_pairs={{0,8},{4,12},{8,0},{12,4},{16,24},{20,28},{24,16},{28,20},{1,9},{5... | collective-permute-start | bytes 1191944 | tf_op jit(solution)/shard_map/ppermute | solution.py:52
  25.3 1.1 copy-start.8
  27.3 24.9 %collective-permute-start.3 = (bf16[1552,128]{1,0:T(8,128)(2,1)S(1)}, bf16[1552,128]{1,0:T(8,128)(2,1)S(1)}, u32[]{:S(2)}, u32[]{:S(2)}) collective-permute-start(bf16[1552,128]{1,0:T(8,128)(2,1)S(1)} %get-tuple-element.47.rest_1_), channel_id=1, source_target_pairs={{0,16},{4,20},{8,24},{12,28},{16,0},{20,4},{24,8},{28,12},{1,17},{... | collective-permute-start | bytes 1191944 | tf_op jit(solution)/shard_map/ppermute | solution.py:52
  34.1 13.0 %collective-permute-start.5 = (bf16[128,1024]{1,0:T(8,128)(2,1)S(1)}, bf16[128,1024]{1,0:T(8,128)(2,1)S(1)}, u32[]{:S(2)}, u32[]{:S(2)}) collective-permute-start(bf16[128,1024]{1,0:T(8,128)(2,1)S(1)} %copy-done.13), channel_id=1, source_target_pairs={{0,2},{1,3},{2,0},{3,1},{4,6},{5,7},{6,4},{7,5},{8,10},{9,11},{10,... | collective-permute-start | bytes 786440 | tf_op jit(solution)/shard_map/ppermute | solution.py:47
  49.6 4.6 %copy-start.12 = (bf16[128,1024]{1,0:T(8,128)(2,1)S(1)}, bf16[128,1024]{1,0:T(8,128)(2,1)}, u32[]{:S(2)}) copy-start(bf16[128,1024]{1,0:T(8,128)(2,1)} %get-tuple-element.50) | copy-start | bytes 786436
  49.7 5.2 %copy-start.11 = (bf16[128,1024]{1,0:T(8,128)(2,1)S(1)}, bf16[128,1024]{1,0:T(8,128)(2,1)}, u32[]{:S(2)}) copy-start(bf16[128,1024]{1,0:T(8,128)(2,1)} %get-tuple-element.51) | copy-start | bytes 786436
  49.7 19.8 %collective-permute-start.7 = (bf16[1552,128]{1,0:T(8,128)(2,1)S(1)}, bf16[1552,128]{1,0:T(8,128)(2,1)S(1)}, u32[]{:S(2)}, u32[]{:S(2)}) collective-permute-start(bf16[1552,128]{1,0:T(8,128)(2,1)S(1)} %shard_map.82.rest_0_.rest_1_.refs_0_), channel_id=1, source_target_pairs={{0,16},{4,20},{8,24},{12,28},{16,0},{20,4},{24,8},{28,12},{1,17},{... | collective-permute-start | bytes 1191944 | tf_op jit(solution)/shard_map/ppermute | solution.py:52
  52.7 16.8 %collective-permute-start.8 = (bf16[1552,128]{1,0:T(8,128)(2,1)S(1)}, bf16[1552,128]{1,0:T(8,128)(2,1)S(1)}, u32[]{:S(2)}, u32[]{:S(2)}) collective-permute-start(bf16[1552,128]{1,0:T(8,128)(2,1)S(1)} %shard_map.84.rest_0_.refs_2_), channel_id=1, source_target_pairs={{0,8},{4,12},{8,0},{12,4},{16,24},{20,28},{24,16},{28,20},{1,9},{5... | collective-permute-start | bytes 1191944 | tf_op jit(solution)/shard_map/ppermute | solution.py:52
  54.2 11.1 %collective-permute-start.6 = (bf16[128,1024]{1,0:T(8,128)(2,1)S(1)}, bf16[128,1024]{1,0:T(8,128)(2,1)S(1)}, u32[]{:S(2)}, u32[]{:S(2)}) collective-permute-start(bf16[128,1024]{1,0:T(8,128)(2,1)S(1)} %copy-done.12), channel_id=1, source_target_pairs={{0,1},{1,2},{2,3},{3,0},{4,5},{5,6},{6,7},{7,4},{8,9},{9,10},{10,1... | collective-permute-start | bytes 786440 | tf_op jit(solution)/shard_map/ppermute | solution.py:47
  54.9 14.6 %collective-permute-start.9 = (bf16[128,1024]{1,0:T(8,128)(2,1)S(1)}, bf16[128,1024]{1,0:T(8,128)(2,1)S(1)}, u32[]{:S(2)}, u32[]{:S(2)}) collective-permute-start(bf16[128,1024]{1,0:T(8,128)(2,1)S(1)} %copy-done.11), channel_id=1, source_target_pairs={{0,3},{1,0},{2,1},{3,2},{4,7},{5,4},{6,5},{7,6},{8,11},{9,8},{10,9... | collective-permute-start | bytes 786440 | tf_op jit(solution)/shard_map/ppermute | solution.py:47
  67.4 2.1 %copy-start.3 = (bf16[2,3,512,512]{3,2,1,0:T(8,128)(2,1)S(1)}, bf16[2,3,512,512]{3,2,1,0:T(8,128)(2,1)}, u32[]{:S(2)}) copy-start(bf16[2,3,512,512]{3,2,1,0:T(8,128)(2,1)} %base_ref.1) | copy-start | bytes 9437188
  69.5 31.6 %slice-start = ((s8[8388608]{0:T(1024)(128)(4,1)}), s8[4194304]{0:T(1024)(128)(4,1)S(1)}, s32[]{:S(2)}) async-start(s8[8388608]{0:T(1024)(128)(4,1)} %bitcast.30), calls=%async_computation | async-start | bytes 8388608
  71.6 8.1 %collective-permute-start.13 = (bf16[3,512,128]{2,1,0:T(8,128)(2,1)S(1)}, bf16[3,512,128]{2,1,0:T(8,128)(2,1)S(1)}, u32[]{:S(2)}, u32[]{:S(2)}) collective-permute-start(bf16[3,512,128]{2,1,0:T(8,128)(2,1)S(1)} %get-tuple-element.53.refs_2_), channel_id=1, source_target_pairs={{0,8},{4,12},{8,0},{12,4},{16,24},{20,28},{24,16},{28,20},{1,9},{5... | collective-permute-start | bytes 1179656 | tf_op jit(solution)/shard_map/ppermute | solution.py:52
  72.2 28.9 %slice-start.1 = ((s8[8388608]{0:T(1024)(128)(4,1)}), s8[4194304]{0:T(1024)(128)(4,1)S(1)}, s32[]{:S(2)}) async-start(s8[8388608]{0:T(1024)(128)(4,1)} %bitcast.30), calls=%async_computation.1 | async-start | bytes 8388608
  72.2 8.0 %collective-permute-start.10 = (bf16[3,512,128]{2,1,0:T(8,128)(2,1)S(1)}, bf16[3,512,128]{2,1,0:T(8,128)(2,1)S(1)}, u32[]{:S(2)}, u32[]{:S(2)}) collective-permute-start(bf16[3,512,128]{2,1,0:T(8,128)(2,1)S(1)} %get-tuple-element.52.refs_2_), channel_id=1, source_target_pairs={{0,16},{4,20},{8,24},{12,28},{16,0},{20,4},{24,8},{28,12},{1,17},{... | collective-permute-start | bytes 1179656 | tf_op jit(solution)/shard_map/ppermute | solution.py:52
  73.9 6.3 %collective-permute-start.14 = (bf16[3,512,128]{2,1,0:T(8,128)(2,1)S(1)}, bf16[3,512,128]{2,1,0:T(8,128)(2,1)S(1)}, u32[]{:S(2)}, u32[]{:S(2)}) collective-permute-start(bf16[3,512,128]{2,1,0:T(8,128)(2,1)S(1)} %get-tuple-element.53.refs_2_), channel_id=1, source_target_pairs={{0,4},{4,0},{8,12},{12,8},{16,20},{20,16},{24,28},{28,24},{1,5},{5... | collective-permute-start | bytes 1179656 | tf_op jit(solution)/shard_map/ppermute | solution.py:52
  79.7 1.7 collective-permute-start.15
  79.7 11.5 %collective-permute-start.11 = (bf16[3,512,128]{2,1,0:T(8,128)(2,1)S(1)}, bf16[3,512,128]{2,1,0:T(8,128)(2,1)S(1)}, u32[]{:S(2)}, u32[]{:S(2)}) collective-permute-start(bf16[3,512,128]{2,1,0:T(8,128)(2,1)S(1)} %get-tuple-element.52.refs_2_), channel_id=1, source_target_pairs={{0,4},{4,0},{8,12},{12,8},{16,20},{20,16},{24,28},{28,24},{1,5},{5... | collective-permute-start | bytes 1179656 | tf_op jit(solution)/shard_map/ppermute | solution.py:52
  80.2 11.0 %collective-permute-start.12 = (bf16[3,512,128]{2,1,0:T(8,128)(2,1)S(1)}, bf16[3,512,128]{2,1,0:T(8,128)(2,1)S(1)}, u32[]{:S(2)}, u32[]{:S(2)}) collective-permute-start(bf16[3,512,128]{2,1,0:T(8,128)(2,1)S(1)} %collective-permute-done.10.refs_3_), channel_id=1, source_target_pairs={{0,4},{4,0},{8,12},{12,8},{16,20},{20,16},{24,28},{28,24},{1,5},{5... | collective-permute-start | bytes 1179656 | tf_op jit(solution)/shard_map/ppermute | solution.py:52
  84.7 22.2 %collective-permute-start.18 = (bf16[512,512]{1,0:T(8,128)(2,1)S(1)}, bf16[512,512]{1,0:T(8,128)(2,1)S(1)}, u32[]{:S(2)}, u32[]{:S(2)}) collective-permute-start(bf16[512,512]{1,0:T(8,128)(2,1)S(1)} %get-tuple-element.58.refs_0_), channel_id=1, source_target_pairs={{0,1},{1,2},{2,3},{4,5},{5,6},{6,7},{8,9},{9,10},{10,11},{12,13},{... | collective-permute-start | bytes 1572872 | tf_op jit(solution)/shard_map/ppermute | solution.py:42
  89.9 16.9 %collective-permute-start.19 = (bf16[512,512]{1,0:T(8,128)(2,1)S(1)}, bf16[512,512]{1,0:T(8,128)(2,1)S(1)}, u32[]{:S(2)}, u32[]{:S(2)}) collective-permute-start(bf16[512,512]{1,0:T(8,128)(2,1)S(1)} %get-tuple-element.58.refs_0_), channel_id=1, source_target_pairs={{1,0},{2,1},{3,2},{5,4},{6,5},{7,6},{9,8},{10,9},{11,10},{13,12},{... | collective-permute-start | bytes 1572872 | tf_op jit(solution)/shard_map/ppermute | solution.py:42
  94.5 19.3 %collective-permute-start.16 = (bf16[512,512]{1,0:T(8,128)(2,1)S(1)}, bf16[512,512]{1,0:T(8,128)(2,1)S(1)}, u32[]{:S(2)}, u32[]{:S(2)}) collective-permute-start(bf16[512,512]{1,0:T(8,128)(2,1)S(1)} %get-tuple-element.55.refs_3_.refs_1_), channel_id=1, source_target_pairs={{0,1},{1,2},{2,3},{4,5},{5,6},{6,7},{8,9},{9,10},{10,11},{12,13},{... | collective-permute-start | bytes 1572872 | tf_op jit(solution)/shard_map/ppermute | solution.py:42
  99.1 18.8 %collective-permute-start.17 = (bf16[512,512]{1,0:T(8,128)(2,1)S(1)}, bf16[512,512]{1,0:T(8,128)(2,1)S(1)}, u32[]{:S(2)}, u32[]{:S(2)}) collective-permute-start(bf16[512,512]{1,0:T(8,128)(2,1)S(1)} %get-tuple-element.55.refs_3_.refs_1_), channel_id=1, source_target_pairs={{1,0},{2,1},{3,2},{5,4},{6,5},{7,6},{9,8},{10,9},{11,10},{13,12},{... | collective-permute-start | bytes 1572872 | tf_op jit(solution)/shard_map/ppermute | solution.py:42
  100.5 23.2 %collective-permute-start.32 = (bf16[1,3,128,1024]{3,2,1,0:T(8,128)(2,1)S(1)}, bf16[1,3,128,1024]{3,2,1,0:T(8,128)(2,1)S(1)}, u32[]{:S(2)}, u32[]{:S(2)}) collective-permute-start(bf16[1,3,128,1024]{3,2,1,0:T(8,128)(2,1)S(1)} %bitcast.32), channel_id=1, source_target_pairs={{0,16},{4,20},{8,24},{12,28},{16,0},{20,4},{24,8},{28,12},{1,17},{... | collective-permute-start | bytes 2359304 | tf_op jit(solution)/shard_map/ppermute | solution.py:52
  106.8 54.9 %copy-start.5 = (bf16[4,512,1024]{2,1,0:T(8,128)(2,1)}, bf16[4,512,1024]{2,1,0:T(8,128)(2,1)S(1)}, u32[]{:S(2)}) copy-start(bf16[4,512,1024]{2,1,0:T(8,128)(2,1)S(1)} %shard_map.91.p_hbm) | copy-start | bytes 12582916
  107.9 17.0 %collective-permute-start.22 = (bf16[512,512]{1,0:T(8,128)(2,1)S(1)}, bf16[512,512]{1,0:T(8,128)(2,1)S(1)}, u32[]{:S(2)}, u32[]{:S(2)}) collective-permute-start(bf16[512,512]{1,0:T(8,128)(2,1)S(1)} %get-tuple-element.63), channel_id=1, source_target_pairs={{0,1},{1,2},{2,3},{4,5},{5,6},{6,7},{8,9},{9,10},{10,11},{12,13},{... | collective-permute-start | bytes 1572872 | tf_op jit(solution)/shard_map/ppermute | solution.py:42
  112.5 16.8 %collective-permute-start.23 = (bf16[512,512]{1,0:T(8,128)(2,1)S(1)}, bf16[512,512]{1,0:T(8,128)(2,1)S(1)}, u32[]{:S(2)}, u32[]{:S(2)}) collective-permute-start(bf16[512,512]{1,0:T(8,128)(2,1)S(1)} %get-tuple-element.60.refs_1_), channel_id=1, source_target_pairs={{1,0},{2,1},{3,2},{5,4},{6,5},{7,6},{9,8},{10,9},{11,10},{13,12},{... | collective-permute-start | bytes 1572872 | tf_op jit(solution)/shard_map/ppermute | solution.py:42
  118.9 17.2 %collective-permute-start.20 = (bf16[512,512]{1,0:T(8,128)(2,1)S(1)}, bf16[512,512]{1,0:T(8,128)(2,1)S(1)}, u32[]{:S(2)}, u32[]{:S(2)}) collective-permute-start(bf16[512,512]{1,0:T(8,128)(2,1)S(1)} %get-tuple-element.61), channel_id=1, source_target_pairs={{0,1},{1,2},{2,3},{4,5},{5,6},{6,7},{8,9},{9,10},{10,11},{12,13},{... | collective-permute-start | bytes 1572872 | tf_op jit(solution)/shard_map/ppermute | solution.py:42
  122.1 18.5 %collective-permute-start.21 = (bf16[512,512]{1,0:T(8,128)(2,1)S(1)}, bf16[512,512]{1,0:T(8,128)(2,1)S(1)}, u32[]{:S(2)}, u32[]{:S(2)}) collective-permute-start(bf16[512,512]{1,0:T(8,128)(2,1)S(1)} %get-tuple-element.62.refs_1_.refs_2_), channel_id=1, source_target_pairs={{1,0},{2,1},{3,2},{5,4},{6,5},{7,6},{9,8},{10,9},{11,10},{13,12},{... | collective-permute-start | bytes 1572872 | tf_op jit(solution)/shard_map/ppermute | solution.py:42
  123.7 39.0 %collective-permute-start.33 = (bf16[2,3,128,1024]{3,2,1,0:T(8,128)(2,1)S(1)}, bf16[2,3,128,1024]{3,2,1,0:T(8,128)(2,1)S(1)}, u32[]{:S(2)}, u32[]{:S(2)}) collective-permute-start(bf16[2,3,128,1024]{3,2,1,0:T(8,128)(2,1)S(1)} %shard_map.98.refs_0_), channel_id=1, source_target_pairs={{0,8},{4,12},{8,0},{12,4},{16,24},{20,28},{24,16},{28,20},{1,9},{5... | collective-permute-start | bytes 4718600 | tf_op jit(solution)/shard_map/ppermute | solution.py:52
  130.3 17.0 %collective-permute-start.26 = (bf16[512,512]{1,0:T(8,128)(2,1)S(1)}, bf16[512,512]{1,0:T(8,128)(2,1)S(1)}, u32[]{:S(2)}, u32[]{:S(2)}) collective-permute-start(bf16[512,512]{1,0:T(8,128)(2,1)S(1)} %get-tuple-element.69), channel_id=1, source_target_pairs={{0,1},{1,2},{2,3},{4,5},{5,6},{6,7},{8,9},{9,10},{10,11},{12,13},{... | collective-permute-start | bytes 1572872 | tf_op jit(solution)/shard_map/ppermute | solution.py:42
  133.4 18.4 %collective-permute-start.27 = (bf16[512,512]{1,0:T(8,128)(2,1)S(1)}, bf16[512,512]{1,0:T(8,128)(2,1)S(1)}, u32[]{:S(2)}, u32[]{:S(2)}) collective-permute-start(bf16[512,512]{1,0:T(8,128)(2,1)S(1)} %get-tuple-element.66.refs_1_), channel_id=1, source_target_pairs={{1,0},{2,1},{3,2},{5,4},{6,5},{7,6},{9,8},{10,9},{11,10},{13,12},{... | collective-permute-start | bytes 1572872 | tf_op jit(solution)/shard_map/ppermute | solution.py:42
  141.5 16.0 %collective-permute-start.24 = (bf16[512,512]{1,0:T(8,128)(2,1)S(1)}, bf16[512,512]{1,0:T(8,128)(2,1)S(1)}, u32[]{:S(2)}, u32[]{:S(2)}) collective-permute-start(bf16[512,512]{1,0:T(8,128)(2,1)S(1)} %get-tuple-element.67), channel_id=1, source_target_pairs={{0,1},{1,2},{2,3},{4,5},{5,6},{6,7},{8,9},{9,10},{10,11},{12,13},{... | collective-permute-start | bytes 1572872 | tf_op jit(solution)/shard_map/ppermute | solution.py:42
  144.6 17.1 %collective-permute-start.25 = (bf16[512,512]{1,0:T(8,128)(2,1)S(1)}, bf16[512,512]{1,0:T(8,128)(2,1)S(1)}, u32[]{:S(2)}, u32[]{:S(2)}) collective-permute-start(bf16[512,512]{1,0:T(8,128)(2,1)S(1)} %get-tuple-element.68.refs_1_), channel_id=1, source_target_pairs={{1,0},{2,1},{3,2},{5,4},{6,5},{7,6},{9,8},{10,9},{11,10},{13,12},{... | collective-permute-start | bytes 1572872 | tf_op jit(solution)/shard_map/ppermute | solution.py:42
  162.9 12.4 %copy-start.4 = (bf16[4,3,128,1024]{3,2,1,0:T(8,128)(2,1)}, bf16[4,3,128,1024]{3,2,1,0:T(8,128)(2,1)S(1)}, u32[]{:S(2)}) copy-start(bf16[4,3,128,1024]{3,2,1,0:T(8,128)(2,1)S(1)} %shard_map.99.refs_4_) | copy-start | bytes 9437188
  162.9 10.6 %collective-permute-start.34 = (bf16[4,3,128,1024]{3,2,1,0:T(8,128)(2,1)S(1)}, bf16[4,3,128,1024]{3,2,1,0:T(8,128)(2,1)S(1)}, u32[]{:S(2)}, u32[]{:S(2)}) collective-permute-start(bf16[4,3,128,1024]{3,2,1,0:T(8,128)(2,1)S(1)} %shard_map.99.refs_4_), channel_id=1, source_target_pairs={{0,4},{4,0},{8,12},{12,8},{16,20},{20,16},{24,28},{28,24},{1,5},{5... | collective-permute-start | bytes 9437192 | tf_op jit(solution)/shard_map/ppermute | solution.py:52
  163.0 21.0 %collective-permute-start.30 = (bf16[512,512]{1,0:T(8,128)(2,1)S(1)}, bf16[512,512]{1,0:T(8,128)(2,1)S(1)}, u32[]{:S(2)}, u32[]{:S(2)}) collective-permute-start(bf16[512,512]{1,0:T(8,128)(2,1)S(1)} %get-tuple-element.75), channel_id=1, source_target_pairs={{0,1},{1,2},{2,3},{4,5},{5,6},{6,7},{8,9},{9,10},{10,11},{12,13},{... | collective-permute-start | bytes 1572872 | tf_op jit(solution)/shard_map/ppermute | solution.py:42
  166.4 17.7 %collective-permute-start.31 = (bf16[512,512]{1,0:T(8,128)(2,1)S(1)}, bf16[512,512]{1,0:T(8,128)(2,1)S(1)}, u32[]{:S(2)}, u32[]{:S(2)}) collective-permute-start(bf16[512,512]{1,0:T(8,128)(2,1)S(1)} %get-tuple-element.72.refs_1_), channel_id=1, source_target_pairs={{1,0},{2,1},{3,2},{5,4},{6,5},{7,6},{9,8},{10,9},{11,10},{13,12},{... | collective-permute-start | bytes 1572872 | tf_op jit(solution)/shard_map/ppermute | solution.py:42
  167.7 21.7 %collective-permute-start.28 = (bf16[512,512]{1,0:T(8,128)(2,1)S(1)}, bf16[512,512]{1,0:T(8,128)(2,1)S(1)}, u32[]{:S(2)}, u32[]{:S(2)}) collective-permute-start(bf16[512,512]{1,0:T(8,128)(2,1)S(1)} %get-tuple-element.73), channel_id=1, source_target_pairs={{0,1},{1,2},{2,3},{4,5},{5,6},{6,7},{8,9},{9,10},{10,11},{12,13},{... | collective-permute-start | bytes 1572872 | tf_op jit(solution)/shard_map/ppermute | solution.py:42
  172.2 21.3 %collective-permute-start.29 = (bf16[512,512]{1,0:T(8,128)(2,1)S(1)}, bf16[512,512]{1,0:T(8,128)(2,1)S(1)}, u32[]{:S(2)}, u32[]{:S(2)}) collective-permute-start(bf16[512,512]{1,0:T(8,128)(2,1)S(1)} %get-tuple-element.74.refs_2_.refs_6_), channel_id=1, source_target_pairs={{1,0},{2,1},{3,2},{5,4},{6,5},{7,6},{9,8},{10,9},{11,10},{13,12},{... | collective-permute-start | bytes 1572872 | tf_op jit(solution)/shard_map/ppermute | solution.py:42
  173.6 1.8 copy-start.10
  175.3 8.8 %copy-start.6 = (bf16[4,512,1024]{2,1,0:T(8,128)(2,1)S(1)}, bf16[4,512,1024]{2,1,0:T(8,128)(2,1)}, u32[]{:S(2)}) copy-start(bf16[4,512,1024]{2,1,0:T(8,128)(2,1)} %copy-done.5) | copy-start | bytes 12582916

commit v6 on v4

--- a/solution.py
+++ b/solution.py
@@ -664,10 +664,12 @@
         pull.append(p)
         far.append(swap(p, order[h][-1]))
         att = attend([p])
+        if h == 0:
+            att = attend([att])
     while len(pieces) < per_head * heads:
         att = attend([att])
     both = [x for h in range(heads) for x in (pull[h], far[h])]
-    new = renorm(ids, tokens_all, fast_weights, both, [att] + strips[:1])
+    new = renorm(ids, tokens_all, fast_weights, both, [att, strips[0]] + strips[2:])
 
     cut = rows // 2
     merged, rest, weights = [], [], None
@@ -676,7 +678,7 @@
         near = swap(new[h], b)
         blocks = [new[h], near, swap(new[h], 1), swap(near, 1)]
         own = pieces[h * per_head : (h + 1) * per_head]
-        m, r, weights = apply(h, heads, ids, query, own, blocks, cut, weights, strips[2:] if h else [])
+        m, r, weights = apply(h, heads, ids, query, own, blocks, cut, weights, [])
         merged.append(m)
         rest.append(r)
     to_right = [[shift(m, "head", 1) for m in merged]]

time: 202 us -> 189 us (0.936)
  waiting for transfers between devices: 67.1 us -> 58.8 us
  starting transfers between devices: 69.7 us -> 64.3 us
    ppermute x3, waiting for transfers between devices: 25.1 us -> 11.7 us  [rotate(): lax.ppermute(block, axis, [(i, (i + distance) % n) for i in range(n)])]
    ppermute x17, waiting for transfers between devices: 32.5 us -> 38.2 us  [shift(): lax.ppermute(block, axis, [(i, i + distance) for i in range(n) if 0 <= i...]
    ppermute x17, starting transfers between devices: 44.9 us -> 40.1 us  [shift(): lax.ppermute(block, axis, [(i, i + distance) for i in range(n) if 0 <= i...]
    ppermute x3, starting transfers between devices: 8.9 us -> 6.41 us  [rotate(): lax.ppermute(block, axis, [(i, (i + distance) % n) for i in range(n)])]
  transfers between devices with their start and end apart: 35 -> 35, of which waited for: 17 -> 17; matrix products, arithmetic and copies ran while one was open for 0% -> 0% of each run, Pallas kernels for 23% -> 25%
where the time goes in v6:
time: 189 us; the launch traced here: 188 us
  starting transfers between devices  64.3 us (34%)
  Pallas kernels  60 us (32%)
  waiting for transfers between devices  58.8 us (31%)
  local copies, waits for them, and re-layouts  3.64 us (2%)
    ppermute x17, starting transfers between devices, shift(): lax.ppermute(block, axis, [(i, i + distance) for i in range(n) if 0 <= i...  40.1 us
    ppermute x17, waiting for transfers between devices, shift(): lax.ppermute(block, axis, [(i, i + distance) for i in range(n) if 0 <= i...  38.2 us
    ppermute x15, starting transfers between devices, swap(): return lax.ppermute(block, 'ctx', [(i, i ^ bit) for i in range(n)])  17.8 us
    pallas_call x2, Pallas kernels, grads(): pl.pallas_call(functools.partial(grads_kernel, h, at), grid=(1,), in_spec...  16 us
    ppermute x3, waiting for transfers between devices, rotate(): lax.ppermute(block, axis, [(i, (i + distance) % n) for i in range(n)])  11.7 us
    ppermute x15, waiting for transfers between devices, swap(): return lax.ppermute(block, 'ctx', [(i, i ^ bit) for i in range(n)])  8.97 us
    pallas_call x1, Pallas kernels, gathered(): pl.pallas_call(functools.partial(gathered_kernel, n, heads, parts, at), g...  8.73 us
    pallas_call x4, Pallas kernels, attention(): pl.pallas_call(attn_kernel, grid=(1,), in_specs=[SMEM, col, col, col, of_...  8.25 us
  transfers between devices with their start and end apart: 35, of which 17 were waited for; matrix products, arithmetic and copies ran while one was open for 0% of the time, Pallas kernels for 25%

profile of v6, /device:TPU:0, one launch (start us, length us, event | category | flops | bytes accessed | tf_op | source)
XLA Modules:
  0.0 188.3 jit_solution(3008518472033773923)
XLA Ops:
  1.5 8.7 %shard_map.77 = (bf16[3088,128]{1,0:T(8,128)(2,1)}, bf16[3088,128]{1,0:T(8,128)(2,1)}, bf16[512,1024]{1,0:T(8,128)(2,1)}, bf16[128,1024]{1,0:T(8,128)(2,1)}, bf1...) custom-call(s32[31]{0:T(128)} %stack.137.ids_ref, s32[2,1024]{1,0:T(2,128)} %bitcast.38, bf16[1024,1024]{1,0:T(8,128)(2,1)} %k_ref.11, ...), custom_call_target="tpu_custom_call" | custom-call | flops 960000000 | tf_op jit(solution)/shard_map/pallas_call | solution.py:151
  10.2 2.6 %collective-permute-start = (bf16[512,1024]{1,0:T(8,128)(2,1)}, bf16[512,1024]{1,0:T(8,128)(2,1)S(1)}, u32[]{:S(2)}, u32[]{:S(2)}) collective-permute-start(bf16[512,1024]{1,0:T(8,128)(2,1)} %get-tuple-element.40), channel_id=1, source_target_pairs={{0,4},{4,8},{8,12},{12,16},{16,20},{20,24},{24,28},{1,5},{5,9},{9,... | collective-permute-start | bytes 3145736 | tf_op jit(solution)/shard_map/ppermute | solution.py:42
  12.9 2.6 %collective-permute-start.1 = (bf16[3088,128]{1,0:T(8,128)(2,1)}, bf16[3088,128]{1,0:T(8,128)(2,1)S(1)}, u32[]{:S(2)}, u32[]{:S(2)}) collective-permute-start(bf16[3088,128]{1,0:T(8,128)(2,1)} %get-tuple-element.42), channel_id=1, source_target_pairs={{0,4},{4,0},{8,12},{12,8},{16,20},{20,16},{24,28},{28,24},{1,5},{5... | collective-permute-start | bytes 2371592 | tf_op jit(solution)/shard_map/ppermute | solution.py:52
  15.5 7.2 %shard_map.79 = (bf16[3088,128]{1,0:T(8,128)(2,1)}, bf16[3088,128]{1,0:T(8,128)(2,1)}) custom-call(s32[31]{0:T(128)} %stack.137.ids_ref, s32[2,1024]{1,0:T(2,128)} %bitcast.39, bf16[1024,1024]{1,0:T(8,128)(2,1)} %k_ref.11, bf16[1024,1024]{1,0:T(8,128)(2,1)} %v_ref.11, bf16[2,3,512,512]{3,2,1,0:T(8,128)(2,1)} %base_ref.1, ...), custom_call_target="tpu_custom_call" | custom-call | flops 960000000 | tf_op jit(solution)/shard_map/pallas_call | solution.py:151
  22.8 0.9 shard_map.78
  23.7 1.6 collective-permute-start.2
  25.3 1.1 copy-done.8
  26.4 0.9 shard_map.80
  27.3 6.8 %collective-permute-start.4 = (bf16[1552,128]{1,0:T(8,128)(2,1)S(1)}, bf16[1552,128]{1,0:T(8,128)(2,1)S(1)}, u32[]{:S(2)}, u32[]{:S(2)}) collective-permute-start(bf16[1552,128]{1,0:T(8,128)(2,1)S(1)} %get-tuple-element.47.rest_1_), channel_id=1, source_target_pairs={{0,16},{4,20},{8,24},{12,28},{16,0},{20,4},{24,8},{28,12},{1,17},{... | collective-permute-start | bytes 1191944 | tf_op jit(solution)/shard_map/ppermute | solution.py:52
  34.1 2.6 %collective-permute-start.5 = (bf16[128,1024]{1,0:T(8,128)(2,1)S(1)}, bf16[128,1024]{1,0:T(8,128)(2,1)S(1)}, u32[]{:S(2)}, u32[]{:S(2)}) collective-permute-start(bf16[128,1024]{1,0:T(8,128)(2,1)S(1)} %copy-done.13), channel_id=1, source_target_pairs={{0,2},{1,3},{2,0},{3,1},{4,6},{5,7},{6,4},{7,5},{8,10},{9,11},{10,... | collective-permute-start | bytes 786440 | tf_op jit(solution)/shard_map/ppermute | solution.py:47
  36.7 2.1 %shard_map.81.rest_0_.refs_0_ = bf16[1024,256]{1,0:T(8,128)(2,1)S(1)} custom-call(s32[31]{0:T(128)S(1)} %copy-done.9, bf16[1024,1024]{1,0:T(8,128)(2,1)S(1)} %copy-done.2, bf16[1024,1024]{1,0:T(8,128)(2,1)S(1)} %copy-done, bf16[1024,1024]{1,0:T(8,128)(2,1)S(1)} %copy-done.1, bf16[512,1024]{1,0:T(8,128)(2,1)S(1)} %collective-permute-done.refs_1_.rim_ref, ...), custom_call_target="tpu_custom_call" | custom-call | flops 252000000 | tf_op jit(solution)/shard_map/pallas_call | solution.py:315
  39.4 2.1 %shard_map.83.rest_0_.refs_1_ = bf16[1024,256]{1,0:T(8,128)(2,1)S(1)} custom-call(s32[31]{0:T(128)S(1)} %copy-done.9, bf16[1024,1024]{1,0:T(8,128)(2,1)S(1)} %copy-done.2, bf16[1024,1024]{1,0:T(8,128)(2,1)S(1)} %copy-done, bf16[1024,1024]{1,0:T(8,128)(2,1)S(1)} %copy-done.1, bf16[512,1024]{1,0:T(8,128)(2,1)S(1)} %collective-permute-done.refs_1_.rim_ref, ...), custom_call_target="tpu_custom_call" | custom-call | flops 252000000 | tf_op jit(solution)/shard_map/pallas_call | solution.py:315
  41.5 2.1 %shard_map.84.rest_0_.refs_0_ = bf16[1024,256]{1,0:T(8,128)(2,1)S(1)} custom-call(s32[31]{0:T(128)S(1)} %copy-done.9, bf16[1024,1024]{1,0:T(8,128)(2,1)S(1)} %copy-done.2, bf16[1024,1024]{1,0:T(8,128)(2,1)S(1)} %copy-done, bf16[1024,1024]{1,0:T(8,128)(2,1)S(1)} %copy-done.1, bf16[512,1024]{1,0:T(8,128)(2,1)S(1)} %collective-permute-done.refs_1_.rim_ref, ...), custom_call_target="tpu_custom_call" | custom-call | flops 252000000 | tf_op jit(solution)/shard_map/pallas_call | solution.py:315
  43.6 3.5 %collective-permute-done.5.rest_2_ = bf16[128,1024]{1,0:T(8,128)(2,1)S(1)} collective-permute-done((bf16[128,1024]{1,0:T(8,128)(2,1)S(1)}, bf16[128,1024]{1,0:T(8,128)(2,1)S(1)}, u32[]{:S(2)}, u32[]{:S(2)}) %collective-permute-start.5) | collective-permute-done | bytes 262176 | tf_op jit(solution)/shard_map/ppermute | solution.py:47
  48.5 3.2 %collective-permute-start.9 = (bf16[128,1024]{1,0:T(8,128)(2,1)S(1)}, bf16[128,1024]{1,0:T(8,128)(2,1)S(1)}, u32[]{:S(2)}, u32[]{:S(2)}) collective-permute-start(bf16[128,1024]{1,0:T(8,128)(2,1)S(1)} %copy-done.11), channel_id=1, source_target_pairs={{0,3},{1,0},{2,1},{3,2},{4,7},{5,4},{6,5},{7,6},{8,11},{9,8},{10,9... | collective-permute-start | bytes 786440 | tf_op jit(solution)/shard_map/ppermute | solution.py:47
  51.6 2.1 %shard_map.86.refs_4_.refs_1_ = bf16[1024,256]{1,0:T(8,128)(2,1)S(1)} custom-call(s32[31]{0:T(128)S(1)} %copy-done.9, bf16[1024,1024]{1,0:T(8,128)(2,1)S(1)} %copy-done.2, bf16[1024,1024]{1,0:T(8,128)(2,1)S(1)} %copy-done, bf16[1024,1024]{1,0:T(8,128)(2,1)S(1)} %copy-done.1, bf16[512,1024]{1,0:T(8,128)(2,1)S(1)} %collective-permute-done.refs_1_.rim_ref, ...), custom_call_target="tpu_custom_call" | custom-call | flops 252000000 | tf_op jit(solution)/shard_map/pallas_call | solution.py:315
  53.7 5.1 %collective-permute-done.8.refs_5_ = bf16[128,1024]{1,0:T(8,128)(2,1)S(1)} collective-permute-done((bf16[128,1024]{1,0:T(8,128)(2,1)S(1)}, bf16[128,1024]{1,0:T(8,128)(2,1)S(1)}, u32[]{:S(2)}, u32[]{:S(2)}) %collective-permute-start.8) | collective-permute-done | bytes 262176 | tf_op jit(solution)/shard_map/ppermute | solution.py:47
  58.8 3.1 %collective-permute-done.9.refs_6_ = bf16[128,1024]{1,0:T(8,128)(2,1)S(1)} collective-permute-done((bf16[128,1024]{1,0:T(8,128)(2,1)S(1)}, bf16[128,1024]{1,0:T(8,128)(2,1)S(1)}, u32[]{:S(2)}, u32[]{:S(2)}) %collective-permute-start.9) | collective-permute-done | bytes 262176 | tf_op jit(solution)/shard_map/ppermute | solution.py:47
  62.0 2.1 %shard_map.87 = (bf16[3,512,128]{2,1,0:T(8,128)(2,1)S(1)}, bf16[3,512,128]{2,1,0:T(8,128)(2,1)S(1)}) custom-call(s32[31]{0:T(128)S(1)} %copy-done.9, bf16[2,3,512,512]{3,2,1,0:T(8,128)(2,1)S(1)} %copy-done.3, bf16[1552,128]{1,0:T(8,128)(2,1)S(1)} %shard_map.82.rest_0_.rest_1_.refs_0_, bf16[1552,128]{1,0:T(8,128)(2,1)S(1)} %collective-permute-done.6.refs_1_, ...), custom_call_target="tpu_custom_call" | custom-call | flops 252000000 | tf_op jit(solution)/shard_map/pallas_call | solution.py:264
  64.1 1.7 collective-permute-start.13
  66.2 7.7 %collective-permute-done.13.refs_3_ = bf16[3,512,128]{2,1,0:T(8,128)(2,1)S(1)} collective-permute-done((bf16[3,512,128]{2,1,0:T(8,128)(2,1)S(1)}, bf16[3,512,128]{2,1,0:T(8,128)(2,1)S(1)}, u32[]{:S(2)}, u32[]{:S(2)}) %collective-permute-start.13) | collective-permute-done | bytes 393248 | tf_op jit(solution)/shard_map/ppermute | solution.py:52
  74.4 0.7 collective-permute-done.10.refs_3_
  75.6 3.2 %shard_map.88 = (bf16[512,512]{1,0:T(8,128)(2,1)S(1)}, bf16[512,512]{1,0:T(8,128)(2,1)S(1)}, bf16[2,3,512,512]{3,2,1,0:T(8,128)(2,1)}) custom-call(s32[31]{0:T(128)S(1)} %copy-done.9, bf16[1024,1024]{1,0:T(8,128)(2,1)S(1)} %copy-done.2, bf16[1024,256]{1,0:T(8,128)(2,1)S(1)} %shard_map.81.rest_0_.refs_0_, bf16[1024,256]{1,0:T(8,128)(2,1)S(1)} %shard_map.83.rest_0_.refs_1_, ...), custom_call_target="tpu_custom_call" | custom-call | flops 396000000 | tf_op jit(solution)/shard_map/pallas_call | solution.py:375
  78.8 5.1 %collective-permute-start.18 = (bf16[512,512]{1,0:T(8,128)(2,1)S(1)}, bf16[512,512]{1,0:T(8,128)(2,1)S(1)}, u32[]{:S(2)}, u32[]{:S(2)}) collective-permute-start(bf16[512,512]{1,0:T(8,128)(2,1)S(1)} %get-tuple-element.58.refs_0_), channel_id=1, source_target_pairs={{0,1},{1,2},{2,3},{4,5},{5,6},{6,7},{8,9},{9,10},{10,11},{12,13},{... | collective-permute-start | bytes 1572872 | tf_op jit(solution)/shard_map/ppermute | solution.py:42
  84.0 1.3 collective-permute-start.19
  85.3 3.2 %shard_map.89 = (bf16[512,512]{1,0:T(8,128)(2,1)S(1)}, bf16[512,512]{1,0:T(8,128)(2,1)S(1)}, bf16[2,3,512,512]{3,2,1,0:T(8,128)(2,1)}) custom-call(s32[31]{0:T(128)S(1)} %copy-done.9, bf16[1024,1024]{1,0:T(8,128)(2,1)S(1)} %copy-done.2, bf16[1024,256]{1,0:T(8,128)(2,1)S(1)} %shard_map.84.rest_0_.refs_0_, ...), custom_call_target="tpu_custom_call", output_to_operand_aliasing={{2}: (8, {})} | custom-call | flops 396000000 | tf_op jit(solution)/shard_map/pallas_call | solution.py:375
  88.5 4.6 %collective-permute-start.16 = (bf16[512,512]{1,0:T(8,128)(2,1)S(1)}, bf16[512,512]{1,0:T(8,128)(2,1)S(1)}, u32[]{:S(2)}, u32[]{:S(2)}) collective-permute-start(bf16[512,512]{1,0:T(8,128)(2,1)S(1)} %get-tuple-element.55.refs_3_.refs_1_), channel_id=1, source_target_pairs={{0,1},{1,2},{2,3},{4,5},{5,6},{6,7},{8,9},{9,10},{10,11},{12,13},{... | collective-permute-start | bytes 1572872 | tf_op jit(solution)/shard_map/ppermute | solution.py:42
  93.1 1.3 collective-permute-start.17
  94.5 1.5 collective-permute-start.32
  96.0 5.7 %shard_map.91.p_hbm = bf16[4,512,1024]{2,1,0:T(8,128)(2,1)S(1)} custom-call(bf16[512,512]{1,0:T(8,128)(2,1)S(1)} %get-tuple-element.56.refs_0_, bf16[512,512]{1,0:T(8,128)(2,1)S(1)} %get-tuple-element.57.refs_1_, bf16[1024,4096]{1,0:T(8,128)(2,1)S(1)} %bitcast.31, bf16[3,128,1024]{2,1,0:T(8,128)(2,1)S(1)} %shard_map.90.refs_3_), custom_call_target="tpu_custom_call" | custom-call | flops 120000000 | tf_op jit(solution)/shard_map/pallas_call | solution.py:415
  101.8 1.0 shard_map.92
  102.8 4.7 %collective-permute-start.22 = (bf16[512,512]{1,0:T(8,128)(2,1)S(1)}, bf16[512,512]{1,0:T(8,128)(2,1)S(1)}, u32[]{:S(2)}, u32[]{:S(2)}) collective-permute-start(bf16[512,512]{1,0:T(8,128)(2,1)S(1)} %get-tuple-element.63), channel_id=1, source_target_pairs={{0,1},{1,2},{2,3},{4,5},{5,6},{6,7},{8,9},{9,10},{10,11},{12,13},{... | collective-permute-start | bytes 1572872 | tf_op jit(solution)/shard_map/ppermute | solution.py:42
  107.5 1.3 collective-permute-start.23
  108.8 2.4 %collective-permute-done.17.left_hbm = bf16[512,512]{1,0:T(8,128)(2,1)S(1)} collective-permute-done((bf16[512,512]{1,0:T(8,128)(2,1)S(1)}, bf16[512,512]{1,0:T(8,128)(2,1)S(1)}, u32[]{:S(2)}, u32[]{:S(2)}) %collective-permute-start.17) | collective-permute-done | bytes 524320 | tf_op jit(solution)/shard_map/ppermute | solution.py:42
  111.2 1.0 shard_map.93
  112.2 2.3 %collective-permute-start.20 = (bf16[512,512]{1,0:T(8,128)(2,1)S(1)}, bf16[512,512]{1,0:T(8,128)(2,1)S(1)}, u32[]{:S(2)}, u32[]{:S(2)}) collective-permute-start(bf16[512,512]{1,0:T(8,128)(2,1)S(1)} %get-tuple-element.61), channel_id=1, source_target_pairs={{0,1},{1,2},{2,3},{4,5},{5,6},{6,7},{8,9},{9,10},{10,11},{12,13},{... | collective-permute-start | bytes 1572872 | tf_op jit(solution)/shard_map/ppermute | solution.py:42
  114.5 1.3 collective-permute-start.21
  115.9 2.1 %collective-permute-start.33 = (bf16[2,3,128,1024]{3,2,1,0:T(8,128)(2,1)S(1)}, bf16[2,3,128,1024]{3,2,1,0:T(8,128)(2,1)S(1)}, u32[]{:S(2)}, u32[]{:S(2)}) collective-permute-start(bf16[2,3,128,1024]{3,2,1,0:T(8,128)(2,1)S(1)} %shard_map.98.refs_0_), channel_id=1, source_target_pairs={{0,8},{4,12},{8,0},{12,4},{16,24},{20,28},{24,16},{28,20},{1,9},{5... | collective-permute-start | bytes 4718600 | tf_op jit(solution)/shard_map/ppermute | solution.py:52
  118.1 1.8 collective-permute-done.22.right_hbm
  119.8 4.4 %collective-permute-done.23.left_hbm = bf16[512,512]{1,0:T(8,128)(2,1)S(1)} collective-permute-done((bf16[512,512]{1,0:T(8,128)(2,1)S(1)}, bf16[512,512]{1,0:T(8,128)(2,1)S(1)}, u32[]{:S(2)}, u32[]{:S(2)}) %collective-permute-start.23) | collective-permute-done | bytes 524320 | tf_op jit(solution)/shard_map/ppermute | solution.py:42
  124.2 1.0 shard_map.94
  125.2 1.9 %collective-permute-start.26 = (bf16[512,512]{1,0:T(8,128)(2,1)S(1)}, bf16[512,512]{1,0:T(8,128)(2,1)S(1)}, u32[]{:S(2)}, u32[]{:S(2)}) collective-permute-start(bf16[512,512]{1,0:T(8,128)(2,1)S(1)} %get-tuple-element.69), channel_id=1, source_target_pairs={{0,1},{1,2},{2,3},{4,5},{5,6},{6,7},{8,9},{9,10},{10,11},{12,13},{... | collective-permute-start | bytes 1572872 | tf_op jit(solution)/shard_map/ppermute | solution.py:42
  127.2 1.3 collective-permute-start.27
  128.5 2.6 %collective-permute-done.20.right_hbm = bf16[512,512]{1,0:T(8,128)(2,1)S(1)} collective-permute-done((bf16[512,512]{1,0:T(8,128)(2,1)S(1)}, bf16[512,512]{1,0:T(8,128)(2,1)S(1)}, u32[]{:S(2)}, u32[]{:S(2)}) %collective-permute-start.20) | collective-permute-done | bytes 524320 | tf_op jit(solution)/shard_map/ppermute | solution.py:42
  131.0 4.4 %collective-permute-done.21.left_hbm = bf16[512,512]{1,0:T(8,128)(2,1)S(1)} collective-permute-done((bf16[512,512]{1,0:T(8,128)(2,1)S(1)}, bf16[512,512]{1,0:T(8,128)(2,1)S(1)}, u32[]{:S(2)}, u32[]{:S(2)}) %collective-permute-start.21) | collective-permute-done | bytes 524320 | tf_op jit(solution)/shard_map/ppermute | solution.py:42
  135.5 1.0 shard_map.95
  136.5 1.9 %collective-permute-start.24 = (bf16[512,512]{1,0:T(8,128)(2,1)S(1)}, bf16[512,512]{1,0:T(8,128)(2,1)S(1)}, u32[]{:S(2)}, u32[]{:S(2)}) collective-permute-start(bf16[512,512]{1,0:T(8,128)(2,1)S(1)} %get-tuple-element.67), channel_id=1, source_target_pairs={{0,1},{1,2},{2,3},{4,5},{5,6},{6,7},{8,9},{9,10},{10,11},{12,13},{... | collective-permute-start | bytes 1572872 | tf_op jit(solution)/shard_map/ppermute | solution.py:42
  138.4 1.3 collective-permute-start.25
  139.7 2.6 %collective-permute-done.26.right_hbm = bf16[512,512]{1,0:T(8,128)(2,1)S(1)} collective-permute-done((bf16[512,512]{1,0:T(8,128)(2,1)S(1)}, bf16[512,512]{1,0:T(8,128)(2,1)S(1)}, u32[]{:S(2)}, u32[]{:S(2)}) %collective-permute-start.26) | collective-permute-done | bytes 524320 | tf_op jit(solution)/shard_map/ppermute | solution.py:42
  142.3 4.4 %collective-permute-done.27.left_hbm = bf16[512,512]{1,0:T(8,128)(2,1)S(1)} collective-permute-done((bf16[512,512]{1,0:T(8,128)(2,1)S(1)}, bf16[512,512]{1,0:T(8,128)(2,1)S(1)}, u32[]{:S(2)}, u32[]{:S(2)}) %collective-permute-start.27) | collective-permute-done | bytes 524320 | tf_op jit(solution)/shard_map/ppermute | solution.py:42
  146.7 1.2 shard_map.96
  148.0 3.7 %collective-permute-done.24.right_hbm = bf16[512,512]{1,0:T(8,128)(2,1)S(1)} collective-permute-done((bf16[512,512]{1,0:T(8,128)(2,1)S(1)}, bf16[512,512]{1,0:T(8,128)(2,1)S(1)}, u32[]{:S(2)}, u32[]{:S(2)}) %collective-permute-start.24) | collective-permute-done | bytes 524320 | tf_op jit(solution)/shard_map/ppermute | solution.py:42
  151.6 4.1 %collective-permute-done.25.left_hbm = bf16[512,512]{1,0:T(8,128)(2,1)S(1)} collective-permute-done((bf16[512,512]{1,0:T(8,128)(2,1)S(1)}, bf16[512,512]{1,0:T(8,128)(2,1)S(1)}, u32[]{:S(2)}, u32[]{:S(2)}) %collective-permute-start.25) | collective-permute-done | bytes 524320 | tf_op jit(solution)/shard_map/ppermute | solution.py:42
  155.8 1.0 shard_map.97
  157.1 2.1 %collective-permute-start.30 = (bf16[512,512]{1,0:T(8,128)(2,1)S(1)}, bf16[512,512]{1,0:T(8,128)(2,1)S(1)}, u32[]{:S(2)}, u32[]{:S(2)}) collective-permute-start(bf16[512,512]{1,0:T(8,128)(2,1)S(1)} %get-tuple-element.75), channel_id=1, source_target_pairs={{0,1},{1,2},{2,3},{4,5},{5,6},{6,7},{8,9},{9,10},{10,11},{12,13},{... | collective-permute-start | bytes 1572872 | tf_op jit(solution)/shard_map/ppermute | solution.py:42
  159.2 1.3 collective-permute-start.31
  160.5 4.6 %collective-permute-start.28 = (bf16[512,512]{1,0:T(8,128)(2,1)S(1)}, bf16[512,512]{1,0:T(8,128)(2,1)S(1)}, u32[]{:S(2)}, u32[]{:S(2)}) collective-permute-start(bf16[512,512]{1,0:T(8,128)(2,1)S(1)} %get-tuple-element.73), channel_id=1, source_target_pairs={{0,1},{1,2},{2,3},{4,5},{5,6},{6,7},{8,9},{9,10},{10,11},{12,13},{... | collective-permute-start | bytes 1572872 | tf_op jit(solution)/shard_map/ppermute | solution.py:42
  165.1 1.3 collective-permute-start.29
  166.5 1.7 copy-done.10
  168.2 8.7 %shard_map.100.out_in = bf16[1024,1024]{1,0:T(8,128)(2,1)} custom-call(s32[31]{0:T(128)S(1)} %copy-done.9, bf16[512,512]{1,0:T(8,128)(2,1)S(1)} %get-tuple-element.58.refs_0_, bf16[512,512]{1,0:T(8,128)(2,1)S(1)} %get-tuple-element.55.refs_3_.refs_1_, bf16[3,512,1024]{2,1,0:T(8,128)(2,1)S(1)} %get-tuple-element.76.refs_2_, bf16[1024,4096]{1,0:T(8,128)(2,1)} %refs_3_.1, ...), custom_call_target="tpu_custom_call" | custom-call | flops 1080000000 | tf_op jit(solution)/shard_map/pallas_call | solution.py:529
  177.0 1.7 shard_map.101.out_in
  178.7 3.6 %collective-permute-done.28.right_hbm = bf16[512,512]{1,0:T(8,128)(2,1)S(1)} collective-permute-done((bf16[512,512]{1,0:T(8,128)(2,1)S(1)}, bf16[512,512]{1,0:T(8,128)(2,1)S(1)}, u32[]{:S(2)}, u32[]{:S(2)}) %collective-permute-start.28) | collective-permute-done | bytes 524320 | tf_op jit(solution)/shard_map/ppermute | solution.py:42
  182.3 4.1 %collective-permute-done.29.left_hbm = bf16[512,512]{1,0:T(8,128)(2,1)S(1)} collective-permute-done((bf16[512,512]{1,0:T(8,128)(2,1)S(1)}, bf16[512,512]{1,0:T(8,128)(2,1)S(1)}, u32[]{:S(2)}, u32[]{:S(2)}) %collective-permute-start.29) | collective-permute-done | bytes 524320 | tf_op jit(solution)/shard_map/ppermute | solution.py:42
  186.4 1.7 shard_map.102
  (66 shorter events, 4.8 us)
Async XLA Ops:
  10.2 15.0 %collective-permute-start = (bf16[512,1024]{1,0:T(8,128)(2,1)}, bf16[512,1024]{1,0:T(8,128)(2,1)S(1)}, u32[]{:S(2)}, u32[]{:S(2)}) collective-permute-start(bf16[512,1024]{1,0:T(8,128)(2,1)} %get-tuple-element.40), channel_id=1, source_target_pairs={{0,4},{4,8},{8,12},{12,16},{16,20},{20,24},{24,28},{1,5},{5,9},{9,... | collective-permute-start | bytes 3145736 | tf_op jit(solution)/shard_map/ppermute | solution.py:42
  12.9 10.0 %collective-permute-start.1 = (bf16[3088,128]{1,0:T(8,128)(2,1)}, bf16[3088,128]{1,0:T(8,128)(2,1)S(1)}, u32[]{:S(2)}, u32[]{:S(2)}) collective-permute-start(bf16[3088,128]{1,0:T(8,128)(2,1)} %get-tuple-element.42), channel_id=1, source_target_pairs={{0,4},{4,0},{8,12},{12,8},{16,20},{20,16},{24,28},{28,24},{1,5},{5... | collective-permute-start | bytes 2371592 | tf_op jit(solution)/shard_map/ppermute | solution.py:52
  15.5 7.4 %copy-start.7 = (bf16[3088,128]{1,0:T(8,128)(2,1)S(1)}, bf16[3088,128]{1,0:T(8,128)(2,1)}, u32[]{:S(2)}) copy-start(bf16[3088,128]{1,0:T(8,128)(2,1)} %get-tuple-element.41.keep_hbm.refs_0_) | copy-start | bytes 2371588
  15.5 7.4 %copy-start.9 = (s32[31]{0:T(128)S(1)}, s32[31]{0:T(128)}, u32[]{:S(2)}) copy-start(s32[31]{0:T(128)} %stack.137.ids_ref) | copy-start | bytes 376
  15.5 18.6 %copy-start.13 = (bf16[128,1024]{1,0:T(8,128)(2,1)S(1)}, bf16[128,1024]{1,0:T(8,128)(2,1)}, u32[]{:S(2)}) copy-start(bf16[128,1024]{1,0:T(8,128)(2,1)} %get-tuple-element.49) | copy-start | bytes 786436
  15.5 21.2 %copy-start.2 = (bf16[1024,1024]{1,0:T(8,128)(2,1)S(1)}, bf16[1024,1024]{1,0:T(8,128)(2,1)}, u32[]{:S(2)}) copy-start(bf16[1024,1024]{1,0:T(8,128)(2,1)} %q_hbm.3) | copy-start | bytes 6291460
  22.7 14.0 %copy-start = (bf16[1024,1024]{1,0:T(8,128)(2,1)S(1)}, bf16[1024,1024]{1,0:T(8,128)(2,1)}, u32[]{:S(2)}) copy-start(bf16[1024,1024]{1,0:T(8,128)(2,1)} %k_ref.11) | copy-start | bytes 6291460
  22.7 14.0 %copy-start.1 = (bf16[1024,1024]{1,0:T(8,128)(2,1)S(1)}, bf16[1024,1024]{1,0:T(8,128)(2,1)}, u32[]{:S(2)}) copy-start(bf16[1024,1024]{1,0:T(8,128)(2,1)} %v_ref.11) | copy-start | bytes 6291460
  22.7 2.6 %collective-permute-start.3 = (bf16[3088,128]{1,0:T(8,128)(2,1)}, bf16[3088,128]{1,0:T(8,128)(2,1)S(1)}, u32[]{:S(2)}, u32[]{:S(2)}) collective-permute-start(bf16[3088,128]{1,0:T(8,128)(2,1)} %get-tuple-element.46), channel_id=1, source_target_pairs={{0,4},{4,0},{8,12},{12,8},{16,20},{20,16},{24,28},{28,24},{1,5},{5... | collective-permute-start | bytes 2371592 | tf_op jit(solution)/shard_map/ppermute | solution.py:52
  23.7 15.1 %collective-permute-start.2 = (bf16[1552,128]{1,0:T(8,128)(2,1)S(1)}, bf16[1552,128]{1,0:T(8,128)(2,1)S(1)}, u32[]{:S(2)}, u32[]{:S(2)}) collective-permute-start(bf16[1552,128]{1,0:T(8,128)(2,1)S(1)} %get-tuple-element.44.refs_0_.rest_0_), channel_id=1, source_target_pairs={{0,8},{4,12},{8,0},{12,4},{16,24},{20,28},{24,16},{28,20},{1,9},{5... | collective-permute-start | bytes 1191944 | tf_op jit(solution)/shard_map/ppermute | solution.py:52
  25.3 1.1 copy-start.8
  27.3 19.8 %collective-permute-start.4 = (bf16[1552,128]{1,0:T(8,128)(2,1)S(1)}, bf16[1552,128]{1,0:T(8,128)(2,1)S(1)}, u32[]{:S(2)}, u32[]{:S(2)}) collective-permute-start(bf16[1552,128]{1,0:T(8,128)(2,1)S(1)} %get-tuple-element.47.rest_1_), channel_id=1, source_target_pairs={{0,16},{4,20},{8,24},{12,28},{16,0},{20,4},{24,8},{28,12},{1,17},{... | collective-permute-start | bytes 1191944 | tf_op jit(solution)/shard_map/ppermute | solution.py:52
  34.1 13.0 %collective-permute-start.5 = (bf16[128,1024]{1,0:T(8,128)(2,1)S(1)}, bf16[128,1024]{1,0:T(8,128)(2,1)S(1)}, u32[]{:S(2)}, u32[]{:S(2)}) collective-permute-start(bf16[128,1024]{1,0:T(8,128)(2,1)S(1)} %copy-done.13), channel_id=1, source_target_pairs={{0,2},{1,3},{2,0},{3,1},{4,6},{5,7},{6,4},{7,5},{8,10},{9,11},{10,... | collective-permute-start | bytes 786440 | tf_op jit(solution)/shard_map/ppermute | solution.py:47
  39.3 22.7 %collective-permute-start.6 = (bf16[1552,128]{1,0:T(8,128)(2,1)S(1)}, bf16[1552,128]{1,0:T(8,128)(2,1)S(1)}, u32[]{:S(2)}, u32[]{:S(2)}) collective-permute-start(bf16[1552,128]{1,0:T(8,128)(2,1)S(1)} %shard_map.82.rest_0_.rest_1_.refs_0_), channel_id=1, source_target_pairs={{0,16},{4,20},{8,24},{12,28},{16,0},{20,4},{24,8},{28,12},{1,17},{... | collective-permute-start | bytes 1191944 | tf_op jit(solution)/shard_map/ppermute | solution.py:52
  41.5 6.3 %copy-start.12 = (bf16[128,1024]{1,0:T(8,128)(2,1)S(1)}, bf16[128,1024]{1,0:T(8,128)(2,1)}, u32[]{:S(2)}) copy-start(bf16[128,1024]{1,0:T(8,128)(2,1)} %get-tuple-element.50) | copy-start | bytes 786436
  41.5 7.0 %copy-start.11 = (bf16[128,1024]{1,0:T(8,128)(2,1)S(1)}, bf16[128,1024]{1,0:T(8,128)(2,1)}, u32[]{:S(2)}) copy-start(bf16[128,1024]{1,0:T(8,128)(2,1)} %get-tuple-element.51) | copy-start | bytes 786436
  47.5 14.4 %collective-permute-start.7 = (bf16[1552,128]{1,0:T(8,128)(2,1)S(1)}, bf16[1552,128]{1,0:T(8,128)(2,1)S(1)}, u32[]{:S(2)}, u32[]{:S(2)}) collective-permute-start(bf16[1552,128]{1,0:T(8,128)(2,1)S(1)} %shard_map.85.rest_0_.refs_2_), channel_id=1, source_target_pairs={{0,8},{4,12},{8,0},{12,4},{16,24},{20,28},{24,16},{28,20},{1,9},{5... | collective-permute-start | bytes 1191944 | tf_op jit(solution)/shard_map/ppermute | solution.py:52
  47.8 11.0 %collective-permute-start.8 = (bf16[128,1024]{1,0:T(8,128)(2,1)S(1)}, bf16[128,1024]{1,0:T(8,128)(2,1)S(1)}, u32[]{:S(2)}, u32[]{:S(2)}) collective-permute-start(bf16[128,1024]{1,0:T(8,128)(2,1)S(1)} %copy-done.12), channel_id=1, source_target_pairs={{0,1},{1,2},{2,3},{3,0},{4,5},{5,6},{6,7},{7,4},{8,9},{9,10},{10,1... | collective-permute-start | bytes 786440 | tf_op jit(solution)/shard_map/ppermute | solution.py:47
  48.5 13.5 %copy-start.3 = (bf16[2,3,512,512]{3,2,1,0:T(8,128)(2,1)S(1)}, bf16[2,3,512,512]{3,2,1,0:T(8,128)(2,1)}, u32[]{:S(2)}) copy-start(bf16[2,3,512,512]{3,2,1,0:T(8,128)(2,1)} %base_ref.1) | copy-start | bytes 9437188
  48.5 13.5 %collective-permute-start.9 = (bf16[128,1024]{1,0:T(8,128)(2,1)S(1)}, bf16[128,1024]{1,0:T(8,128)(2,1)S(1)}, u32[]{:S(2)}, u32[]{:S(2)}) collective-permute-start(bf16[128,1024]{1,0:T(8,128)(2,1)S(1)} %copy-done.11), channel_id=1, source_target_pairs={{0,3},{1,0},{2,1},{3,2},{4,7},{5,4},{6,5},{7,6},{8,11},{9,8},{10,9... | collective-permute-start | bytes 786440 | tf_op jit(solution)/shard_map/ppermute | solution.py:47
  61.9 34.1 %slice-start = ((s8[8388608]{0:T(1024)(128)(4,1)}), s8[4194304]{0:T(1024)(128)(4,1)S(1)}, s32[]{:S(2)}) async-start(s8[8388608]{0:T(1024)(128)(4,1)} %bitcast.30), calls=%async_computation | async-start | bytes 8388608
  64.1 9.8 %collective-permute-start.13 = (bf16[3,512,128]{2,1,0:T(8,128)(2,1)S(1)}, bf16[3,512,128]{2,1,0:T(8,128)(2,1)S(1)}, u32[]{:S(2)}, u32[]{:S(2)}) collective-permute-start(bf16[3,512,128]{2,1,0:T(8,128)(2,1)S(1)} %get-tuple-element.53.refs_2_), channel_id=1, source_target_pairs={{0,8},{4,12},{8,0},{12,4},{16,24},{20,28},{24,16},{28,20},{1,9},{5... | collective-permute-start | bytes 1179656 | tf_op jit(solution)/shard_map/ppermute | solution.py:52
  65.8 30.2 %slice-start.1 = ((s8[8388608]{0:T(1024)(128)(4,1)}), s8[4194304]{0:T(1024)(128)(4,1)S(1)}, s32[]{:S(2)}) async-start(s8[8388608]{0:T(1024)(128)(4,1)} %bitcast.30), calls=%async_computation.1 | async-start | bytes 8388608
  65.8 9.4 %collective-permute-start.10 = (bf16[3,512,128]{2,1,0:T(8,128)(2,1)S(1)}, bf16[3,512,128]{2,1,0:T(8,128)(2,1)S(1)}, u32[]{:S(2)}, u32[]{:S(2)}) collective-permute-start(bf16[3,512,128]{2,1,0:T(8,128)(2,1)S(1)} %get-tuple-element.52.refs_2_), channel_id=1, source_target_pairs={{0,16},{4,20},{8,24},{12,28},{16,0},{20,4},{24,8},{28,12},{1,17},{... | collective-permute-start | bytes 1179656 | tf_op jit(solution)/shard_map/ppermute | solution.py:52
  66.2 9.0 %collective-permute-start.14 = (bf16[3,512,128]{2,1,0:T(8,128)(2,1)S(1)}, bf16[3,512,128]{2,1,0:T(8,128)(2,1)S(1)}, u32[]{:S(2)}, u32[]{:S(2)}) collective-permute-start(bf16[3,512,128]{2,1,0:T(8,128)(2,1)S(1)} %get-tuple-element.53.refs_2_), channel_id=1, source_target_pairs={{0,4},{4,0},{8,12},{12,8},{16,20},{20,16},{24,28},{28,24},{1,5},{5... | collective-permute-start | bytes 1179656 | tf_op jit(solution)/shard_map/ppermute | solution.py:52
  73.9 1.7 collective-permute-start.15
  73.9 11.4 %collective-permute-start.11 = (bf16[3,512,128]{2,1,0:T(8,128)(2,1)S(1)}, bf16[3,512,128]{2,1,0:T(8,128)(2,1)S(1)}, u32[]{:S(2)}, u32[]{:S(2)}) collective-permute-start(bf16[3,512,128]{2,1,0:T(8,128)(2,1)S(1)} %get-tuple-element.52.refs_2_), channel_id=1, source_target_pairs={{0,4},{4,0},{8,12},{12,8},{16,20},{20,16},{24,28},{28,24},{1,5},{5... | collective-permute-start | bytes 1179656 | tf_op jit(solution)/shard_map/ppermute | solution.py:52
  75.1 10.1 %collective-permute-start.12 = (bf16[3,512,128]{2,1,0:T(8,128)(2,1)S(1)}, bf16[3,512,128]{2,1,0:T(8,128)(2,1)S(1)}, u32[]{:S(2)}, u32[]{:S(2)}) collective-permute-start(bf16[3,512,128]{2,1,0:T(8,128)(2,1)S(1)} %collective-permute-done.10.refs_3_), channel_id=1, source_target_pairs={{0,4},{4,0},{8,12},{12,8},{16,20},{20,16},{24,28},{28,24},{1,5},{5... | collective-permute-start | bytes 1179656 | tf_op jit(solution)/shard_map/ppermute | solution.py:52
  78.8 22.9 %collective-permute-start.18 = (bf16[512,512]{1,0:T(8,128)(2,1)S(1)}, bf16[512,512]{1,0:T(8,128)(2,1)S(1)}, u32[]{:S(2)}, u32[]{:S(2)}) collective-permute-start(bf16[512,512]{1,0:T(8,128)(2,1)S(1)} %get-tuple-element.58.refs_0_), channel_id=1, source_target_pairs={{0,1},{1,2},{2,3},{4,5},{5,6},{6,7},{8,9},{9,10},{10,11},{12,13},{... | collective-permute-start | bytes 1572872 | tf_op jit(solution)/shard_map/ppermute | solution.py:42
  84.0 17.8 %collective-permute-start.19 = (bf16[512,512]{1,0:T(8,128)(2,1)S(1)}, bf16[512,512]{1,0:T(8,128)(2,1)S(1)}, u32[]{:S(2)}, u32[]{:S(2)}) collective-permute-start(bf16[512,512]{1,0:T(8,128)(2,1)S(1)} %get-tuple-element.58.refs_0_), channel_id=1, source_target_pairs={{1,0},{2,1},{3,2},{5,4},{6,5},{7,6},{9,8},{10,9},{11,10},{13,12},{... | collective-permute-start | bytes 1572872 | tf_op jit(solution)/shard_map/ppermute | solution.py:42
  88.5 20.2 %collective-permute-start.16 = (bf16[512,512]{1,0:T(8,128)(2,1)S(1)}, bf16[512,512]{1,0:T(8,128)(2,1)S(1)}, u32[]{:S(2)}, u32[]{:S(2)}) collective-permute-start(bf16[512,512]{1,0:T(8,128)(2,1)S(1)} %get-tuple-element.55.refs_3_.refs_1_), channel_id=1, source_target_pairs={{0,1},{1,2},{2,3},{4,5},{5,6},{6,7},{8,9},{9,10},{10,11},{12,13},{... | collective-permute-start | bytes 1572872 | tf_op jit(solution)/shard_map/ppermute | solution.py:42
  93.1 18.1 %collective-permute-start.17 = (bf16[512,512]{1,0:T(8,128)(2,1)S(1)}, bf16[512,512]{1,0:T(8,128)(2,1)S(1)}, u32[]{:S(2)}, u32[]{:S(2)}) collective-permute-start(bf16[512,512]{1,0:T(8,128)(2,1)S(1)} %get-tuple-element.55.refs_3_.refs_1_), channel_id=1, source_target_pairs={{1,0},{2,1},{3,2},{5,4},{6,5},{7,6},{9,8},{10,9},{11,10},{13,12},{... | collective-permute-start | bytes 1572872 | tf_op jit(solution)/shard_map/ppermute | solution.py:42
  94.5 21.3 %collective-permute-start.32 = (bf16[1,3,128,1024]{3,2,1,0:T(8,128)(2,1)S(1)}, bf16[1,3,128,1024]{3,2,1,0:T(8,128)(2,1)S(1)}, u32[]{:S(2)}, u32[]{:S(2)}) collective-permute-start(bf16[1,3,128,1024]{3,2,1,0:T(8,128)(2,1)S(1)} %bitcast.32), channel_id=1, source_target_pairs={{0,16},{4,20},{8,24},{12,28},{16,0},{20,4},{24,8},{28,12},{1,17},{... | collective-permute-start | bytes 2359304 | tf_op jit(solution)/shard_map/ppermute | solution.py:52
  101.8 54.0 %copy-start.5 = (bf16[4,512,1024]{2,1,0:T(8,128)(2,1)}, bf16[4,512,1024]{2,1,0:T(8,128)(2,1)S(1)}, u32[]{:S(2)}) copy-start(bf16[4,512,1024]{2,1,0:T(8,128)(2,1)S(1)} %shard_map.91.p_hbm) | copy-start | bytes 12582916
  102.8 17.0 %collective-permute-start.22 = (bf16[512,512]{1,0:T(8,128)(2,1)S(1)}, bf16[512,512]{1,0:T(8,128)(2,1)S(1)}, u32[]{:S(2)}, u32[]{:S(2)}) collective-permute-start(bf16[512,512]{1,0:T(8,128)(2,1)S(1)} %get-tuple-element.63), channel_id=1, source_target_pairs={{0,1},{1,2},{2,3},{4,5},{5,6},{6,7},{8,9},{9,10},{10,11},{12,13},{... | collective-permute-start | bytes 1572872 | tf_op jit(solution)/shard_map/ppermute | solution.py:42
  107.5 16.8 %collective-permute-start.23 = (bf16[512,512]{1,0:T(8,128)(2,1)S(1)}, bf16[512,512]{1,0:T(8,128)(2,1)S(1)}, u32[]{:S(2)}, u32[]{:S(2)}) collective-permute-start(bf16[512,512]{1,0:T(8,128)(2,1)S(1)} %get-tuple-element.60.refs_1_), channel_id=1, source_target_pairs={{1,0},{2,1},{3,2},{5,4},{6,5},{7,6},{9,8},{10,9},{11,10},{13,12},{... | collective-permute-start | bytes 1572872 | tf_op jit(solution)/shard_map/ppermute | solution.py:42
  112.2 18.8 %collective-permute-start.20 = (bf16[512,512]{1,0:T(8,128)(2,1)S(1)}, bf16[512,512]{1,0:T(8,128)(2,1)S(1)}, u32[]{:S(2)}, u32[]{:S(2)}) collective-permute-start(bf16[512,512]{1,0:T(8,128)(2,1)S(1)} %get-tuple-element.61), channel_id=1, source_target_pairs={{0,1},{1,2},{2,3},{4,5},{5,6},{6,7},{8,9},{9,10},{10,11},{12,13},{... | collective-permute-start | bytes 1572872 | tf_op jit(solution)/shard_map/ppermute | solution.py:42
  114.5 21.0 %collective-permute-start.21 = (bf16[512,512]{1,0:T(8,128)(2,1)S(1)}, bf16[512,512]{1,0:T(8,128)(2,1)S(1)}, u32[]{:S(2)}, u32[]{:S(2)}) collective-permute-start(bf16[512,512]{1,0:T(8,128)(2,1)S(1)} %get-tuple-element.62.refs_1_.refs_2_), channel_id=1, source_target_pairs={{1,0},{2,1},{3,2},{5,4},{6,5},{7,6},{9,8},{10,9},{11,10},{13,12},{... | collective-permute-start | bytes 1572872 | tf_op jit(solution)/shard_map/ppermute | solution.py:42
  115.9 40.9 %collective-permute-start.33 = (bf16[2,3,128,1024]{3,2,1,0:T(8,128)(2,1)S(1)}, bf16[2,3,128,1024]{3,2,1,0:T(8,128)(2,1)S(1)}, u32[]{:S(2)}, u32[]{:S(2)}) collective-permute-start(bf16[2,3,128,1024]{3,2,1,0:T(8,128)(2,1)S(1)} %shard_map.98.refs_0_), channel_id=1, source_target_pairs={{0,8},{4,12},{8,0},{12,4},{16,24},{20,28},{24,16},{28,20},{1,9},{5... | collective-permute-start | bytes 4718600 | tf_op jit(solution)/shard_map/ppermute | solution.py:52
  125.2 17.0 %collective-permute-start.26 = (bf16[512,512]{1,0:T(8,128)(2,1)S(1)}, bf16[512,512]{1,0:T(8,128)(2,1)S(1)}, u32[]{:S(2)}, u32[]{:S(2)}) collective-permute-start(bf16[512,512]{1,0:T(8,128)(2,1)S(1)} %get-tuple-element.69), channel_id=1, source_target_pairs={{0,1},{1,2},{2,3},{4,5},{5,6},{6,7},{8,9},{9,10},{10,11},{12,13},{... | collective-permute-start | bytes 1572872 | tf_op jit(solution)/shard_map/ppermute | solution.py:42
  127.2 19.5 %collective-permute-start.27 = (bf16[512,512]{1,0:T(8,128)(2,1)S(1)}, bf16[512,512]{1,0:T(8,128)(2,1)S(1)}, u32[]{:S(2)}, u32[]{:S(2)}) collective-permute-start(bf16[512,512]{1,0:T(8,128)(2,1)S(1)} %get-tuple-element.66.refs_1_), channel_id=1, source_target_pairs={{1,0},{2,1},{3,2},{5,4},{6,5},{7,6},{9,8},{10,9},{11,10},{13,12},{... | collective-permute-start | bytes 1572872 | tf_op jit(solution)/shard_map/ppermute | solution.py:42
  136.5 15.2 %collective-permute-start.24 = (bf16[512,512]{1,0:T(8,128)(2,1)S(1)}, bf16[512,512]{1,0:T(8,128)(2,1)S(1)}, u32[]{:S(2)}, u32[]{:S(2)}) collective-permute-start(bf16[512,512]{1,0:T(8,128)(2,1)S(1)} %get-tuple-element.67), channel_id=1, source_target_pairs={{0,1},{1,2},{2,3},{4,5},{5,6},{6,7},{8,9},{9,10},{10,11},{12,13},{... | collective-permute-start | bytes 1572872 | tf_op jit(solution)/shard_map/ppermute | solution.py:42
  138.4 17.4 %collective-permute-start.25 = (bf16[512,512]{1,0:T(8,128)(2,1)S(1)}, bf16[512,512]{1,0:T(8,128)(2,1)S(1)}, u32[]{:S(2)}, u32[]{:S(2)}) collective-permute-start(bf16[512,512]{1,0:T(8,128)(2,1)S(1)} %get-tuple-element.68.refs_1_), channel_id=1, source_target_pairs={{1,0},{2,1},{3,2},{5,4},{6,5},{7,6},{9,8},{10,9},{11,10},{13,12},{... | collective-permute-start | bytes 1572872 | tf_op jit(solution)/shard_map/ppermute | solution.py:42
  157.0 11.2 %copy-start.4 = (bf16[4,3,128,1024]{3,2,1,0:T(8,128)(2,1)}, bf16[4,3,128,1024]{3,2,1,0:T(8,128)(2,1)S(1)}, u32[]{:S(2)}) copy-start(bf16[4,3,128,1024]{3,2,1,0:T(8,128)(2,1)S(1)} %shard_map.99.refs_4_) | copy-start | bytes 9437188
  157.0 9.4 %collective-permute-start.34 = (bf16[4,3,128,1024]{3,2,1,0:T(8,128)(2,1)S(1)}, bf16[4,3,128,1024]{3,2,1,0:T(8,128)(2,1)S(1)}, u32[]{:S(2)}, u32[]{:S(2)}) collective-permute-start(bf16[4,3,128,1024]{3,2,1,0:T(8,128)(2,1)S(1)} %shard_map.99.refs_4_), channel_id=1, source_target_pairs={{0,4},{4,0},{8,12},{12,8},{16,20},{20,16},{24,28},{28,24},{1,5},{5... | collective-permute-start | bytes 9437192 | tf_op jit(solution)/shard_map/ppermute | solution.py:52
  157.1 19.8 %collective-permute-start.30 = (bf16[512,512]{1,0:T(8,128)(2,1)S(1)}, bf16[512,512]{1,0:T(8,128)(2,1)S(1)}, u32[]{:S(2)}, u32[]{:S(2)}) collective-permute-start(bf16[512,512]{1,0:T(8,128)(2,1)S(1)} %get-tuple-element.75), channel_id=1, source_target_pairs={{0,1},{1,2},{2,3},{4,5},{5,6},{6,7},{8,9},{9,10},{10,11},{12,13},{... | collective-permute-start | bytes 1572872 | tf_op jit(solution)/shard_map/ppermute | solution.py:42
  159.2 17.7 %collective-permute-start.31 = (bf16[512,512]{1,0:T(8,128)(2,1)S(1)}, bf16[512,512]{1,0:T(8,128)(2,1)S(1)}, u32[]{:S(2)}, u32[]{:S(2)}) collective-permute-start(bf16[512,512]{1,0:T(8,128)(2,1)S(1)} %get-tuple-element.72.refs_1_), channel_id=1, source_target_pairs={{1,0},{2,1},{3,2},{5,4},{6,5},{7,6},{9,8},{10,9},{11,10},{13,12},{... | collective-permute-start | bytes 1572872 | tf_op jit(solution)/shard_map/ppermute | solution.py:42
  160.5 21.7 %collective-permute-start.28 = (bf16[512,512]{1,0:T(8,128)(2,1)S(1)}, bf16[512,512]{1,0:T(8,128)(2,1)S(1)}, u32[]{:S(2)}, u32[]{:S(2)}) collective-permute-start(bf16[512,512]{1,0:T(8,128)(2,1)S(1)} %get-tuple-element.73), channel_id=1, source_target_pairs={{0,1},{1,2},{2,3},{4,5},{5,6},{6,7},{8,9},{9,10},{10,11},{12,13},{... | collective-permute-start | bytes 1572872 | tf_op jit(solution)/shard_map/ppermute | solution.py:42
  165.1 21.3 %collective-permute-start.29 = (bf16[512,512]{1,0:T(8,128)(2,1)S(1)}, bf16[512,512]{1,0:T(8,128)(2,1)S(1)}, u32[]{:S(2)}, u32[]{:S(2)}) collective-permute-start(bf16[512,512]{1,0:T(8,128)(2,1)S(1)} %get-tuple-element.74.refs_2_.refs_6_), channel_id=1, source_target_pairs={{1,0},{2,1},{3,2},{5,4},{6,5},{7,6},{9,8},{10,9},{11,10},{13,12},{... | collective-permute-start | bytes 1572872 | tf_op jit(solution)/shard_map/ppermute | solution.py:42
  166.4 1.8 copy-start.10
  168.2 8.8 %copy-start.6 = (bf16[4,512,1024]{2,1,0:T(8,128)(2,1)S(1)}, bf16[4,512,1024]{2,1,0:T(8,128)(2,1)}, u32[]{:S(2)}) copy-start(bf16[4,512,1024]{2,1,0:T(8,128)(2,1)} %copy-done.5) | copy-start | bytes 12582916

commit v7 on v6

--- a/solution.py
+++ b/solution.py
@@ -86,22 +86,24 @@
 
 
 def grads_kernel(h, at, ids_ref, code_ref, k_ref, v_ref, w_ref, *refs):
-    lhs, rhs, sem = refs[-3:]
-    copies = []
+    copies, outs = [], []
     if h == 0:
-        k_hbm, v_hbm, ow_hbm, keep_ref, send_ref, rim_ref = refs[:6]
+        k_hbm, v_hbm, ow_hbm, keep_ref, send_ref = refs[:5]
+        n = (len(refs) - 9) // 2
+        out_hbm, held, (lhs, rhs, sem, osem) = refs[5 : 5 + n], refs[5 + n : 5 + 2 * n], refs[-4:]
         last = pl.ds(k_hbm.shape[0] - WINDOW, WINDOW)
         copies = [
-            pltpu.make_async_copy(k_hbm.at[last, :], rim_ref.at[pl.ds(0, WINDOW), :], sem.at[0]),
+            pltpu.make_async_copy(k_hbm.at[last, :], held[0].at[pl.ds(0, WINDOW), :], sem.at[0]),
             pltpu.make_async_copy(
-                v_hbm.at[last, :], rim_ref.at[pl.ds(WINDOW, WINDOW), :], sem.at[1]
+                v_hbm.at[last, :], held[0].at[pl.ds(WINDOW, WINDOW), :], sem.at[1]
             ),
         ] + [
             strip_copy(ids_ref, at + 2 * i, ow_hbm, strip_ref, sem.at[2 + i])
-            for i, strip_ref in enumerate(refs[6:-3])
+            for i, strip_ref in enumerate(held[1:])
         ]
+        outs = [pltpu.make_async_copy(a, b, osem.at[i]) for i, (a, b) in enumerate(zip(held, out_hbm))]
     else:
-        keep_ref, send_ref = refs[-5:-3]
+        keep_ref, send_ref, lhs, rhs = refs[-4:]
     for copy in copies:
         copy.start()
     rows = k_ref.shape[0]
@@ -125,6 +127,11 @@
             lhs[FW + j * wide : FW + (j + 1) * wide, sl] = (gs * up).astype(BF).T
             rhs[sl, cs] = (back * up * (s + gs * (1.0 - s))).astype(BF)
             rhs[sl, FW + j * wide : FW + (j + 1) * wide] = (back * gs).astype(BF)
+        if t == 0:
+            for copy in copies:
+                copy.wait()
+            for copy in outs:
+                copy.start()
     lhs[:FW, :] = k_ref[...].T
     tail = split_rows(jnp.broadcast_to(jnp.sum(codes, axis=1, keepdims=True), (1, LANES)))
     pairs = HALF // 2
@@ -138,7 +145,7 @@
             r = mm(left, right).astype(BF)
             ref[pl.ds(2 * i * FW, FW), :] = r[:, :LANES]
             ref[pl.ds((2 * i + 1) * FW, FW), :] = r[:, LANES:]
-    for copy in copies:
+    for copy in outs:
         copy.wait()
 
 
@@ -159,13 +166,12 @@
             pl.BlockSpec((1, 3, FW, FW), lambda i: (h, 0, 0, 0)),
         ]
         + [ANY] * len(more),
-        out_specs=[full(x) for x in outs],
+        out_specs=[full(x) for x in outs[:2]] + [ANY] * len(outs[2:]),
         out_shape=[jax.ShapeDtypeStruct(x, BF) for x in outs],
-        scratch_shapes=[
-            pltpu.VMEM((2 * FW, rows), BF),
-            pltpu.VMEM((rows, 3 * FW), BF),
-            pltpu.SemaphoreType.DMA((2 + len(strips),)),
-        ],
+        scratch_shapes=[pltpu.VMEM(x, BF) for x in outs[2:]]
+        + [pltpu.VMEM((2 * FW, rows), BF), pltpu.VMEM((rows, 3 * FW), BF)]
+        + [pltpu.SemaphoreType.DMA((2 + i,)) for i in (len(strips), 0) if h == 0 and i]
+        + [pltpu.SemaphoreType.DMA((1 + len(strips),)) for _ in range(1) if h == 0],
         compiler_params=room(58),
         cost_estimate=cost(8 * rows / 1024),
     )(ids, codes, keys, values, fast_weights, *more)

time: 189 us -> 188 us (level)
  no operation moved by 1% of the time
where the time goes in v7:
time: 188 us
  starting transfers between devices  64.4 us (34%)
  Pallas kernels  59.3 us (32%)
  waiting for transfers between devices  58.9 us (31%)
  local copies, waits for them, and re-layouts  3.64 us (2%)
    ppermute x17, starting transfers between devices, shift(): lax.ppermute(block, axis, [(i, i + distance) for i in range(n) if 0 <= i...  40.1 us
    ppermute x17, waiting for transfers between devices, shift(): lax.ppermute(block, axis, [(i, i + distance) for i in range(n) if 0 <= i...  38.2 us
    ppermute x15, starting transfers between devices, swap(): return lax.ppermute(block, 'ctx', [(i, i ^ bit) for i in range(n)])  17.9 us
    pallas_call x2, Pallas kernels, grads(): pl.pallas_call(functools.partial(grads_kernel, h, at), grid=(1,), in_spec...  15.3 us
    ppermute x3, waiting for transfers between devices, rotate(): lax.ppermute(block, axis, [(i, (i + distance) % n) for i in range(n)])  11.7 us
    ppermute x15, waiting for transfers between devices, swap(): return lax.ppermute(block, 'ctx', [(i, i ^ bit) for i in range(n)])  8.99 us
    pallas_call x1, Pallas kernels, gathered(): pl.pallas_call(functools.partial(gathered_kernel, n, heads, parts, at), g...  8.73 us
    pallas_call x4, Pallas kernels, attention(): pl.pallas_call(attn_kernel, grid=(1,), in_specs=[SMEM, col, col, col, of_...  8.26 us
  transfers between devices with their start and end apart: 35, of which 17 were waited for; matrix products, arithmetic and copies ran while one was open for 0% of the time, Pallas kernels for 25%

profile of v7, /device:TPU:0, one launch (start us, length us, event | category | flops | bytes accessed | tf_op | source)
XLA Modules:
  0.0 187.8 jit_solution(2459559608355813190)
XLA Ops:
  1.5 8.1 %shard_map.77 = (bf16[3088,128]{1,0:T(8,128)(2,1)}, bf16[3088,128]{1,0:T(8,128)(2,1)}, bf16[512,1024]{1,0:T(8,128)(2,1)}, bf16[128,1024]{1,0:T(8,128)(2,1)}, bf1...) custom-call(s32[31]{0:T(128)} %stack.137.ids_ref, s32[2,1024]{1,0:T(2,128)} %bitcast.38, bf16[1024,1024]{1,0:T(8,128)(2,1)} %k_ref.11, ...), custom_call_target="tpu_custom_call" | custom-call | flops 960000000 | tf_op jit(solution)/shard_map/pallas_call | solution.py:158
  9.6 2.6 %collective-permute-start = (bf16[512,1024]{1,0:T(8,128)(2,1)}, bf16[512,1024]{1,0:T(8,128)(2,1)S(1)}, u32[]{:S(2)}, u32[]{:S(2)}) collective-permute-start(bf16[512,1024]{1,0:T(8,128)(2,1)} %get-tuple-element.40), channel_id=1, source_target_pairs={{0,4},{4,8},{8,12},{12,16},{16,20},{20,24},{24,28},{1,5},{5,9},{9,... | collective-permute-start | bytes 3145736 | tf_op jit(solution)/shard_map/ppermute | solution.py:42
  12.2 2.6 %collective-permute-start.1 = (bf16[3088,128]{1,0:T(8,128)(2,1)}, bf16[3088,128]{1,0:T(8,128)(2,1)S(1)}, u32[]{:S(2)}, u32[]{:S(2)}) collective-permute-start(bf16[3088,128]{1,0:T(8,128)(2,1)} %get-tuple-element.42), channel_id=1, source_target_pairs={{0,4},{4,0},{8,12},{12,8},{16,20},{20,16},{24,28},{28,24},{1,5},{5... | collective-permute-start | bytes 2371592 | tf_op jit(solution)/shard_map/ppermute | solution.py:52
  14.9 7.2 %shard_map.79 = (bf16[3088,128]{1,0:T(8,128)(2,1)}, bf16[3088,128]{1,0:T(8,128)(2,1)}) custom-call(s32[31]{0:T(128)} %stack.137.ids_ref, s32[2,1024]{1,0:T(2,128)} %bitcast.39, bf16[1024,1024]{1,0:T(8,128)(2,1)} %k_ref.11, bf16[1024,1024]{1,0:T(8,128)(2,1)} %v_ref.11, bf16[2,3,512,512]{3,2,1,0:T(8,128)(2,1)} %base_ref.1, ...), custom_call_target="tpu_custom_call" | custom-call | flops 960000000 | tf_op jit(solution)/shard_map/pallas_call | solution.py:158
  22.1 0.9 shard_map.78
  23.0 1.5 collective-permute-start.2
  24.6 1.1 copy-done.8
  25.7 0.9 shard_map.80
  26.6 6.9 %collective-permute-start.4 = (bf16[1552,128]{1,0:T(8,128)(2,1)S(1)}, bf16[1552,128]{1,0:T(8,128)(2,1)S(1)}, u32[]{:S(2)}, u32[]{:S(2)}) collective-permute-start(bf16[1552,128]{1,0:T(8,128)(2,1)S(1)} %get-tuple-element.47.rest_1_), channel_id=1, source_target_pairs={{0,16},{4,20},{8,24},{12,28},{16,0},{20,4},{24,8},{28,12},{1,17},{... | collective-permute-start | bytes 1191944 | tf_op jit(solution)/shard_map/ppermute | solution.py:52
  33.5 2.6 %collective-permute-start.5 = (bf16[128,1024]{1,0:T(8,128)(2,1)S(1)}, bf16[128,1024]{1,0:T(8,128)(2,1)S(1)}, u32[]{:S(2)}, u32[]{:S(2)}) collective-permute-start(bf16[128,1024]{1,0:T(8,128)(2,1)S(1)} %copy-done.13), channel_id=1, source_target_pairs={{0,2},{1,3},{2,0},{3,1},{4,6},{5,7},{6,4},{7,5},{8,10},{9,11},{10,... | collective-permute-start | bytes 786440 | tf_op jit(solution)/shard_map/ppermute | solution.py:47
  36.1 2.1 %shard_map.81.rest_0_.refs_0_ = bf16[1024,256]{1,0:T(8,128)(2,1)S(1)} custom-call(s32[31]{0:T(128)S(1)} %copy-done.9, bf16[1024,1024]{1,0:T(8,128)(2,1)S(1)} %copy-done.2, bf16[1024,1024]{1,0:T(8,128)(2,1)S(1)} %copy-done, bf16[1024,1024]{1,0:T(8,128)(2,1)S(1)} %copy-done.1, bf16[512,1024]{1,0:T(8,128)(2,1)S(1)} %collective-permute-done.refs_1_.rim_ref, ...), custom_call_target="tpu_custom_call" | custom-call | flops 252000000 | tf_op jit(solution)/shard_map/pallas_call | solution.py:321
  38.9 2.1 %shard_map.83.rest_0_.refs_1_ = bf16[1024,256]{1,0:T(8,128)(2,1)S(1)} custom-call(s32[31]{0:T(128)S(1)} %copy-done.9, bf16[1024,1024]{1,0:T(8,128)(2,1)S(1)} %copy-done.2, bf16[1024,1024]{1,0:T(8,128)(2,1)S(1)} %copy-done, bf16[1024,1024]{1,0:T(8,128)(2,1)S(1)} %copy-done.1, bf16[512,1024]{1,0:T(8,128)(2,1)S(1)} %collective-permute-done.refs_1_.rim_ref, ...), custom_call_target="tpu_custom_call" | custom-call | flops 252000000 | tf_op jit(solution)/shard_map/pallas_call | solution.py:321
  41.0 2.1 %shard_map.84.rest_0_.refs_0_ = bf16[1024,256]{1,0:T(8,128)(2,1)S(1)} custom-call(s32[31]{0:T(128)S(1)} %copy-done.9, bf16[1024,1024]{1,0:T(8,128)(2,1)S(1)} %copy-done.2, bf16[1024,1024]{1,0:T(8,128)(2,1)S(1)} %copy-done, bf16[1024,1024]{1,0:T(8,128)(2,1)S(1)} %copy-done.1, bf16[512,1024]{1,0:T(8,128)(2,1)S(1)} %collective-permute-done.refs_1_.rim_ref, ...), custom_call_target="tpu_custom_call" | custom-call | flops 252000000 | tf_op jit(solution)/shard_map/pallas_call | solution.py:321
  43.0 3.5 %collective-permute-done.5.rest_2_ = bf16[128,1024]{1,0:T(8,128)(2,1)S(1)} collective-permute-done((bf16[128,1024]{1,0:T(8,128)(2,1)S(1)}, bf16[128,1024]{1,0:T(8,128)(2,1)S(1)}, u32[]{:S(2)}, u32[]{:S(2)}) %collective-permute-start.5) | collective-permute-done | bytes 262176 | tf_op jit(solution)/shard_map/ppermute | solution.py:47
  47.9 3.1 %collective-permute-start.9 = (bf16[128,1024]{1,0:T(8,128)(2,1)S(1)}, bf16[128,1024]{1,0:T(8,128)(2,1)S(1)}, u32[]{:S(2)}, u32[]{:S(2)}) collective-permute-start(bf16[128,1024]{1,0:T(8,128)(2,1)S(1)} %copy-done.11), channel_id=1, source_target_pairs={{0,3},{1,0},{2,1},{3,2},{4,7},{5,4},{6,5},{7,6},{8,11},{9,8},{10,9... | collective-permute-start | bytes 786440 | tf_op jit(solution)/shard_map/ppermute | solution.py:47
  51.1 2.1 %shard_map.86.refs_4_.refs_1_ = bf16[1024,256]{1,0:T(8,128)(2,1)S(1)} custom-call(s32[31]{0:T(128)S(1)} %copy-done.9, bf16[1024,1024]{1,0:T(8,128)(2,1)S(1)} %copy-done.2, bf16[1024,1024]{1,0:T(8,128)(2,1)S(1)} %copy-done, bf16[1024,1024]{1,0:T(8,128)(2,1)S(1)} %copy-done.1, bf16[512,1024]{1,0:T(8,128)(2,1)S(1)} %collective-permute-done.refs_1_.rim_ref, ...), custom_call_target="tpu_custom_call" | custom-call | flops 252000000 | tf_op jit(solution)/shard_map/pallas_call | solution.py:321
  53.1 5.1 %collective-permute-done.8.refs_5_ = bf16[128,1024]{1,0:T(8,128)(2,1)S(1)} collective-permute-done((bf16[128,1024]{1,0:T(8,128)(2,1)S(1)}, bf16[128,1024]{1,0:T(8,128)(2,1)S(1)}, u32[]{:S(2)}, u32[]{:S(2)}) %collective-permute-start.8) | collective-permute-done | bytes 262176 | tf_op jit(solution)/shard_map/ppermute | solution.py:47
  58.3 3.1 %collective-permute-done.9.refs_6_ = bf16[128,1024]{1,0:T(8,128)(2,1)S(1)} collective-permute-done((bf16[128,1024]{1,0:T(8,128)(2,1)S(1)}, bf16[128,1024]{1,0:T(8,128)(2,1)S(1)}, u32[]{:S(2)}, u32[]{:S(2)}) %collective-permute-start.9) | collective-permute-done | bytes 262176 | tf_op jit(solution)/shard_map/ppermute | solution.py:47
  61.4 2.1 %shard_map.87 = (bf16[3,512,128]{2,1,0:T(8,128)(2,1)S(1)}, bf16[3,512,128]{2,1,0:T(8,128)(2,1)S(1)}) custom-call(s32[31]{0:T(128)S(1)} %copy-done.9, bf16[2,3,512,512]{3,2,1,0:T(8,128)(2,1)S(1)} %copy-done.3, bf16[1552,128]{1,0:T(8,128)(2,1)S(1)} %shard_map.82.rest_0_.rest_1_.refs_0_, bf16[1552,128]{1,0:T(8,128)(2,1)S(1)} %collective-permute-done.6.refs_1_, ...), custom_call_target="tpu_custom_call" | custom-call | flops 252000000 | tf_op jit(solution)/shard_map/pallas_call | solution.py:270
  63.5 1.7 collective-permute-start.13
  65.6 7.7 %collective-permute-done.13.refs_3_ = bf16[3,512,128]{2,1,0:T(8,128)(2,1)S(1)} collective-permute-done((bf16[3,512,128]{2,1,0:T(8,128)(2,1)S(1)}, bf16[3,512,128]{2,1,0:T(8,128)(2,1)S(1)}, u32[]{:S(2)}, u32[]{:S(2)}) %collective-permute-start.13) | collective-permute-done | bytes 393248 | tf_op jit(solution)/shard_map/ppermute | solution.py:52
  73.9 0.7 collective-permute-done.10.refs_3_
  75.1 3.2 %shard_map.88 = (bf16[512,512]{1,0:T(8,128)(2,1)S(1)}, bf16[512,512]{1,0:T(8,128)(2,1)S(1)}, bf16[2,3,512,512]{3,2,1,0:T(8,128)(2,1)}) custom-call(s32[31]{0:T(128)S(1)} %copy-done.9, bf16[1024,1024]{1,0:T(8,128)(2,1)S(1)} %copy-done.2, bf16[1024,256]{1,0:T(8,128)(2,1)S(1)} %shard_map.81.rest_0_.refs_0_, bf16[1024,256]{1,0:T(8,128)(2,1)S(1)} %shard_map.83.rest_0_.refs_1_, ...), custom_call_target="tpu_custom_call" | custom-call | flops 396000000 | tf_op jit(solution)/shard_map/pallas_call | solution.py:381
  78.3 5.1 %collective-permute-start.18 = (bf16[512,512]{1,0:T(8,128)(2,1)S(1)}, bf16[512,512]{1,0:T(8,128)(2,1)S(1)}, u32[]{:S(2)}, u32[]{:S(2)}) collective-permute-start(bf16[512,512]{1,0:T(8,128)(2,1)S(1)} %get-tuple-element.58.refs_0_), channel_id=1, source_target_pairs={{0,1},{1,2},{2,3},{4,5},{5,6},{6,7},{8,9},{9,10},{10,11},{12,13},{... | collective-permute-start | bytes 1572872 | tf_op jit(solution)/shard_map/ppermute | solution.py:42
  83.4 1.3 collective-permute-start.19
  84.8 3.2 %shard_map.89 = (bf16[512,512]{1,0:T(8,128)(2,1)S(1)}, bf16[512,512]{1,0:T(8,128)(2,1)S(1)}, bf16[2,3,512,512]{3,2,1,0:T(8,128)(2,1)}) custom-call(s32[31]{0:T(128)S(1)} %copy-done.9, bf16[1024,1024]{1,0:T(8,128)(2,1)S(1)} %copy-done.2, bf16[1024,256]{1,0:T(8,128)(2,1)S(1)} %shard_map.84.rest_0_.refs_0_, ...), custom_call_target="tpu_custom_call", output_to_operand_aliasing={{2}: (8, {})} | custom-call | flops 396000000 | tf_op jit(solution)/shard_map/pallas_call | solution.py:381
  88.0 4.6 %collective-permute-start.16 = (bf16[512,512]{1,0:T(8,128)(2,1)S(1)}, bf16[512,512]{1,0:T(8,128)(2,1)S(1)}, u32[]{:S(2)}, u32[]{:S(2)}) collective-permute-start(bf16[512,512]{1,0:T(8,128)(2,1)S(1)} %get-tuple-element.55.refs_3_.refs_1_), channel_id=1, source_target_pairs={{0,1},{1,2},{2,3},{4,5},{5,6},{6,7},{8,9},{9,10},{10,11},{12,13},{... | collective-permute-start | bytes 1572872 | tf_op jit(solution)/shard_map/ppermute | solution.py:42
  92.6 1.3 collective-permute-start.17
  94.0 1.5 collective-permute-start.32
  95.5 5.7 %shard_map.91.p_hbm = bf16[4,512,1024]{2,1,0:T(8,128)(2,1)S(1)} custom-call(bf16[512,512]{1,0:T(8,128)(2,1)S(1)} %get-tuple-element.56.refs_0_, bf16[512,512]{1,0:T(8,128)(2,1)S(1)} %get-tuple-element.57.refs_1_, bf16[1024,4096]{1,0:T(8,128)(2,1)S(1)} %bitcast.31, bf16[3,128,1024]{2,1,0:T(8,128)(2,1)S(1)} %shard_map.90.refs_3_), custom_call_target="tpu_custom_call" | custom-call | flops 120000000 | tf_op jit(solution)/shard_map/pallas_call | solution.py:421
  101.3 1.0 shard_map.92
  102.3 4.6 %collective-permute-start.22 = (bf16[512,512]{1,0:T(8,128)(2,1)S(1)}, bf16[512,512]{1,0:T(8,128)(2,1)S(1)}, u32[]{:S(2)}, u32[]{:S(2)}) collective-permute-start(bf16[512,512]{1,0:T(8,128)(2,1)S(1)} %get-tuple-element.63), channel_id=1, source_target_pairs={{0,1},{1,2},{2,3},{4,5},{5,6},{6,7},{8,9},{9,10},{10,11},{12,13},{... | collective-permute-start | bytes 1572872 | tf_op jit(solution)/shard_map/ppermute | solution.py:42
  106.9 1.3 collective-permute-start.23
  108.2 2.5 %collective-permute-done.17.left_hbm = bf16[512,512]{1,0:T(8,128)(2,1)S(1)} collective-permute-done((bf16[512,512]{1,0:T(8,128)(2,1)S(1)}, bf16[512,512]{1,0:T(8,128)(2,1)S(1)}, u32[]{:S(2)}, u32[]{:S(2)}) %collective-permute-start.17) | collective-permute-done | bytes 524320 | tf_op jit(solution)/shard_map/ppermute | solution.py:42
  110.7 1.0 shard_map.93
  111.7 2.3 %collective-permute-start.20 = (bf16[512,512]{1,0:T(8,128)(2,1)S(1)}, bf16[512,512]{1,0:T(8,128)(2,1)S(1)}, u32[]{:S(2)}, u32[]{:S(2)}) collective-permute-start(bf16[512,512]{1,0:T(8,128)(2,1)S(1)} %get-tuple-element.61), channel_id=1, source_target_pairs={{0,1},{1,2},{2,3},{4,5},{5,6},{6,7},{8,9},{9,10},{10,11},{12,13},{... | collective-permute-start | bytes 1572872 | tf_op jit(solution)/shard_map/ppermute | solution.py:42
  114.0 1.3 collective-permute-start.21
  115.4 2.1 %collective-permute-start.33 = (bf16[2,3,128,1024]{3,2,1,0:T(8,128)(2,1)S(1)}, bf16[2,3,128,1024]{3,2,1,0:T(8,128)(2,1)S(1)}, u32[]{:S(2)}, u32[]{:S(2)}) collective-permute-start(bf16[2,3,128,1024]{3,2,1,0:T(8,128)(2,1)S(1)} %shard_map.98.refs_0_), channel_id=1, source_target_pairs={{0,8},{4,12},{8,0},{12,4},{16,24},{20,28},{24,16},{28,20},{1,9},{5... | collective-permute-start | bytes 4718600 | tf_op jit(solution)/shard_map/ppermute | solution.py:52
  117.5 1.7 collective-permute-done.22.right_hbm
  119.2 4.4 %collective-permute-done.23.left_hbm = bf16[512,512]{1,0:T(8,128)(2,1)S(1)} collective-permute-done((bf16[512,512]{1,0:T(8,128)(2,1)S(1)}, bf16[512,512]{1,0:T(8,128)(2,1)S(1)}, u32[]{:S(2)}, u32[]{:S(2)}) %collective-permute-start.23) | collective-permute-done | bytes 524320 | tf_op jit(solution)/shard_map/ppermute | solution.py:42
  123.7 1.0 shard_map.94
  124.7 1.9 %collective-permute-start.26 = (bf16[512,512]{1,0:T(8,128)(2,1)S(1)}, bf16[512,512]{1,0:T(8,128)(2,1)S(1)}, u32[]{:S(2)}, u32[]{:S(2)}) collective-permute-start(bf16[512,512]{1,0:T(8,128)(2,1)S(1)} %get-tuple-element.69), channel_id=1, source_target_pairs={{0,1},{1,2},{2,3},{4,5},{5,6},{6,7},{8,9},{9,10},{10,11},{12,13},{... | collective-permute-start | bytes 1572872 | tf_op jit(solution)/shard_map/ppermute | solution.py:42
  126.6 1.3 collective-permute-start.27
  127.9 2.6 %collective-permute-done.20.right_hbm = bf16[512,512]{1,0:T(8,128)(2,1)S(1)} collective-permute-done((bf16[512,512]{1,0:T(8,128)(2,1)S(1)}, bf16[512,512]{1,0:T(8,128)(2,1)S(1)}, u32[]{:S(2)}, u32[]{:S(2)}) %collective-permute-start.20) | collective-permute-done | bytes 524320 | tf_op jit(solution)/shard_map/ppermute | solution.py:42
  130.5 4.4 %collective-permute-done.21.left_hbm = bf16[512,512]{1,0:T(8,128)(2,1)S(1)} collective-permute-done((bf16[512,512]{1,0:T(8,128)(2,1)S(1)}, bf16[512,512]{1,0:T(8,128)(2,1)S(1)}, u32[]{:S(2)}, u32[]{:S(2)}) %collective-permute-start.21) | collective-permute-done | bytes 524320 | tf_op jit(solution)/shard_map/ppermute | solution.py:42
  134.9 1.0 shard_map.95
  135.9 1.9 %collective-permute-start.24 = (bf16[512,512]{1,0:T(8,128)(2,1)S(1)}, bf16[512,512]{1,0:T(8,128)(2,1)S(1)}, u32[]{:S(2)}, u32[]{:S(2)}) collective-permute-start(bf16[512,512]{1,0:T(8,128)(2,1)S(1)} %get-tuple-element.67), channel_id=1, source_target_pairs={{0,1},{1,2},{2,3},{4,5},{5,6},{6,7},{8,9},{9,10},{10,11},{12,13},{... | collective-permute-start | bytes 1572872 | tf_op jit(solution)/shard_map/ppermute | solution.py:42
  137.8 1.3 collective-permute-start.25
  139.1 2.6 %collective-permute-done.26.right_hbm = bf16[512,512]{1,0:T(8,128)(2,1)S(1)} collective-permute-done((bf16[512,512]{1,0:T(8,128)(2,1)S(1)}, bf16[512,512]{1,0:T(8,128)(2,1)S(1)}, u32[]{:S(2)}, u32[]{:S(2)}) %collective-permute-start.26) | collective-permute-done | bytes 524320 | tf_op jit(solution)/shard_map/ppermute | solution.py:42
  141.7 4.4 %collective-permute-done.27.left_hbm = bf16[512,512]{1,0:T(8,128)(2,1)S(1)} collective-permute-done((bf16[512,512]{1,0:T(8,128)(2,1)S(1)}, bf16[512,512]{1,0:T(8,128)(2,1)S(1)}, u32[]{:S(2)}, u32[]{:S(2)}) %collective-permute-start.27) | collective-permute-done | bytes 524320 | tf_op jit(solution)/shard_map/ppermute | solution.py:42
  146.1 1.2 shard_map.96
  147.4 3.7 %collective-permute-done.24.right_hbm = bf16[512,512]{1,0:T(8,128)(2,1)S(1)} collective-permute-done((bf16[512,512]{1,0:T(8,128)(2,1)S(1)}, bf16[512,512]{1,0:T(8,128)(2,1)S(1)}, u32[]{:S(2)}, u32[]{:S(2)}) %collective-permute-start.24) | collective-permute-done | bytes 524320 | tf_op jit(solution)/shard_map/ppermute | solution.py:42
  151.1 4.1 %collective-permute-done.25.left_hbm = bf16[512,512]{1,0:T(8,128)(2,1)S(1)} collective-permute-done((bf16[512,512]{1,0:T(8,128)(2,1)S(1)}, bf16[512,512]{1,0:T(8,128)(2,1)S(1)}, u32[]{:S(2)}, u32[]{:S(2)}) %collective-permute-start.25) | collective-permute-done | bytes 524320 | tf_op jit(solution)/shard_map/ppermute | solution.py:42
  155.3 1.0 shard_map.97
  156.6 2.1 %collective-permute-start.30 = (bf16[512,512]{1,0:T(8,128)(2,1)S(1)}, bf16[512,512]{1,0:T(8,128)(2,1)S(1)}, u32[]{:S(2)}, u32[]{:S(2)}) collective-permute-start(bf16[512,512]{1,0:T(8,128)(2,1)S(1)} %get-tuple-element.75), channel_id=1, source_target_pairs={{0,1},{1,2},{2,3},{4,5},{5,6},{6,7},{8,9},{9,10},{10,11},{12,13},{... | collective-permute-start | bytes 1572872 | tf_op jit(solution)/shard_map/ppermute | solution.py:42
  158.7 1.3 collective-permute-start.31
  160.0 4.6 %collective-permute-start.28 = (bf16[512,512]{1,0:T(8,128)(2,1)S(1)}, bf16[512,512]{1,0:T(8,128)(2,1)S(1)}, u32[]{:S(2)}, u32[]{:S(2)}) collective-permute-start(bf16[512,512]{1,0:T(8,128)(2,1)S(1)} %get-tuple-element.73), channel_id=1, source_target_pairs={{0,1},{1,2},{2,3},{4,5},{5,6},{6,7},{8,9},{9,10},{10,11},{12,13},{... | collective-permute-start | bytes 1572872 | tf_op jit(solution)/shard_map/ppermute | solution.py:42
  164.6 1.3 collective-permute-start.29
  165.9 1.7 copy-done.10
  167.7 8.7 %shard_map.100.out_in = bf16[1024,1024]{1,0:T(8,128)(2,1)} custom-call(s32[31]{0:T(128)S(1)} %copy-done.9, bf16[512,512]{1,0:T(8,128)(2,1)S(1)} %get-tuple-element.58.refs_0_, bf16[512,512]{1,0:T(8,128)(2,1)S(1)} %get-tuple-element.55.refs_3_.refs_1_, bf16[3,512,1024]{2,1,0:T(8,128)(2,1)S(1)} %get-tuple-element.76.refs_2_, bf16[1024,4096]{1,0:T(8,128)(2,1)} %refs_3_.1, ...), custom_call_target="tpu_custom_call" | custom-call | flops 1080000000 | tf_op jit(solution)/shard_map/pallas_call | solution.py:535
  176.4 1.7 shard_map.101.out_in
  178.1 3.6 %collective-permute-done.28.right_hbm = bf16[512,512]{1,0:T(8,128)(2,1)S(1)} collective-permute-done((bf16[512,512]{1,0:T(8,128)(2,1)S(1)}, bf16[512,512]{1,0:T(8,128)(2,1)S(1)}, u32[]{:S(2)}, u32[]{:S(2)}) %collective-permute-start.28) | collective-permute-done | bytes 524320 | tf_op jit(solution)/shard_map/ppermute | solution.py:42
  181.7 4.1 %collective-permute-done.29.left_hbm = bf16[512,512]{1,0:T(8,128)(2,1)S(1)} collective-permute-done((bf16[512,512]{1,0:T(8,128)(2,1)S(1)}, bf16[512,512]{1,0:T(8,128)(2,1)S(1)}, u32[]{:S(2)}, u32[]{:S(2)}) %collective-permute-start.29) | collective-permute-done | bytes 524320 | tf_op jit(solution)/shard_map/ppermute | solution.py:42
  185.9 1.7 shard_map.102
  (66 shorter events, 4.8 us)
Async XLA Ops:
  9.6 15.0 %collective-permute-start = (bf16[512,1024]{1,0:T(8,128)(2,1)}, bf16[512,1024]{1,0:T(8,128)(2,1)S(1)}, u32[]{:S(2)}, u32[]{:S(2)}) collective-permute-start(bf16[512,1024]{1,0:T(8,128)(2,1)} %get-tuple-element.40), channel_id=1, source_target_pairs={{0,4},{4,8},{8,12},{12,16},{16,20},{20,24},{24,28},{1,5},{5,9},{9,... | collective-permute-start | bytes 3145736 | tf_op jit(solution)/shard_map/ppermute | solution.py:42
  12.2 9.9 %collective-permute-start.1 = (bf16[3088,128]{1,0:T(8,128)(2,1)}, bf16[3088,128]{1,0:T(8,128)(2,1)S(1)}, u32[]{:S(2)}, u32[]{:S(2)}) collective-permute-start(bf16[3088,128]{1,0:T(8,128)(2,1)} %get-tuple-element.42), channel_id=1, source_target_pairs={{0,4},{4,0},{8,12},{12,8},{16,20},{20,16},{24,28},{28,24},{1,5},{5... | collective-permute-start | bytes 2371592 | tf_op jit(solution)/shard_map/ppermute | solution.py:52
  14.8 7.3 %copy-start.7 = (bf16[3088,128]{1,0:T(8,128)(2,1)S(1)}, bf16[3088,128]{1,0:T(8,128)(2,1)}, u32[]{:S(2)}) copy-start(bf16[3088,128]{1,0:T(8,128)(2,1)} %get-tuple-element.41.keep_hbm.refs_0_) | copy-start | bytes 2371588
  14.9 7.3 %copy-start.9 = (s32[31]{0:T(128)S(1)}, s32[31]{0:T(128)}, u32[]{:S(2)}) copy-start(s32[31]{0:T(128)} %stack.137.ids_ref) | copy-start | bytes 376
  14.9 18.7 %copy-start.13 = (bf16[128,1024]{1,0:T(8,128)(2,1)S(1)}, bf16[128,1024]{1,0:T(8,128)(2,1)}, u32[]{:S(2)}) copy-start(bf16[128,1024]{1,0:T(8,128)(2,1)} %get-tuple-element.49) | copy-start | bytes 786436
  14.9 21.3 %copy-start.2 = (bf16[1024,1024]{1,0:T(8,128)(2,1)S(1)}, bf16[1024,1024]{1,0:T(8,128)(2,1)}, u32[]{:S(2)}) copy-start(bf16[1024,1024]{1,0:T(8,128)(2,1)} %q_hbm.3) | copy-start | bytes 6291460
  22.0 14.1 %copy-start = (bf16[1024,1024]{1,0:T(8,128)(2,1)S(1)}, bf16[1024,1024]{1,0:T(8,128)(2,1)}, u32[]{:S(2)}) copy-start(bf16[1024,1024]{1,0:T(8,128)(2,1)} %k_ref.11) | copy-start | bytes 6291460
  22.0 14.1 %copy-start.1 = (bf16[1024,1024]{1,0:T(8,128)(2,1)S(1)}, bf16[1024,1024]{1,0:T(8,128)(2,1)}, u32[]{:S(2)}) copy-start(bf16[1024,1024]{1,0:T(8,128)(2,1)} %v_ref.11) | copy-start | bytes 6291460
  22.0 2.6 %collective-permute-start.3 = (bf16[3088,128]{1,0:T(8,128)(2,1)}, bf16[3088,128]{1,0:T(8,128)(2,1)S(1)}, u32[]{:S(2)}, u32[]{:S(2)}) collective-permute-start(bf16[3088,128]{1,0:T(8,128)(2,1)} %get-tuple-element.46), channel_id=1, source_target_pairs={{0,4},{4,0},{8,12},{12,8},{16,20},{20,16},{24,28},{28,24},{1,5},{5... | collective-permute-start | bytes 2371592 | tf_op jit(solution)/shard_map/ppermute | solution.py:52
  23.0 15.2 %collective-permute-start.2 = (bf16[1552,128]{1,0:T(8,128)(2,1)S(1)}, bf16[1552,128]{1,0:T(8,128)(2,1)S(1)}, u32[]{:S(2)}, u32[]{:S(2)}) collective-permute-start(bf16[1552,128]{1,0:T(8,128)(2,1)S(1)} %get-tuple-element.44.refs_0_.rest_0_), channel_id=1, source_target_pairs={{0,8},{4,12},{8,0},{12,4},{16,24},{20,28},{24,16},{28,20},{1,9},{5... | collective-permute-start | bytes 1191944 | tf_op jit(solution)/shard_map/ppermute | solution.py:52
  24.6 1.1 copy-start.8
  26.6 19.9 %collective-permute-start.4 = (bf16[1552,128]{1,0:T(8,128)(2,1)S(1)}, bf16[1552,128]{1,0:T(8,128)(2,1)S(1)}, u32[]{:S(2)}, u32[]{:S(2)}) collective-permute-start(bf16[1552,128]{1,0:T(8,128)(2,1)S(1)} %get-tuple-element.47.rest_1_), channel_id=1, source_target_pairs={{0,16},{4,20},{8,24},{12,28},{16,0},{20,4},{24,8},{28,12},{1,17},{... | collective-permute-start | bytes 1191944 | tf_op jit(solution)/shard_map/ppermute | solution.py:52
  33.5 13.0 %collective-permute-start.5 = (bf16[128,1024]{1,0:T(8,128)(2,1)S(1)}, bf16[128,1024]{1,0:T(8,128)(2,1)S(1)}, u32[]{:S(2)}, u32[]{:S(2)}) collective-permute-start(bf16[128,1024]{1,0:T(8,128)(2,1)S(1)} %copy-done.13), channel_id=1, source_target_pairs={{0,2},{1,3},{2,0},{3,1},{4,6},{5,7},{6,4},{7,5},{8,10},{9,11},{10,... | collective-permute-start | bytes 786440 | tf_op jit(solution)/shard_map/ppermute | solution.py:47
  38.7 22.7 %collective-permute-start.6 = (bf16[1552,128]{1,0:T(8,128)(2,1)S(1)}, bf16[1552,128]{1,0:T(8,128)(2,1)S(1)}, u32[]{:S(2)}, u32[]{:S(2)}) collective-permute-start(bf16[1552,128]{1,0:T(8,128)(2,1)S(1)} %shard_map.82.rest_0_.rest_1_.refs_0_), channel_id=1, source_target_pairs={{0,16},{4,20},{8,24},{12,28},{16,0},{20,4},{24,8},{28,12},{1,17},{... | collective-permute-start | bytes 1191944 | tf_op jit(solution)/shard_map/ppermute | solution.py:52
  41.0 6.3 %copy-start.12 = (bf16[128,1024]{1,0:T(8,128)(2,1)S(1)}, bf16[128,1024]{1,0:T(8,128)(2,1)}, u32[]{:S(2)}) copy-start(bf16[128,1024]{1,0:T(8,128)(2,1)} %get-tuple-element.50) | copy-start | bytes 786436
  41.0 6.9 %copy-start.11 = (bf16[128,1024]{1,0:T(8,128)(2,1)S(1)}, bf16[128,1024]{1,0:T(8,128)(2,1)}, u32[]{:S(2)}) copy-start(bf16[128,1024]{1,0:T(8,128)(2,1)} %get-tuple-element.51) | copy-start | bytes 786436
  47.0 14.4 %collective-permute-start.7 = (bf16[1552,128]{1,0:T(8,128)(2,1)S(1)}, bf16[1552,128]{1,0:T(8,128)(2,1)S(1)}, u32[]{:S(2)}, u32[]{:S(2)}) collective-permute-start(bf16[1552,128]{1,0:T(8,128)(2,1)S(1)} %shard_map.85.rest_0_.refs_2_), channel_id=1, source_target_pairs={{0,8},{4,12},{8,0},{12,4},{16,24},{20,28},{24,16},{28,20},{1,9},{5... | collective-permute-start | bytes 1191944 | tf_op jit(solution)/shard_map/ppermute | solution.py:52
  47.2 11.0 %collective-permute-start.8 = (bf16[128,1024]{1,0:T(8,128)(2,1)S(1)}, bf16[128,1024]{1,0:T(8,128)(2,1)S(1)}, u32[]{:S(2)}, u32[]{:S(2)}) collective-permute-start(bf16[128,1024]{1,0:T(8,128)(2,1)S(1)} %copy-done.12), channel_id=1, source_target_pairs={{0,1},{1,2},{2,3},{3,0},{4,5},{5,6},{6,7},{7,4},{8,9},{9,10},{10,1... | collective-permute-start | bytes 786440 | tf_op jit(solution)/shard_map/ppermute | solution.py:47
  47.9 13.5 %copy-start.3 = (bf16[2,3,512,512]{3,2,1,0:T(8,128)(2,1)S(1)}, bf16[2,3,512,512]{3,2,1,0:T(8,128)(2,1)}, u32[]{:S(2)}) copy-start(bf16[2,3,512,512]{3,2,1,0:T(8,128)(2,1)} %base_ref.1) | copy-start | bytes 9437188
  47.9 13.5 %collective-permute-start.9 = (bf16[128,1024]{1,0:T(8,128)(2,1)S(1)}, bf16[128,1024]{1,0:T(8,128)(2,1)S(1)}, u32[]{:S(2)}, u32[]{:S(2)}) collective-permute-start(bf16[128,1024]{1,0:T(8,128)(2,1)S(1)} %copy-done.11), channel_id=1, source_target_pairs={{0,3},{1,0},{2,1},{3,2},{4,7},{5,4},{6,5},{7,6},{8,11},{9,8},{10,9... | collective-permute-start | bytes 786440 | tf_op jit(solution)/shard_map/ppermute | solution.py:47
  61.4 34.1 %slice-start = ((s8[8388608]{0:T(1024)(128)(4,1)}), s8[4194304]{0:T(1024)(128)(4,1)S(1)}, s32[]{:S(2)}) async-start(s8[8388608]{0:T(1024)(128)(4,1)} %bitcast.30), calls=%async_computation | async-start | bytes 8388608
  63.5 9.8 %collective-permute-start.13 = (bf16[3,512,128]{2,1,0:T(8,128)(2,1)S(1)}, bf16[3,512,128]{2,1,0:T(8,128)(2,1)S(1)}, u32[]{:S(2)}, u32[]{:S(2)}) collective-permute-start(bf16[3,512,128]{2,1,0:T(8,128)(2,1)S(1)} %get-tuple-element.53.refs_2_), channel_id=1, source_target_pairs={{0,8},{4,12},{8,0},{12,4},{16,24},{20,28},{24,16},{28,20},{1,9},{5... | collective-permute-start | bytes 1179656 | tf_op jit(solution)/shard_map/ppermute | solution.py:52
  65.3 30.2 %slice-start.1 = ((s8[8388608]{0:T(1024)(128)(4,1)}), s8[4194304]{0:T(1024)(128)(4,1)S(1)}, s32[]{:S(2)}) async-start(s8[8388608]{0:T(1024)(128)(4,1)} %bitcast.30), calls=%async_computation.1 | async-start | bytes 8388608
  65.3 9.4 %collective-permute-start.10 = (bf16[3,512,128]{2,1,0:T(8,128)(2,1)S(1)}, bf16[3,512,128]{2,1,0:T(8,128)(2,1)S(1)}, u32[]{:S(2)}, u32[]{:S(2)}) collective-permute-start(bf16[3,512,128]{2,1,0:T(8,128)(2,1)S(1)} %get-tuple-element.52.refs_2_), channel_id=1, source_target_pairs={{0,16},{4,20},{8,24},{12,28},{16,0},{20,4},{24,8},{28,12},{1,17},{... | collective-permute-start | bytes 1179656 | tf_op jit(solution)/shard_map/ppermute | solution.py:52
  65.6 9.0 %collective-permute-start.14 = (bf16[3,512,128]{2,1,0:T(8,128)(2,1)S(1)}, bf16[3,512,128]{2,1,0:T(8,128)(2,1)S(1)}, u32[]{:S(2)}, u32[]{:S(2)}) collective-permute-start(bf16[3,512,128]{2,1,0:T(8,128)(2,1)S(1)} %get-tuple-element.53.refs_2_), channel_id=1, source_target_pairs={{0,4},{4,0},{8,12},{12,8},{16,20},{20,16},{24,28},{28,24},{1,5},{5... | collective-permute-start | bytes 1179656 | tf_op jit(solution)/shard_map/ppermute | solution.py:52
  73.4 1.7 collective-permute-start.15
  73.4 11.4 %collective-permute-start.11 = (bf16[3,512,128]{2,1,0:T(8,128)(2,1)S(1)}, bf16[3,512,128]{2,1,0:T(8,128)(2,1)S(1)}, u32[]{:S(2)}, u32[]{:S(2)}) collective-permute-start(bf16[3,512,128]{2,1,0:T(8,128)(2,1)S(1)} %get-tuple-element.52.refs_2_), channel_id=1, source_target_pairs={{0,4},{4,0},{8,12},{12,8},{16,20},{20,16},{24,28},{28,24},{1,5},{5... | collective-permute-start | bytes 1179656 | tf_op jit(solution)/shard_map/ppermute | solution.py:52
  74.6 10.1 %collective-permute-start.12 = (bf16[3,512,128]{2,1,0:T(8,128)(2,1)S(1)}, bf16[3,512,128]{2,1,0:T(8,128)(2,1)S(1)}, u32[]{:S(2)}, u32[]{:S(2)}) collective-permute-start(bf16[3,512,128]{2,1,0:T(8,128)(2,1)S(1)} %collective-permute-done.10.refs_3_), channel_id=1, source_target_pairs={{0,4},{4,0},{8,12},{12,8},{16,20},{20,16},{24,28},{28,24},{1,5},{5... | collective-permute-start | bytes 1179656 | tf_op jit(solution)/shard_map/ppermute | solution.py:52
  78.3 22.9 %collective-permute-start.18 = (bf16[512,512]{1,0:T(8,128)(2,1)S(1)}, bf16[512,512]{1,0:T(8,128)(2,1)S(1)}, u32[]{:S(2)}, u32[]{:S(2)}) collective-permute-start(bf16[512,512]{1,0:T(8,128)(2,1)S(1)} %get-tuple-element.58.refs_0_), channel_id=1, source_target_pairs={{0,1},{1,2},{2,3},{4,5},{5,6},{6,7},{8,9},{9,10},{10,11},{12,13},{... | collective-permute-start | bytes 1572872 | tf_op jit(solution)/shard_map/ppermute | solution.py:42
  83.4 17.8 %collective-permute-start.19 = (bf16[512,512]{1,0:T(8,128)(2,1)S(1)}, bf16[512,512]{1,0:T(8,128)(2,1)S(1)}, u32[]{:S(2)}, u32[]{:S(2)}) collective-permute-start(bf16[512,512]{1,0:T(8,128)(2,1)S(1)} %get-tuple-element.58.refs_0_), channel_id=1, source_target_pairs={{1,0},{2,1},{3,2},{5,4},{6,5},{7,6},{9,8},{10,9},{11,10},{13,12},{... | collective-permute-start | bytes 1572872 | tf_op jit(solution)/shard_map/ppermute | solution.py:42
  88.0 20.2 %collective-permute-start.16 = (bf16[512,512]{1,0:T(8,128)(2,1)S(1)}, bf16[512,512]{1,0:T(8,128)(2,1)S(1)}, u32[]{:S(2)}, u32[]{:S(2)}) collective-permute-start(bf16[512,512]{1,0:T(8,128)(2,1)S(1)} %get-tuple-element.55.refs_3_.refs_1_), channel_id=1, source_target_pairs={{0,1},{1,2},{2,3},{4,5},{5,6},{6,7},{8,9},{9,10},{10,11},{12,13},{... | collective-permute-start | bytes 1572872 | tf_op jit(solution)/shard_map/ppermute | solution.py:42
  92.6 18.1 %collective-permute-start.17 = (bf16[512,512]{1,0:T(8,128)(2,1)S(1)}, bf16[512,512]{1,0:T(8,128)(2,1)S(1)}, u32[]{:S(2)}, u32[]{:S(2)}) collective-permute-start(bf16[512,512]{1,0:T(8,128)(2,1)S(1)} %get-tuple-element.55.refs_3_.refs_1_), channel_id=1, source_target_pairs={{1,0},{2,1},{3,2},{5,4},{6,5},{7,6},{9,8},{10,9},{11,10},{13,12},{... | collective-permute-start | bytes 1572872 | tf_op jit(solution)/shard_map/ppermute | solution.py:42
  94.0 21.3 %collective-permute-start.32 = (bf16[1,3,128,1024]{3,2,1,0:T(8,128)(2,1)S(1)}, bf16[1,3,128,1024]{3,2,1,0:T(8,128)(2,1)S(1)}, u32[]{:S(2)}, u32[]{:S(2)}) collective-permute-start(bf16[1,3,128,1024]{3,2,1,0:T(8,128)(2,1)S(1)} %bitcast.32), channel_id=1, source_target_pairs={{0,16},{4,20},{8,24},{12,28},{16,0},{20,4},{24,8},{28,12},{1,17},{... | collective-permute-start | bytes 2359304 | tf_op jit(solution)/shard_map/ppermute | solution.py:52
  101.2 54.0 %copy-start.5 = (bf16[4,512,1024]{2,1,0:T(8,128)(2,1)}, bf16[4,512,1024]{2,1,0:T(8,128)(2,1)S(1)}, u32[]{:S(2)}) copy-start(bf16[4,512,1024]{2,1,0:T(8,128)(2,1)S(1)} %shard_map.91.p_hbm) | copy-start | bytes 12582916
  102.3 17.0 %collective-permute-start.22 = (bf16[512,512]{1,0:T(8,128)(2,1)S(1)}, bf16[512,512]{1,0:T(8,128)(2,1)S(1)}, u32[]{:S(2)}, u32[]{:S(2)}) collective-permute-start(bf16[512,512]{1,0:T(8,128)(2,1)S(1)} %get-tuple-element.63), channel_id=1, source_target_pairs={{0,1},{1,2},{2,3},{4,5},{5,6},{6,7},{8,9},{9,10},{10,11},{12,13},{... | collective-permute-start | bytes 1572872 | tf_op jit(solution)/shard_map/ppermute | solution.py:42
  106.9 16.8 %collective-permute-start.23 = (bf16[512,512]{1,0:T(8,128)(2,1)S(1)}, bf16[512,512]{1,0:T(8,128)(2,1)S(1)}, u32[]{:S(2)}, u32[]{:S(2)}) collective-permute-start(bf16[512,512]{1,0:T(8,128)(2,1)S(1)} %get-tuple-element.60.refs_1_), channel_id=1, source_target_pairs={{1,0},{2,1},{3,2},{5,4},{6,5},{7,6},{9,8},{10,9},{11,10},{13,12},{... | collective-permute-start | bytes 1572872 | tf_op jit(solution)/shard_map/ppermute | solution.py:42
  111.7 18.8 %collective-permute-start.20 = (bf16[512,512]{1,0:T(8,128)(2,1)S(1)}, bf16[512,512]{1,0:T(8,128)(2,1)S(1)}, u32[]{:S(2)}, u32[]{:S(2)}) collective-permute-start(bf16[512,512]{1,0:T(8,128)(2,1)S(1)} %get-tuple-element.61), channel_id=1, source_target_pairs={{0,1},{1,2},{2,3},{4,5},{5,6},{6,7},{8,9},{9,10},{10,11},{12,13},{... | collective-permute-start | bytes 1572872 | tf_op jit(solution)/shard_map/ppermute | solution.py:42
  114.0 20.9 %collective-permute-start.21 = (bf16[512,512]{1,0:T(8,128)(2,1)S(1)}, bf16[512,512]{1,0:T(8,128)(2,1)S(1)}, u32[]{:S(2)}, u32[]{:S(2)}) collective-permute-start(bf16[512,512]{1,0:T(8,128)(2,1)S(1)} %get-tuple-element.62.refs_1_.refs_2_), channel_id=1, source_target_pairs={{1,0},{2,1},{3,2},{5,4},{6,5},{7,6},{9,8},{10,9},{11,10},{13,12},{... | collective-permute-start | bytes 1572872 | tf_op jit(solution)/shard_map/ppermute | solution.py:42
  115.4 40.9 %collective-permute-start.33 = (bf16[2,3,128,1024]{3,2,1,0:T(8,128)(2,1)S(1)}, bf16[2,3,128,1024]{3,2,1,0:T(8,128)(2,1)S(1)}, u32[]{:S(2)}, u32[]{:S(2)}) collective-permute-start(bf16[2,3,128,1024]{3,2,1,0:T(8,128)(2,1)S(1)} %shard_map.98.refs_0_), channel_id=1, source_target_pairs={{0,8},{4,12},{8,0},{12,4},{16,24},{20,28},{24,16},{28,20},{1,9},{5... | collective-permute-start | bytes 4718600 | tf_op jit(solution)/shard_map/ppermute | solution.py:52
  124.7 17.0 %collective-permute-start.26 = (bf16[512,512]{1,0:T(8,128)(2,1)S(1)}, bf16[512,512]{1,0:T(8,128)(2,1)S(1)}, u32[]{:S(2)}, u32[]{:S(2)}) collective-permute-start(bf16[512,512]{1,0:T(8,128)(2,1)S(1)} %get-tuple-element.69), channel_id=1, source_target_pairs={{0,1},{1,2},{2,3},{4,5},{5,6},{6,7},{8,9},{9,10},{10,11},{12,13},{... | collective-permute-start | bytes 1572872 | tf_op jit(solution)/shard_map/ppermute | solution.py:42
  126.6 19.5 %collective-permute-start.27 = (bf16[512,512]{1,0:T(8,128)(2,1)S(1)}, bf16[512,512]{1,0:T(8,128)(2,1)S(1)}, u32[]{:S(2)}, u32[]{:S(2)}) collective-permute-start(bf16[512,512]{1,0:T(8,128)(2,1)S(1)} %get-tuple-element.66.refs_1_), channel_id=1, source_target_pairs={{1,0},{2,1},{3,2},{5,4},{6,5},{7,6},{9,8},{10,9},{11,10},{13,12},{... | collective-permute-start | bytes 1572872 | tf_op jit(solution)/shard_map/ppermute | solution.py:42
  135.9 15.2 %collective-permute-start.24 = (bf16[512,512]{1,0:T(8,128)(2,1)S(1)}, bf16[512,512]{1,0:T(8,128)(2,1)S(1)}, u32[]{:S(2)}, u32[]{:S(2)}) collective-permute-start(bf16[512,512]{1,0:T(8,128)(2,1)S(1)} %get-tuple-element.67), channel_id=1, source_target_pairs={{0,1},{1,2},{2,3},{4,5},{5,6},{6,7},{8,9},{9,10},{10,11},{12,13},{... | collective-permute-start | bytes 1572872 | tf_op jit(solution)/shard_map/ppermute | solution.py:42
  137.8 17.4 %collective-permute-start.25 = (bf16[512,512]{1,0:T(8,128)(2,1)S(1)}, bf16[512,512]{1,0:T(8,128)(2,1)S(1)}, u32[]{:S(2)}, u32[]{:S(2)}) collective-permute-start(bf16[512,512]{1,0:T(8,128)(2,1)S(1)} %get-tuple-element.68.refs_1_), channel_id=1, source_target_pairs={{1,0},{2,1},{3,2},{5,4},{6,5},{7,6},{9,8},{10,9},{11,10},{13,12},{... | collective-permute-start | bytes 1572872 | tf_op jit(solution)/shard_map/ppermute | solution.py:42
  156.5 11.2 %copy-start.4 = (bf16[4,3,128,1024]{3,2,1,0:T(8,128)(2,1)}, bf16[4,3,128,1024]{3,2,1,0:T(8,128)(2,1)S(1)}, u32[]{:S(2)}) copy-start(bf16[4,3,128,1024]{3,2,1,0:T(8,128)(2,1)S(1)} %shard_map.99.refs_4_) | copy-start | bytes 9437188
  156.5 9.4 %collective-permute-start.34 = (bf16[4,3,128,1024]{3,2,1,0:T(8,128)(2,1)S(1)}, bf16[4,3,128,1024]{3,2,1,0:T(8,128)(2,1)S(1)}, u32[]{:S(2)}, u32[]{:S(2)}) collective-permute-start(bf16[4,3,128,1024]{3,2,1,0:T(8,128)(2,1)S(1)} %shard_map.99.refs_4_), channel_id=1, source_target_pairs={{0,4},{4,0},{8,12},{12,8},{16,20},{20,16},{24,28},{28,24},{1,5},{5... | collective-permute-start | bytes 9437192 | tf_op jit(solution)/shard_map/ppermute | solution.py:52
  156.6 19.8 %collective-permute-start.30 = (bf16[512,512]{1,0:T(8,128)(2,1)S(1)}, bf16[512,512]{1,0:T(8,128)(2,1)S(1)}, u32[]{:S(2)}, u32[]{:S(2)}) collective-permute-start(bf16[512,512]{1,0:T(8,128)(2,1)S(1)} %get-tuple-element.75), channel_id=1, source_target_pairs={{0,1},{1,2},{2,3},{4,5},{5,6},{6,7},{8,9},{9,10},{10,11},{12,13},{... | collective-permute-start | bytes 1572872 | tf_op jit(solution)/shard_map/ppermute | solution.py:42
  158.7 17.7 %collective-permute-start.31 = (bf16[512,512]{1,0:T(8,128)(2,1)S(1)}, bf16[512,512]{1,0:T(8,128)(2,1)S(1)}, u32[]{:S(2)}, u32[]{:S(2)}) collective-permute-start(bf16[512,512]{1,0:T(8,128)(2,1)S(1)} %get-tuple-element.72.refs_1_), channel_id=1, source_target_pairs={{1,0},{2,1},{3,2},{5,4},{6,5},{7,6},{9,8},{10,9},{11,10},{13,12},{... | collective-permute-start | bytes 1572872 | tf_op jit(solution)/shard_map/ppermute | solution.py:42
  160.0 21.7 %collective-permute-start.28 = (bf16[512,512]{1,0:T(8,128)(2,1)S(1)}, bf16[512,512]{1,0:T(8,128)(2,1)S(1)}, u32[]{:S(2)}, u32[]{:S(2)}) collective-permute-start(bf16[512,512]{1,0:T(8,128)(2,1)S(1)} %get-tuple-element.73), channel_id=1, source_target_pairs={{0,1},{1,2},{2,3},{4,5},{5,6},{6,7},{8,9},{9,10},{10,11},{12,13},{... | collective-permute-start | bytes 1572872 | tf_op jit(solution)/shard_map/ppermute | solution.py:42
  164.6 21.3 %collective-permute-start.29 = (bf16[512,512]{1,0:T(8,128)(2,1)S(1)}, bf16[512,512]{1,0:T(8,128)(2,1)S(1)}, u32[]{:S(2)}, u32[]{:S(2)}) collective-permute-start(bf16[512,512]{1,0:T(8,128)(2,1)S(1)} %get-tuple-element.74.refs_2_.refs_6_), channel_id=1, source_target_pairs={{1,0},{2,1},{3,2},{5,4},{6,5},{7,6},{9,8},{10,9},{11,10},{13,12},{... | collective-permute-start | bytes 1572872 | tf_op jit(solution)/shard_map/ppermute | solution.py:42
  165.9 1.8 copy-start.10
  167.7 8.8 %copy-start.6 = (bf16[4,512,1024]{2,1,0:T(8,128)(2,1)S(1)}, bf16[4,512,1024]{2,1,0:T(8,128)(2,1)}, u32[]{:S(2)}) copy-start(bf16[4,512,1024]{2,1,0:T(8,128)(2,1)} %copy-done.5) | copy-start | bytes 12582916
